TPU v7x, 32 devices: a whole 2x2x4 slice. The times are simulated.
32 devices in a mesh: expert: 8 (over y, x, core), tensor: 4 (over z).
Axes of the slice: x: 2, y: 2, z: 4, core: 2. Of those that a mesh axis runs over, the one named last changes fastest.
Arguments:
- hidden_in: bfloat16 [8192, 2048], P(('expert', 'tensor')), may hold values from -6 to 6
- attn_gain: bfloat16 [2048], replicated, may hold values from 0.099609375 to 1.8984375
- query_gain: bfloat16 [128], replicated, may hold values from 0.099609375 to 1.8984375
- key_gain: bfloat16 [128], replicated, may hold values from 0.099609375 to 1.8984375
- w_qkv: bfloat16 [2048, 5120], P(None, 'tensor'), may hold values from -0.125 to 0.125
- w_out: bfloat16 [4096, 2048], P('tensor'), may hold values from -2 to 2
- moe_gain: bfloat16 [2048], replicated, may hold values from 0.099609375 to 1.8984375
- w_router: bfloat16 [2048, 32], replicated, may hold values from -0.0625 to 0.0625
- w_gate: bfloat16 [32, 2048, 768], P('expert', None, 'tensor'), may hold values from -0.125 to 0.125
- w_up: bfloat16 [32, 2048, 768], P('expert', None, 'tensor'), may hold values from -0.125 to 0.125
- w_down: bfloat16 [32, 768, 2048], P('expert', 'tensor'), may hold values from -0.875 to 0.875
- routes: int32 [8192, 8], P('expert'), may hold values from 0 to 31, as said below
- pair_rank: int32 [8, 8192], P('expert'), may hold values from 0 to 8191, as said below
- out_grad: bfloat16 [8192, 2048], P(('expert', 'tensor')), may hold values from -6 to 6
Outputs:
- layer_out: bfloat16 [8192, 2048], P(('expert', 'tensor'))
- grad_in: float32 [8192, 2048], P(('expert', 'tensor'))
- grad_attn_gain: float32 [2048], replicated
- grad_query_gain: float32 [128], replicated
- grad_key_gain: float32 [128], replicated
- grad_qkv: float32 [2048, 5120], P('expert', 'tensor')
- grad_out: float32 [4096, 2048], P('tensor', 'expert')
- grad_moe_gain: float32 [2048], replicated
- grad_router: float32 [2048, 32], replicated
- grad_gate: float32 [32, 2048, 768], P('expert', None, 'tensor')
- grad_up: float32 [32, 2048, 768], P('expert', None, 'tensor')
- grad_down: float32 [32, 768, 2048], P('expert', 'tensor')
Inputs may be any that keep to these rules, and one draw needn't show every extreme that they name: `routes`: each row names 8 different experts, and every expert is named by some row. `pair_rank`: each row is a permutation; entry i * 8 + k is the priority of route k of the row's token i.
All inputs are finite; a program needn't handle non-finite values.
Results may differ from a plain program's by a relative error of at most 0.029.
Values may be sent and summed in bfloat16 or wider, within the bound.
No kernel may reach another device: no remote copies, remote signals or barrier semaphores. Data moves between devices by JAX's collectives and lax.ppermute only.
A program may use at most 512 MiB of HBM per device.

v0:
```python
import jax
import jax.numpy as jnp
from jax import lax
from jax.sharding import PartitionSpec as P

HD = 128
TOPK = 8
SEQ = 1024
ATT_BLOCK = 256
QBLOCK = 512


norm_eps = 1e-06
rope_base = 1000000.0


def row_norm(values, gain):
    return values * lax.rsqrt(jnp.mean(values * values, axis=-1, keepdims=True) + norm_eps) * gain


def rotate(values, positions):
    middle_at = values.shape[-1] // 2
    fraction = jnp.arange(middle_at).astype(jnp.float32) * (2.0 / values.shape[-1])
    freqs = jnp.power(rope_base, -fraction)
    angles = positions[:, None] * freqs[None, :]
    cosine = jnp.concatenate([jnp.cos(angles), jnp.cos(angles)], axis=-1)[:, None, :]
    sine = jnp.concatenate([jnp.sin(angles), jnp.sin(angles)], axis=-1)[:, None, :]
    turned = jnp.concatenate([-values[..., middle_at:], values[..., :middle_at]], axis=-1)
    return values * cosine + turned * sine


def pair_slots(route_rows, rank_row, n_experts, capacity):
    pairs = route_rows.shape[0] * route_rows.shape[1]
    experts_flat = route_rows.reshape(pairs)
    order = jnp.zeros((pairs,), jnp.int32).at[rank_row].set(jnp.arange(pairs, dtype=jnp.int32))
    ranked = experts_flat[order]
    onehot = (ranked[:, None] == jnp.arange(n_experts, dtype=jnp.int32)[None, :]).astype(jnp.int32)
    filled = jnp.sum(jnp.cumsum(onehot, axis=0) * onehot, axis=1) - 1
    slots = jnp.zeros((pairs,), jnp.int32).at[order].set(filled)
    return (experts_flat, slots, slots < capacity)


def local(
    hidden_in,
    attn_gain,
    query_gain,
    key_gain,
    w_qkv,
    w_out,
    moe_gain,
    w_router,
    w_gate,
    w_up,
    w_down,
    routes,
    pair_rank,
    out_grad,
):
    tok_dev, width = hidden_in.shape
    n_tensor = lax.axis_size("tensor")
    n_expert = lax.axis_size("expert")
    member = lax.axis_index("tensor")
    group = tok_dev * n_tensor
    local_experts = w_gate.shape[0]
    n_experts = local_experts * n_expert
    capacity = 9 * group * TOPK // (8 * n_experts)
    local_q = w_out.shape[0] // HD
    local_kv = (w_qkv.shape[1] // HD - local_q) // 2
    repeat = local_q // local_kv
    scale = HD ** (-0.5)
    bf16 = jnp.bfloat16
    f32 = jnp.float32
    hidden_f = hidden_in.astype(f32)
    attn_normed, attn_pull = jax.vjp(row_norm, hidden_f, attn_gain.astype(f32))
    gathered = lax.all_gather(attn_normed.astype(bf16), "tensor", axis=0, tiled=True)
    projected = jnp.dot(gathered, w_qkv, preferred_element_type=f32)
    raw_query = projected[:, : local_q * HD].reshape(group, local_q, HD)
    raw_key = projected[:, local_q * HD : (local_q + local_kv) * HD].reshape(group, local_kv, HD)
    values_bf = projected[:, (local_q + local_kv) * HD :].reshape(group, local_kv, HD).astype(bf16)
    positions = (jnp.arange(group) % SEQ).astype(f32)

    def shape_heads(query_in, key_in, gain_query, gain_key):
        return (
            rotate(row_norm(query_in, gain_query), positions),
            rotate(row_norm(key_in, gain_key), positions),
        )

    rotated, heads_pull = jax.vjp(
        shape_heads, raw_query, raw_key, query_gain.astype(f32), key_gain.astype(f32)
    )
    queries = rotated[0].astype(bf16).reshape(group, local_kv, repeat, HD)
    keys_bf = rotated[1].astype(bf16)
    n_blocks = group // QBLOCK
    key_block = jnp.arange(SEQ) // ATT_BLOCK

    def block_scores(index):
        start = index * QBLOCK
        seq_start = start // SEQ * SEQ
        query_blk = lax.dynamic_slice_in_dim(queries, start, QBLOCK, 0)
        scores = (
            jnp.einsum("qkrd,skd->qkrs", query_blk, keys_bf, preferred_element_type=f32) * scale
        )
        row_block = (start - seq_start + jnp.arange(QBLOCK)) // ATT_BLOCK
        allowed = key_block[None, :] <= row_block[:, None]
        scores = jnp.where(allowed[:, None, None, :], scores, -jnp.inf)
        return (start, seq_start, query_blk, keys_bf, values_bf, scores)

    def attend_block(index):
        start, seq_start, query_blk, key_blk, value_blk, scores = block_scores(index)
        top_score = jnp.max(scores, axis=-1, keepdims=True)
        log_total = top_score + jnp.log(
            jnp.sum(jnp.exp(scores - top_score), axis=-1, keepdims=True)
        )
        probs = jnp.exp(scores - log_total).astype(bf16)
        mixed = jnp.einsum("qkrs,skd->qkrd", probs, value_blk, preferred_element_type=f32)
        return (mixed.astype(bf16).reshape(QBLOCK, local_q * HD), log_total)

    mixed_blocks, log_totals = lax.map(attend_block, jnp.arange(n_blocks))
    mixed_all = mixed_blocks.reshape(group, local_q * HD)
    attn = lax.psum_scatter(
        jnp.dot(mixed_all, w_out, preferred_element_type=f32).astype(jnp.bfloat16),
        "tensor",
        scatter_dimension=0,
        tiled=True,
    ).astype(jnp.float32)
    middle = hidden_f + attn
    moe_normed, moe_pull = jax.vjp(row_norm, middle, moe_gain.astype(f32))
    moe_in = moe_normed.astype(bf16)
    logits = jnp.dot(moe_in, w_router, preferred_element_type=f32)
    own_routes = lax.dynamic_slice_in_dim(routes, member * tok_dev, tok_dev, 0)
    picks = (
        own_routes[:, :, None] == jnp.arange(n_experts, dtype=jnp.int32)[None, None, :]
    ).astype(f32)
    chosen = jnp.sum(picks * logits[:, None, :], axis=-1)
    gates = jax.nn.softmax(chosen, axis=-1)
    all_moe_in, all_gates, all_grad = (
        lax.all_gather(moe_in, "tensor", axis=0, tiled=True),
        lax.all_gather(gates.astype(bf16), "tensor", axis=0, tiled=True),
        lax.all_gather(out_grad, "tensor", axis=0, tiled=True),
    )
    experts_flat, slots, keep = pair_slots(routes, pair_rank[0], n_experts, capacity)
    pairs = group * TOPK
    total = n_experts * capacity
    target = jnp.where(keep, experts_flat * capacity + slots, total)
    owners = jnp.arange(pairs, dtype=jnp.int32) // TOPK
    source = jnp.full((total,), group, jnp.int32).at[target].set(owners, mode="drop")
    slot_gate = (
        jnp.zeros((total,), f32).at[target].set(all_gates.reshape(pairs).astype(f32), mode="drop")
    )
    source = source.reshape(n_expert, local_experts, capacity).transpose(1, 0, 2)
    slot_gate = slot_gate.reshape(n_expert, local_experts, capacity).transpose(1, 0, 2)
    pad_rows = jnp.zeros((1, width), bf16)
    sent_rows = jnp.concatenate([all_moe_in, pad_rows], axis=0)[source]
    sent_grad = (
        jnp.concatenate([all_grad, pad_rows], axis=0)[source].astype(f32) * slot_gate[..., None]
    ).astype(bf16)
    got_rows, got_grad = (
        lax.all_to_all(sent_rows, "expert", split_axis=1, concat_axis=1, tiled=True),
        lax.all_to_all(sent_grad, "expert", split_axis=1, concat_axis=1, tiled=True),
    )
    rows_in = got_rows.reshape(local_experts, -1, width)
    rows_grad = got_grad.reshape(local_experts, -1, width)
    gate_pre = jnp.einsum("erd,edf->erf", rows_in, w_gate, preferred_element_type=f32)
    up_pre = jnp.einsum("erd,edf->erf", rows_in, w_up, preferred_element_type=f32)
    sigma = jax.nn.sigmoid(gate_pre)
    active = gate_pre * sigma
    hidden_bf = (active * up_pre).astype(bf16)
    expert_out = jnp.einsum("erf,efd->erd", hidden_bf, w_down, preferred_element_type=f32).astype(
        bf16
    )
    hidden_grad = jnp.einsum("erd,efd->erf", rows_grad, w_down, preferred_element_type=f32)
    gate_back = (hidden_grad * up_pre * sigma * (1.0 + gate_pre * (1.0 - sigma))).astype(bf16)
    up_back = (hidden_grad * active).astype(bf16)
    rows_back = (
        jnp.einsum("erf,edf->erd", gate_back, w_gate, preferred_element_type=f32)
        + jnp.einsum("erf,edf->erd", up_back, w_up, preferred_element_type=f32)
    ).astype(bf16)
    grad_down = jnp.einsum("erf,erd->efd", hidden_bf, rows_grad, preferred_element_type=f32)
    grad_gate = jnp.einsum("erd,erf->edf", rows_in, gate_back, preferred_element_type=f32)
    grad_up = jnp.einsum("erd,erf->edf", rows_in, up_back, preferred_element_type=f32)
    back_out, back_grad = (
        lax.all_to_all(
            expert_out.reshape(got_rows.shape), "expert", split_axis=1, concat_axis=1, tiled=True
        ),
        lax.all_to_all(
            rows_back.reshape(got_rows.shape), "expert", split_axis=1, concat_axis=1, tiled=True
        ),
    )
    placed = jnp.where(
        keep,
        experts_flat % local_experts * (n_expert * capacity)
        + experts_flat // local_experts * capacity
        + slots,
        total,
    ).reshape(group, TOPK)
    out_table = jnp.concatenate([back_out.reshape(total, width), pad_rows], axis=0)
    grad_table = jnp.concatenate([back_grad.reshape(total, width), pad_rows], axis=0)
    moe_part = jnp.zeros((group, width), f32)
    back_part = jnp.zeros((group, width), f32)
    score_terms = []
    for route_slot in range(TOPK):
        picked = out_table[placed[:, route_slot]].astype(f32)
        moe_part = moe_part + all_gates[:, route_slot : route_slot + 1].astype(f32) * picked
        back_part = back_part + grad_table[placed[:, route_slot]].astype(f32)
        score_terms.append(jnp.sum(all_grad.astype(f32) * picked, axis=1))
    score_part = jnp.stack(score_terms, axis=1)
    moe_out, moe_back, gate_score = (
        lax.psum_scatter(
            moe_part.astype(jnp.bfloat16), "tensor", scatter_dimension=0, tiled=True
        ).astype(jnp.float32),
        lax.psum_scatter(
            back_part.astype(jnp.bfloat16), "tensor", scatter_dimension=0, tiled=True
        ).astype(jnp.float32),
        lax.psum_scatter(
            score_part.astype(jnp.bfloat16), "tensor", scatter_dimension=0, tiled=True
        ).astype(jnp.float32),
    )
    layer_out = (middle + moe_out).astype(bf16)
    inner_gate = jnp.sum(gates * gate_score, axis=-1, keepdims=True)
    chosen_grad = gates * (gate_score - inner_gate)
    logit_grad = jnp.sum(picks * chosen_grad[:, :, None], axis=1).astype(bf16)
    router_grad = jnp.einsum("td,te->de", moe_in, logit_grad, preferred_element_type=f32)
    moe_in_grad = moe_back + jnp.einsum(
        "te,de->td", logit_grad, w_router, preferred_element_type=f32
    )
    middle_part, moe_gain_grad = moe_pull(moe_in_grad)
    middle_grad = out_grad.astype(f32) + middle_part
    piece = lax.all_gather(middle_grad.astype(bf16), "tensor", axis=0, tiled=True)
    part = jnp.einsum("rd,hd->rh", piece, w_out, preferred_element_type=f32)
    mixed_grad = part
    mixed_grad, out_weight_grad = (
        mixed_grad,
        jnp.einsum("rh,rd->hd", mixed_all, piece, preferred_element_type=f32),
    )
    mixed_grad_bf = mixed_grad.astype(bf16).reshape(group, local_kv, repeat, HD)

    def attend_back(carry, index):
        key_acc, value_acc = carry
        start, seq_start, query_blk, key_blk, value_blk, scores = block_scores(index)
        probs = jnp.exp(scores - log_totals[index])
        grad_blk = lax.dynamic_slice_in_dim(mixed_grad_bf, start, QBLOCK, 0)
        prob_grad = jnp.einsum("qkrd,skd->qkrs", grad_blk, value_blk, preferred_element_type=f32)
        inner_prob = jnp.sum(probs * prob_grad, axis=-1, keepdims=True)
        score_grad = (probs * (prob_grad - inner_prob)).astype(bf16)
        query_part = (
            jnp.einsum("qkrs,skd->qkrd", score_grad, key_blk, preferred_element_type=f32) * scale
        )
        key_part = (
            jnp.einsum("qkrs,qkrd->skd", score_grad, query_blk, preferred_element_type=f32) * scale
        )
        value_part = jnp.einsum(
            "qkrs,qkrd->skd", probs.astype(bf16), grad_blk, preferred_element_type=f32
        )
        key_acc = key_acc + key_part
        value_acc = value_acc + value_part
        return ((key_acc, value_acc), query_part.reshape(QBLOCK, local_q, HD))

    kv_start = (jnp.zeros((group, local_kv, HD), f32), jnp.zeros((group, local_kv, HD), f32))
    kv_grads, query_blocks = lax.scan(attend_back, kv_start, jnp.arange(n_blocks))
    query_grad = query_blocks.reshape(group, local_q, HD)
    raw_q_grad, raw_k_grad, query_gain_grad, key_gain_grad = heads_pull((query_grad, kv_grads[0]))
    qkv_grad = jnp.concatenate(
        [
            raw_q_grad.reshape(group, -1),
            raw_k_grad.reshape(group, -1),
            kv_grads[1].reshape(group, -1),
        ],
        axis=1,
    ).astype(bf16)
    qkv_weight_grad = jnp.einsum("gd,gc->dc", gathered, qkv_grad, preferred_element_type=f32)
    normed_grad = lax.psum_scatter(
        jnp.einsum("rc,dc->rd", qkv_grad, w_qkv, preferred_element_type=f32).astype(jnp.bfloat16),
        "tensor",
        scatter_dimension=0,
        tiled=True,
    ).astype(jnp.float32)
    hidden_part, attn_gain_grad = attn_pull(normed_grad)
    input_grad = middle_grad + hidden_part
    grad_qkv, grad_out = (
        lax.psum_scatter(
            qkv_weight_grad.astype(jnp.bfloat16), "expert", scatter_dimension=0, tiled=True
        ).astype(jnp.float32),
        lax.psum_scatter(
            out_weight_grad.astype(jnp.bfloat16), "expert", scatter_dimension=1, tiled=True
        ).astype(jnp.float32),
    )
    summed = lax.psum(
        (attn_gain_grad, query_gain_grad, key_gain_grad, moe_gain_grad, router_grad),
        ("expert", "tensor"),
    )
    return (
        layer_out,
        input_grad,
        summed[0],
        summed[1],
        summed[2],
        grad_qkv,
        grad_out,
        summed[3],
        summed[4],
        grad_gate,
        grad_up,
        grad_down,
    )


def solution(mesh):
    in_specs = (
        P(("expert", "tensor"), None),
        P(),
        P(),
        P(),
        P(None, "tensor"),
        P("tensor", None),
        P(),
        P(),
        P("expert", None, "tensor"),
        P("expert", None, "tensor"),
        P("expert", "tensor", None),
        P("expert", None),
        P("expert", None),
        P(("expert", "tensor"), None),
    )
    out_specs = (
        P(("expert", "tensor"), None),
        P(("expert", "tensor"), None),
        P(),
        P(),
        P(),
        P("expert", "tensor"),
        P("tensor", "expert"),
        P(),
        P(),
        P("expert", None, "tensor"),
        P("expert", None, "tensor"),
        P("expert", "tensor", None),
    )
    return jax.shard_map(local, mesh=mesh, in_specs=in_specs, out_specs=out_specs, check_vma=False)
```

profile of v0, /device:TPU:0, one launch (start us, length us, event | category | flops | bytes accessed | tf_op | source)
XLA Modules:
  0.0 3488.6 jit_solution(3265933404754009145)
XLA Ops:
  17.3 79.6 %all-gather.5.cloned.1.call-done = bf16[1024,2048]{1,0:T(8,128)(2,1)} async-done(((bf16[256,2048]{1,0:T(8,128)(2,1)}), bf16[1024,2048]{1,0:T(8,128)(2,1)}) %all-gather.5.cloned.1.call-update) | async-done | bytes 4194320 | tf_op jit(solution)/shard_map/all_gather | solution.py:75
  134.9 41.0 %while.34 = (s32[]{:T(128)}, bf16[2,512,1024]{2,1,0:T(8,128)(2,1)}, f32[2,512,1,8,1]{1,3,4,2,0:T(8,128)S(1)}, s32[2]{0:T(128)S(1)}, bf16[1024,1,8,128]{3,0,2,1:T...) while((s32[]{:T(128)}, bf16[2,512,1024]{2,1,0:T(8,128)(2,1)}, ...), condition=%wide.region_6.7_spmd.clone, body=%wide.region_3.6_spmd.clone.sunk | while | flops 2194681856 | bytes 60436888 | solution.py:118
  188.4 30.5 scatter_custom_fusion
  218.9 45.9 %gather_fusion = s32[8192]{0:T(1024)S(1)} fusion(s32[8192]{0:T(1024)S(1)} %reshape.601, s32[8192]{0:T(1024)S(1)} %get-tuple-element.578), kind=kCustom, calls=%fused_computation | custom fusion | bytes 98304 | tf_op jit(solution)/shard_map/gather | solution.py:36
  265.9 18.8 reduce-window.6
  289.4 30.5 scatter_custom_fusion.1
  320.6 30.5 scatter_custom_fusion.2
  356.2 71.6 %gather_fusion.10 = bf16[9216,2048]{1,0:T(8,128)(2,1)} fusion(bf16[1025,2048]{1,0:T(8,128)(2,1)} %concatenate.56, s32[9216]{0:T(1024)S(1)} %broadcast_clamp_fusion), kind=kCustom, calls=%fused_computation.10 | custom fusion | bytes 75534336 | tf_op jit(solution)/shard_map/gather | solution.py:155
  435.6 13.1 all_gather.16
  451.0 30.5 scatter_custom_fusion.3
  481.5 25.6 fusion.66
  515.1 81.9 %all-gather.7.cloned.1.call-done = bf16[1024,2048]{1,0:T(8,128)(2,1)} async-done(((bf16[256,2048]{1,0:T(8,128)(2,1)}), bf16[1024,2048]{1,0:T(8,128)(2,1)}) %all-gather.7.cloned.1.call-update) | async-done | bytes 4194320 | tf_op jit(solution)/shard_map/all_gather | solution.py:137
  601.8 71.8 %gather_fusion.1 = bf16[9216,2048]{1,0:T(8,128)(2,1)} fusion(bf16[1025,2048]{1,0:T(8,128)(2,1)} %concatenate.54, s32[9216]{0:T(1024)S(1)} %broadcast_clamp_fusion), kind=kCustom, calls=%fused_computation.1 | custom fusion | bytes 75534336 | tf_op jit(solution)/shard_map/gather | solution.py:153
  673.6 25.4 copy.161
  699.0 224.2 %all-to-all-done.2 = bf16[4,8,288,2048]{3,2,0,1:T(8,128)(2,1)} async-done(((bf16[4,8,288,2048]{3,2,0,1:T(8,128)(2,1)}), bf16[4,8,288,2048]{3,2,0,1:T(8,128)(2,1)}, u32[]{:S(2)}, u32[]{:S(2)}) %all-to-all-start.2) | async-done | bytes 37748768 | tf_op jit(solution)/shard_map/all_to_all | solution.py:159
  930.7 25.4 copy.167
  956.1 383.3 %all-to-all-done = bf16[4,8,288,2048]{3,2,0,1:T(8,128)(2,1)} async-done(((bf16[4,8,288,2048]{3,2,0,1:T(8,128)(2,1)}), bf16[4,8,288,2048]{3,2,0,1:T(8,128)(2,1)}, u32[]{:S(2)}, u32[]{:S(2)}) %all-to-all-start) | async-done | bytes 37748768 | tf_op jit(solution)/shard_map/all_to_all | solution.py:158
  1339.4 25.4 copy.162
  1364.8 21.3 fusion.167
  1386.0 21.2 fusion.166
  1407.3 24.1 multiply_convert_fusion
  1431.4 17.8 convolution_convert_fusion
  1449.2 25.4 copy.163
  1482.3 28.2 fusion.168
  1510.6 39.6 %add_convert_fusion = bf16[4,2304,2048]{2,1,0:T(8,128)(2,1)} fusion(f32[4,2304,2048]{2,1,0:T(8,128)} %fusion.168, bf16[4,2304,192]{1,2,0:T(8,128)(2,1)} %get-tuple-element.560, bf16[4,2048,192]{1,2,0:T(8,128)(2,1)} %param.27), kind=kOutput, calls=%fused_computation.117 | convolution fusion | flops 7285506048 | bytes 119930880 | tf_op jit(solution)/shard_map/erf,edf->erd/dot_general | solution.py:176
  1550.2 25.4 copy.168
  1575.6 315.4 %all-to-all-done.1 = bf16[4,8,288,2048]{3,2,0,1:T(8,128)(2,1)} async-done(((bf16[4,8,288,2048]{3,2,0,1:T(8,128)(2,1)}), bf16[4,8,288,2048]{3,2,0,1:T(8,128)(2,1)}, u32[]{:S(2)}, u32[]{:S(2)}) %all-to-all-start.1) | async-done | bytes 37748768 | tf_op jit(solution)/shard_map/all_to_all | solution.py:182
  1902.8 25.8 copy.164
  1928.6 25.6 concatenate.55
  1954.2 26.2 gather_fusion.9
  1980.4 26.6 gather_fusion.8
  2007.0 300.1 %all-to-all-done.3 = bf16[4,8,288,2048]{3,2,0,1:T(8,128)(2,1)} async-done(((bf16[4,8,288,2048]{3,2,0,1:T(8,128)(2,1)}), bf16[4,8,288,2048]{3,2,0,1:T(8,128)(2,1)}, u32[]{:S(2)}, u32[]{:S(2)}) %all-to-all-start.3) | async-done | bytes 37748768 | tf_op jit(solution)/shard_map/all_to_all | solution.py:185
  2307.1 25.3 copy.169
  2332.4 25.5 concatenate.57
  2357.9 26.1 gather_fusion.18
  2384.0 26.7 gather_fusion.17
  2410.8 26.3 gather_fusion.7
  2437.1 26.6 gather_fusion.16
  2463.6 27.7 gather_fusion.6
  2491.3 27.7 gather_fusion.15
  2519.0 28.4 gather_fusion.5
  2547.4 28.4 gather_fusion.14
  2575.7 29.1 gather_fusion.4
  2604.8 29.0 gather_fusion.13
  2633.8 29.5 gather_fusion.3
  2663.3 29.6 gather_fusion.12
  2692.8 31.9 gather_fusion.2
  2724.7 32.0 gather_fusion.11
  2756.8 21.3 fusion.82
  2779.0 16.2 add_convert_fusion.1
  2797.7 76.0 %reduce-scatter.12.cloned.1.call-done = bf16[256,2048]{1,0:T(8,128)(2,1)} async-done(((bf16[1024,2048]{1,0:T(8,128)(2,1)}), bf16[256,2048]{1,0:T(8,128)(2,1)}) %reduce-scatter.12.cloned.1.call-update) | async-done | bytes 1048592 | tf_op jit(solution)/shard_map/reduce_scatter | solution.py:211
  2880.3 80.9 %all-gather.11.cloned.1.call-done = bf16[1024,2048]{1,0:T(8,128)(2,1)} async-done(((bf16[256,2048]{1,0:T(8,128)(2,1)}), bf16[1024,2048]{1,0:T(8,128)(2,1)}) %all-gather.11.cloned.1.call-update) | async-done | bytes 4194320 | tf_op jit(solution)/shard_map/all_gather | solution.py:228
  2980.2 108.3 %while.35 = (s32[]{:T(128)}, f32[1024,1,128]{0,2,1:T(8,128)}, f32[1024,1,128]{0,2,1:T(8,128)}, f32[2,512,8,128]{3,2,1,0:T(8,128)}, s32[2]{0:T(128)S(1)}, /*index...) while((s32[]{:T(128)}, f32[1024,1,128]{0,2,1:T(8,128)}, ...), condition=%wide.region_35.36_spmd.clone, body=%wide.region_33.35_spmd.clone.sunk | while | flops 5408174080 | bytes 241005088 | solution.py:259
  2993.8 12.3 fusion.240
  3006.1 11.9 fusion.241
  3047.6 12.2 fusion.240
  3059.8 11.5 fusion.241
  3144.7 20.7 fusion.169
  3165.5 20.0 fusion.171
  3185.5 20.1 fusion.170
  3211.0 56.8 %reduce-scatter.16.cloned.1.call-done = bf16[256,2048]{1,0:T(8,128)(2,1)} async-done(((bf16[1024,2048]{1,0:T(8,128)(2,1)}), bf16[256,2048]{1,0:T(8,128)(2,1)}) %reduce-scatter.16.cloned.1.call-update) | async-done | bytes 1048592 | tf_op jit(solution)/shard_map/reduce_scatter | solution.py:271
  3270.2 77.3 %reduce-scatter.10.cloned.1.call-done = bf16[256,2048]{1,0:T(8,128)(2,1)} async-done(((bf16[1024,2048]{1,0:T(8,128)(2,1)}), bf16[256,2048]{1,0:T(8,128)(2,1)}) %reduce-scatter.10.cloned.1.call-update) | async-done | bytes 1048592 | tf_op jit(solution)/shard_map/reduce_scatter | solution.py:208
  3353.8 41.1 %all-reduce.8 = (f32[2048]{0:T(1024)}, f32[128]{0:T(128)}, f32[128]{0:T(128)}, f32[2048]{0:T(1024)}) all-reduce(f32[2048]{0:T(1024)S(1)} %get-tuple-element.504, f32[128]{0:T(128)S(1)} %get-tuple-element.494, f32[128]{0:T(128)S(1)} %get-tuple-element.490, ...), channel_id=1, replica_groups=mesh['expert'=8,'tensor'=4] {'expert','tensor'}, use_global_device_ids=true, to_apply=%region_41.42 | all-reduce | flops 4352 | bytes 34816 | tf_op jit(solution)/shard_map/psum | solution.py:287
  3395.0 84.9 %all-reduce.11.cloned.1.call-done = f32[2048,32]{0,1:T(8,128)} async-done(((f32[2048,32]{0,1:T(8,128)}), f32[2048,32]{0,1:T(8,128)}) %all-reduce.11.cloned.1.call-update) | async-done | bytes 262160 | tf_op jit(solution)/shard_map/psum | solution.py:287
  (385 shorter events, 315.8 us)
Async XLA Ops:
  7.2 1400.1 %copy-start = (bf16[4,192,2048]{2,1,0:T(8,128)(2,1)S(1)}, bf16[4,192,2048]{2,1,0:T(8,128)(2,1)}, u32[]{:S(2)}) copy-start(bf16[4,192,2048]{2,1,0:T(8,128)(2,1)} %param.28) | copy-start | bytes 9437188
  7.2 89.7 %all-gather.5.cloned.1.call-start = ((), (), s32[]{:S(2)}) async-start(), calls=%async_computation.11 | async-start | bytes 5242880 | tf_op jit(solution)/shard_map/all_gather | solution.py:75
  13.3 338.0 %all-gather.9.cloned.1.call-start = ((), (), s32[]{:S(2)}) async-start(), calls=%async_computation.15 | async-start | bytes 5242880 | tf_op jit(solution)/shard_map/all_gather | solution.py:139
  14.1 413.7 %reduce-scatter.8.cloned.1.call-start = ((), (), s32[]{:S(2)}) async-start(), calls=%async_computation.12 | async-start | bytes 5242880 | tf_op jit(solution)/shard_map/reduce_scatter | solution.py:120
  14.2 116.0 %copy-start.85 = (f32[128]{0:T(128)}, f32[128]{0:T(128)S(1)}, u32[]{:S(2)}) copy-start(f32[128]{0:T(128)S(1)} %convert_element_type.266) | copy-start | bytes 1540
  14.2 113.6 %copy-start.87 = (f32[128]{0:T(128)}, f32[128]{0:T(128)S(1)}, u32[]{:S(2)}) copy-start(f32[128]{0:T(128)S(1)} %convert_element_type.270) | copy-start | bytes 1540
  109.5 18.3 copy-start.48
  175.9 9.4 copy-start.6
  175.9 9.4 copy-start.38
  186.1 243.7 %copy-start.42 = (f32[2048]{0:T(1024)}, f32[2048]{0:T(1024)S(1)}, u32[]{:S(2)}) copy-start(f32[2048]{0:T(1024)S(1)} %convert_element_type.276) | copy-start | bytes 24580
  351.3 83.1 %copy-start.50 = (s32[256,8]{0,1:T(8,128)}, s32[256,8]{0,1:T(8,128)S(1)}, u32[]{:S(2)}) copy-start(s32[256,8]{0,1:T(8,128)S(1)} %constant_dynamic-slice_fusion) | copy-start | bytes 24580
  434.4 72.6 %copy-start.33 = (f32[256,8]{0,1:T(8,128)}, f32[256,8]{0,1:T(8,128)S(1)}, u32[]{:S(2)}) copy-start(f32[256,8]{0,1:T(8,128)S(1)} %select_reduce_fusion.1) | copy-start | bytes 24580
  448.8 58.3 %copy-start.35 = (bf16[1024,8]{0,1:T(8,128)(2,1)}, bf16[1024,8]{0,1:T(8,128)(2,1)S(1)}, u32[]{:S(2)}) copy-start(bf16[1024,8]{0,1:T(8,128)(2,1)S(1)} %all_gather.16) | copy-start | bytes 49156
  507.1 416.1 %all-to-all-start.2 = ((bf16[4,8,288,2048]{3,2,0,1:T(8,128)(2,1)}), bf16[4,8,288,2048]{3,2,0,1:T(8,128)(2,1)}, u32[]{:S(2)}, u32[]{:S(2)}) async-start(bf16[4,8,288,2048]{3,2,0,1:T(8,128)(2,1)} %fusion.66), calls=%async_computation.4 | async-start | bytes 75497472 | tf_op jit(solution)/shard_map/all_to_all | solution.py:159
  514.6 82.5 %all-gather.7.cloned.1.call-start = ((), (), s32[]{:S(2)}) async-start(), calls=%async_computation.13 | async-start | bytes 5242880 | tf_op jit(solution)/shard_map/all_gather | solution.py:137
  923.2 416.2 %all-to-all-start = ((bf16[4,8,288,2048]{3,2,0,1:T(8,128)(2,1)}), bf16[4,8,288,2048]{3,2,0,1:T(8,128)(2,1)}, u32[]{:S(2)}, u32[]{:S(2)}) async-start(bf16[4,8,288,2048]{3,2,0,1:T(8,128)(2,1)} %copy.161), calls=%async_computation.1 | async-start | bytes 75497472 | tf_op jit(solution)/shard_map/all_to_all | solution.py:158
  1474.6 416.4 %all-to-all-start.1 = ((bf16[4,8,288,2048]{3,2,0,1:T(8,128)(2,1)}), bf16[4,8,288,2048]{3,2,0,1:T(8,128)(2,1)}, u32[]{:S(2)}, u32[]{:S(2)}) async-start(bf16[4,8,288,2048]{3,2,0,1:T(8,128)(2,1)} %copy.163), calls=%async_computation.2 | async-start | bytes 75497472 | tf_op jit(solution)/shard_map/all_to_all | solution.py:182
  1575.6 323.0 %copy-start.47 = (s32[8192]{0:T(1024)S(1)}, s32[8192]{0:T(1024)}, u32[]{:S(2)}) copy-start(s32[8192]{0:T(1024)} %get-tuple-element.576) | copy-start | bytes 98308
  1891.0 416.1 %all-to-all-start.3 = ((bf16[4,8,288,2048]{3,2,0,1:T(8,128)(2,1)}), bf16[4,8,288,2048]{3,2,0,1:T(8,128)(2,1)}, u32[]{:S(2)}, u32[]{:S(2)}) async-start(bf16[4,8,288,2048]{3,2,0,1:T(8,128)(2,1)} %copy.168), calls=%async_computation.5 | async-start | bytes 75497472 | tf_op jit(solution)/shard_map/all_to_all | solution.py:185
  1898.5 897.5 %reduce-scatter.14.cloned.1.call-start = ((), (), s32[]{:S(2)}) async-start(), calls=%async_computation.17 | async-start | bytes 20480 | tf_op jit(solution)/shard_map/reduce_scatter | solution.py:214
  2491.3 27.7 copy-start.58
  2547.4 28.4 copy-start.56
  2604.8 29.0 copy-start.57
  2663.3 29.6 copy-start.55
  2724.7 32.1 copy-start.69
  2724.7 32.1 copy-start.70
  2724.7 32.1 copy-start.71
  2724.7 32.1 copy-start.72
  2724.7 32.1 copy-start.73
  2724.7 32.1 copy-start.74
  2724.7 32.1 copy-start.75
  2724.7 32.1 copy-start.76
  2779.0 94.7 %reduce-scatter.12.cloned.1.call-start = ((), (), s32[]{:S(2)}) async-start(), calls=%async_computation.16 | async-start | bytes 5242880 | tf_op jit(solution)/shard_map/reduce_scatter | solution.py:211
  2795.2 78.4 %copy-start.8 = (bf16[256,2048]{1,0:T(8,128)(2,1)S(1)}, bf16[256,2048]{1,0:T(8,128)(2,1)}, u32[]{:S(2)}) copy-start(bf16[256,2048]{1,0:T(8,128)(2,1)} %param.18) | copy-start | bytes 3145732
  2795.2 78.4 %copy-start.12 = (bf16[256,2048]{1,0:T(8,128)(2,1)S(1)}, bf16[256,2048]{1,0:T(8,128)(2,1)}, u32[]{:S(2)}) copy-start(bf16[256,2048]{1,0:T(8,128)(2,1)} %reduce-scatter.8.cloned.1.call-done) | copy-start | bytes 3145732
  2795.2 78.4 %copy-start.43 = (f32[2048]{0:T(1024)S(1)}, f32[2048]{0:T(1024)}, u32[]{:S(2)}) copy-start(f32[2048]{0:T(1024)} %copy-done.42) | copy-start | bytes 24580
  2795.2 78.4 %copy-start.46 = (bf16[2048,32]{0,1:T(8,128)(2,1)S(1)}, bf16[2048,32]{0,1:T(8,128)(2,1)}, u32[]{:S(2)}) copy-start(bf16[2048,32]{0,1:T(8,128)(2,1)} %param.25) | copy-start | bytes 393220
  2795.3 78.4 %copy-start.67 = (f32[256]{0:T(256)S(1)}, f32[256]{0:T(256)}, u32[]{:S(2)}) copy-start(f32[256]{0:T(256)} %copy-done.66) | copy-start | bytes 3076
  2795.3 81.3 %copy-start.84 = (f32[256]{0:T(256)S(1)}, f32[256]{0:T(256)}, u32[]{:S(2)}) copy-start(f32[256]{0:T(256)} %copy-done.83) | copy-start | bytes 3076
  2795.3 82.6 %copy-start.21 = (bf16[256,2048]{1,0:T(8,128)(2,1)S(1)}, bf16[256,2048]{1,0:T(8,128)(2,1)}, u32[]{:S(2)}) copy-start(bf16[256,2048]{1,0:T(8,128)(2,1)} %param.31) | copy-start | bytes 3145732
  2795.3 165.9 %all-gather.11.cloned.1.call-start = ((), (), s32[]{:S(2)}) async-start(), calls=%async_computation.18 | async-start | bytes 5242880 | tf_op jit(solution)/shard_map/all_gather | solution.py:228
  2797.7 82.1 %copy-start.52 = (bf16[256,32]{0,1:T(8,128)(2,1)}, bf16[256,32]{0,1:T(8,128)(2,1)S(1)}, u32[]{:S(2)}) copy-start(bf16[256,32]{0,1:T(8,128)(2,1)S(1)} %select_reduce_fusion) | copy-start | bytes 49156
  2876.5 94.2 %copy-start.79 = (f32[256]{0:T(256)}, f32[256]{0:T(256)S(1)}, u32[]{:S(2)}) copy-start(f32[256]{0:T(256)S(1)} %multiply_multiply_fusion.4) | copy-start | bytes 3076
  2879.8 326.9 %reduce-scatter.20.cloned.1.call-start = ((), (), s32[]{:S(2)}) async-start(), calls=%async_computation.21 | async-start | bytes 4718592 | tf_op jit(solution)/shard_map/reduce_scatter | solution.py:283
  2970.7 9.4 copy-start.7
  2970.8 9.4 copy-start.19
  2970.8 9.4 copy-start.39
  2970.8 238.0 %reduce-scatter.18.cloned.1.call-start = ((), (), s32[]{:S(2)}) async-start(), calls=%async_computation.20 | async-start | bytes 5898240 | tf_op jit(solution)/shard_map/reduce_scatter | solution.py:280
  3006.1 16.0 copy-start.2
  3059.8 15.4 copy-start.2
  3133.4 134.5 %reduce-scatter.16.cloned.1.call-start = ((), (), s32[]{:S(2)}) async-start(), calls=%async_computation.19 | async-start | bytes 5242880 | tf_op jit(solution)/shard_map/reduce_scatter | solution.py:271
  3144.7 202.8 %reduce-scatter.10.cloned.1.call-start = ((), (), s32[]{:S(2)}) async-start(), calls=%async_computation.14 | async-start | bytes 5242880 | tf_op jit(solution)/shard_map/reduce_scatter | solution.py:208
  3165.5 314.4 %all-reduce.11.cloned.1.call-start = ((), (), s32[]{:S(2)}) async-start(), calls=%async_computation.22 | async-start | bytes 524288 | tf_op jit(solution)/shard_map/psum | solution.py:287
  3185.5 20.1 copy-start.11
  3185.5 20.1 copy-start.53
  3205.6 62.3 %copy-start.9 = (bf16[256,2048]{1,0:T(8,128)(2,1)S(1)}, bf16[256,2048]{1,0:T(8,128)(2,1)}, u32[]{:S(2)}) copy-start(bf16[256,2048]{1,0:T(8,128)(2,1)} %param.18) | copy-start | bytes 3145732
  3205.6 62.3 %copy-start.41 = (f32[2048]{0:T(1024)S(1)}, f32[2048]{0:T(1024)}, u32[]{:S(2)}) copy-start(f32[2048]{0:T(1024)} %copy-done.40) | copy-start | bytes 24580
  3205.6 62.3 %copy-start.65 = (f32[256]{0:T(256)S(1)}, f32[256]{0:T(256)}, u32[]{:S(2)}) copy-start(f32[256]{0:T(256)} %copy-done.64) | copy-start | bytes 3076
  3205.6 64.5 %copy-start.82 = (f32[256]{0:T(256)S(1)}, f32[256]{0:T(256)}, u32[]{:S(2)}) copy-start(f32[256]{0:T(256)} %copy-done.81) | copy-start | bytes 3076
  3205.6 141.8 %copy-start.44 = (f32[2048]{0:T(1024)S(1)}, f32[2048]{0:T(1024)}, u32[]{:S(2)}) copy-start(f32[2048]{0:T(1024)} %copy-done.42) | copy-start | bytes 24580
  3205.7 141.8 %copy-start.68 = (f32[256]{0:T(256)S(1)}, f32[256]{0:T(256)}, u32[]{:S(2)}) copy-start(f32[256]{0:T(256)} %copy-done.66) | copy-start | bytes 3076
  3205.7 141.8 %copy-start.80 = (f32[256]{0:T(256)S(1)}, f32[256]{0:T(256)}, u32[]{:S(2)}) copy-start(f32[256]{0:T(256)} %copy-done.79) | copy-start | bytes 3076
  3270.2 211.4 %copy-start.1 = (bf16[4,192,2048]{2,1,0:T(8,128)(2,1)S(1)}, bf16[4,192,2048]{2,1,0:T(8,128)(2,1)}, u32[]{:S(2)}) copy-start(bf16[4,192,2048]{2,1,0:T(8,128)(2,1)} %param.28) | copy-start | bytes 9437188
  3270.2 83.6 %copy-start.89 = (f32[2048]{0:T(1024)S(1)}, f32[2048]{0:T(1024)}, u32[]{:S(2)}) copy-start(f32[2048]{0:T(1024)} %get-tuple-element.492) | copy-start | bytes 24580
  (49 other events, 156.5 us)
Sparse Core Ops, SparseCore 0:
  13.4 83.4 all-gather.4
  98.5 79.2 all-gather.8
  185.4 75.4 reduce-scatter.7
  517.3 79.6 all-gather.6
  2779.1 16.8 reduce-scatter.13
  2798.7 74.8 reduce-scatter.11
  2879.9 81.2 all-gather.10
  2970.9 49.8 reduce-scatter.19
  3133.5 55.2 reduce-scatter.17
  3191.1 76.7 reduce-scatter.15
  3270.2 77.2 reduce-scatter.9
  3354.3 125.5 all-reduce.10
where the time goes:
time: 3510 us; the launch traced here: 3490 us
  waiting for transfers between devices  1760 us (50%)
  local copies, waits for them, and re-layouts  1060 us (30%)
  matrix products  357 us (10%)
  other arithmetic  199 us (6%)
  blocking collectives  54.3 us (2%)
    all_to_all x1, waiting for transfers between devices, local(): lax.all_to_all(sent_rows, 'expert', split_axis=1, concat_axis=1, tiled=True)  383 us
    all_to_all x1, waiting for transfers between devices, local(): lax.all_to_all(expert_out.reshape(got_rows.shape), 'expert', split_axis=1...  315 us
    all_to_all x1, waiting for transfers between devices, local(): lax.all_to_all(rows_back.reshape(got_rows.shape), 'expert', split_axis=1,...  300 us
    gather x8, local copies, waits for them, and re-layouts, local(): back_part = back_part + grad_table[placed[:, route_slot]].astype(f32)  226 us
    gather x8, local copies, waits for them, and re-layouts, local(): picked = out_table[placed[:, route_slot]].astype(f32)  226 us
    all_to_all x1, waiting for transfers between devices, local(): lax.all_to_all(sent_grad, 'expert', split_axis=1, concat_axis=1, tiled=True)  224 us
    gather x2, local copies, waits for them, and re-layouts, local(): sent_rows = jnp.concatenate([all_moe_in, pad_rows], axis=0)[source]  97.1 us
    psum x1, waiting for transfers between devices, local(): lax.psum((attn_gain_grad, query_gain_grad, key_gain_grad, moe_gain_grad,...  84.9 us
  transfers between devices with their start and end apart: 16, of which 12 were waited for; matrix products, arithmetic and copies ran while one was open for 26% of the time, Pallas kernels for 0%

commit v1 on v0

v1 whole, which is shorter than its diff:
```python
import functools

import jax
import jax.numpy as jnp
from jax import lax
from jax.experimental import pallas as pl
from jax.experimental.pallas import tpu as pltpu
from jax.sharding import PartitionSpec as P

HD = 128
ATT_BLOCK = 256
norm_eps = 1e-06
rope_base = 1000000.0
bf16 = jnp.bfloat16
f32 = jnp.float32
MIB = 1 << 20


def dot(a, b, contract=((1,), (0,))):
    return lax.dot_general(a, b, (contract, ((), ())), preferred_element_type=f32)


NT = ((1,), (1,))
TN = ((0,), (0,))


def rope_tables(length):
    half = HD // 2
    freqs = jnp.power(rope_base, -(jnp.arange(half).astype(f32) * (2.0 / HD)))
    angles = jnp.arange(length).astype(f32)[:, None] * freqs[None, :]
    cosine, sine = jnp.cos(angles), jnp.sin(angles)
    return jnp.concatenate([cosine, cosine], axis=1), jnp.concatenate([-sine, sine], axis=1)


def project_kernel(local_q, local_kv, x_ref, w_ref, qg_ref, kg_ref, cos_ref, sin_ref, raw_ref, q_ref, k_ref, v_ref):
    raw = dot(x_ref[...], w_ref[...])
    cosine, sine = cos_ref[...], sin_ref[...]
    raw_ref[...] = raw[:, : (local_q + local_kv) * HD]
    for h in range(local_q + local_kv):
        head = raw[:, h * HD : (h + 1) * HD]
        gain = qg_ref[...] if h < local_q else kg_ref[...]
        normed = head * lax.rsqrt(jnp.mean(head * head, axis=1, keepdims=True) + norm_eps) * gain
        turned = (normed * cosine + pltpu.roll(normed, HD // 2, 1) * sine).astype(bf16)
        if h < local_q:
            q_ref[:, h * HD : (h + 1) * HD] = turned
        else:
            k_ref[:, (h - local_q) * HD : (h - local_q + 1) * HD] = turned
    v_ref[...] = raw[:, (local_q + local_kv) * HD :].astype(bf16)


def project(x, w, q_gain, k_gain, cosine, sine, local_q, local_kv):
    rows, width = x.shape
    tile = 256
    cols = w.shape[1]
    full = lambda shape: pl.BlockSpec(shape, lambda i: (0,) * len(shape))
    row = lambda n: pl.BlockSpec((tile, n), lambda i: (i, 0))
    heads = local_q + local_kv
    return pl.pallas_call(
        functools.partial(project_kernel, local_q, local_kv),
        grid=(rows // tile,),
        in_specs=[row(width), full((width, cols)), full((1, HD)), full((1, HD)), row(HD), row(HD)],
        out_specs=[row(heads * HD), row(local_q * HD), row(local_kv * HD), row(local_kv * HD)],
        out_shape=[
            jax.ShapeDtypeStruct((rows, heads * HD), f32),
            jax.ShapeDtypeStruct((rows, local_q * HD), bf16),
            jax.ShapeDtypeStruct((rows, local_kv * HD), bf16),
            jax.ShapeDtypeStruct((rows, local_kv * HD), bf16),
        ],
        compiler_params=pltpu.CompilerParams(vmem_limit_bytes=40 * MIB),
        cost_estimate=pl.CostEstimate(flops=2 * rows * width * cols, bytes_accessed=rows * width * 2 + width * cols * 2 + rows * cols * 6, transcendentals=0),
        name="project",
    )(x, w, q_gain, k_gain, cosine, sine)


def attend_kernel(scale, q_ref, k_ref, vt_ref, o_ref):
    for b in range(q_ref.shape[0] // ATT_BLOCK):
        n = (b + 1) * ATT_BLOCK
        at = slice(b * ATT_BLOCK, n)
        weight = jnp.exp(dot(k_ref[:n, :], q_ref[at, :], NT) * scale)
        total = jnp.sum(weight, axis=0, keepdims=True)
        mixed = dot(vt_ref[:, :n], weight.astype(bf16)) * (1.0 / total)
        o_ref[at, :] = mixed.T.astype(bf16)


def attend(q, k, v_t, local_q, local_kv):
    rows = q.shape[0]
    repeat = local_q // local_kv
    return pl.pallas_call(
        functools.partial(attend_kernel, HD**-0.5),
        grid=(local_q,),
        in_specs=[
            pl.BlockSpec((rows, HD), lambda h: (0, h)),
            pl.BlockSpec((rows, HD), lambda h: (0, h // repeat)),
            pl.BlockSpec((HD, rows), lambda h: (h // repeat, 0)),
        ],
        out_specs=pl.BlockSpec((rows, HD), lambda h: (0, h)),
        out_shape=jax.ShapeDtypeStruct((rows, local_q * HD), bf16),
        compiler_params=pltpu.CompilerParams(vmem_limit_bytes=32 * MIB),
        cost_estimate=pl.CostEstimate(flops=local_q * rows * rows * HD * 3, bytes_accessed=rows * local_q * HD * 4, transcendentals=local_q * rows * rows),
        name="attend",
    )(q, k, v_t)


def unturn(grad, raw, gain, cosine, sine):
    grad = grad * cosine - pltpu.roll(grad, HD // 2, 1) * sine
    inv = lax.rsqrt(jnp.mean(raw * raw, axis=1, keepdims=True) + norm_eps)
    part = gain * grad
    back = inv * part - raw * (inv * inv * inv) * jnp.mean(raw * part, axis=1, keepdims=True)
    return back, jnp.sum(grad * raw * inv, axis=0, keepdims=True)


def attend_back_kernel(
    scale, repeat, q_ref, do_ref, raw_ref, k_ref, kt_ref, v_ref, rawk_ref, qg_ref, kg_ref, cos_ref, sin_ref,
    dq_ref, dk_ref, dv_ref, dqg_ref, dkg_ref, dqs, dks, dvs,
):
    h = pl.program_id(0)

    @pl.when(h == 0)
    def _():
        dqg_ref[...] = jnp.zeros_like(dqg_ref)
        dkg_ref[...] = jnp.zeros_like(dkg_ref)

    @pl.when(lax.rem(h, repeat) == 0)
    def _():
        dks[...] = jnp.zeros_like(dks)
        dvs[...] = jnp.zeros_like(dvs)

    for b in range(q_ref.shape[0] // ATT_BLOCK):
        n = (b + 1) * ATT_BLOCK
        at = slice(b * ATT_BLOCK, n)
        query, given = q_ref[at, :], do_ref[at, :]
        weight = jnp.exp(dot(k_ref[:n, :], query, NT) * scale)
        prob = weight * (1.0 / jnp.sum(weight, axis=0, keepdims=True))
        prob_grad = dot(v_ref[:n, :], given, NT)
        inner = jnp.sum(prob * prob_grad, axis=0, keepdims=True)
        score_grad = (prob * (prob_grad - inner)).astype(bf16)
        dks[:n, :] += dot(score_grad, query)
        dvs[:n, :] += dot(prob.astype(bf16), given)
        dqs[at, :] = dot(kt_ref[:, :n], score_grad).T * scale
    back, gain_part = unturn(dqs[...], raw_ref[...], qg_ref[...], cos_ref[...], sin_ref[...])
    dq_ref[...] = back.astype(bf16)
    dqg_ref[...] += gain_part

    @pl.when(lax.rem(h, repeat) == repeat - 1)
    def _():
        back_k, gain_k = unturn(dks[...] * scale, rawk_ref[...], kg_ref[...], cos_ref[...], sin_ref[...])
        dk_ref[...] = back_k.astype(bf16)
        dv_ref[...] = dvs[...].astype(bf16)
        dkg_ref[...] += gain_k


def attend_back(q, given, raw, k, k_t, v, q_gain, k_gain, cosine, sine, local_q, local_kv):
    rows = q.shape[0]
    repeat = local_q // local_kv
    head = pl.BlockSpec((rows, HD), lambda h: (0, h))
    shared = pl.BlockSpec((rows, HD), lambda h: (0, h // repeat))
    whole = pl.BlockSpec((rows, HD), lambda h: (0, 0))
    gain = pl.BlockSpec((1, HD), lambda h: (0, 0))
    return pl.pallas_call(
        functools.partial(attend_back_kernel, HD**-0.5, repeat),
        grid=(local_q,),
        in_specs=[
            head, head, head, shared, pl.BlockSpec((HD, rows), lambda h: (h // repeat, 0)), shared,
            pl.BlockSpec((rows, HD), lambda h: (0, local_q + h // repeat)), gain, gain, whole, whole,
        ],
        out_specs=[head, shared, shared, gain, gain],
        out_shape=[
            jax.ShapeDtypeStruct((rows, local_q * HD), bf16),
            jax.ShapeDtypeStruct((rows, local_kv * HD), bf16),
            jax.ShapeDtypeStruct((rows, local_kv * HD), bf16),
            jax.ShapeDtypeStruct((1, HD), f32),
            jax.ShapeDtypeStruct((1, HD), f32),
        ],
        scratch_shapes=[pltpu.VMEM((rows, HD), f32)] * 3,
        compiler_params=pltpu.CompilerParams(vmem_limit_bytes=40 * MIB),
        cost_estimate=pl.CostEstimate(flops=local_q * rows * rows * HD * 7, bytes_accessed=rows * local_q * HD * 10, transcendentals=local_q * rows * rows),
        name="attend_back",
    )(q, given, raw, k, k_t, v, raw, q_gain, k_gain, cosine, sine)


def experts_kernel(
    table, x_ref, g_ref, gate_ref, spread_ref, wg_ref, wu_ref, wd_ref, hw_ref, gb_ref, ub_ref, score_ref, back_ref
):
    x = x_ref[...]
    gate_pre = dot(x, wg_ref[...])
    sigma = 1.0 / (1.0 + jnp.exp(-gate_pre))
    active = gate_pre * sigma
    up_pre = dot(x, wu_ref[...])
    pre = dot(g_ref[...], wd_ref[...], NT)
    hidden = active * up_pre
    score_ref[...] = dot(spread_ref[...], (hidden * pre).astype(bf16), NT)
    weight = dot(gate_ref[...], spread_ref[...])
    hw_ref[...] = (hidden * weight).astype(bf16)
    hidden_grad = pre * weight
    up_back = (hidden_grad * active).astype(bf16)
    gate_back = (hidden_grad * up_pre * sigma * (1.0 + gate_pre * (1.0 - sigma))).astype(bf16)
    gb_ref[...] = gate_back
    ub_ref[...] = up_back
    back_ref[...] = (dot(gate_back, wg_ref[...], NT) + dot(up_back, wu_ref[...], NT)).astype(bf16)


def experts(order, x, g, gates, spread, gate_w, up_w, down_w, tile):
    rows, width = x.shape
    hidden = gate_w.shape[1]
    lanes = spread.shape[0]
    at = lambda n: pl.BlockSpec((tile, n), lambda j, order: (order[j], 0))
    full = lambda shape: pl.BlockSpec(shape, lambda j, order: (0, 0), pipeline_mode=pl.Buffered(1))
    return pl.pallas_call(
        experts_kernel,
        grid_spec=pltpu.PrefetchScalarGridSpec(
            num_scalar_prefetch=1,
            grid=(rows // tile,),
            in_specs=[
                at(width), at(width), at(lanes), full((lanes, hidden)),
                full((width, hidden)), full((width, hidden)), full((hidden, width)),
            ],
            out_specs=[
                at(hidden), at(hidden), at(hidden),
                pl.BlockSpec((lanes, tile), lambda j, order: (0, order[j])),
                pl.BlockSpec((tile, width), lambda j, order: (j, 0)),
            ],
        ),
        out_shape=[
            jax.ShapeDtypeStruct((rows, hidden), bf16),
            jax.ShapeDtypeStruct((rows, hidden), bf16),
            jax.ShapeDtypeStruct((rows, hidden), bf16),
            jax.ShapeDtypeStruct((lanes, rows), f32),
            jax.ShapeDtypeStruct((rows, width), bf16),
        ],
        compiler_params=pltpu.CompilerParams(vmem_limit_bytes=58 * MIB),
        cost_estimate=pl.CostEstimate(flops=10 * rows * width * hidden, bytes_accessed=rows * width * 6 + rows * hidden * 6, transcendentals=rows * hidden),
        name="experts",
    )(order, x, g, gates, spread, gate_w, up_w, down_w)


TOPK = 8


def row_norm(values, gain):
    return values * lax.rsqrt(jnp.mean(values * values, axis=-1, keepdims=True) + norm_eps) * gain


def after(value, *others):
    return lax.optimization_barrier((value, *others))[0]


def hop(block, bit, axis):
    size = lax.axis_size(axis)
    return lax.ppermute(block, axis, [(i, i ^ bit) for i in range(size)])


def bits_of(size):
    return [1 << k for k in range(size.bit_length() - 1)]


def add_up(value):
    for axis in ("expert", "tensor"):
        for bit in bits_of(lax.axis_size(axis)):
            value = value + hop(value, bit, axis)
    return value


def to_members(parts):
    size, me = lax.axis_size("tensor"), lax.axis_index("tensor")
    found = [lax.dynamic_index_in_dim(parts, me, 0, keepdims=False)]
    for step in range(1, size):
        block = lax.dynamic_index_in_dim(parts, lax.rem(me + step, size), 0, keepdims=False)
        found.append(lax.ppermute(block, "tensor", [(i, (i + step) % size) for i in range(size)]))
    return found


def step_order(bits):
    order = [0]
    for bit in reversed(bits):
        order = [r | bit for r in order] + order
    return order


def scatter_sum(blocks, bits):
    for bit in bits:
        half = blocks.shape[0] // 2
        moved = hop(blocks[:half], bit, "expert")
        blocks = (blocks[half:].astype(f32) + moved.astype(f32)).astype(bf16)
    return blocks


def local(
    hidden_in,
    attn_gain,
    query_gain,
    key_gain,
    w_qkv,
    w_out,
    moe_gain,
    w_router,
    w_gate,
    w_up,
    w_down,
    routes,
    pair_rank,
    out_grad,
):
    tok_dev, width = hidden_in.shape
    n_tensor = lax.axis_size("tensor")
    n_expert = lax.axis_size("expert")
    member = lax.axis_index("tensor")
    place = lax.axis_index("expert")
    group = tok_dev * n_tensor
    local_experts = w_gate.shape[0]
    quarter = w_gate.shape[2]
    n_experts = local_experts * n_expert
    hidden_loc = local_experts * quarter
    capacity = 9 * group * TOPK // (8 * n_experts)
    local_q = w_out.shape[0] // HD
    local_kv = (w_qkv.shape[1] // HD - local_q) // 2
    both = ("expert", "tensor")
    bits = bits_of(n_expert)
    chunks = 2 * max(n_expert // 8, 1)
    piece = tok_dev // chunks
    rows = n_tensor * piece
    total = n_expert * rows
    lanes = 8 * (-(-local_experts // 8))

    hidden_f = hidden_in.astype(f32)
    attn_normed, attn_pull = jax.vjp(row_norm, hidden_f, attn_gain.astype(f32))
    gathered = lax.all_gather(attn_normed.astype(bf16), "tensor", axis=0, tiled=True)
    given = after(out_grad, gathered)

    def spread_out(values, c):
        return lax.all_gather(values[c * piece : (c + 1) * piece], both, axis=0, tiled=True)

    cosine, sine = rope_tables(group)
    q_gain, k_gain = query_gain.astype(f32)[None, :], key_gain.astype(f32)[None, :]
    raw, queries, keys, values = project(gathered, w_qkv, q_gain, k_gain, cosine, sine, local_q, local_kv)
    mixed_all = attend(queries, keys, values.T, local_q, local_kv)
    attn = lax.psum_scatter(
        dot(mixed_all, w_out).astype(bf16), "tensor", scatter_dimension=0, tiled=True
    )
    middle = hidden_f + attn.astype(f32)
    moe_normed, moe_pull = jax.vjp(row_norm, middle, moe_gain.astype(f32))
    moe_in = moe_normed.astype(bf16)

    expert_ids = jnp.arange(n_experts, dtype=jnp.int32)
    hits = routes.T[None, :, :] == expert_ids[:, None, None]
    ranks = jnp.where(hits, pair_rank[0].reshape(group, TOPK).T[None, :, :] + 1, 0).sum(axis=1)
    ranks = jnp.where(ranks == 0, group * TOPK + 1, ranks)
    own_ranks = lax.dynamic_slice_in_dim(ranks, member * tok_dev, tok_dev, 1)
    before = (ranks[:, :, None] < own_ranks[:, None, :]).astype(f32).sum(axis=1)
    routed = own_ranks <= group * TOPK
    keep = routed & (before < capacity)

    logits = dot(w_router, moe_in, ((0,), (1,)))
    gates = jax.nn.softmax(jnp.where(routed, logits, -jnp.inf), axis=0)
    sent_gates = jnp.where(keep, gates, 0.0).astype(bf16).astype(f32)
    gates_in = lax.all_to_all(
        sent_gates.reshape(n_expert, local_experts, tok_dev), "expert", 0, 0, tiled=True
    )
    gates_in = jnp.stack(to_members(jnp.broadcast_to(gates_in[None], (n_tensor, *gates_in.shape))))
    gates_in = jnp.take(gates_in, lax.rem(member - jnp.arange(n_tensor) + n_tensor, n_tensor), axis=0)
    gates_in = gates_in.reshape(n_tensor, n_expert, local_experts, chunks, piece)
    gates_in = gates_in.transpose(3, 1, 0, 4, 2).reshape(chunks, total, local_experts)
    gates_in = jnp.pad(gates_in, ((0, 0), (0, 0), (0, lanes - local_experts))).astype(bf16)

    gate_w = w_gate.transpose(1, 0, 2).reshape(width, hidden_loc)
    up_w = w_up.transpose(1, 0, 2).reshape(width, hidden_loc)
    down_w = w_down.reshape(hidden_loc, width)
    spread = (jnp.arange(hidden_loc)[None, :] // quarter == jnp.arange(lanes)[:, None]).astype(bf16)

    def run_experts(c, x_c, g_c):
        way = [bits[0]] + (bits[1:] if c % 2 else bits[:0:-1])
        order = place ^ jnp.array(step_order(way), jnp.int32)
        hidden_wt, gate_back, up_back, score, back = experts(
            order, x_c, g_c, gates_in[c], spread, gate_w, up_w, down_w, rows
        )
        return way, order, hidden_wt, gate_back, up_back, score, back

    def out_of(hidden_wt, way, order):
        blocks = hidden_wt.reshape(n_expert, rows, hidden_loc)
        blocks = jnp.take(blocks, order, axis=0).reshape(total, hidden_loc)
        return scatter_sum(dot(blocks, down_w).astype(bf16), way)

    def weight_grads(x_c, g_c, hidden_wt, gate_back, up_back):
        return dot(hidden_wt, g_c, TN), dot(x_c, gate_back, TN), dot(x_c, up_back, TN)

    def own_rows(part):
        return lax.psum_scatter(part, "tensor", scatter_dimension=0, tiled=True)

    if chunks == 2:
        grad_all = [spread_out(given, c) for c in range(chunks)]
        moe_all = [spread_out(moe_in, c) for c in range(chunks)]
        done = [run_experts(c, moe_all[c], grad_all[c]) for c in range(chunks)]
        back_own = [own_rows(scatter_sum(d[6], d[0])) for d in done]
        scores = [d[5] for d in done]
        out_own = [own_rows(out_of(after(d[2], done[1][6]), d[0], d[1])) for d in done]
        grads = [
            weight_grads(moe_all[c], grad_all[c], *done[c][2:5]) for c in range(chunks)
        ]
        grads = [sum(parts) for parts in zip(*grads)]
    else:
        def one_chunk(sums, c):
            x_c = lax.all_gather(lax.dynamic_slice_in_dim(moe_in, c * piece, piece, 0), both, axis=0, tiled=True)
            g_c = lax.all_gather(lax.dynamic_slice_in_dim(given, c * piece, piece, 0), both, axis=0, tiled=True)
            way = bits
            order = place ^ jnp.array(step_order(way), jnp.int32)
            hidden_wt, gate_back, up_back, score, back = experts(
                order, x_c, g_c, lax.dynamic_index_in_dim(gates_in, c, 0, keepdims=False), spread, gate_w, up_w, down_w, rows
            )
            parts = weight_grads(x_c, g_c, hidden_wt, gate_back, up_back)
            sums = tuple(a + b for a, b in zip(sums, parts))
            return sums, (own_rows(scatter_sum(back, way)), score, own_rows(out_of(hidden_wt, way, order)))

        zeros = (
            jnp.zeros((hidden_loc, width), f32),
            jnp.zeros((width, hidden_loc), f32),
            jnp.zeros((width, hidden_loc), f32),
        )
        grads, (back_own, scores, out_own) = lax.scan(one_chunk, zeros, jnp.arange(chunks))
    grad_down = grads[0].reshape(local_experts, quarter, width)
    grad_gate, grad_up = (
        part.reshape(width, local_experts, quarter).transpose(1, 0, 2) for part in grads[1:]
    )
    moe_back = jnp.concatenate(list(back_own), axis=0).astype(f32)
    moe_out = jnp.concatenate(list(out_own), axis=0).astype(f32)

    scores = jnp.stack([s[:local_experts] for s in scores]).reshape(
        chunks, local_experts, n_expert, n_tensor, piece
    )
    scores = scores.transpose(2, 3, 1, 0, 4).reshape(n_expert, n_tensor, local_experts, tok_dev)
    scores = lax.all_to_all(scores, "expert", 0, 0, tiled=True)
    scores = sum(to_members(scores.transpose(1, 0, 2, 3)))
    scores = jnp.where(keep, scores.reshape(n_experts, tok_dev), 0.0)

    layer_out = (middle + moe_out).astype(bf16)
    inner_gate = jnp.sum(gates * scores, axis=0, keepdims=True)
    logit_grad = (gates * (scores - inner_gate)).astype(bf16)
    router_grad = dot(logit_grad, moe_in)
    moe_in_grad = moe_back + dot(logit_grad, w_router, ((0,), (1,)))
    middle_part, moe_gain_grad = moe_pull(moe_in_grad)
    middle_grad = out_grad.astype(f32) + middle_part

    middle_all = lax.all_gather(middle_grad.astype(bf16), "tensor", axis=0, tiled=True)
    mixed_grad = dot(middle_all, w_out, NT).astype(bf16)
    dq, dk, dv, query_gain_grad, key_gain_grad = attend_back(
        queries, mixed_grad, raw, keys, keys.T, values, q_gain, k_gain, cosine, sine, local_q, local_kv
    )
    out_weight_grad = dot(mixed_all, middle_all, TN).astype(bf16)
    grad_out = lax.psum_scatter(out_weight_grad, "expert", scatter_dimension=1, tiled=True).astype(f32)
    qkv_grad = jnp.concatenate([dq, dk, dv], axis=1)
    normed_part = dot(qkv_grad, w_qkv, NT)
    normed_grad = lax.psum_scatter(
        normed_part.astype(bf16), "tensor", scatter_dimension=0, tiled=True
    ).astype(f32)
    attn_gain_grad = jnp.sum(normed_part * gathered.astype(f32), axis=0) / attn_gain.astype(f32)
    qkv_weight_grad = dot(gathered, qkv_grad, TN).astype(bf16)
    order = place ^ jnp.array(step_order(bits), jnp.int32)
    blocks = jnp.take(qkv_weight_grad.reshape(n_expert, -1, w_qkv.shape[1]), order, axis=0)
    grad_qkv = scatter_sum(blocks.reshape(qkv_weight_grad.shape), bits).astype(f32)
    hidden_part, _ = attn_pull(normed_grad)
    input_grad = middle_grad + hidden_part
    small = jnp.concatenate(
        [attn_gain_grad[None, :], jnp.pad(query_gain_grad, ((0, 0), (0, width - HD))), jnp.pad(key_gain_grad, ((0, 0), (0, width - HD)))],
        axis=0,
    )
    small = add_up(small)
    router_sum = add_up(jnp.concatenate([router_grad, moe_gain_grad[None, :]], axis=0))
    return (
        layer_out,
        input_grad,
        small[0],
        small[1, :HD],
        small[2, :HD],
        grad_qkv,
        grad_out,
        router_sum[n_experts],
        router_sum[:n_experts].T,
        grad_gate,
        grad_up,
        grad_down,
    )


def solution(mesh):
    in_specs = (
        P(("expert", "tensor"), None),
        P(),
        P(),
        P(),
        P(None, "tensor"),
        P("tensor", None),
        P(),
        P(),
        P("expert", None, "tensor"),
        P("expert", None, "tensor"),
        P("expert", "tensor", None),
        P("expert", None),
        P("expert", None),
        P(("expert", "tensor"), None),
    )
    out_specs = (
        P(("expert", "tensor"), None),
        P(("expert", "tensor"), None),
        P(),
        P(),
        P(),
        P("expert", "tensor"),
        P("tensor", "expert"),
        P(),
        P(),
        P("expert", None, "tensor"),
        P("expert", None, "tensor"),
        P("expert", "tensor", None),
    )
    return jax.shard_map(local, mesh=mesh, in_specs=in_specs, out_specs=out_specs, check_vma=False)
```

time: 3510 us -> 1590 us (0.45)
  local copies, waits for them, and re-layouts: 1060 us -> 122 us
  waiting for transfers between devices: 1760 us -> 856 us
  Pallas kernels: 0 us -> 220 us
  matrix products: 357 us -> 212 us
  other arithmetic: 199 us -> 110 us
  blocking collectives: 54.3 us -> 0 us
    all_to_all x4 -> x2, waiting for transfers between devices: 1220 us -> 43.6 us  [the longest x1 38.9 us: local(): scores = lax.all_to_all(scores, 'expert', 0, 0, tiled=True)]
    gather x20 -> x5, local copies, waits for them, and re-layouts: 666 us -> 19.1 us  [the longest x2 12.6 us: out_of(): blocks = jnp.take(blocks, order, axis=0).reshape(total, hidden_loc)]
    ppermute x0 -> x31, waiting for transfers between devices: none -> 278 us  [the longest x25 278 us: hop(): return lax.ppermute(block, axis, [(i, i ^ bit) for i in range(size)])]
    all_gather x2 -> x4, waiting for transfers between devices: 81.9 us -> 327 us  [spread_out(): lax.all_gather(values[c * piece:(c + 1) * piece], both, axis=0, tiled=True)]
    pallas_call x0 -> x5, Pallas kernels: none -> 220 us  [the longest x2 171 us: experts(): pl.pallas_call(experts_kernel, grid_spec=pltpu.PrefetchScalarGridSpec(num...]
    dot_general x32 -> x16, matrix products: 357 us -> 212 us  [dot(): lax.dot_general(a, b, (contract, ((), ())), preferred_element_type=f32)]
    scatter x4 -> x0, local copies, waits for them, and re-layouts: 122 us -> none  [the longest x1 30.5 us: pair_slots(): jnp.zeros((pairs,), jnp.int32).at[rank_row]]
    reduce_scatter x7, waiting for transfers between devices: 211 us -> 91.4 us  [the longest x1 72.9 us: local(): lax.psum_scatter(dot(mixed_all, w_out).astype(bf16), 'tensor', scatter_di...]
  transfers between devices with their start and end apart: 16 -> 46, of which waited for: 12 -> 20; matrix products, arithmetic and copies ran while one was open for 26% -> 25% of each run, Pallas kernels for 0% -> 13%
where the time goes in v1:
time: 1590 us; the launch traced here: 1570 us
  waiting for transfers between devices  856 us (54%)
  Pallas kernels  220 us (14%)
  matrix products  212 us (13%)
  local copies, waits for them, and re-layouts  122 us (8%)
  other arithmetic  110 us (7%)
  starting transfers between devices  36.5 us (2%)
    all_gather x4, waiting for transfers between devices, spread_out(): lax.all_gather(values[c * piece:(c + 1) * piece], both, axis=0, tiled=True)  327 us
    ppermute x25, waiting for transfers between devices, hop(): return lax.ppermute(block, axis, [(i, i ^ bit) for i in range(size)])  278 us
    dot_general x16, matrix products, dot(): lax.dot_general(a, b, (contract, ((), ())), preferred_element_type=f32)  212 us
    pallas_call x2, Pallas kernels, experts(): pl.pallas_call(experts_kernel, grid_spec=pltpu.PrefetchScalarGridSpec(num...  171 us
    all_gather x1, waiting for transfers between devices, local(): lax.all_gather(attn_normed.astype(bf16), 'tensor', axis=0, tiled=True)  81.2 us
    reduce_scatter x1, waiting for transfers between devices, local(): lax.psum_scatter(dot(mixed_all, w_out).astype(bf16), 'tensor', scatter_di...  72.9 us
    convert_element_type x14, other arithmetic, scatter_sum(): blocks = (blocks[half:].astype(f32) + moved.astype(f32)).astype(bf16)  62.2 us
    slice x14, local copies, waits for them, and re-layouts, scatter_sum(): moved = hop(blocks[:half], bit, 'expert')  47.7 us
  transfers between devices with their start and end apart: 46, of which 20 were waited for; matrix products, arithmetic and copies ran while one was open for 25% of the time, Pallas kernels for 13%

profile of v1, /device:TPU:0, one launch (start us, length us, event | category | flops | bytes accessed | tf_op | source)
XLA Modules:
  0.0 1571.9 jit_solution(18000126482543546714)
XLA Ops:
  15.0 81.2 %all-gather.7.cloned.1.call-done.x_ref = bf16[1024,2048]{1,0:T(8,128)(2,1)} async-done(((bf16[256,2048]{1,0:T(8,128)(2,1)}), bf16[1024,2048]{1,0:T(8,128)(2,1)}) %all-gather.7.cloned.1.call-update) | async-done | bytes 4194320 | tf_op jit(solution)/shard_map/all_gather | solution.py:326
  98.4 9.5 project.1
  113.2 11.7 attend.1
  126.2 6.0 convolution_convert_fusion.4
  134.7 72.9 %reduce-scatter.8.cloned.1.call-done = bf16[256,2048]{1,0:T(8,128)(2,1)} async-done(((bf16[1024,2048]{1,0:T(8,128)(2,1)}), bf16[256,2048]{1,0:T(8,128)(2,1)}) %reduce-scatter.8.cloned.1.call-update) | async-done | bytes 1048592 | tf_op jit(solution)/shard_map/reduce_scatter | solution.py:336
  217.4 5.6 convert_reduce_fusion
  226.6 3.7 all-to-all-start
  230.3 4.7 all-to-all-done
  240.2 5.0 copy.83.wg_ref
  245.2 4.7 copy.84.wu_ref
  255.7 70.8 %all-gather.11.cloned.1.call-done.g_ref = bf16[4096,2048]{1,0:T(8,128)(2,1)} async-done(((bf16[128,2048]{1,0:T(8,128)(2,1)}), bf16[4096,2048]{1,0:T(8,128)(2,1)}) %all-gather.11.cloned.1.call-update) | async-done | bytes 16777232 | tf_op jit(solution)/shard_map/all_gather | solution.py:330
  326.5 116.9 %all-gather.9.cloned.1.call-done.x_ref = bf16[4096,2048]{1,0:T(8,128)(2,1)} async-done(((bf16[128,2048]{1,0:T(8,128)(2,1)}), bf16[4096,2048]{1,0:T(8,128)(2,1)}) %all-gather.9.cloned.1.call-update) | async-done | bytes 16777232 | tf_op jit(solution)/shard_map/all_gather | solution.py:330
  443.4 85.3 %experts.2 = (bf16[4096,768]{1,0:T(8,128)(2,1)}, bf16[4096,768]{1,0:T(8,128)(2,1)}, bf16[4096,768]{1,0:T(8,128)(2,1)}, f32[8,4096]{1,0:T(8,128)}, bf16[4096,2048]{1,0:T(8,128)(2,1)}) custom-call(s32[8]{0:T(128)} %broadcast_xor_fusion.1.table, bf16[4096,2048]{1,0:T(8,128)(2,1)} %all-gather.9.cloned.1.call-done.x_ref, ...), custom_call_target="tpu_custom_call" | custom-call | flops 64424509440 | bytes 69206016 | tf_op jit(solution)/shard_map/experts/pallas_call | solution.py:208
  528.7 8.4 slice.152
  537.3 22.5 %all-gather.15.cloned.1.call-done.g_ref = bf16[4096,2048]{1,0:T(8,128)(2,1)} async-done(((bf16[128,2048]{1,0:T(8,128)(2,1)}), bf16[4096,2048]{1,0:T(8,128)(2,1)}) %all-gather.15.cloned.1.call-update) | async-done | bytes 16777232 | tf_op jit(solution)/shard_map/all_gather | solution.py:330
  559.8 116.9 %all-gather.13.cloned.1.call-done.x_ref = bf16[4096,2048]{1,0:T(8,128)(2,1)} async-done(((bf16[128,2048]{1,0:T(8,128)(2,1)}), bf16[4096,2048]{1,0:T(8,128)(2,1)}) %all-gather.13.cloned.1.call-update) | async-done | bytes 16777232 | tf_op jit(solution)/shard_map/all_gather | solution.py:330
  676.8 85.7 %experts.3 = (bf16[4096,768]{1,0:T(8,128)(2,1)}, bf16[4096,768]{1,0:T(8,128)(2,1)}, bf16[4096,768]{1,0:T(8,128)(2,1)}, f32[8,4096]{1,0:T(8,128)}, bf16[4096,2048]{1,0:T(8,128)(2,1)}) custom-call(s32[8]{0:T(128)} %broadcast_xor_fusion.table, bf16[4096,2048]{1,0:T(8,128)(2,1)} %all-gather.13.cloned.1.call-done.x_ref, ...), custom_call_target="tpu_custom_call" | custom-call | flops 64424509440 | bytes 69206016 | tf_op jit(solution)/shard_map/experts/pallas_call | solution.py:208
  762.4 8.3 slice.158
  771.0 6.3 gather_fusion.2
  777.3 3.5 broadcast_select_fusion.1
  780.8 18.1 %convolution_convert_fusion.1 = bf16[4096,2048]{1,0:T(8,128)(2,1)} fusion(bf16[4096,768]{1,0:T(8,128)(2,1)S(1)} %bitcast.133, bf16[768,2048]{1,0:T(8,128)(2,1)} %bitcast.156), kind=kOutput, calls=%fused_computation.10 | convolution fusion | flops 12893290496 | bytes 26214400 | tf_op jit(solution)/shard_map/dot_general | solution.py:20
  798.9 8.3 slice.188
  807.4 6.3 gather_fusion.3
  813.7 6.0 broadcast_select_fusion
  819.8 8.3 add_convert_fusion.1
  830.5 3.4 copy-done.17
  835.4 5.8 add_convert_fusion
  846.9 18.8 %convolution_convert_fusion = bf16[4096,2048]{1,0:T(8,128)(2,1)} fusion(bf16[4096,768]{1,0:T(8,128)(2,1)} %bitcast.132, bf16[768,2048]{1,0:T(8,128)(2,1)S(1)} %bitcast.157), kind=kOutput, calls=%fused_computation.9 | convolution fusion | flops 12893290496 | bytes 26214400 | tf_op jit(solution)/shard_map/dot_general | solution.py:20
  865.7 8.4 slice.194
  874.2 52.7 %collective-permute-done.10 = bf16[1024,2048]{1,0:T(8,128)(2,1)} collective-permute-done((bf16[1024,2048]{1,0:T(8,128)(2,1)}, bf16[1024,2048]{1,0:T(8,128)(2,1)}, u32[]{:S(2)}, u32[]{:S(2)}) %collective-permute-start.10) | collective-permute-done | bytes 4194336 | tf_op jit(solution)/shard_map/ppermute | solution.py:249
  926.9 5.4 add_convert_fusion.5
  935.0 5.1 collective-permute-done.13
  940.1 4.1 add_convert_fusion.4
  947.6 36.3 %collective-permute-done.11 = bf16[512,2048]{1,0:T(8,128)(2,1)S(1)} collective-permute-done((bf16[512,2048]{1,0:T(8,128)(2,1)}, bf16[512,2048]{1,0:T(8,128)(2,1)S(1)}, u32[]{:S(2)}, u32[]{:S(2)}) %collective-permute-start.11) | collective-permute-done | bytes 2097184 | tf_op jit(solution)/shard_map/ppermute | solution.py:249
  986.7 7.7 add_convert_fusion.3
  1001.6 33.3 %collective-permute-done.14 = bf16[512,2048]{1,0:T(8,128)(2,1)S(1)} collective-permute-done((bf16[512,2048]{1,0:T(8,128)(2,1)}, bf16[512,2048]{1,0:T(8,128)(2,1)S(1)}, u32[]{:S(2)}, u32[]{:S(2)}) %collective-permute-start.14) | collective-permute-done | bytes 2097184 | tf_op jit(solution)/shard_map/ppermute | solution.py:249
  1037.2 8.1 add_convert_fusion.2
  1050.6 72.5 %collective-permute-done.4 = bf16[1024,2048]{1,0:T(8,128)(2,1)} collective-permute-done((bf16[1024,2048]{1,0:T(8,128)(2,1)}, bf16[1024,2048]{1,0:T(8,128)(2,1)}, u32[]{:S(2)}, u32[]{:S(2)}) %collective-permute-start.4) | collective-permute-done | bytes 4194336 | tf_op jit(solution)/shard_map/ppermute | solution.py:249
  1123.0 5.4 add_convert_fusion.7
  1129.3 54.3 %collective-permute-done.5 = bf16[512,2048]{1,0:T(8,128)(2,1)S(1)} collective-permute-done((bf16[512,2048]{1,0:T(8,128)(2,1)S(1)}, bf16[512,2048]{1,0:T(8,128)(2,1)S(1)}, u32[]{:S(2)}, u32[]{:S(2)}) %collective-permute-start.5) | collective-permute-done | bytes 2097184 | tf_op jit(solution)/shard_map/ppermute | solution.py:249
  1185.7 5.4 add_convert_fusion.6
  1196.4 3.4 all-to-all-start.1
  1200.0 38.9 %all-to-all-done.1 = f32[8,4,4,256]{3,2,1,0:T(4,128)S(1)} async-done(((f32[8,4,4,256]{3,2,1,0:T(4,128)}), f32[8,4,4,256]{3,2,1,0:T(4,128)S(1)}, u32[]{:S(2)}, u32[]{:S(2)}) %all-to-all-start.1) | async-done | bytes 131104 | tf_op jit(solution)/shard_map/all_to_all | solution.py:429
  1242.4 4.4 add_convert_fusion.10
  1247.0 20.9 %fusion.39 = f32[2048,768]{0,1:T(8,128)} fusion(bf16[4096,2048]{1,0:T(8,128)(2,1)} %all-gather.9.cloned.1.call-done.x_ref, bf16[4096,768]{1,0:T(8,128)(2,1)} %get-tuple-element.55), kind=kOutput, calls=%fused_computation.158 | convolution fusion | flops 12884901888 | bytes 29360128 | tf_op jit(solution)/shard_map/dot_general | solution.py:20
  1269.6 3.8 multiply_reduce_fusion.1
  1274.2 15.7 reduce-scatter.12.cloned.1.call-done
  1289.9 5.9 fusion.31
  1295.9 21.6 %convolution_add_fusion.1 = f32[2048,768]{0,1:T(8,128)} fusion(f32[2048,768]{0,1:T(8,128)} %fusion.39, bf16[4096,2048]{1,0:T(8,128)(2,1)} %all-gather.13.cloned.1.call-done.x_ref, bf16[4096,768]{1,0:T(8,128)(2,1)} %get-tuple-element.56), kind=kOutput, calls=%fused_computation.32 | convolution fusion | flops 12886474752 | bytes 35651584 | tf_op jit(solution)/shard_map/dot_general | solution.py:20
  1319.9 20.8 %fusion.38 = f32[2048,768]{0,1:T(8,128)} fusion(bf16[4096,2048]{1,0:T(8,128)(2,1)} %all-gather.9.cloned.1.call-done.x_ref, bf16[4096,768]{1,0:T(8,128)(2,1)} %get-tuple-element.53), kind=kOutput, calls=%fused_computation.157 | convolution fusion | flops 12884901888 | bytes 29360128 | tf_op jit(solution)/shard_map/dot_general | solution.py:20
  1342.3 33.8 %all-gather.17.cloned.1.call-done = bf16[1024,2048]{1,0:T(8,128)(2,1)} async-done(((bf16[256,2048]{1,0:T(8,128)(2,1)}), bf16[1024,2048]{1,0:T(8,128)(2,1)}) %all-gather.17.cloned.1.call-update) | async-done | bytes 4194320 | tf_op jit(solution)/shard_map/all_gather | solution.py:441
  1376.1 9.4 convolution_convert_fusion.3
  1385.5 22.0 %convolution_add_fusion.2 = f32[2048,768]{0,1:T(8,128)} fusion(f32[2048,768]{0,1:T(8,128)} %fusion.38, bf16[4096,2048]{1,0:T(8,128)(2,1)} %all-gather.13.cloned.1.call-done.x_ref, bf16[4096,768]{1,0:T(8,128)(2,1)} %get-tuple-element.54), kind=kOutput, calls=%fused_computation.33 | convolution fusion | flops 12886474752 | bytes 35651584 | tf_op jit(solution)/shard_map/dot_general | solution.py:20
  1407.7 8.1 convolution_convert_fusion.5.do_ref
  1415.9 27.7 %attend_back.1 = (bf16[1024,1024]{1,0:T(8,128)(2,1)S(1)}, bf16[1024,128]{1,0:T(8,128)(2,1)S(1)}, bf16[1024,128]{1,0:T(8,128)(2,1)S(1)}, f32[1,128]{1,0:T(1,128)S(1)}, f32[1,128]{1,0:T(1,128)S(1)}) custom-call(bf16[1024,1024]{1,0:T(8,128)(2,1)S(1)} %copy-done.11, bf16[1024,1024]{1,0:T(8,128)(2,1)S(1)} %convolution_convert_fusion.5.do_ref, ...), custom_call_target="tpu_custom_call" | custom-call | flops 7516192768 | bytes 10485760 | tf_op jit(solution)/shard_map/attend_back/pallas_call | solution.py:159
  1445.9 7.4 convolution_convert_fusion.2
  1453.2 5.9 gather_fusion.1
  1459.2 10.9 multiply_reduce_fusion
  1479.5 20.7 %fusion.40 = f32[768,2048]{1,0:T(8,128)} fusion(bf16[4096,768]{1,0:T(8,128)(2,1)} %get-tuple-element.41, bf16[4096,2048]{1,0:T(8,128)(2,1)} %all-gather.11.cloned.1.call-done.g_ref), kind=kOutput, calls=%fused_computation.159 | convolution fusion | flops 12884901888 | bytes 29360128 | tf_op jit(solution)/shard_map/dot_general | solution.py:20
  1505.9 20.0 %convolution_add_fusion = f32[768,2048]{1,0:T(8,128)} fusion(f32[768,2048]{1,0:T(8,128)} %fusion.40, bf16[4096,768]{1,0:T(8,128)(2,1)S(1)} %bitcast.130, bf16[4096,2048]{1,0:T(8,128)(2,1)} %all-gather.15.cloned.1.call-done.g_ref), kind=kOutput, calls=%fused_computation.31 | convolution fusion | flops 12886474752 | bytes 35651584 | tf_op jit(solution)/shard_map/dot_general | solution.py:20
  1525.9 13.7 collective-permute-done.30
  1542.6 4.1 collective-permute-done.22
  1547.9 5.5 collective-permute-done.25
  1561.1 3.8 fusion.2
  (331 shorter events, 124.5 us)
Async XLA Ops:
  7.2 215.9 %copy-start = (bf16[2048,32]{0,1:T(8,128)(2,1)S(1)}, bf16[2048,32]{0,1:T(8,128)(2,1)}, u32[]{:S(2)}) copy-start(bf16[2048,32]{0,1:T(8,128)(2,1)} %param.26) | copy-start | bytes 393220
  7.2 89.0 %all-gather.7.cloned.1.call-start = ((), (), s32[]{:S(2)}) async-start(), calls=%async_computation.9 | async-start | bytes 5242880 | tf_op jit(solution)/shard_map/all_gather | solution.py:326
  12.6 195.0 %reduce-scatter.8.cloned.1.call-start = ((), (), s32[]{:S(2)}) async-start(), calls=%async_computation.10 | async-start | bytes 5242880 | tf_op jit(solution)/shard_map/reduce_scatter | solution.py:336
  15.0 93.0 %copy-start.1 = (f32[1,128]{1,0:T(1,128)}, f32[1,128]{1,0:T(1,128)S(1)}, u32[]{:S(2)}) copy-start(f32[1,128]{1,0:T(1,128)S(1)} %get-tuple-element.97.kg_ref) | copy-start | bytes 1540
  15.0 93.0 %copy-start.3 = (f32[1,128]{1,0:T(1,128)}, f32[1,128]{1,0:T(1,128)S(1)}, u32[]{:S(2)}) copy-start(f32[1,128]{1,0:T(1,128)S(1)} %get-tuple-element.98.qg_ref) | copy-start | bytes 1540
  132.2 75.5 %copy-start.12 = (bf16[256,2048]{1,0:T(8,128)(2,1)S(1)}, bf16[256,2048]{1,0:T(8,128)(2,1)}, u32[]{:S(2)}) copy-start(bf16[256,2048]{1,0:T(8,128)(2,1)} %param.19) | copy-start | bytes 3145732
  132.2 194.3 %all-gather.11.cloned.1.call-start = ((), (), s32[]{:S(2)}) async-start(), calls=%async_computation.12 | async-start | bytes 17301504 | tf_op jit(solution)/shard_map/all_gather | solution.py:330
  134.6 308.8 %all-gather.9.cloned.1.call-start = ((), (), s32[]{:S(2)}) async-start(), calls=%async_computation.11 | async-start | bytes 17301504 | tf_op jit(solution)/shard_map/all_gather | solution.py:330
  134.7 79.5 %copy-start.30 = (f32[2048]{0:T(1024)}, f32[2048]{0:T(1024)S(1)}, u32[]{:S(2)}) copy-start(f32[2048]{0:T(1024)S(1)} %convert_element_type.261) | copy-start | bytes 24580
  134.7 80.1 %copy-start.34 = (s32[1,8192]{1,0:T(1,128)S(1)}, s32[1,8192]{1,0:T(1,128)}, u32[]{:S(2)}) copy-start(s32[1,8192]{1,0:T(1,128)} %param.31) | copy-start | bytes 98308
  213.6 346.2 %all-gather.15.cloned.1.call-start = ((), (), s32[]{:S(2)}) async-start(), calls=%async_computation.14 | async-start | bytes 17301504 | tf_op jit(solution)/shard_map/all_gather | solution.py:330
  214.2 462.5 %all-gather.13.cloned.1.call-start = ((), (), s32[]{:S(2)}) async-start(), calls=%async_computation.13 | async-start | bytes 17301504 | tf_op jit(solution)/shard_map/all_gather | solution.py:330
  226.6 8.4 all-to-all-start
  230.3 1039.3 %reduce-scatter.14.cloned.1.call-start = ((), (), s32[]{:S(2)}) async-start(), calls=%async_computation.17 | async-start | bytes 2621440 | tf_op jit(solution)/shard_map/reduce_scatter | solution.py:386
  235.0 14.8 collective-permute-start
  236.5 13.3 collective-permute-start.2
  239.1 10.8 collective-permute-start.1
  537.1 282.7 %collective-permute-start.9 = (bf16[2048,2048]{1,0:T(8,128)(2,1)}, bf16[2048,2048]{1,0:T(8,128)(2,1)}, u32[]{:S(2)}, u32[]{:S(2)}) collective-permute-start(bf16[2048,2048]{1,0:T(8,128)(2,1)} %slice.152), channel_id=1, source_target_pairs={{0,4},{4,0},{8,12},{12,8},{16,20},{20,16},{24,28},{28,24},{1,5},{5... | collective-permute-start | bytes 25165832 | tf_op jit(solution)/shard_map/ppermute | solution.py:249
  770.7 64.6 %collective-permute-start.12 = (bf16[2048,2048]{1,0:T(8,128)(2,1)}, bf16[2048,2048]{1,0:T(8,128)(2,1)}, u32[]{:S(2)}, u32[]{:S(2)}) collective-permute-start(bf16[2048,2048]{1,0:T(8,128)(2,1)} %slice.158), channel_id=1, source_target_pairs={{0,4},{4,0},{8,12},{12,8},{16,20},{20,16},{24,28},{28,24},{1,5},{5... | collective-permute-start | bytes 25165832 | tf_op jit(solution)/shard_map/ppermute | solution.py:249
  771.0 42.7 %copy-start.50 = (pred[8]{0:T(512)(128)(4,1)}, pred[8]{0:T(512)(128)(4,1)S(1)}, u32[]{:S(2)}) copy-start(pred[8]{0:T(512)(128)(4,1)S(1)} %get-tuple-element.63) | copy-start | bytes 28
  771.0 36.4 %copy-start.49 = (s32[1024]{0:T(1024)}, s32[1024]{0:T(1024)S(1)}, u32[]{:S(2)}) copy-start(s32[1024]{0:T(1024)S(1)} %pad_clamp_fusion) | copy-start | bytes 12292
  807.1 179.6 %collective-permute-start.3 = (bf16[2048,2048]{1,0:T(8,128)(2,1)}, bf16[2048,2048]{1,0:T(8,128)(2,1)}, u32[]{:S(2)}, u32[]{:S(2)}) collective-permute-start(bf16[2048,2048]{1,0:T(8,128)(2,1)} %slice.188), channel_id=1, source_target_pairs={{0,4},{4,0},{8,12},{12,8},{16,20},{20,16},{24,28},{28,24},{1,5},{5... | collective-permute-start | bytes 25165832 | tf_op jit(solution)/shard_map/ppermute | solution.py:249
  833.8 93.1 %collective-permute-start.10 = (bf16[1024,2048]{1,0:T(8,128)(2,1)}, bf16[1024,2048]{1,0:T(8,128)(2,1)}, u32[]{:S(2)}, u32[]{:S(2)}) collective-permute-start(bf16[1024,2048]{1,0:T(8,128)(2,1)} %slice.200), channel_id=1, source_target_pairs={{0,16},{4,20},{8,24},{12,28},{16,0},{20,4},{24,8},{28,12},{1,17},{... | collective-permute-start | bytes 12582920 | tf_op jit(solution)/shard_map/ppermute | solution.py:249
  846.3 93.8 %collective-permute-start.13 = (bf16[1024,2048]{1,0:T(8,128)(2,1)}, bf16[1024,2048]{1,0:T(8,128)(2,1)}, u32[]{:S(2)}, u32[]{:S(2)}) collective-permute-start(bf16[1024,2048]{1,0:T(8,128)(2,1)} %slice.204), channel_id=1, source_target_pairs={{0,8},{4,12},{8,0},{12,4},{16,24},{20,28},{24,16},{28,20},{1,9},{5... | collective-permute-start | bytes 12582920 | tf_op jit(solution)/shard_map/ppermute | solution.py:249
  865.7 74.4 %slice-start.2 = ((s8[8388608]{0:T(1024)(128)(4,1)}), s8[4194304]{0:T(1024)(128)(4,1)S(1)}, s32[]{:S(2)}) async-start(s8[8388608]{0:T(1024)(128)(4,1)} %bitcast.123), calls=%async_computation.24 | async-start | bytes 8388608
  874.2 65.9 %slice-start.3 = ((s8[8388608]{0:T(1024)(128)(4,1)}), s8[4194304]{0:T(1024)(128)(4,1)S(1)}, s32[]{:S(2)}) async-start(s8[8388608]{0:T(1024)(128)(4,1)} %bitcast.123), calls=%async_computation.25 | async-start | bytes 8388608
  874.2 163.0 %collective-permute-start.6 = (bf16[2048,2048]{1,0:T(8,128)(2,1)}, bf16[2048,2048]{1,0:T(8,128)(2,1)}, u32[]{:S(2)}, u32[]{:S(2)}) collective-permute-start(bf16[2048,2048]{1,0:T(8,128)(2,1)} %slice.194), channel_id=1, source_target_pairs={{0,4},{4,0},{8,12},{12,8},{16,20},{20,16},{24,28},{28,24},{1,5},{5... | collective-permute-start | bytes 25165832 | tf_op jit(solution)/shard_map/ppermute | solution.py:249
  933.7 50.2 %collective-permute-start.11 = (bf16[512,2048]{1,0:T(8,128)(2,1)}, bf16[512,2048]{1,0:T(8,128)(2,1)S(1)}, u32[]{:S(2)}, u32[]{:S(2)}) collective-permute-start(bf16[512,2048]{1,0:T(8,128)(2,1)} %slice.202), channel_id=1, source_target_pairs={{0,8},{4,12},{8,0},{12,4},{16,24},{20,28},{24,16},{28,20},{1,9},{5... | collective-permute-start | bytes 6291464 | tf_op jit(solution)/shard_map/ppermute | solution.py:249
  986.1 283.5 %reduce-scatter.16.cloned.1.call-start = ((), (), s32[]{:S(2)}) async-start(), calls=%async_computation.18 | async-start | bytes 2621440 | tf_op jit(solution)/shard_map/reduce_scatter | solution.py:386
  986.1 48.8 %collective-permute-start.14 = (bf16[512,2048]{1,0:T(8,128)(2,1)}, bf16[512,2048]{1,0:T(8,128)(2,1)S(1)}, u32[]{:S(2)}, u32[]{:S(2)}) collective-permute-start(bf16[512,2048]{1,0:T(8,128)(2,1)} %slice.206), channel_id=1, source_target_pairs={{0,16},{4,20},{8,24},{12,28},{16,0},{20,4},{24,8},{28,12},{1,17},{... | collective-permute-start | bytes 6291464 | tf_op jit(solution)/shard_map/ppermute | solution.py:249
  994.4 40.6 %copy-start.22 = (bf16[1024,2048]{1,0:T(8,128)(2,1)S(1)}, bf16[1024,2048]{1,0:T(8,128)(2,1)}, u32[]{:S(2)}) copy-start(bf16[1024,2048]{1,0:T(8,128)(2,1)} %copy-done.21) | copy-start | bytes 12582916
  1000.0 123.0 %collective-permute-start.4 = (bf16[1024,2048]{1,0:T(8,128)(2,1)}, bf16[1024,2048]{1,0:T(8,128)(2,1)}, u32[]{:S(2)}, u32[]{:S(2)}) collective-permute-start(bf16[1024,2048]{1,0:T(8,128)(2,1)} %slice.190), channel_id=1, source_target_pairs={{0,16},{4,20},{8,24},{12,28},{16,0},{20,4},{24,8},{28,12},{1,17},{... | collective-permute-start | bytes 12582920 | tf_op jit(solution)/shard_map/ppermute | solution.py:249
  1037.1 237.1 %reduce-scatter.10.cloned.1.call-start = ((), (), s32[]{:S(2)}) async-start(), calls=%async_computation.15 | async-start | bytes 2621440 | tf_op jit(solution)/shard_map/reduce_scatter | solution.py:386
  1049.9 135.8 %collective-permute-start.7 = (bf16[1024,2048]{1,0:T(8,128)(2,1)}, bf16[1024,2048]{1,0:T(8,128)(2,1)}, u32[]{:S(2)}, u32[]{:S(2)}) collective-permute-start(bf16[1024,2048]{1,0:T(8,128)(2,1)} %slice.196), channel_id=1, source_target_pairs={{0,8},{4,12},{8,0},{12,4},{16,24},{20,28},{24,16},{28,20},{1,9},{5... | collective-permute-start | bytes 12582920 | tf_op jit(solution)/shard_map/ppermute | solution.py:249
  1128.7 54.9 %collective-permute-start.5 = (bf16[512,2048]{1,0:T(8,128)(2,1)S(1)}, bf16[512,2048]{1,0:T(8,128)(2,1)S(1)}, u32[]{:S(2)}, u32[]{:S(2)}) collective-permute-start(bf16[512,2048]{1,0:T(8,128)(2,1)S(1)} %slice.192), channel_id=1, source_target_pairs={{0,8},{4,12},{8,0},{12,4},{16,24},{20,28},{24,16},{28,20},{1,9},{5... | collective-permute-start | bytes 6291464 | tf_op jit(solution)/shard_map/ppermute | solution.py:249
  1194.6 47.8 %collective-permute-start.8 = (bf16[512,2048]{1,0:T(8,128)(2,1)}, bf16[512,2048]{1,0:T(8,128)(2,1)}, u32[]{:S(2)}, u32[]{:S(2)}) collective-permute-start(bf16[512,2048]{1,0:T(8,128)(2,1)} %slice.198), channel_id=1, source_target_pairs={{0,16},{4,20},{8,24},{12,28},{16,0},{20,4},{24,8},{28,12},{1,17},{... | collective-permute-start | bytes 6291464 | tf_op jit(solution)/shard_map/ppermute | solution.py:249
  1196.4 42.5 %all-to-all-start.1 = ((f32[8,4,4,256]{3,2,1,0:T(4,128)}), f32[8,4,4,256]{3,2,1,0:T(4,128)S(1)}, u32[]{:S(2)}, u32[]{:S(2)}) async-start(f32[8,4,4,256]{3,2,1,0:T(4,128)} %copy.89), calls=%async_computation.6 | async-start | bytes 262144 | tf_op jit(solution)/shard_map/all_to_all | solution.py:429
  1199.8 90.1 %reduce-scatter.12.cloned.1.call-start = ((), (), s32[]{:S(2)}) async-start(), calls=%async_computation.16 | async-start | bytes 2621440 | tf_op jit(solution)/shard_map/reduce_scatter | solution.py:386
  1238.9 28.9 %collective-permute-start.17 = (f32[8,4,256]{2,0,1:T(8,128)S(1)}, f32[8,4,256]{2,0,1:T(8,128)S(1)}, u32[]{:S(2)}, u32[]{:S(2)}) collective-permute-start(f32[8,4,256]{2,0,1:T(8,128)S(1)} %bitcast.147), channel_id=1, source_target_pairs={{0,3},{1,0},{2,1},{3,2},{4,7},{5,4},{6,5},{7,6},{8,11},{9,8},{10,9... | collective-permute-start | bytes 98312 | tf_op jit(solution)/shard_map/ppermute | solution.py:268
  1240.3 27.6 %collective-permute-start.15 = (f32[8,4,256]{2,0,1:T(8,128)S(1)}, f32[8,4,256]{2,0,1:T(8,128)S(1)}, u32[]{:S(2)}, u32[]{:S(2)}) collective-permute-start(f32[8,4,256]{2,0,1:T(8,128)S(1)} %bitcast.146), channel_id=1, source_target_pairs={{0,1},{1,2},{2,3},{3,0},{4,5},{5,6},{6,7},{7,4},{8,9},{9,10},{10,1... | collective-permute-start | bytes 98312 | tf_op jit(solution)/shard_map/ppermute | solution.py:268
  1241.0 26.8 %collective-permute-start.16 = (f32[8,4,256]{2,0,1:T(8,128)S(1)}, f32[8,4,256]{2,0,1:T(8,128)S(1)}, u32[]{:S(2)}, u32[]{:S(2)}) collective-permute-start(f32[8,4,256]{2,0,1:T(8,128)S(1)} %bitcast.145), channel_id=1, source_target_pairs={{0,2},{1,3},{2,0},{3,1},{4,6},{5,7},{6,4},{7,5},{8,10},{9,11},{10,... | collective-permute-start | bytes 98312 | tf_op jit(solution)/shard_map/ppermute | solution.py:268
  1246.8 129.3 %all-gather.17.cloned.1.call-start = ((), (), s32[]{:S(2)}) async-start(), calls=%async_computation.19 | async-start | bytes 5242880 | tf_op jit(solution)/shard_map/all_gather | solution.py:441
  1246.9 21.1 %copy-start.26 = (f32[32,256]{1,0:T(8,128)S(1)}, f32[32,256]{1,0:T(8,128)}, u32[]{:S(2)}) copy-start(f32[32,256]{1,0:T(8,128)} %copy-done.25) | copy-start | bytes 98308
  1246.9 21.1 %copy-start.29 = (pred[32,256]{1,0:T(8,128)(4,1)S(1)}, pred[32,256]{1,0:T(8,128)(4,1)}, u32[]{:S(2)}) copy-start(pred[32,256]{1,0:T(8,128)(4,1)} %get-tuple-element.66) | copy-start | bytes 24580
  1246.9 22.7 %copy-start.13 = (bf16[256,2048]{1,0:T(8,128)(2,1)S(1)}, bf16[256,2048]{1,0:T(8,128)(2,1)}, u32[]{:S(2)}) copy-start(bf16[256,2048]{1,0:T(8,128)(2,1)} %param.19) | copy-start | bytes 3145732
  1246.9 22.7 %copy-start.31 = (f32[2048]{0:T(1024)S(1)}, f32[2048]{0:T(1024)}, u32[]{:S(2)}) copy-start(f32[2048]{0:T(1024)} %copy-done.30) | copy-start | bytes 24580
  1246.9 22.7 %copy-start.44 = (f32[256]{0:T(256)S(1)}, f32[256]{0:T(256)}, u32[]{:S(2)}) copy-start(f32[256]{0:T(256)} %copy-done.43) | copy-start | bytes 3076
  1274.2 43.3 %collective-permute-start.26 = (f32[33,2048]{1,0:T(8,128)}, f32[33,2048]{1,0:T(8,128)}, u32[]{:S(2)}, u32[]{:S(2)}) collective-permute-start(f32[33,2048]{1,0:T(8,128)} %pad_maximum_fusion.2), channel_id=1, source_target_pairs={{0,4},{4,0},{8,12},{12,8},{16,20},{20,16},{24,28},{28,24},{1,5},{5... | collective-permute-start | bytes 811016 | tf_op jit(solution)/shard_map/ppermute | solution.py:249
  1295.8 258.8 %reduce-scatter.20.cloned.1.call-start = ((), (), s32[]{:S(2)}) async-start(), calls=%async_computation.21 | async-start | bytes 4718592 | tf_op jit(solution)/shard_map/reduce_scatter | solution.py:447
  1318.5 22.2 %collective-permute-start.27 = (f32[33,2048]{1,0:T(8,128)S(1)}, f32[33,2048]{1,0:T(8,128)S(1)}, u32[]{:S(2)}, u32[]{:S(2)}) collective-permute-start(f32[33,2048]{1,0:T(8,128)S(1)} %fusion.29), channel_id=1, source_target_pairs={{0,8},{4,12},{8,0},{12,4},{16,24},{20,28},{24,16},{28,20},{1,9},{5... | collective-permute-start | bytes 811016 | tf_op jit(solution)/shard_map/ppermute | solution.py:249
  1340.8 66.8 %collective-permute-start.28 = (f32[33,2048]{1,0:T(8,128)S(1)}, f32[33,2048]{1,0:T(8,128)S(1)}, u32[]{:S(2)}, u32[]{:S(2)}) collective-permute-start(f32[33,2048]{1,0:T(8,128)S(1)} %add.283), channel_id=1, source_target_pairs={{0,16},{4,20},{8,24},{12,28},{16,0},{20,4},{24,8},{28,12},{1,17},{... | collective-permute-start | bytes 811016 | tf_op jit(solution)/shard_map/ppermute | solution.py:249
  1385.5 173.9 %reduce-scatter.18.cloned.1.call-start = ((), (), s32[]{:S(2)}) async-start(), calls=%async_computation.20 | async-start | bytes 5242880 | tf_op jit(solution)/shard_map/reduce_scatter | solution.py:450
  1407.7 92.6 %collective-permute-start.29 = (f32[33,2048]{1,0:T(8,128)S(1)}, f32[33,2048]{1,0:T(8,128)S(1)}, u32[]{:S(2)}, u32[]{:S(2)}) collective-permute-start(f32[33,2048]{1,0:T(8,128)S(1)} %add.284), channel_id=1, source_target_pairs={{0,1},{1,0},{2,3},{3,2},{4,5},{5,4},{6,7},{7,6},{8,9},{9,8},{10,11... | collective-permute-start | bytes 811016 | tf_op jit(solution)/shard_map/ppermute | solution.py:249
  1470.1 3.0 collective-permute-start.18
  1473.1 4.8 collective-permute-start.19
  1474.6 31.3 %slice-start.8 = ((s8[6291456]{0:T(1024)(128)(4,1)}), s8[4194304]{0:T(1024)(128)(4,1)S(1)}, s32[]{:S(2)}) async-start(s8[6291456]{0:T(1024)(128)(4,1)} %bitcast.129), calls=%async_computation.30 | async-start | bytes 8388608
  1477.7 26.5 %collective-permute-start.23 = (bf16[1024,1280]{1,0:T(8,128)(2,1)S(1)}, bf16[1024,1280]{1,0:T(8,128)(2,1)S(1)}, u32[]{:S(2)}, u32[]{:S(2)}) collective-permute-start(bf16[1024,1280]{1,0:T(8,128)(2,1)S(1)} %bitcast.137), channel_id=1, source_target_pairs={{0,4},{4,0},{8,12},{12,8},{16,20},{20,16},{24,28},{28,24},{1,5},{5... | collective-permute-start | bytes 7864328 | tf_op jit(solution)/shard_map/ppermute | solution.py:249
  1478.0 28.0 %slice-start.9 = ((s8[6291456]{0:T(1024)(128)(4,1)}), s8[2097152]{0:T(1024)(128)(4,1)S(1)}, s32[]{:S(2)}) async-start(s8[6291456]{0:T(1024)(128)(4,1)} %bitcast.129), calls=%async_computation.31 | async-start | bytes 4194304
  1478.0 24.4 %collective-permute-start.20 = (f32[3,2048]{1,0:T(4,128)S(1)}, f32[3,2048]{1,0:T(4,128)S(1)}, u32[]{:S(2)}, u32[]{:S(2)}) collective-permute-start(f32[3,2048]{1,0:T(4,128)S(1)} %fusion.73), channel_id=1, source_target_pairs={{0,16},{4,20},{8,24},{12,28},{16,0},{20,4},{24,8},{28,12},{1,17},{... | collective-permute-start | bytes 73736 | tf_op jit(solution)/shard_map/ppermute | solution.py:249
  1500.3 39.3 %collective-permute-start.30 = (f32[33,2048]{1,0:T(8,128)S(1)}, f32[33,2048]{1,0:T(8,128)S(1)}, u32[]{:S(2)}, u32[]{:S(2)}) collective-permute-start(f32[33,2048]{1,0:T(8,128)S(1)} %add.285), channel_id=1, source_target_pairs={{0,2},{1,3},{2,0},{3,1},{4,6},{5,7},{6,4},{7,5},{8,10},{9,11},{10,... | collective-permute-start | bytes 811016 | tf_op jit(solution)/shard_map/ppermute | solution.py:249
  1502.4 37.3 %collective-permute-start.21 = (f32[3,2048]{1,0:T(4,128)S(1)}, f32[3,2048]{1,0:T(4,128)S(1)}, u32[]{:S(2)}, u32[]{:S(2)}) collective-permute-start(f32[3,2048]{1,0:T(4,128)S(1)} %add.275), channel_id=1, source_target_pairs={{0,1},{1,0},{2,3},{3,2},{4,5},{5,4},{6,7},{7,6},{8,9},{9,8},{10,11... | collective-permute-start | bytes 73736 | tf_op jit(solution)/shard_map/ppermute | solution.py:249
  1505.1 34.6 %collective-permute-start.24 = (bf16[512,1280]{1,0:T(8,128)(2,1)S(1)}, bf16[512,1280]{1,0:T(8,128)(2,1)S(1)}, u32[]{:S(2)}, u32[]{:S(2)}) collective-permute-start(bf16[512,1280]{1,0:T(8,128)(2,1)S(1)} %slice.213), channel_id=1, source_target_pairs={{0,8},{4,12},{8,0},{12,4},{16,24},{20,28},{24,16},{28,20},{1,9},{5... | collective-permute-start | bytes 3932168 | tf_op jit(solution)/shard_map/ppermute | solution.py:249
  1539.7 7.0 collective-permute-start.22
  1540.2 13.2 collective-permute-start.25
  (51 other events, 375.9 us)
Sparse Core Ops, SparseCore 0:
  12.7 83.4 all-gather.6
  132.3 75.2 reduce-scatter.7
  211.1 115.3 all-gather.10
  330.4 113.0 all-gather.8
  446.7 113.0 all-gather.14
  563.7 113.0 all-gather.12
  986.2 41.7 reduce-scatter.13
  1037.3 41.7 reduce-scatter.15
  1185.8 41.8 reduce-scatter.9
  1247.0 42.9 reduce-scatter.11
  1296.0 80.0 all-gather.16
  1385.6 49.8 reduce-scatter.19
  1473.2 86.1 reduce-scatter.17

commit v2 on v1

--- a/solution.py
+++ b/solution.py
@@ -1,5 +1,5 @@
 import functools
-
+import itertools
 import jax
 import jax.numpy as jnp
 from jax import lax
@@ -179,58 +179,106 @@
 
 
 def experts_kernel(
-    table, x_ref, g_ref, gate_ref, spread_ref, wg_ref, wu_ref, wd_ref, hw_ref, gb_ref, ub_ref, score_ref, back_ref
+    held, order, x_ref, pre_ref, gate_ref, spread_ref, wg_ref, wu_ref, *refs
 ):
+    hw_ref, gb_ref, ub_ref, score_ref, back_ref = refs[held:]
     x = x_ref[...]
     gate_pre = dot(x, wg_ref[...])
     sigma = 1.0 / (1.0 + jnp.exp(-gate_pre))
     active = gate_pre * sigma
     up_pre = dot(x, wu_ref[...])
-    pre = dot(g_ref[...], wd_ref[...], NT)
+    pre = pre_ref[...].reshape(gate_pre.shape)
     hidden = active * up_pre
     score_ref[...] = dot(spread_ref[...], (hidden * pre).astype(bf16), NT)
     weight = dot(gate_ref[...], spread_ref[...])
-    hw_ref[...] = (hidden * weight).astype(bf16)
+    hw_ref[...] = (hidden * weight).astype(bf16).reshape(hw_ref.shape)
     hidden_grad = pre * weight
     up_back = (hidden_grad * active).astype(bf16)
     gate_back = (hidden_grad * up_pre * sigma * (1.0 + gate_pre * (1.0 - sigma))).astype(bf16)
     gb_ref[...] = gate_back
     ub_ref[...] = up_back
-    back_ref[...] = (dot(gate_back, wg_ref[...], NT) + dot(up_back, wu_ref[...], NT)).astype(bf16)
-
-
-def experts(order, x, g, gates, spread, gate_w, up_w, down_w, tile):
+    back = (dot(gate_back, wg_ref[...], NT) + dot(up_back, wu_ref[...], NT)).astype(bf16)
+    back_ref[...] = back
+
+
+def row_block(array, c):
+    _, members, _, piece, columns = array.shape
+    return pl.BlockSpec((1, members, 1, piece, columns), lambda j, order: (order[j], 0, c, 0, 0))
+
+
+def experts(order, c, x, pre, gates, spread, gate_w, up_w, held=()):
     rows, width = x.shape
+    tile = rows // pre.shape[0]
     hidden = gate_w.shape[1]
     lanes = spread.shape[0]
+    steps = order.shape[0]
     at = lambda n: pl.BlockSpec((tile, n), lambda j, order: (order[j], 0))
     full = lambda shape: pl.BlockSpec(shape, lambda j, order: (0, 0), pipeline_mode=pl.Buffered(1))
     return pl.pallas_call(
-        experts_kernel,
+        functools.partial(experts_kernel, len(held)),
         grid_spec=pltpu.PrefetchScalarGridSpec(
             num_scalar_prefetch=1,
-            grid=(rows // tile,),
+            grid=(steps,),
             in_specs=[
-                at(width), at(width), at(lanes), full((lanes, hidden)),
-                full((width, hidden)), full((width, hidden)), full((hidden, width)),
+                at(width), row_block(pre, c), at(lanes), full((lanes, hidden)), full((width, hidden)), full((width, hidden)),
+                *[pl.BlockSpec(memory_space=pl.ANY)] * len(held),
             ],
             out_specs=[
-                at(hidden), at(hidden), at(hidden),
-                pl.BlockSpec((lanes, tile), lambda j, order: (0, order[j])),
+                row_block(pre, c), at(hidden), at(hidden), pl.BlockSpec((lanes, tile), lambda j, order: (0, order[j])),
                 pl.BlockSpec((tile, width), lambda j, order: (j, 0)),
             ],
         ),
         out_shape=[
-            jax.ShapeDtypeStruct((rows, hidden), bf16),
+            jax.ShapeDtypeStruct(pre.shape, bf16),
             jax.ShapeDtypeStruct((rows, hidden), bf16),
             jax.ShapeDtypeStruct((rows, hidden), bf16),
             jax.ShapeDtypeStruct((lanes, rows), f32),
-            jax.ShapeDtypeStruct((rows, width), bf16),
+            jax.ShapeDtypeStruct((steps * tile, width), bf16),
         ],
+        input_output_aliases={7 + i: output for i, (output, _) in enumerate(held)},
         compiler_params=pltpu.CompilerParams(vmem_limit_bytes=58 * MIB),
-        cost_estimate=pl.CostEstimate(flops=10 * rows * width * hidden, bytes_accessed=rows * width * 6 + rows * hidden * 6, transcendentals=rows * hidden),
+        cost_estimate=pl.CostEstimate(flops=8 * steps * tile * width * hidden, bytes_accessed=steps * tile * (width * 4 + hidden * 10), transcendentals=steps * tile * hidden),
         name="experts",
-    )(order, x, g, gates, spread, gate_w, up_w, down_w)
+    )(order, x, pre, gates, spread, gate_w, up_w, *[array for _, array in held])
+
+
+def outputs_kernel(half, order, h_ref, w_ref, far_ref, near_ref):
+    hidden = h_ref[...].reshape(far_ref.shape[0], w_ref.shape[0])
+    value = dot(hidden, w_ref[...]).astype(bf16)
+
+    @pl.when(pl.program_id(0) < half)
+    def _():
+        far_ref[...] = value
+
+    @pl.when(pl.program_id(0) >= half)
+    def _():
+        near_ref[...] = value
+
+
+def outputs(order, c, hidden_wt, down_w):
+    steps, members, _, piece, hidden = hidden_wt.shape
+    tile = members * piece
+    width = down_w.shape[1]
+    half = steps // 2
+    return pl.pallas_call(
+        functools.partial(outputs_kernel, half),
+        grid_spec=pltpu.PrefetchScalarGridSpec(
+            num_scalar_prefetch=1,
+            grid=(steps,),
+            in_specs=[
+                row_block(hidden_wt, c),
+                pl.BlockSpec((hidden, width), lambda j, order: (0, 0), pipeline_mode=pl.Buffered(1)),
+            ],
+            out_specs=[
+                pl.BlockSpec((tile, width), lambda j, order: (jnp.minimum(j, half - 1), 0)),
+                pl.BlockSpec((tile, width), lambda j, order: (jnp.maximum(j - half, 0), 0)),
+            ],
+        ),
+        out_shape=[jax.ShapeDtypeStruct((half * tile, width), bf16)] * 2,
+        compiler_params=pltpu.CompilerParams(vmem_limit_bytes=32 * MIB),
+        cost_estimate=pl.CostEstimate(flops=2 * steps * tile * width * hidden, bytes_accessed=steps * tile * (width + hidden) * 2, transcendentals=0),
+        name="outputs",
+    )(order, hidden_wt, down_w)
 
 
 TOPK = 8
@@ -253,10 +301,9 @@
     return [1 << k for k in range(size.bit_length() - 1)]
 
 
-def add_up(value):
-    for axis in ("expert", "tensor"):
-        for bit in bits_of(lax.axis_size(axis)):
-            value = value + hop(value, bit, axis)
+def add_up(value, axis):
+    for bit in bits_of(lax.axis_size(axis)):
+        value = value + hop(value, bit, axis)
     return value
 
 
@@ -276,12 +323,106 @@
     return order
 
 
-def scatter_sum(blocks, bits):
-    for bit in bits:
-        half = blocks.shape[0] // 2
-        moved = hop(blocks[:half], bit, "expert")
-        blocks = (blocks[half:].astype(f32) + moved.astype(f32)).astype(bf16)
-    return blocks
+class Exchange:
+    def __init__(self, far, near, bits):
+        self.moved = [hop(far, bits[0], "expert")]
+        self.near, self.rest = near, bits[1:]
+        self.left = [list(range(len(self.rest))) for _ in range(2)]
+        self.sides = None
+
+    def wait(self, behind):
+        if self.sides is None:
+            moved = after(self.moved, *behind) if behind else self.moved
+            rows, width = self.near.shape[0] >> len(self.rest), self.near.shape[1]
+            near, moved = self.near.reshape(-1, rows, width), moved[0].reshape(-1, rows, width)
+            spots = itertools.product(range(2), repeat=len(self.rest))
+            index = {spot: i for i, spot in enumerate(spots)}
+            self.sides = []
+            for part in (slice(0, rows // 2), slice(rows // 2, None)):
+                self.sides.append({spot: [near[i, part], moved[i, part]] for spot, i in index.items()})
+        else:
+            for number, (side, got) in enumerate(zip(self.sides, self.got)):
+                got = after(got, *behind) if behind else got
+                self.sides[number] = {spot: [*parts, got[i]] for i, (spot, parts) in enumerate(side.items())}
+
+    def send(self, *behind):
+        self.wait(behind)
+        sent, self.got = [], []
+        add = lambda parts: sum(p.astype(f32) for p in parts).astype(bf16)
+        for number, side in enumerate(self.sides):
+            at = len(self.left[number]) - 1 if number else 0
+            bit = self.rest[self.left[number].pop(at)]
+            spots = sorted({spot[:at] + spot[at + 1 :] for spot in side})
+            block = jnp.stack([add(side[spot[:at] + (0,) + spot[at:]]) for spot in spots])
+            self.got.append(hop(block, bit, "expert"))
+            sent.append(block)
+            self.sides[number] = {spot: side[spot[:at] + (1,) + spot[at:]] for spot in spots}
+        return sent
+
+    def total(self, *behind):
+        while any(self.left):
+            self.send()
+        self.wait(behind)
+        parts = [sum(p.astype(f32) for p in side[()]).astype(bf16) for side in self.sides]
+        return jnp.concatenate(parts, axis=0)
+
+
+def neighbours():
+    size = lax.axis_size("tensor")
+    up = lambda v: lax.ppermute(v, "tensor", [(i, (i + 1) % size) for i in range(size)])
+    down = lambda v: lax.ppermute(v, "tensor", [(i, (i - 1) % size) for i in range(size)])
+    return up, down
+
+
+def gather_line(block, behind=()):
+    size, me = lax.axis_size("tensor"), lax.axis_index("tensor")
+    if size != 4:
+        return lax.all_gather(block, "tensor", axis=0, tiled=True)
+    rows = block.shape[0]
+    cut = rows // 2
+    up, down = neighbours()
+    low, high = up(block), down(block)
+    if behind:
+        low, high = after((low, high), *behind)
+    far_low, far_high = up(low[:cut]), down(high[cut:])
+    whole = jnp.zeros((rows * size, block.shape[1]), block.dtype)
+    for part, member, shift in ((block, 0, 0), (low, 3, 0), (high, 1, 0), (far_low, 2, 0), (far_high, 2, cut)):
+        at = lax.rem(me + member, size) * rows + shift
+        whole = lax.dynamic_update_slice(whole, part, (at, 0))
+    return whole
+
+
+class Line:
+    def __init__(self, part):
+        self.size, self.me = lax.axis_size("tensor"), lax.axis_index("tensor")
+        self.part, self.rows = part, part.shape[0] // self.size
+        self.got = None
+
+    def of(self, member, start, end):
+        at = lax.rem(self.me + member, self.size) * self.rows
+        return lax.dynamic_slice_in_dim(self.part, at + start, end - start, 0)
+
+    def send(self, *behind):
+        cut, rows = self.rows // 2, self.rows
+        if self.size != 4:
+            return []
+        if behind:
+            self.got = after(self.got, *behind)
+        if self.got is None:
+            low, high = self.of(2, cut, rows), self.of(2, 0, cut)
+        else:
+            from_low, from_high = (part.astype(f32) for part in self.got)
+            low = jnp.concatenate([self.of(1, 0, cut), (self.of(1, cut, rows).astype(f32) + from_low).astype(bf16)])
+            high = jnp.concatenate([(self.of(3, 0, cut).astype(f32) + from_high).astype(bf16), self.of(3, cut, rows)])
+        up, down = neighbours()
+        self.got = up(low), down(high)
+        return [low, high]
+
+    def total(self, *behind):
+        if self.size != 4:
+            return lax.psum_scatter(self.part, "tensor", scatter_dimension=0, tiled=True).astype(f32)
+        low, high = after(self.got, *behind) if behind else self.got
+        return self.of(0, 0, self.rows).astype(f32) + low.astype(f32) + high.astype(f32)
 
 
 def local(
@@ -321,22 +462,37 @@
     total = n_expert * rows
     lanes = 8 * (-(-local_experts // 8))
 
+    gate_w = w_gate.transpose(1, 0, 2).reshape(width, hidden_loc)
+    up_w = w_up.transpose(1, 0, 2).reshape(width, hidden_loc)
+    down_w = w_down.reshape(hidden_loc, width)
+    spread = (jnp.arange(hidden_loc)[None, :] // quarter == jnp.arange(lanes)[:, None]).astype(bf16)
+
     hidden_f = hidden_in.astype(f32)
     attn_normed, attn_pull = jax.vjp(row_norm, hidden_f, attn_gain.astype(f32))
-    gathered = lax.all_gather(attn_normed.astype(bf16), "tensor", axis=0, tiled=True)
+    gathered = gather_line(attn_normed.astype(bf16))
     given = after(out_grad, gathered)
-
-    def spread_out(values, c):
-        return lax.all_gather(values[c * piece : (c + 1) * piece], both, axis=0, tiled=True)
 
     cosine, sine = rope_tables(group)
     q_gain, k_gain = query_gain.astype(f32)[None, :], key_gain.astype(f32)[None, :]
+    by_chunk = (n_expert, n_tensor, 1, piece, hidden_loc)
+    if chunks == 2:
+        gathered = after(gathered, gate_w, up_w)
     raw, queries, keys, values = project(gathered, w_qkv, q_gain, k_gain, cosine, sine, local_q, local_kv)
     mixed_all = attend(queries, keys, values.T, local_q, local_kv)
-    attn = lax.psum_scatter(
-        dot(mixed_all, w_out).astype(bf16), "tensor", scatter_dimension=0, tiled=True
-    )
-    middle = hidden_f + attn.astype(f32)
+    attn = mixed_all
+    if chunks == 2:
+        grad_line = [
+            gather_line(given[:piece], (queries,)),
+            gather_line(after(given[piece:], queries), (mixed_all,)),
+        ]
+        grad_all = [lax.all_gather(part, "expert", axis=0, tiled=True) for part in grad_line]
+        pre = [dot(part, down_w, NT).reshape(by_chunk) for part in grad_all]
+        attn = after(attn, *grad_line)
+    attn = Line(dot(attn, w_out).astype(bf16))
+    attn.send()
+    attn.send()
+    attn = attn.total()
+    middle = hidden_f + attn
     moe_normed, moe_pull = jax.vjp(row_norm, middle, moe_gain.astype(f32))
     moe_in = moe_normed.astype(bf16)
 
@@ -361,53 +517,65 @@
     gates_in = gates_in.transpose(3, 1, 0, 4, 2).reshape(chunks, total, local_experts)
     gates_in = jnp.pad(gates_in, ((0, 0), (0, 0), (0, lanes - local_experts))).astype(bf16)
 
-    gate_w = w_gate.transpose(1, 0, 2).reshape(width, hidden_loc)
-    up_w = w_up.transpose(1, 0, 2).reshape(width, hidden_loc)
-    down_w = w_down.reshape(hidden_loc, width)
-    spread = (jnp.arange(hidden_loc)[None, :] // quarter == jnp.arange(lanes)[:, None]).astype(bf16)
-
-    def run_experts(c, x_c, g_c):
-        way = [bits[0]] + (bits[1:] if c % 2 else bits[:0:-1])
-        order = place ^ jnp.array(step_order(way), jnp.int32)
-        hidden_wt, gate_back, up_back, score, back = experts(
-            order, x_c, g_c, gates_in[c], spread, gate_w, up_w, down_w, rows
-        )
-        return way, order, hidden_wt, gate_back, up_back, score, back
-
-    def out_of(hidden_wt, way, order):
-        blocks = hidden_wt.reshape(n_expert, rows, hidden_loc)
-        blocks = jnp.take(blocks, order, axis=0).reshape(total, hidden_loc)
-        return scatter_sum(dot(blocks, down_w).astype(bf16), way)
-
-    def weight_grads(x_c, g_c, hidden_wt, gate_back, up_back):
-        return dot(hidden_wt, g_c, TN), dot(x_c, gate_back, TN), dot(x_c, up_back, TN)
+    order = place ^ jnp.array(step_order(bits), jnp.int32)
 
     def own_rows(part):
         return lax.psum_scatter(part, "tensor", scatter_dimension=0, tiled=True)
 
+    def to_tokens(scores):
+        scores = jnp.stack([s[:local_experts] for s in scores])
+        scores = scores.reshape(chunks, local_experts, n_expert, n_tensor, piece)
+        scores = scores.transpose(2, 3, 1, 0, 4).reshape(n_expert, n_tensor, local_experts, tok_dev)
+        scores = lax.all_to_all(scores, "expert", 0, 0, tiled=True)
+        scores = sum(to_members(scores.transpose(1, 0, 2, 3)))
+        return jnp.where(keep, scores.reshape(n_experts, tok_dev), 0.0)
+
     if chunks == 2:
-        grad_all = [spread_out(given, c) for c in range(chunks)]
-        moe_all = [spread_out(moe_in, c) for c in range(chunks)]
-        done = [run_experts(c, moe_all[c], grad_all[c]) for c in range(chunks)]
-        back_own = [own_rows(scatter_sum(d[6], d[0])) for d in done]
-        scores = [d[5] for d in done]
-        out_own = [own_rows(out_of(after(d[2], done[1][6]), d[0], d[1])) for d in done]
-        grads = [
-            weight_grads(moe_all[c], grad_all[c], *done[c][2:5]) for c in range(chunks)
-        ]
-        grads = [sum(parts) for parts in zip(*grads)]
+        moe_line = [gather_line(moe_in[:piece], (pre[0],)), gather_line(moe_in[piece:])]
+        moe_line[0] = after(moe_line[0], grad_all[1])
+        moe_all = [lax.all_gather(part, "expert", axis=0, tiled=True) for part in moe_line]
+        front, rear = order[: n_expert // 2], order[n_expert // 2 :]
+        fixed = (spread, gate_w, up_w)
+        x_0 = after(moe_all[0], pre[1])
+        *kept_0, back_0 = experts(jnp.arange(n_expert, dtype=jnp.int32), 0, x_0, pre[0], gates_in[0], *fixed)
+        back_0 = lax.psum_scatter(back_0, "expert", scatter_dimension=0, tiled=True)
+        back_own = [own_rows(back_0)]
+        outs = [outputs(order, 0, kept_0[0], down_w)]
+        x_1 = after(moe_all[1], *outs[0])
+        *kept_1, near = experts(rear, 0, x_1, pre[1], gates_in[1], *fixed)
+        *kept_1, far = experts(front, 0, x_1, pre[1], gates_in[1], *fixed, list(enumerate(kept_1)))
+        back_1 = Exchange(far, near, bits)
+        outs.append(outputs(order, 0, kept_1[0], down_w))
+        sent = back_1.send(*outs[1])
+        scores = to_tokens(after([kept_0[3], kept_1[3]], *sent))
+        x_0 = after(moe_all[0], *sent)
+        gate_grad = dot(x_0, kept_0[1], TN)
+        sent = back_1.send(gate_grad, scores, back_0)
+        out_0, out_1 = (Exchange(*out, bits) for out in outs)
+        sent = out_0.send(*sent)
+        up_grad = dot(after(x_0, *sent), kept_0[2], TN)
+        back_1 = back_1.total(up_grad, back_own[0])
+        back_own.append(own_rows(back_1))
+        x_1, g_0 = after((moe_all[1], grad_all[0]), back_1)
+        gate_grad = gate_grad + dot(x_1, kept_1[1], TN)
+        down_grad = dot(kept_0[0].reshape(-1, hidden_loc), g_0, TN)
+        sent = out_0.send(gate_grad, down_grad)
+        back_own = after(back_own, *sent)
     else:
         def one_chunk(sums, c):
             x_c = lax.all_gather(lax.dynamic_slice_in_dim(moe_in, c * piece, piece, 0), both, axis=0, tiled=True)
             g_c = lax.all_gather(lax.dynamic_slice_in_dim(given, c * piece, piece, 0), both, axis=0, tiled=True)
-            way = bits
-            order = place ^ jnp.array(step_order(way), jnp.int32)
-            hidden_wt, gate_back, up_back, score, back = experts(
-                order, x_c, g_c, lax.dynamic_index_in_dim(gates_in, c, 0, keepdims=False), spread, gate_w, up_w, down_w, rows
-            )
-            parts = weight_grads(x_c, g_c, hidden_wt, gate_back, up_back)
+            gates_c = lax.dynamic_index_in_dim(gates_in, c, 0, keepdims=False)
+            pre = dot(g_c, down_w, NT).reshape(n_expert, n_tensor, 1, piece, hidden_loc)
+            given_c = (0, x_c, pre, gates_c, spread, gate_w, up_w)
+            *kept, far = experts(order[: n_expert // 2], *given_c)
+            *kept, near = experts(order[n_expert // 2 :], *given_c, list(enumerate(kept)))
+            hw, gate_back, up_back, score = kept
+            parts = (dot(hw.reshape(-1, hidden_loc), g_c, TN), dot(x_c, gate_back, TN), dot(x_c, up_back, TN))
             sums = tuple(a + b for a, b in zip(sums, parts))
-            return sums, (own_rows(scatter_sum(back, way)), score, own_rows(out_of(hidden_wt, way, order)))
+            back = own_rows(Exchange(far, near, bits).total())
+            out = own_rows(Exchange(*outputs(order, 0, hw, down_w), bits).total())
+            return sums, (back, score, out)
 
         zeros = (
             jnp.zeros((hidden_loc, width), f32),
@@ -415,22 +583,10 @@
             jnp.zeros((width, hidden_loc), f32),
         )
         grads, (back_own, scores, out_own) = lax.scan(one_chunk, zeros, jnp.arange(chunks))
-    grad_down = grads[0].reshape(local_experts, quarter, width)
-    grad_gate, grad_up = (
-        part.reshape(width, local_experts, quarter).transpose(1, 0, 2) for part in grads[1:]
-    )
+        scores = to_tokens(scores)
+        moe_out = jnp.concatenate(list(out_own), axis=0)
     moe_back = jnp.concatenate(list(back_own), axis=0).astype(f32)
-    moe_out = jnp.concatenate(list(out_own), axis=0).astype(f32)
-
-    scores = jnp.stack([s[:local_experts] for s in scores]).reshape(
-        chunks, local_experts, n_expert, n_tensor, piece
-    )
-    scores = scores.transpose(2, 3, 1, 0, 4).reshape(n_expert, n_tensor, local_experts, tok_dev)
-    scores = lax.all_to_all(scores, "expert", 0, 0, tiled=True)
-    scores = sum(to_members(scores.transpose(1, 0, 2, 3)))
-    scores = jnp.where(keep, scores.reshape(n_experts, tok_dev), 0.0)
-
-    layer_out = (middle + moe_out).astype(bf16)
+
     inner_gate = jnp.sum(gates * scores, axis=0, keepdims=True)
     logit_grad = (gates * (scores - inner_gate)).astype(bf16)
     router_grad = dot(logit_grad, moe_in)
@@ -439,40 +595,68 @@
     middle_grad = out_grad.astype(f32) + middle_part
 
     middle_all = lax.all_gather(middle_grad.astype(bf16), "tensor", axis=0, tiled=True)
+    if chunks == 2:
+        sent = out_1.send(middle_grad)
+        x_1, g_1 = after((moe_all[1], grad_all[1]), *sent)
+        up_grad = up_grad + dot(x_1, kept_1[2], TN)
+        out_0 = out_0.total(up_grad)
+        down_grad = down_grad + dot(kept_1[0].reshape(-1, hidden_loc), after(g_1, out_0), TN)
+        sent = out_1.send(down_grad)
+        middle_all = after(middle_all, *sent)
     mixed_grad = dot(middle_all, w_out, NT).astype(bf16)
+    out_weight_grad = dot(middle_all, mixed_all, TN).astype(bf16)
+    mixed_grad, out_weight_grad = lax.optimization_barrier((mixed_grad, out_weight_grad))
+    if chunks == 2:
+        out_1 = out_1.total(out_weight_grad)
+        mixed_grad = after(mixed_grad, out_1)
+    grad_out = lax.psum_scatter(out_weight_grad, "expert", scatter_dimension=0, tiled=True)
     dq, dk, dv, query_gain_grad, key_gain_grad = attend_back(
         queries, mixed_grad, raw, keys, keys.T, values, q_gain, k_gain, cosine, sine, local_q, local_kv
     )
-    out_weight_grad = dot(mixed_all, middle_all, TN).astype(bf16)
-    grad_out = lax.psum_scatter(out_weight_grad, "expert", scatter_dimension=1, tiled=True).astype(f32)
     qkv_grad = jnp.concatenate([dq, dk, dv], axis=1)
+    if chunks == 2:
+        out_own = [own_rows(part) for part in (out_0, out_1)]
+        qkv_grad = after(qkv_grad, *out_own)
+        moe_out = jnp.concatenate(out_own, axis=0)
     normed_part = dot(qkv_grad, w_qkv, NT)
-    normed_grad = lax.psum_scatter(
-        normed_part.astype(bf16), "tensor", scatter_dimension=0, tiled=True
-    ).astype(f32)
+    normed_low = normed_part.astype(bf16)
+    normed_line = Line(normed_low)
+    sent = normed_line.send()
+    weight_grad = dot(after(gathered, *sent), qkv_grad, TN).astype(bf16)
     attn_gain_grad = jnp.sum(normed_part * gathered.astype(f32), axis=0) / attn_gain.astype(f32)
-    qkv_weight_grad = dot(gathered, qkv_grad, TN).astype(bf16)
-    order = place ^ jnp.array(step_order(bits), jnp.int32)
-    blocks = jnp.take(qkv_weight_grad.reshape(n_expert, -1, w_qkv.shape[1]), order, axis=0)
-    grad_qkv = scatter_sum(blocks.reshape(qkv_weight_grad.shape), bits).astype(f32)
+    gain_rows = [attn_gain_grad[None, :], moe_gain_grad[None, :]]
+    gain_rows += [jnp.pad(part, ((0, 0), (0, width - HD))) for part in (query_gain_grad, key_gain_grad)]
+    small = add_up(jnp.concatenate([router_grad, *gain_rows], axis=0), "expert")
+    blocks = weight_grad.reshape(n_expert, -1, weight_grad.shape[1])
+    blocks = [lax.dynamic_index_in_dim(blocks, order[r], 0, keepdims=False) for r in range(n_expert)]
+    far, near = (
+        jnp.concatenate(part, axis=0) for part in (blocks[: n_expert // 2], blocks[n_expert // 2 :])
+    )
+    grad_qkv = Exchange(far, near, bits)
+    sent = normed_line.send(small, far, near)
+    small = add_up(after(small, *sent), "tensor") if sent else add_up(small, "tensor")
+    sent = sum([grad_qkv.send(*sent) for _ in bits[1:]], [])
+    grad_qkv = grad_qkv.total().astype(f32)
+    normed_grad = normed_line.total(*sent)
+    layer_out = (middle + moe_out.astype(f32)).astype(bf16)
+    if chunks == 2:
+        grads = [down_grad, gate_grad, up_grad]
+    grad_down = grads[0].reshape(local_experts, quarter, width)
+    grad_gate, grad_up = (
+        part.reshape(width, local_experts, quarter).transpose(1, 0, 2) for part in grads[1:]
+    )
     hidden_part, _ = attn_pull(normed_grad)
     input_grad = middle_grad + hidden_part
-    small = jnp.concatenate(
-        [attn_gain_grad[None, :], jnp.pad(query_gain_grad, ((0, 0), (0, width - HD))), jnp.pad(key_gain_grad, ((0, 0), (0, width - HD)))],
-        axis=0,
-    )
-    small = add_up(small)
-    router_sum = add_up(jnp.concatenate([router_grad, moe_gain_grad[None, :]], axis=0))
     return (
         layer_out,
         input_grad,
-        small[0],
-        small[1, :HD],
-        small[2, :HD],
+        small[n_experts],
+        small[n_experts + 2, :HD],
+        small[n_experts + 3, :HD],
         grad_qkv,
-        grad_out,
-        router_sum[n_experts],
-        router_sum[:n_experts].T,
+        grad_out.astype(f32).T,
+        small[n_experts + 1],
+        small[:n_experts].T,
         grad_gate,
         grad_up,
         grad_down,

time: 1590 us -> 1110 us (0.70)
  waiting for transfers between devices: 856 us -> 332 us
  starting transfers between devices: 36.5 us -> 94.7 us
  local copies, waits for them, and re-layouts: 122 us -> 103 us
    all_gather x5 -> x4, waiting for transfers between devices: 408 us -> 9.44 us  [local(): lax.all_gather(part, 'expert', axis=0, tiled=True)]
    ppermute x0 -> x28, waiting for transfers between devices: none -> 185 us  [the longest x14 97.1 us: neighbours(): lax.ppermute(v, 'tensor', [(i, (i - 1) % size) for i in range(size)])]
    ppermute x25, waiting for transfers between devices: 278 us -> 108 us  [hop(): return lax.ppermute(block, axis, [(i, i ^ bit) for i in range(size)])]
    reduce_scatter x3 -> x2, waiting for transfers between devices: 75.6 us -> 0.01 us  [the longest x1 0.01 us: local(): back_0 = lax.psum_scatter(back_0, 'expert', scatter_dimension=0, tiled=True)]
    ppermute x0 -> x28, starting transfers between devices: none -> 45.2 us  [the longest x14 32.8 us: neighbours(): lax.ppermute(v, 'tensor', [(i, (i - 1) % size) for i in range(size)])]
    slice x21 -> x17, local copies, waits for them, and re-layouts: 55.3 us -> 11.2 us  [the longest x10 6.8 us: gather_line(): far_low, far_high = (up(low[:cut]), down(high[cut:]))]
    all_to_all x1, waiting for transfers between devices: 38.9 us -> 5.39 us  [to_tokens(): scores = lax.all_to_all(scores, 'expert', 0, 0, tiled=True)]
    all_gather x1, waiting for transfers between devices: 33.8 us -> 1.52 us  [local(): lax.all_gather(middle_grad.astype(bf16), 'tensor', axis=0, tiled=True)]
  transfers between devices with their start and end apart: 46 -> 72, of which waited for: 20 -> 37; matrix products, arithmetic and copies ran while one was open for 25% -> 34% of each run, Pallas kernels for 13% -> 20%
where the time goes in v2:
time: 1110 us; the launch traced here: 1100 us
  waiting for transfers between devices  332 us (30%)
  Pallas kernels  225 us (20%)
  matrix products  213 us (19%)
  local copies, waits for them, and re-layouts  103 us (9%)
  other arithmetic  102 us (9%)
  starting transfers between devices  94.7 us (9%)
  between operations  31 us (3%)
    dot_general x16, matrix products, dot(): lax.dot_general(a, b, (contract, ((), ())), preferred_element_type=f32)  213 us
    pallas_call x3, Pallas kernels, experts(): pl.pallas_call(functools.partial(experts_kernel, len(held)), grid_spec=pl...  140 us
    ppermute x25, waiting for transfers between devices, hop(): return lax.ppermute(block, axis, [(i, i ^ bit) for i in range(size)])  108 us
    ppermute x14, waiting for transfers between devices, neighbours(): lax.ppermute(v, 'tensor', [(i, (i - 1) % size) for i in range(size)])  97.1 us
    ppermute x14, waiting for transfers between devices, neighbours(): lax.ppermute(v, 'tensor', [(i, (i + 1) % size) for i in range(size)])  88 us
    pallas_call x2, Pallas kernels, outputs(): pl.pallas_call(functools.partial(outputs_kernel, half), grid_spec=pltpu.P...  36.1 us
    convert_element_type x8, other arithmetic, send(): add = lambda parts: sum((p.astype(f32) for p in parts)).astype(bf16)  33.3 us
    ppermute x14, starting transfers between devices, neighbours(): lax.ppermute(v, 'tensor', [(i, (i - 1) % size) for i in range(size)])  32.8 us
  transfers between devices with their start and end apart: 72, of which 37 were waited for; matrix products, arithmetic and copies ran while one was open for 34% of the time, Pallas kernels for 20%

profile of v2, /device:TPU:0, one launch (start us, length us, event | category | flops | bytes accessed | tf_op | source)
XLA Modules:
  0.0 1101.3 jit_solution(14982618359218755895)
XLA Ops:
  22.3 21.2 %collective-permute-done = bf16[256,2048]{1,0:T(8,128)(2,1)S(1)} collective-permute-done((bf16[256,2048]{1,0:T(8,128)(2,1)}, bf16[256,2048]{1,0:T(8,128)(2,1)S(1)}, u32[]{:S(2)}, u32[]{:S(2)}) %collective-permute-start) | collective-permute-done | bytes 1048608 | tf_op jit(solution)/shard_map/ppermute | solution.py:372
  44.4 20.4 %collective-permute-done.1 = bf16[256,2048]{1,0:T(8,128)(2,1)} collective-permute-done((bf16[256,2048]{1,0:T(8,128)(2,1)}, bf16[256,2048]{1,0:T(8,128)(2,1)}, u32[]{:S(2)}, u32[]{:S(2)}) %collective-permute-start.1) | collective-permute-done | bytes 1048608 | tf_op jit(solution)/shard_map/ppermute | solution.py:373
  72.4 7.6 collective-permute-done.2
  81.9 5.7 collective-permute-done.3
  95.6 9.9 project.1
  108.9 8.1 collective-permute-done.5
  124.9 8.6 collective-permute-done.6
  139.7 11.7 %attend.1 = bf16[1024,1024]{1,0:T(8,128)(2,1)S(1)} custom-call(bf16[1024,1024]{1,0:T(8,128)(2,1)S(1)} %copy-done.15, bf16[1024,128]{1,0:T(8,128)(2,1)S(1)} %get-tuple-element.95.k_ref, bf16[128,1024]{1,0:T(8,128)(2,1)S(1)} %bitcast.174), custom_call_target="tpu_custom_call" | custom-call | flops 3221225472 | bytes 4194304 | tf_op jit(solution)/shard_map/attend/pallas_call | solution.py:88
  152.8 6.9 collective-permute-done.8
  175.5 8.8 convolution_convert_fusion.2
  188.8 22.3 %collective-permute-done.14 = bf16[128,2048]{1,0:T(8,128)(2,1)} collective-permute-done((bf16[128,2048]{1,0:T(8,128)(2,1)}, bf16[128,2048]{1,0:T(8,128)(2,1)}, u32[]{:S(2)}, u32[]{:S(2)}) %collective-permute-start.14) | collective-permute-done | bytes 524320 | tf_op jit(solution)/shard_map/ppermute | solution.py:373
  215.9 21.7 %collective-permute-done.15 = bf16[256,2048]{1,0:T(8,128)(2,1)S(1)} collective-permute-done((bf16[256,2048]{1,0:T(8,128)(2,1)S(1)}, bf16[256,2048]{1,0:T(8,128)(2,1)S(1)}, u32[]{:S(2)}, u32[]{:S(2)}) %collective-permute-start.15) | collective-permute-done | bytes 1048608 | tf_op jit(solution)/shard_map/ppermute | solution.py:373
  237.6 23.7 %collective-permute-done.13 = bf16[256,2048]{1,0:T(8,128)(2,1)S(1)} collective-permute-done((bf16[256,2048]{1,0:T(8,128)(2,1)S(1)}, bf16[256,2048]{1,0:T(8,128)(2,1)S(1)}, u32[]{:S(2)}, u32[]{:S(2)}) %collective-permute-start.13) | collective-permute-done | bytes 1048608 | tf_op jit(solution)/shard_map/ppermute | solution.py:372
  267.1 3.8 collective-permute-start.17
  270.9 20.5 %convolution_bitcast_fusion.1.pre_ref = f32[8,4,1,128,768]{4,3,2,1,0:T(8,128)} fusion(bf16[8,4,128,2048]{3,2,1,0:T(8,128)(2,1)} %bitcast.214, bf16[768,2048,1,1]{1,0,3,2:T(8,128)(2,1)} %bitcast.175), kind=kOutput, calls=%fused_computation.5 | convolution fusion | flops 12884901888 | bytes 32505856 | tf_op jit(solution)/shard_map/dot_general | solution.py:20
  299.1 4.4 collective-permute-done.18
  307.4 9.4 all-gather.8.cloned.1.call-done
  323.2 10.6 collective-permute-done.24
  333.9 9.9 collective-permute-done.25
  351.4 4.2 collective-permute-done.27
  357.9 5.6 convert_reduce_fusion
  369.3 4.8 all-to-all-done
  374.6 13.7 %collective-permute-start.22 = (bf16[8,4,256]{2,0,1:T(8,128)(2,1)S(1)}, bf16[8,4,256]{2,0,1:T(8,128)(2,1)S(1)}, u32[]{:S(2)}, u32[]{:S(2)}) collective-permute-start(bf16[8,4,256]{2,0,1:T(8,128)(2,1)S(1)} %copy.131), channel_id=1, source_target_pairs={{0,3},{1,0},{2,1},{3,2},{4,7},{5,4},{6,5},{7,6},{8,11},{9,8},{10,9... | collective-permute-start | bytes 49160 | tf_op jit(solution)/shard_map/ppermute | solution.py:315
  388.3 4.8 copy.95.wg_ref
  393.1 4.7 copy.96.wu_ref
  400.4 3.4 fusion.8
  403.8 19.9 %convolution_bitcast_fusion.pre_ref = f32[8,4,1,128,768]{4,3,2,1,0:T(8,128)} fusion(bf16[8,4,128,2048]{3,2,1,0:T(8,128)(2,1)} %bitcast.213, bf16[768,2048,1,1]{1,0,3,2:T(8,128)(2,1)S(1)} %bitcast.176), kind=kOutput, calls=%fused_computation.4 | convolution fusion | flops 12884901888 | bytes 32505856 | tf_op jit(solution)/shard_map/dot_general | solution.py:20
  424.2 65.8 %experts.3 = (bf16[8,4,1,128,768]{4,3,2,1,0:T(8,128)(2,1)}, bf16[4096,768]{1,0:T(8,128)(2,1)}, bf16[4096,768]{1,0:T(8,128)(2,1)}, f32[8,4096]{1,0:T(8,128)}, bf16[4096,2048]{1,0:T(8,128)(2,1)}) custom-call(s32[8]{0:T(128)} %iota.50.order, bf16[4096,2048]{1,0:T(8,128)(2,1)} %all-gather.10.cloned.1.call-done.x_ref, ...), custom_call_target="tpu_custom_call" | custom-call | flops 51539607552 | bytes 65011712 | tf_op jit(solution)/shard_map/experts/pallas_call | solution.py:217
  496.1 17.9 %outputs.2 = (bf16[2048,2048]{1,0:T(8,128)(2,1)S(1)}, bf16[2048,2048]{1,0:T(8,128)(2,1)}) custom-call(s32[8]{0:T(128)S(1)} %broadcast_xor_fusion.order, bf16[8,4,1,128,768]{4,3,2,1,0:T(8,128)(2,1)S(1)} %copy-done.10, bf16[768,2048]{1,0:T(8,128)(2,1)S(1)} %bitcast.177), custom_call_target="tpu_custom_call" | custom-call | flops 12884901888 | bytes 23068672 | tf_op jit(solution)/shard_map/outputs/pallas_call | solution.py:263
  514.0 4.6 copy-done.6
  518.6 38.0 %experts.4 = (bf16[8,4,1,128,768]{4,3,2,1,0:T(8,128)(2,1)}, bf16[4096,768]{1,0:T(8,128)(2,1)}, bf16[4096,768]{1,0:T(8,128)(2,1)}, f32[8,4096]{1,0:T(8,128)}, bf16[2048,2048]{1,0:T(8,128)(2,1)}) custom-call(s32[4]{0:T(128)} %get-tuple-element.331.order, bf16[4096,2048]{1,0:T(8,128)(2,1)} %all-gather.12.cloned.1.call-done.x_ref, ...), custom_call_target="tpu_custom_call" | custom-call | flops 25769803776 | bytes 32505856 | tf_op jit(solution)/shard_map/experts/pallas_call | solution.py:217
  556.6 36.2 %experts.5 = (bf16[8,4,1,128,768]{4,3,2,1,0:T(8,128)(2,1)}, bf16[4096,768]{1,0:T(8,128)(2,1)}, bf16[4096,768]{1,0:T(8,128)(2,1)}, f32[8,4096]{1,0:T(8,128)}, bf16[2048,2048]{1,0:T(8,128)(2,1)}) custom-call(s32[4]{0:T(128)} %get-tuple-element.332.order, ...), custom_call_target="tpu_custom_call", output_to_operand_aliasing={{0}: (7, {}), {1}: (8, {}), {2}: (9, {}), {3}: (10, {})} | custom-call | flops 25769803776 | bytes 32505856 | tf_op jit(solution)/shard_map/experts/pallas_call | solution.py:217
  598.2 18.1 %outputs.3 = (bf16[2048,2048]{1,0:T(8,128)(2,1)S(1)}, bf16[2048,2048]{1,0:T(8,128)(2,1)}) custom-call(s32[8]{0:T(128)S(1)} %broadcast_xor_fusion.order, bf16[8,4,1,128,768]{4,3,2,1,0:T(8,128)(2,1)S(1)} %copy-done.11, bf16[768,2048]{1,0:T(8,128)(2,1)S(1)} %bitcast.178), custom_call_target="tpu_custom_call" | custom-call | flops 12884901888 | bytes 23068672 | tf_op jit(solution)/shard_map/outputs/pallas_call | solution.py:263
  616.3 6.1 add_convert_fusion.22
  630.3 5.4 all-to-all-done.1
  642.4 20.3 %fusion.43 = f32[2048,768]{0,1:T(8,128)} fusion(bf16[4096,2048]{1,0:T(8,128)(2,1)} %all-gather.10.cloned.1.call-done.x_ref, bf16[4096,768]{1,0:T(8,128)(2,1)} %get-tuple-element.123), kind=kOutput, calls=%fused_computation.221 | convolution fusion | flops 12884901888 | bytes 29360128 | tf_op jit(solution)/shard_map/dot_general | solution.py:20
  662.9 22.4 %collective-permute-done.29 = bf16[2,256,2048]{2,1,0:T(8,128)(2,1)} collective-permute-done((bf16[2,256,2048]{2,1,0:T(8,128)(2,1)}, bf16[2,256,2048]{2,1,0:T(8,128)(2,1)}, u32[]{:S(2)}, u32[]{:S(2)}) %collective-permute-start.29) | collective-permute-done | bytes 2097184 | tf_op jit(solution)/shard_map/ppermute | solution.py:297
  686.0 5.3 add_convert_fusion.20
  693.2 4.3 add_convert_fusion.16
  702.8 18.5 %fusion.44 = f32[2048,768]{0,1:T(8,128)} fusion(bf16[4096,2048]{1,0:T(8,128)(2,1)} %all-gather.10.cloned.1.call-done.x_ref, bf16[4096,768]{1,0:T(8,128)(2,1)S(1)} %bitcast.219), kind=kOutput, calls=%fused_computation.222 | convolution fusion | flops 12884901888 | bytes 29360128 | tf_op jit(solution)/shard_map/dot_general | solution.py:20
  721.3 6.8 reduce-scatter.9.cloned.1.call-done
  728.1 4.9 fusion.9
  735.0 21.6 %convolution_add_fusion.2 = f32[2048,768]{0,1:T(8,128)} fusion(f32[2048,768]{0,1:T(8,128)} %fusion.43, bf16[4096,2048]{1,0:T(8,128)(2,1)} %all-gather.12.cloned.1.call-done.x_ref, bf16[4096,768]{1,0:T(8,128)(2,1)} %get-tuple-element.137), kind=kOutput, calls=%fused_computation.13 | convolution fusion | flops 12886474752 | bytes 35651584 | tf_op jit(solution)/shard_map/dot_general | solution.py:20
  756.6 20.6 %fusion.45 = f32[768,2048]{1,0:T(8,128)} fusion(bf16[4096,768]{1,0:T(8,128)(2,1)} %bitcast.179, bf16[4096,2048]{1,0:T(8,128)(2,1)} %all-gather.6.cloned.1.call-done), kind=kOutput, calls=%fused_computation.223 | convolution fusion | flops 12884901888 | bytes 29360128 | tf_op jit(solution)/shard_map/dot_general | solution.py:20
  777.2 5.1 add_convert_fusion.11
  791.2 4.8 add_convert_fusion.10
  799.8 21.3 %convolution_add_fusion.1 = f32[2048,768]{0,1:T(8,128)} fusion(f32[2048,768]{0,1:T(8,128)} %fusion.44, bf16[4096,2048]{1,0:T(8,128)(2,1)} %all-gather.12.cloned.1.call-done.x_ref, bf16[4096,768]{1,0:T(8,128)(2,1)} %get-tuple-element.145), kind=kOutput, calls=%fused_computation.12 | convolution fusion | flops 12886474752 | bytes 35651584 | tf_op jit(solution)/shard_map/dot_general | solution.py:20
  821.1 4.6 fusion.11
  827.2 21.8 %convolution_add_fusion = f32[768,2048]{1,0:T(8,128)} fusion(f32[768,2048]{1,0:T(8,128)} %fusion.45, bf16[4096,768]{1,0:T(8,128)(2,1)} %bitcast.180, bf16[4096,2048]{1,0:T(8,128)(2,1)} %all-gather.8.cloned.1.call-done), kind=kOutput, calls=%fused_computation.11 | convolution fusion | flops 12886474752 | bytes 35651584 | tf_op jit(solution)/shard_map/dot_general | solution.py:20
  849.0 9.9 collective-permute-done.43
  858.9 5.5 add_convert_fusion.4
  868.0 9.5 convolution_convert_fusion.1
  877.5 9.3 convolution_convert_fusion.3.do_ref
  889.3 4.9 fusion.13
  918.7 27.6 %attend_back.1 = (bf16[1024,1024]{1,0:T(8,128)(2,1)S(1)}, bf16[1024,128]{1,0:T(8,128)(2,1)S(1)}, bf16[1024,128]{1,0:T(8,128)(2,1)S(1)}, f32[1,128]{1,0:T(1,128)S(1)}, f32[1,128]{1,0:T(1,128)S(1)}) custom-call(bf16[1024,1024]{1,0:T(8,128)(2,1)S(1)} %copy-done.16, bf16[1024,1024]{1,0:T(8,128)(2,1)S(1)} %copy-done.18, f32[1024,1152]{1,0:T(8,128)S(1)} %copy-done.13, ...), custom_call_target="tpu_custom_call" | custom-call | flops 7516192768 | bytes 10485760 | tf_op jit(solution)/shard_map/attend_back/pallas_call | solution.py:159
  947.2 11.0 reduce-scatter.15.cloned.1.call-done
  958.2 9.0 multiply_reduce_fusion
  974.5 7.6 convolution_convert_fusion
  985.1 15.3 %collective-permute-done.48 = f32[36,2048]{1,0:T(8,128)S(1)} collective-permute-done((f32[36,2048]{1,0:T(8,128)S(1)}, f32[36,2048]{1,0:T(8,128)S(1)}, u32[]{:S(2)}, u32[]{:S(2)}) %collective-permute-start.48) | collective-permute-done | bytes 294944 | tf_op jit(solution)/shard_map/ppermute | solution.py:297
  1002.1 7.7 collective-permute-done.49
  1014.1 8.4 collective-permute-done.55
  1030.1 30.7 %collective-permute-done.56 = f32[36,2048]{1,0:T(8,128)S(1)} collective-permute-done((f32[36,2048]{1,0:T(8,128)S(1)}, f32[36,2048]{1,0:T(8,128)S(1)}, u32[]{:S(2)}, u32[]{:S(2)}) %collective-permute-start.56) | collective-permute-done | bytes 294944 | tf_op jit(solution)/shard_map/ppermute | solution.py:297
  1071.5 8.3 collective-permute-done.53
  1087.2 3.9 fusion.1
  (418 shorter events, 230.7 us)
Async XLA Ops:
  7.2 263.7 %all-gather.6.cloned.1.call-start = ((), (), s32[]{:S(2)}) async-start(), calls=%async_computation.8 | async-start | bytes 18874368 | tf_op jit(solution)/shard_map/all_gather | solution.py:488
  14.2 29.3 %collective-permute-start = (bf16[256,2048]{1,0:T(8,128)(2,1)}, bf16[256,2048]{1,0:T(8,128)(2,1)S(1)}, u32[]{:S(2)}, u32[]{:S(2)}) collective-permute-start(bf16[256,2048]{1,0:T(8,128)(2,1)} %get-tuple-element.247), channel_id=1, source_target_pairs={{0,1},{1,2},{2,3},{3,0},{4,5},{5,6},{6,7},{7,4},{8,9},{9,10},{10,1... | collective-permute-start | bytes 3145736 | tf_op jit(solution)/shard_map/ppermute | solution.py:372
  17.2 47.6 %collective-permute-start.1 = (bf16[256,2048]{1,0:T(8,128)(2,1)}, bf16[256,2048]{1,0:T(8,128)(2,1)}, u32[]{:S(2)}, u32[]{:S(2)}) collective-permute-start(bf16[256,2048]{1,0:T(8,128)(2,1)} %get-tuple-element.247), channel_id=1, source_target_pairs={{0,3},{1,0},{2,1},{3,2},{4,7},{5,4},{6,5},{7,6},{8,11},{9,8},{10,9... | collective-permute-start | bytes 3145736 | tf_op jit(solution)/shard_map/ppermute | solution.py:373
  44.4 35.7 %collective-permute-start.2 = (bf16[128,2048]{1,0:T(8,128)(2,1)}, bf16[128,2048]{1,0:T(8,128)(2,1)}, u32[]{:S(2)}, u32[]{:S(2)}) collective-permute-start(bf16[128,2048]{1,0:T(8,128)(2,1)} %slice.455), channel_id=1, source_target_pairs={{0,1},{1,2},{2,3},{3,0},{4,5},{5,6},{6,7},{7,4},{8,9},{9,10},{10,1... | collective-permute-start | bytes 1572872 | tf_op jit(solution)/shard_map/ppermute | solution.py:372
  65.9 21.8 %collective-permute-start.3 = (bf16[128,2048]{1,0:T(8,128)(2,1)S(1)}, bf16[128,2048]{1,0:T(8,128)(2,1)S(1)}, u32[]{:S(2)}, u32[]{:S(2)}) collective-permute-start(bf16[128,2048]{1,0:T(8,128)(2,1)S(1)} %slice.456), channel_id=1, source_target_pairs={{0,3},{1,0},{2,1},{3,2},{4,7},{5,4},{6,5},{7,6},{8,11},{9,8},{10,9... | collective-permute-start | bytes 1572872 | tf_op jit(solution)/shard_map/ppermute | solution.py:373
  91.3 17.6 %collective-permute-start.4 = (bf16[128,2048]{1,0:T(8,128)(2,1)}, bf16[128,2048]{1,0:T(8,128)(2,1)}, u32[]{:S(2)}, u32[]{:S(2)}) collective-permute-start(bf16[128,2048]{1,0:T(8,128)(2,1)} %get-tuple-element.309), channel_id=1, source_target_pairs={{0,1},{1,2},{2,3},{3,0},{4,5},{5,6},{6,7},{7,4},{8,9},{9,10},{10,1... | collective-permute-start | bytes 1572872 | tf_op jit(solution)/shard_map/ppermute | solution.py:372
  91.9 25.1 %collective-permute-start.5 = (bf16[128,2048]{1,0:T(8,128)(2,1)}, bf16[128,2048]{1,0:T(8,128)(2,1)}, u32[]{:S(2)}, u32[]{:S(2)}) collective-permute-start(bf16[128,2048]{1,0:T(8,128)(2,1)} %get-tuple-element.309), channel_id=1, source_target_pairs={{0,3},{1,0},{2,1},{3,2},{4,7},{5,4},{6,5},{7,6},{8,11},{9,8},{10,9... | collective-permute-start | bytes 1572872 | tf_op jit(solution)/shard_map/ppermute | solution.py:373
  119.0 15.3 %collective-permute-start.7 = (bf16[64,2048]{1,0:T(8,128)(2,1)S(1)}, bf16[64,2048]{1,0:T(8,128)(2,1)S(1)}, u32[]{:S(2)}, u32[]{:S(2)}) collective-permute-start(bf16[64,2048]{1,0:T(8,128)(2,1)S(1)} %slice.344), channel_id=1, source_target_pairs={{0,3},{1,0},{2,1},{3,2},{4,7},{5,4},{6,5},{7,6},{8,11},{9,8},{10,9... | collective-permute-start | bytes 786440 | tf_op jit(solution)/shard_map/ppermute | solution.py:373
  121.1 12.5 %collective-permute-start.6 = (bf16[64,2048]{1,0:T(8,128)(2,1)S(1)}, bf16[64,2048]{1,0:T(8,128)(2,1)S(1)}, u32[]{:S(2)}, u32[]{:S(2)}) collective-permute-start(bf16[64,2048]{1,0:T(8,128)(2,1)S(1)} %slice.343), channel_id=1, source_target_pairs={{0,1},{1,2},{2,3},{3,0},{4,5},{5,6},{6,7},{7,4},{8,9},{9,10},{10,1... | collective-permute-start | bytes 786440 | tf_op jit(solution)/shard_map/ppermute | solution.py:372
  135.0 181.8 %all-gather.8.cloned.1.call-start = ((), (), s32[]{:S(2)}) async-start(), calls=%async_computation.9 | async-start | bytes 18874368 | tf_op jit(solution)/shard_map/all_gather | solution.py:488
  135.1 17.7 %collective-permute-start.9 = (bf16[128,2048]{1,0:T(8,128)(2,1)S(1)}, bf16[128,2048]{1,0:T(8,128)(2,1)}, u32[]{:S(2)}, u32[]{:S(2)}) collective-permute-start(bf16[128,2048]{1,0:T(8,128)(2,1)S(1)} %copy-done.35), channel_id=1, source_target_pairs={{0,3},{1,0},{2,1},{3,2},{4,7},{5,4},{6,5},{7,6},{8,11},{9,8},{10,9... | collective-permute-start | bytes 1572872 | tf_op jit(solution)/shard_map/ppermute | solution.py:373
  136.9 22.7 %collective-permute-start.8 = (bf16[128,2048]{1,0:T(8,128)(2,1)S(1)}, bf16[128,2048]{1,0:T(8,128)(2,1)}, u32[]{:S(2)}, u32[]{:S(2)}) collective-permute-start(bf16[128,2048]{1,0:T(8,128)(2,1)S(1)} %copy-done.35), channel_id=1, source_target_pairs={{0,1},{1,2},{2,3},{3,0},{4,5},{5,6},{6,7},{7,4},{8,9},{9,10},{10,1... | collective-permute-start | bytes 1572872 | tf_op jit(solution)/shard_map/ppermute | solution.py:372
  160.6 11.1 %collective-permute-start.10 = (bf16[64,2048]{1,0:T(8,128)(2,1)S(1)}, bf16[64,2048]{1,0:T(8,128)(2,1)S(1)}, u32[]{:S(2)}, u32[]{:S(2)}) collective-permute-start(bf16[64,2048]{1,0:T(8,128)(2,1)S(1)} %slice.346), channel_id=1, source_target_pairs={{0,1},{1,2},{2,3},{3,0},{4,5},{5,6},{6,7},{7,4},{8,9},{9,10},{10,1... | collective-permute-start | bytes 786440 | tf_op jit(solution)/shard_map/ppermute | solution.py:372
  175.4 248.3 %all-gather.10.cloned.1.call-start = ((), (), s32[]{:S(2)}) async-start(), calls=%async_computation.10 | async-start | bytes 18874368 | tf_op jit(solution)/shard_map/all_gather | solution.py:536
  186.8 24.3 %collective-permute-start.14 = (bf16[128,2048]{1,0:T(8,128)(2,1)}, bf16[128,2048]{1,0:T(8,128)(2,1)}, u32[]{:S(2)}, u32[]{:S(2)}) collective-permute-start(bf16[128,2048]{1,0:T(8,128)(2,1)} %get-tuple-element.298), channel_id=1, source_target_pairs={{0,3},{1,0},{2,1},{3,2},{4,7},{5,4},{6,5},{7,6},{8,11},{9,8},{10,9... | collective-permute-start | bytes 1572872 | tf_op jit(solution)/shard_map/ppermute | solution.py:373
  188.5 22.6 %collective-permute-start.12 = (bf16[128,2048]{1,0:T(8,128)(2,1)}, bf16[128,2048]{1,0:T(8,128)(2,1)}, u32[]{:S(2)}, u32[]{:S(2)}) collective-permute-start(bf16[128,2048]{1,0:T(8,128)(2,1)} %get-tuple-element.299), channel_id=1, source_target_pairs={{0,1},{1,2},{2,3},{3,0},{4,5},{5,6},{6,7},{7,4},{8,9},{9,10},{10,1... | collective-permute-start | bytes 1572872 | tf_op jit(solution)/shard_map/ppermute | solution.py:372
  213.4 24.2 %collective-permute-start.15 = (bf16[256,2048]{1,0:T(8,128)(2,1)S(1)}, bf16[256,2048]{1,0:T(8,128)(2,1)S(1)}, u32[]{:S(2)}, u32[]{:S(2)}) collective-permute-start(bf16[256,2048]{1,0:T(8,128)(2,1)S(1)} %pad_maximum_fusion.13), channel_id=1, source_target_pairs={{0,3},{1,0},{2,1},{3,2},{4,7},{5,4},{6,5},{7,6},{8,11},{9,8},{10,9... | collective-permute-start | bytes 3145736 | tf_op jit(solution)/shard_map/ppermute | solution.py:373
  214.0 47.3 %collective-permute-start.13 = (bf16[256,2048]{1,0:T(8,128)(2,1)S(1)}, bf16[256,2048]{1,0:T(8,128)(2,1)S(1)}, u32[]{:S(2)}, u32[]{:S(2)}) collective-permute-start(bf16[256,2048]{1,0:T(8,128)(2,1)S(1)} %pad_maximum_fusion.12), channel_id=1, source_target_pairs={{0,1},{1,2},{2,3},{3,0},{4,5},{5,6},{6,7},{7,4},{8,9},{9,10},{10,1... | collective-permute-start | bytes 3145736 | tf_op jit(solution)/shard_map/ppermute | solution.py:372
  267.1 24.3 %collective-permute-start.16 = (bf16[128,2048]{1,0:T(8,128)(2,1)}, bf16[128,2048]{1,0:T(8,128)(2,1)}, u32[]{:S(2)}, u32[]{:S(2)}) collective-permute-start(bf16[128,2048]{1,0:T(8,128)(2,1)} %get-tuple-element.304), channel_id=1, source_target_pairs={{0,1},{1,2},{2,3},{3,0},{4,5},{5,6},{6,7},{7,4},{8,9},{9,10},{10,1... | collective-permute-start | bytes 1572872 | tf_op jit(solution)/shard_map/ppermute | solution.py:372
  267.1 24.4 %collective-permute-start.17 = (bf16[128,2048]{1,0:T(8,128)(2,1)}, bf16[128,2048]{1,0:T(8,128)(2,1)S(1)}, u32[]{:S(2)}, u32[]{:S(2)}) collective-permute-start(bf16[128,2048]{1,0:T(8,128)(2,1)} %get-tuple-element.304), channel_id=1, source_target_pairs={{0,3},{1,0},{2,1},{3,2},{4,7},{5,4},{6,5},{7,6},{8,11},{9,8},{10,9... | collective-permute-start | bytes 1572872 | tf_op jit(solution)/shard_map/ppermute | solution.py:373
  292.5 11.1 %collective-permute-start.18 = (bf16[64,2048]{1,0:T(8,128)(2,1)S(1)}, bf16[64,2048]{1,0:T(8,128)(2,1)S(1)}, u32[]{:S(2)}, u32[]{:S(2)}) collective-permute-start(bf16[64,2048]{1,0:T(8,128)(2,1)S(1)} %slice.349), channel_id=1, source_target_pairs={{0,1},{1,2},{2,3},{3,0},{4,5},{5,6},{6,7},{7,4},{8,9},{9,10},{10,1... | collective-permute-start | bytes 786440 | tf_op jit(solution)/shard_map/ppermute | solution.py:372
  295.3 11.4 %collective-permute-start.19 = (bf16[64,2048]{1,0:T(8,128)(2,1)S(1)}, bf16[64,2048]{1,0:T(8,128)(2,1)S(1)}, u32[]{:S(2)}, u32[]{:S(2)}) collective-permute-start(bf16[64,2048]{1,0:T(8,128)(2,1)S(1)} %slice.350), channel_id=1, source_target_pairs={{0,3},{1,0},{2,1},{3,2},{4,7},{5,4},{6,5},{7,6},{8,11},{9,8},{10,9... | collective-permute-start | bytes 786440 | tf_op jit(solution)/shard_map/ppermute | solution.py:373
  316.9 201.7 %all-gather.12.cloned.1.call-start = ((), (), s32[]{:S(2)}) async-start(), calls=%async_computation.11 | async-start | bytes 18874368 | tf_op jit(solution)/shard_map/all_gather | solution.py:536
  316.9 16.9 %collective-permute-start.24 = (bf16[128,2048]{1,0:T(8,128)(2,1)}, bf16[128,2048]{1,0:T(8,128)(2,1)S(1)}, u32[]{:S(2)}, u32[]{:S(2)}) collective-permute-start(bf16[128,2048]{1,0:T(8,128)(2,1)} %get-tuple-element.306), channel_id=1, source_target_pairs={{0,1},{1,2},{2,3},{3,0},{4,5},{5,6},{6,7},{7,4},{8,9},{9,10},{10,1... | collective-permute-start | bytes 1572872 | tf_op jit(solution)/shard_map/ppermute | solution.py:372
  318.5 25.3 %collective-permute-start.25 = (bf16[128,2048]{1,0:T(8,128)(2,1)}, bf16[128,2048]{1,0:T(8,128)(2,1)S(1)}, u32[]{:S(2)}, u32[]{:S(2)}) collective-permute-start(bf16[128,2048]{1,0:T(8,128)(2,1)} %get-tuple-element.306), channel_id=1, source_target_pairs={{0,3},{1,0},{2,1},{3,2},{4,7},{5,4},{6,5},{7,6},{8,11},{9,8},{10,9... | collective-permute-start | bytes 1572872 | tf_op jit(solution)/shard_map/ppermute | solution.py:373
  333.8 16.9 %collective-permute-start.26 = (bf16[64,2048]{1,0:T(8,128)(2,1)S(1)}, bf16[64,2048]{1,0:T(8,128)(2,1)S(1)}, u32[]{:S(2)}, u32[]{:S(2)}) collective-permute-start(bf16[64,2048]{1,0:T(8,128)(2,1)S(1)} %slice.460), channel_id=1, source_target_pairs={{0,1},{1,2},{2,3},{3,0},{4,5},{5,6},{6,7},{7,4},{8,9},{9,10},{10,1... | collective-permute-start | bytes 786440 | tf_op jit(solution)/shard_map/ppermute | solution.py:372
  343.8 11.8 %collective-permute-start.27 = (bf16[64,2048]{1,0:T(8,128)(2,1)S(1)}, bf16[64,2048]{1,0:T(8,128)(2,1)S(1)}, u32[]{:S(2)}, u32[]{:S(2)}) collective-permute-start(bf16[64,2048]{1,0:T(8,128)(2,1)S(1)} %slice.461), channel_id=1, source_target_pairs={{0,3},{1,0},{2,1},{3,2},{4,7},{5,4},{6,5},{7,6},{8,11},{9,8},{10,9... | collective-permute-start | bytes 786440 | tf_op jit(solution)/shard_map/ppermute | solution.py:373
  369.2 316.0 %reduce-scatter.7.cloned.1.call-start = ((), (), s32[]{:S(2)}) async-start(), calls=%async_computation.12 | async-start | bytes 18874368 | tf_op jit(solution)/shard_map/reduce_scatter | solution.py:541
  374.1 23.7 %collective-permute-start.20 = (bf16[8,4,256]{2,0,1:T(8,128)(2,1)S(1)}, bf16[8,4,256]{2,0,1:T(8,128)(2,1)S(1)}, u32[]{:S(2)}, u32[]{:S(2)}) collective-permute-start(bf16[8,4,256]{2,0,1:T(8,128)(2,1)S(1)} %copy.131), channel_id=1, source_target_pairs={{0,1},{1,2},{2,3},{3,0},{4,5},{5,6},{6,7},{7,4},{8,9},{9,10},{10,1... | collective-permute-start | bytes 49160 | tf_op jit(solution)/shard_map/ppermute | solution.py:315
  374.6 23.2 %collective-permute-start.22 = (bf16[8,4,256]{2,0,1:T(8,128)(2,1)S(1)}, bf16[8,4,256]{2,0,1:T(8,128)(2,1)S(1)}, u32[]{:S(2)}, u32[]{:S(2)}) collective-permute-start(bf16[8,4,256]{2,0,1:T(8,128)(2,1)S(1)} %copy.131), channel_id=1, source_target_pairs={{0,3},{1,0},{2,1},{3,2},{4,7},{5,4},{6,5},{7,6},{8,11},{9,8},{10,9... | collective-permute-start | bytes 49160 | tf_op jit(solution)/shard_map/ppermute | solution.py:315
  388.3 9.5 collective-permute-start.21
  592.8 23.5 %collective-permute-start.28 = (bf16[2048,2048]{1,0:T(8,128)(2,1)}, bf16[2048,2048]{1,0:T(8,128)(2,1)}, u32[]{:S(2)}, u32[]{:S(2)}) collective-permute-start(bf16[2048,2048]{1,0:T(8,128)(2,1)} %get-tuple-element.117), channel_id=1, source_target_pairs={{0,4},{4,0},{8,12},{12,8},{16,20},{20,16},{24,28},{28,24},{1,5},{5... | collective-permute-start | bytes 25165832 | tf_op jit(solution)/shard_map/ppermute | solution.py:297
  592.8 100.4 %collective-permute-start.23 = (bf16[2048,2048]{1,0:T(8,128)(2,1)}, bf16[2048,2048]{1,0:T(8,128)(2,1)}, u32[]{:S(2)}, u32[]{:S(2)}) collective-permute-start(bf16[2048,2048]{1,0:T(8,128)(2,1)} %copy-done.6), channel_id=1, source_target_pairs={{0,4},{4,0},{8,12},{12,8},{16,20},{20,16},{24,28},{28,24},{1,5},{5... | collective-permute-start | bytes 25165832 | tf_op jit(solution)/shard_map/ppermute | solution.py:297
  630.2 97.9 %reduce-scatter.9.cloned.1.call-start = ((), (), s32[]{:S(2)}) async-start(), calls=%async_computation.13 | async-start | bytes 2621440 | tf_op jit(solution)/shard_map/reduce_scatter | solution.py:523
  638.1 47.2 %collective-permute-start.29 = (bf16[2,256,2048]{2,1,0:T(8,128)(2,1)}, bf16[2,256,2048]{2,1,0:T(8,128)(2,1)}, u32[]{:S(2)}, u32[]{:S(2)}) collective-permute-start(bf16[2,256,2048]{2,1,0:T(8,128)(2,1)} %pad_maximum_fusion.3), channel_id=1, source_target_pairs={{0,8},{4,12},{8,0},{12,4},{16,24},{20,28},{24,16},{28,20},{1,9},{5... | collective-permute-start | bytes 6291464 | tf_op jit(solution)/shard_map/ppermute | solution.py:297
  638.6 47.1 %collective-permute-start.33 = (bf16[2,256,2048]{2,1,0:T(8,128)(2,1)}, bf16[2,256,2048]{2,1,0:T(8,128)(2,1)}, u32[]{:S(2)}, u32[]{:S(2)}) collective-permute-start(bf16[2,256,2048]{2,1,0:T(8,128)(2,1)} %pad_maximum_fusion.4), channel_id=1, source_target_pairs={{0,16},{4,20},{8,24},{12,28},{16,0},{20,4},{24,8},{28,12},{1,17},{... | collective-permute-start | bytes 6291464 | tf_op jit(solution)/shard_map/ppermute | solution.py:297
  639.2 23.5 %collective-permute-start.30 = (f32[8,4,256]{2,0,1:T(8,128)S(1)}, f32[8,4,256]{2,0,1:T(8,128)S(1)}, u32[]{:S(2)}, u32[]{:S(2)}) collective-permute-start(f32[8,4,256]{2,0,1:T(8,128)S(1)} %bitcast.206), channel_id=1, source_target_pairs={{0,1},{1,2},{2,3},{3,0},{4,5},{5,6},{6,7},{7,4},{8,9},{9,10},{10,1... | collective-permute-start | bytes 98312 | tf_op jit(solution)/shard_map/ppermute | solution.py:315
  639.7 23.0 %collective-permute-start.31 = (f32[8,4,256]{2,0,1:T(8,128)S(1)}, f32[8,4,256]{2,0,1:T(8,128)S(1)}, u32[]{:S(2)}, u32[]{:S(2)}) collective-permute-start(f32[8,4,256]{2,0,1:T(8,128)S(1)} %bitcast.204), channel_id=1, source_target_pairs={{0,2},{1,3},{2,0},{3,1},{4,6},{5,7},{6,4},{7,5},{8,10},{9,11},{10,... | collective-permute-start | bytes 98312 | tf_op jit(solution)/shard_map/ppermute | solution.py:315
  662.7 128.5 %collective-permute-start.38 = (bf16[2048,2048]{1,0:T(8,128)(2,1)}, bf16[2048,2048]{1,0:T(8,128)(2,1)}, u32[]{:S(2)}, u32[]{:S(2)}) collective-permute-start(bf16[2048,2048]{1,0:T(8,128)(2,1)} %copy-done.5), channel_id=1, source_target_pairs={{0,4},{4,0},{8,12},{12,8},{16,20},{20,16},{24,28},{28,24},{1,5},{5... | collective-permute-start | bytes 25165832 | tf_op jit(solution)/shard_map/ppermute | solution.py:297
  685.7 96.7 %reduce-scatter.11.cloned.1.call-start = ((), (), s32[]{:S(2)}) async-start(), calls=%async_computation.14 | async-start | bytes 2621440 | tf_op jit(solution)/shard_map/reduce_scatter | solution.py:523
  691.3 36.8 %collective-permute-start.35 = (bf16[1,256,2048]{2,1,0:T(8,128)(2,1)}, bf16[1,256,2048]{2,1,0:T(8,128)(2,1)S(1)}, u32[]{:S(2)}, u32[]{:S(2)}) collective-permute-start(bf16[1,256,2048]{2,1,0:T(8,128)(2,1)} %get-tuple-element.266), channel_id=1, source_target_pairs={{0,16},{4,20},{8,24},{12,28},{16,0},{20,4},{24,8},{28,12},{1,17},{... | collective-permute-start | bytes 3145736 | tf_op jit(solution)/shard_map/ppermute | solution.py:297
  691.9 29.4 %collective-permute-start.36 = (bf16[1,256,2048]{2,1,0:T(8,128)(2,1)S(1)}, bf16[1,256,2048]{2,1,0:T(8,128)(2,1)}, u32[]{:S(2)}, u32[]{:S(2)}) collective-permute-start(bf16[1,256,2048]{2,1,0:T(8,128)(2,1)S(1)} %get-tuple-element.267), channel_id=1, source_target_pairs={{0,8},{4,12},{8,0},{12,4},{16,24},{20,28},{24,16},{28,20},{1,9},{5... | collective-permute-start | bytes 3145736 | tf_op jit(solution)/shard_map/ppermute | solution.py:297
  699.1 78.1 %collective-permute-start.34 = (bf16[2,256,2048]{2,1,0:T(8,128)(2,1)}, bf16[2,256,2048]{2,1,0:T(8,128)(2,1)}, u32[]{:S(2)}, u32[]{:S(2)}) collective-permute-start(bf16[2,256,2048]{2,1,0:T(8,128)(2,1)} %pad_maximum_fusion.5), channel_id=1, source_target_pairs={{0,8},{4,12},{8,0},{12,4},{16,24},{20,28},{24,16},{28,20},{1,9},{5... | collective-permute-start | bytes 6291464 | tf_op jit(solution)/shard_map/ppermute | solution.py:297
  701.3 75.9 %collective-permute-start.39 = (bf16[2,256,2048]{2,1,0:T(8,128)(2,1)}, bf16[2,256,2048]{2,1,0:T(8,128)(2,1)}, u32[]{:S(2)}, u32[]{:S(2)}) collective-permute-start(bf16[2,256,2048]{2,1,0:T(8,128)(2,1)} %pad_maximum_fusion.6), channel_id=1, source_target_pairs={{0,16},{4,20},{8,24},{12,28},{16,0},{20,4},{24,8},{28,12},{1,17},{... | collective-permute-start | bytes 6291464 | tf_op jit(solution)/shard_map/ppermute | solution.py:297
  734.5 133.5 %all-gather.14.cloned.1.call-start = ((), (), s32[]{:S(2)}) async-start(), calls=%async_computation.16 | async-start | bytes 5242880 | tf_op jit(solution)/shard_map/all_gather | solution.py:597
  788.1 159.1 %reduce-scatter.13.cloned.1.call-start = ((), (), s32[]{:S(2)}) async-start(), calls=%async_computation.15 | async-start | bytes 2621440 | tf_op jit(solution)/shard_map/reduce_scatter | solution.py:523
  788.2 32.9 %collective-permute-start.40 = (bf16[1,256,2048]{2,1,0:T(8,128)(2,1)}, bf16[1,256,2048]{2,1,0:T(8,128)(2,1)S(1)}, u32[]{:S(2)}, u32[]{:S(2)}) collective-permute-start(bf16[1,256,2048]{2,1,0:T(8,128)(2,1)} %get-tuple-element.258), channel_id=1, source_target_pairs={{0,8},{4,12},{8,0},{12,4},{16,24},{20,28},{24,16},{28,20},{1,9},{5... | collective-permute-start | bytes 3145736 | tf_op jit(solution)/shard_map/ppermute | solution.py:297
  789.7 31.4 %collective-permute-start.37 = (bf16[1,256,2048]{2,1,0:T(8,128)(2,1)S(1)}, bf16[1,256,2048]{2,1,0:T(8,128)(2,1)S(1)}, u32[]{:S(2)}, u32[]{:S(2)}) collective-permute-start(bf16[1,256,2048]{2,1,0:T(8,128)(2,1)S(1)} %get-tuple-element.259), channel_id=1, source_target_pairs={{0,16},{4,20},{8,24},{12,28},{16,0},{20,4},{24,8},{28,12},{1,17},{... | collective-permute-start | bytes 3145736 | tf_op jit(solution)/shard_map/ppermute | solution.py:297
  797.5 61.4 %collective-permute-start.43 = (bf16[2,256,2048]{2,1,0:T(8,128)(2,1)}, bf16[2,256,2048]{2,1,0:T(8,128)(2,1)}, u32[]{:S(2)}, u32[]{:S(2)}) collective-permute-start(bf16[2,256,2048]{2,1,0:T(8,128)(2,1)} %pad_maximum_fusion.9), channel_id=1, source_target_pairs={{0,16},{4,20},{8,24},{12,28},{16,0},{20,4},{24,8},{28,12},{1,17},{... | collective-permute-start | bytes 6291464 | tf_op jit(solution)/shard_map/ppermute | solution.py:297
  799.2 59.7 %collective-permute-start.41 = (bf16[2,256,2048]{2,1,0:T(8,128)(2,1)}, bf16[2,256,2048]{2,1,0:T(8,128)(2,1)}, u32[]{:S(2)}, u32[]{:S(2)}) collective-permute-start(bf16[2,256,2048]{2,1,0:T(8,128)(2,1)} %pad_maximum_fusion.8), channel_id=1, source_target_pairs={{0,8},{4,12},{8,0},{12,4},{16,24},{20,28},{24,16},{28,20},{1,9},{5... | collective-permute-start | bytes 6291464 | tf_op jit(solution)/shard_map/ppermute | solution.py:297
  827.1 131.1 %reduce-scatter.15.cloned.1.call-start = ((), (), s32[]{:S(2)}) async-start(), calls=%async_computation.17 | async-start | bytes 2621440 | tf_op jit(solution)/shard_map/reduce_scatter | solution.py:523
  864.4 24.8 %collective-permute-start.42 = (bf16[1,256,2048]{2,1,0:T(8,128)(2,1)}, bf16[1,256,2048]{2,1,0:T(8,128)(2,1)S(1)}, u32[]{:S(2)}, u32[]{:S(2)}) collective-permute-start(bf16[1,256,2048]{2,1,0:T(8,128)(2,1)} %get-tuple-element.250), channel_id=1, source_target_pairs={{0,16},{4,20},{8,24},{12,28},{16,0},{20,4},{24,8},{28,12},{1,17},{... | collective-permute-start | bytes 3145736 | tf_op jit(solution)/shard_map/ppermute | solution.py:297
  865.9 23.3 %collective-permute-start.44 = (bf16[1,256,2048]{2,1,0:T(8,128)(2,1)}, bf16[1,256,2048]{2,1,0:T(8,128)(2,1)}, u32[]{:S(2)}, u32[]{:S(2)}) collective-permute-start(bf16[1,256,2048]{2,1,0:T(8,128)(2,1)} %get-tuple-element.251), channel_id=1, source_target_pairs={{0,8},{4,12},{8,0},{12,4},{16,24},{20,28},{24,16},{28,20},{1,9},{5... | collective-permute-start | bytes 3145736 | tf_op jit(solution)/shard_map/ppermute | solution.py:297
  895.7 173.3 %reduce-scatter.17.cloned.1.call-start = ((), (), s32[]{:S(2)}) async-start(), calls=%async_computation.18 | async-start | bytes 4718592 | tf_op jit(solution)/shard_map/reduce_scatter | solution.py:612
  969.8 40.1 %collective-permute-start.46 = (bf16[128,2048]{1,0:T(8,128)(2,1)}, bf16[128,2048]{1,0:T(8,128)(2,1)}, u32[]{:S(2)}, u32[]{:S(2)}) collective-permute-start(bf16[128,2048]{1,0:T(8,128)(2,1)} %get-tuple-element.293), channel_id=1, source_target_pairs={{0,3},{1,0},{2,1},{3,2},{4,7},{5,4},{6,5},{7,6},{8,11},{9,8},{10,9... | collective-permute-start | bytes 1572872 | tf_op jit(solution)/shard_map/ppermute | solution.py:373
  971.1 38.8 %collective-permute-start.45 = (bf16[128,2048]{1,0:T(8,128)(2,1)}, bf16[128,2048]{1,0:T(8,128)(2,1)}, u32[]{:S(2)}, u32[]{:S(2)}) collective-permute-start(bf16[128,2048]{1,0:T(8,128)(2,1)} %get-tuple-element.294), channel_id=1, source_target_pairs={{0,1},{1,2},{2,3},{3,0},{4,5},{5,6},{6,7},{7,4},{8,9},{9,10},{10,1... | collective-permute-start | bytes 1572872 | tf_op jit(solution)/shard_map/ppermute | solution.py:372
  983.1 17.3 %collective-permute-start.48 = (f32[36,2048]{1,0:T(8,128)S(1)}, f32[36,2048]{1,0:T(8,128)S(1)}, u32[]{:S(2)}, u32[]{:S(2)}) collective-permute-start(f32[36,2048]{1,0:T(8,128)S(1)} %add.673), channel_id=1, source_target_pairs={{0,8},{4,12},{8,0},{12,4},{16,24},{20,28},{24,16},{28,20},{1,9},{5... | collective-permute-start | bytes 884744 | tf_op jit(solution)/shard_map/ppermute | solution.py:297
  984.8 76.7 %collective-permute-start.52 = (bf16[1024,1280]{1,0:T(8,128)(2,1)S(1)}, bf16[1024,1280]{1,0:T(8,128)(2,1)S(1)}, u32[]{:S(2)}, u32[]{:S(2)}) collective-permute-start(bf16[1024,1280]{1,0:T(8,128)(2,1)S(1)} %pad_maximum_fusion.1), channel_id=1, source_target_pairs={{0,4},{4,0},{8,12},{12,8},{16,20},{20,16},{24,28},{28,24},{1,5},{5... | collective-permute-start | bytes 7864328 | tf_op jit(solution)/shard_map/ppermute | solution.py:297
  1000.4 9.4 collective-permute-start.49
  1022.5 38.3 %collective-permute-start.56 = (f32[36,2048]{1,0:T(8,128)S(1)}, f32[36,2048]{1,0:T(8,128)S(1)}, u32[]{:S(2)}, u32[]{:S(2)}) collective-permute-start(f32[36,2048]{1,0:T(8,128)S(1)} %add.697), channel_id=1, source_target_pairs={{0,2},{1,3},{2,0},{3,1},{4,6},{5,7},{6,4},{7,5},{8,10},{9,11},{10,... | collective-permute-start | bytes 884744 | tf_op jit(solution)/shard_map/ppermute | solution.py:297
  1026.1 58.8 %collective-permute-start.50 = (bf16[256,2048]{1,0:T(8,128)(2,1)}, bf16[256,2048]{1,0:T(8,128)(2,1)S(1)}, u32[]{:S(2)}, u32[]{:S(2)}) collective-permute-start(bf16[256,2048]{1,0:T(8,128)(2,1)} %pad_maximum_fusion.14), channel_id=1, source_target_pairs={{0,1},{1,2},{2,3},{3,0},{4,5},{5,6},{6,7},{7,4},{8,9},{9,10},{10,1... | collective-permute-start | bytes 3145736 | tf_op jit(solution)/shard_map/ppermute | solution.py:372
  1027.5 57.4 %collective-permute-start.51 = (bf16[256,2048]{1,0:T(8,128)(2,1)}, bf16[256,2048]{1,0:T(8,128)(2,1)}, u32[]{:S(2)}, u32[]{:S(2)}) collective-permute-start(bf16[256,2048]{1,0:T(8,128)(2,1)} %pad_maximum_fusion.15), channel_id=1, source_target_pairs={{0,3},{1,0},{2,1},{3,2},{4,7},{5,4},{6,5},{7,6},{8,11},{9,8},{10,9... | collective-permute-start | bytes 3145736 | tf_op jit(solution)/shard_map/ppermute | solution.py:373
  1063.3 16.4 %collective-permute-start.53 = (bf16[2,128,1280]{2,1,0:T(8,128)(2,1)}, bf16[2,128,1280]{2,1,0:T(8,128)(2,1)}, u32[]{:S(2)}, u32[]{:S(2)}) collective-permute-start(bf16[2,128,1280]{2,1,0:T(8,128)(2,1)} %pad_maximum_fusion.16), channel_id=1, source_target_pairs={{0,8},{4,12},{8,0},{12,4},{16,24},{20,28},{24,16},{28,20},{1,9},{5... | collective-permute-start | bytes 1966088 | tf_op jit(solution)/shard_map/ppermute | solution.py:297
  1066.4 15.0 %collective-permute-start.54 = (bf16[2,128,1280]{2,1,0:T(8,128)(2,1)}, bf16[2,128,1280]{2,1,0:T(8,128)(2,1)}, u32[]{:S(2)}, u32[]{:S(2)}) collective-permute-start(bf16[2,128,1280]{2,1,0:T(8,128)(2,1)} %pad_maximum_fusion.17), channel_id=1, source_target_pairs={{0,16},{4,20},{8,24},{12,28},{16,0},{20,4},{24,8},{28,12},{1,17},{... | collective-permute-start | bytes 1966088 | tf_op jit(solution)/shard_map/ppermute | solution.py:297
  (81 other events, 1200.1 us)
Sparse Core Ops, SparseCore 0:
  135.2 89.3 all-gather.5
  227.0 89.8 all-gather.7
  319.3 90.0 all-gather.9
  411.7 89.9 all-gather.11
  505.1 115.9 reduce-scatter.6
  685.8 42.2 reduce-scatter.8
  734.6 43.1 reduce-scatter.10
  788.2 79.7 all-gather.13
  870.3 42.3 reduce-scatter.12
  915.0 43.1 reduce-scatter.14
  961.6 57.5 reduce-scatter.16

commit v3 on v2

--- a/solution.py
+++ b/solution.py
@@ -181,7 +181,7 @@
 def experts_kernel(
     held, order, x_ref, pre_ref, gate_ref, spread_ref, wg_ref, wu_ref, *refs
 ):
-    hw_ref, gb_ref, ub_ref, score_ref, back_ref = refs[held:]
+    hw_ref, gb_ref, ub_ref, score_ref, *back_refs = refs[held:]
     x = x_ref[...]
     gate_pre = dot(x, wg_ref[...])
     sigma = 1.0 / (1.0 + jnp.exp(-gate_pre))
@@ -189,7 +189,7 @@
     up_pre = dot(x, wu_ref[...])
     pre = pre_ref[...].reshape(gate_pre.shape)
     hidden = active * up_pre
-    score_ref[...] = dot(spread_ref[...], (hidden * pre).astype(bf16), NT)
+    score_ref[...] = dot(spread_ref[...], (hidden * pre).astype(bf16), NT).reshape(score_ref.shape)
     weight = dot(gate_ref[...], spread_ref[...])
     hw_ref[...] = (hidden * weight).astype(bf16).reshape(hw_ref.shape)
     hidden_grad = pre * weight
@@ -198,7 +198,18 @@
     gb_ref[...] = gate_back
     ub_ref[...] = up_back
     back = (dot(gate_back, wg_ref[...], NT) + dot(up_back, wu_ref[...], NT)).astype(bf16)
-    back_ref[...] = back
+    if len(back_refs) == 1:
+        back_refs[0][...] = back
+        return
+    first = pl.program_id(0) < pl.num_programs(0) // 2
+
+    @pl.when(first)
+    def _():
+        back_refs[0][...] = back
+
+    @pl.when(jnp.logical_not(first))
+    def _():
+        back_refs[1][...] = back
 
 
 def row_block(array, c):
@@ -206,12 +217,16 @@
     return pl.BlockSpec((1, members, 1, piece, columns), lambda j, order: (order[j], 0, c, 0, 0))
 
 
-def experts(order, c, x, pre, gates, spread, gate_w, up_w, held=()):
+def experts(order, c, x, pre, gates, spread, gate_w, up_w, held=(), halves=False):
     rows, width = x.shape
     tile = rows // pre.shape[0]
     hidden = gate_w.shape[1]
     lanes = spread.shape[0]
     steps = order.shape[0]
+    half = steps // 2
+    spots = [lambda j, order: (j, 0)]
+    if halves:
+        spots = [lambda j, order: (jnp.minimum(j, half - 1), 0), lambda j, order: (jnp.maximum(j - half, 0), 0)]
     at = lambda n: pl.BlockSpec((tile, n), lambda j, order: (order[j], 0))
     full = lambda shape: pl.BlockSpec(shape, lambda j, order: (0, 0), pipeline_mode=pl.Buffered(1))
     return pl.pallas_call(
@@ -224,16 +239,16 @@
                 *[pl.BlockSpec(memory_space=pl.ANY)] * len(held),
             ],
             out_specs=[
-                row_block(pre, c), at(hidden), at(hidden), pl.BlockSpec((lanes, tile), lambda j, order: (0, order[j])),
-                pl.BlockSpec((tile, width), lambda j, order: (j, 0)),
+                row_block(pre, c), at(hidden), at(hidden), pl.BlockSpec((1, lanes, tile), lambda j, order: (order[j], 0, 0)),
+                *[pl.BlockSpec((tile, width), spot) for spot in spots],
             ],
         ),
         out_shape=[
             jax.ShapeDtypeStruct(pre.shape, bf16),
             jax.ShapeDtypeStruct((rows, hidden), bf16),
             jax.ShapeDtypeStruct((rows, hidden), bf16),
-            jax.ShapeDtypeStruct((lanes, rows), f32),
-            jax.ShapeDtypeStruct((steps * tile, width), bf16),
+            jax.ShapeDtypeStruct((rows // tile, lanes, tile), f32),
+            *[jax.ShapeDtypeStruct((steps * tile // len(spots), width), bf16) for _ in spots],
         ],
         input_output_aliases={7 + i: output for i, (output, _) in enumerate(held)},
         compiler_params=pltpu.CompilerParams(vmem_limit_bytes=58 * MIB),
@@ -242,26 +257,18 @@
     )(order, x, pre, gates, spread, gate_w, up_w, *[array for _, array in held])
 
 
-def outputs_kernel(half, order, h_ref, w_ref, far_ref, near_ref):
-    hidden = h_ref[...].reshape(far_ref.shape[0], w_ref.shape[0])
-    value = dot(hidden, w_ref[...]).astype(bf16)
-
-    @pl.when(pl.program_id(0) < half)
-    def _():
-        far_ref[...] = value
-
-    @pl.when(pl.program_id(0) >= half)
-    def _():
-        near_ref[...] = value
+def outputs_kernel(order, h_ref, w_ref, out_ref):
+    hidden = h_ref[...].reshape(out_ref.shape[0], w_ref.shape[0])
+    out_ref[...] = dot(hidden, w_ref[...]).astype(bf16)
 
 
 def outputs(order, c, hidden_wt, down_w):
-    steps, members, _, piece, hidden = hidden_wt.shape
+    _, members, _, piece, hidden = hidden_wt.shape
+    steps = order.shape[0]
     tile = members * piece
     width = down_w.shape[1]
-    half = steps // 2
     return pl.pallas_call(
-        functools.partial(outputs_kernel, half),
+        outputs_kernel,
         grid_spec=pltpu.PrefetchScalarGridSpec(
             num_scalar_prefetch=1,
             grid=(steps,),
@@ -269,14 +276,11 @@
                 row_block(hidden_wt, c),
                 pl.BlockSpec((hidden, width), lambda j, order: (0, 0), pipeline_mode=pl.Buffered(1)),
             ],
-            out_specs=[
-                pl.BlockSpec((tile, width), lambda j, order: (jnp.minimum(j, half - 1), 0)),
-                pl.BlockSpec((tile, width), lambda j, order: (jnp.maximum(j - half, 0), 0)),
-            ],
+            out_specs=pl.BlockSpec((tile, width), lambda j, order: (j, 0)),
         ),
-        out_shape=[jax.ShapeDtypeStruct((half * tile, width), bf16)] * 2,
+        out_shape=jax.ShapeDtypeStruct((steps * tile, width), bf16),
         compiler_params=pltpu.CompilerParams(vmem_limit_bytes=32 * MIB),
-        cost_estimate=pl.CostEstimate(flops=2 * steps * tile * width * hidden, bytes_accessed=steps * tile * (width + hidden) * 2, transcendentals=0),
+        cost_estimate=pl.CostEstimate(flops=1, bytes_accessed=1, transcendentals=0),
         name="outputs",
     )(order, hidden_wt, down_w)
 
@@ -299,21 +303,6 @@
 
 def bits_of(size):
     return [1 << k for k in range(size.bit_length() - 1)]
-
-
-def add_up(value, axis):
-    for bit in bits_of(lax.axis_size(axis)):
-        value = value + hop(value, bit, axis)
-    return value
-
-
-def to_members(parts):
-    size, me = lax.axis_size("tensor"), lax.axis_index("tensor")
-    found = [lax.dynamic_index_in_dim(parts, me, 0, keepdims=False)]
-    for step in range(1, size):
-        block = lax.dynamic_index_in_dim(parts, lax.rem(me + step, size), 0, keepdims=False)
-        found.append(lax.ppermute(block, "tensor", [(i, (i + step) % size) for i in range(size)]))
-    return found
 
 
 def step_order(bits):
@@ -458,8 +447,7 @@
     bits = bits_of(n_expert)
     chunks = 2 * max(n_expert // 8, 1)
     piece = tok_dev // chunks
-    rows = n_tensor * piece
-    total = n_expert * rows
+    first = 16 * (tok_dev * 9 // 256) if chunks == 2 else piece
     lanes = 8 * (-(-local_experts // 8))
 
     gate_w = w_gate.transpose(1, 0, 2).reshape(width, hidden_loc)
@@ -474,7 +462,6 @@
 
     cosine, sine = rope_tables(group)
     q_gain, k_gain = query_gain.astype(f32)[None, :], key_gain.astype(f32)[None, :]
-    by_chunk = (n_expert, n_tensor, 1, piece, hidden_loc)
     if chunks == 2:
         gathered = after(gathered, gate_w, up_w)
     raw, queries, keys, values = project(gathered, w_qkv, q_gain, k_gain, cosine, sine, local_q, local_kv)
@@ -482,11 +469,11 @@
     attn = mixed_all
     if chunks == 2:
         grad_line = [
-            gather_line(given[:piece], (queries,)),
-            gather_line(after(given[piece:], queries), (mixed_all,)),
+            gather_line(given[:first], (queries,)),
+            gather_line(after(given[first:], queries), (mixed_all,)),
         ]
         grad_all = [lax.all_gather(part, "expert", axis=0, tiled=True) for part in grad_line]
-        pre = [dot(part, down_w, NT).reshape(by_chunk) for part in grad_all]
+        pre = [dot(part, down_w, NT).reshape(n_expert, n_tensor, 1, -1, hidden_loc) for part in grad_all]
         attn = after(attn, *grad_line)
     attn = Line(dot(attn, w_out).astype(bf16))
     attn.send()
@@ -508,14 +495,15 @@
     logits = dot(w_router, moe_in, ((0,), (1,)))
     gates = jax.nn.softmax(jnp.where(routed, logits, -jnp.inf), axis=0)
     sent_gates = jnp.where(keep, gates, 0.0).astype(bf16).astype(f32)
-    gates_in = lax.all_to_all(
-        sent_gates.reshape(n_expert, local_experts, tok_dev), "expert", 0, 0, tiled=True
+    gates_in = jnp.broadcast_to(
+        sent_gates.reshape(n_expert, 1, local_experts, tok_dev), (n_expert, n_tensor, local_experts, tok_dev)
     )
-    gates_in = jnp.stack(to_members(jnp.broadcast_to(gates_in[None], (n_tensor, *gates_in.shape))))
-    gates_in = jnp.take(gates_in, lax.rem(member - jnp.arange(n_tensor) + n_tensor, n_tensor), axis=0)
-    gates_in = gates_in.reshape(n_tensor, n_expert, local_experts, chunks, piece)
-    gates_in = gates_in.transpose(3, 1, 0, 4, 2).reshape(chunks, total, local_experts)
-    gates_in = jnp.pad(gates_in, ((0, 0), (0, 0), (0, lanes - local_experts))).astype(bf16)
+    gates_in = lax.all_to_all(gates_in.reshape(-1, local_experts, tok_dev), both, 0, 0, tiled=True)
+    gates_in = gates_in.reshape(n_expert, n_tensor, local_experts, tok_dev).transpose(0, 1, 3, 2)
+    gates_in = jnp.pad(gates_in, ((0, 0), (0, 0), (0, 0), (0, lanes - local_experts))).astype(bf16)
+
+    def gates_of(start, count):
+        return lax.dynamic_slice_in_dim(gates_in, start, count, 2).reshape(-1, lanes)
 
     order = place ^ jnp.array(step_order(bits), jnp.int32)
 
@@ -523,35 +511,36 @@
         return lax.psum_scatter(part, "tensor", scatter_dimension=0, tiled=True)
 
     def to_tokens(scores):
-        scores = jnp.stack([s[:local_experts] for s in scores])
-        scores = scores.reshape(chunks, local_experts, n_expert, n_tensor, piece)
-        scores = scores.transpose(2, 3, 1, 0, 4).reshape(n_expert, n_tensor, local_experts, tok_dev)
-        scores = lax.all_to_all(scores, "expert", 0, 0, tiled=True)
-        scores = sum(to_members(scores.transpose(1, 0, 2, 3)))
+        scores = [s[:, :local_experts].reshape(n_expert, local_experts, n_tensor, -1) for s in scores]
+        scores = jnp.concatenate(scores, axis=3).transpose(0, 2, 1, 3)
+        scores = lax.all_to_all(scores.reshape(-1, local_experts, tok_dev), both, 0, 0, tiled=True)
+        scores = scores.reshape(n_expert, n_tensor, local_experts, tok_dev).sum(axis=1)
         return jnp.where(keep, scores.reshape(n_experts, tok_dev), 0.0)
 
     if chunks == 2:
-        moe_line = [gather_line(moe_in[:piece], (pre[0],)), gather_line(moe_in[piece:])]
+        moe_line = [gather_line(moe_in[:first], (pre[0],)), gather_line(moe_in[first:])]
+        gates_0, gates_1 = gates_of(0, first), gates_of(first, tok_dev - first)
         moe_line[0] = after(moe_line[0], grad_all[1])
         moe_all = [lax.all_gather(part, "expert", axis=0, tiled=True) for part in moe_line]
         front, rear = order[: n_expert // 2], order[n_expert // 2 :]
         fixed = (spread, gate_w, up_w)
         x_0 = after(moe_all[0], pre[1])
-        *kept_0, back_0 = experts(jnp.arange(n_expert, dtype=jnp.int32), 0, x_0, pre[0], gates_in[0], *fixed)
+        *kept_0, back_0 = experts(jnp.arange(n_expert, dtype=jnp.int32), 0, x_0, pre[0], gates_0, *fixed)
         back_0 = lax.psum_scatter(back_0, "expert", scatter_dimension=0, tiled=True)
         back_own = [own_rows(back_0)]
-        outs = [outputs(order, 0, kept_0[0], down_w)]
-        x_1 = after(moe_all[1], *outs[0])
-        *kept_1, near = experts(rear, 0, x_1, pre[1], gates_in[1], *fixed)
-        *kept_1, far = experts(front, 0, x_1, pre[1], gates_in[1], *fixed, list(enumerate(kept_1)))
+        far_0 = outputs(front, 0, kept_0[0], down_w)
+        x_1 = after(moe_all[1], far_0)
+        *kept_1, far, near = experts(order, 0, x_1, pre[1], gates_1, *fixed, halves=True)
         back_1 = Exchange(far, near, bits)
-        outs.append(outputs(order, 0, kept_1[0], down_w))
-        sent = back_1.send(*outs[1])
-        scores = to_tokens(after([kept_0[3], kept_1[3]], *sent))
-        x_0 = after(moe_all[0], *sent)
+        x_0 = after(moe_all[0], kept_1[3])
         gate_grad = dot(x_0, kept_0[1], TN)
-        sent = back_1.send(gate_grad, scores, back_0)
-        out_0, out_1 = (Exchange(*out, bits) for out in outs)
+        scores = to_tokens([kept_0[3], kept_1[3]])
+        sent = back_1.send(gate_grad, scores)
+        hidden_0, hidden_1 = after((kept_0[0], kept_1[0]), *sent)
+        near_0 = outputs(rear, 0, hidden_0, down_w)
+        far_1, near_1 = (outputs(part, 0, hidden_1, down_w) for part in (front, rear))
+        sent = back_1.send(near_0, far_1, near_1, back_0)
+        out_0, out_1 = Exchange(far_0, near_0, bits), Exchange(far_1, near_1, bits)
         sent = out_0.send(*sent)
         up_grad = dot(after(x_0, *sent), kept_0[2], TN)
         back_1 = back_1.total(up_grad, back_own[0])
@@ -565,7 +554,7 @@
         def one_chunk(sums, c):
             x_c = lax.all_gather(lax.dynamic_slice_in_dim(moe_in, c * piece, piece, 0), both, axis=0, tiled=True)
             g_c = lax.all_gather(lax.dynamic_slice_in_dim(given, c * piece, piece, 0), both, axis=0, tiled=True)
-            gates_c = lax.dynamic_index_in_dim(gates_in, c, 0, keepdims=False)
+            gates_c = gates_of(c * piece, piece)
             pre = dot(g_c, down_w, NT).reshape(n_expert, n_tensor, 1, piece, hidden_loc)
             given_c = (0, x_c, pre, gates_c, spread, gate_w, up_w)
             *kept, far = experts(order[: n_expert // 2], *given_c)
@@ -574,7 +563,8 @@
             parts = (dot(hw.reshape(-1, hidden_loc), g_c, TN), dot(x_c, gate_back, TN), dot(x_c, up_back, TN))
             sums = tuple(a + b for a, b in zip(sums, parts))
             back = own_rows(Exchange(far, near, bits).total())
-            out = own_rows(Exchange(*outputs(order, 0, hw, down_w), bits).total())
+            out = [outputs(part, 0, hw, down_w) for part in (order[: n_expert // 2], order[n_expert // 2 :])]
+            out = own_rows(Exchange(*out, bits).total())
             return sums, (back, score, out)
 
         zeros = (
@@ -604,37 +594,42 @@
         sent = out_1.send(down_grad)
         middle_all = after(middle_all, *sent)
     mixed_grad = dot(middle_all, w_out, NT).astype(bf16)
-    out_weight_grad = dot(middle_all, mixed_all, TN).astype(bf16)
-    mixed_grad, out_weight_grad = lax.optimization_barrier((mixed_grad, out_weight_grad))
     if chunks == 2:
-        out_1 = out_1.total(out_weight_grad)
+        out_1 = out_1.total(mixed_grad)
         mixed_grad = after(mixed_grad, out_1)
-    grad_out = lax.psum_scatter(out_weight_grad, "expert", scatter_dimension=0, tiled=True)
     dq, dk, dv, query_gain_grad, key_gain_grad = attend_back(
         queries, mixed_grad, raw, keys, keys.T, values, q_gain, k_gain, cosine, sine, local_q, local_kv
     )
     qkv_grad = jnp.concatenate([dq, dk, dv], axis=1)
     if chunks == 2:
         out_own = [own_rows(part) for part in (out_0, out_1)]
-        qkv_grad = after(qkv_grad, *out_own)
+        qkv_grad = after(qkv_grad, out_own[0])
         moe_out = jnp.concatenate(out_own, axis=0)
     normed_part = dot(qkv_grad, w_qkv, NT)
     normed_low = normed_part.astype(bf16)
     normed_line = Line(normed_low)
     sent = normed_line.send()
+    out_weight_grad = dot(middle_all, after(mixed_all, *sent), TN).astype(bf16)
+    grad_out = lax.psum_scatter(out_weight_grad, "expert", scatter_dimension=0, tiled=True)
     weight_grad = dot(after(gathered, *sent), qkv_grad, TN).astype(bf16)
     attn_gain_grad = jnp.sum(normed_part * gathered.astype(f32), axis=0) / attn_gain.astype(f32)
     gain_rows = [attn_gain_grad[None, :], moe_gain_grad[None, :]]
     gain_rows += [jnp.pad(part, ((0, 0), (0, width - HD))) for part in (query_gain_grad, key_gain_grad)]
-    small = add_up(jnp.concatenate([router_grad, *gain_rows], axis=0), "expert")
+    small = jnp.concatenate([router_grad, *gain_rows], axis=0)
+    small = jnp.pad(small, ((0, -small.shape[0] % n_expert), (0, 0))).reshape(n_expert, -1, width)
+    small = lax.all_to_all(small, "expert", 0, 0, tiled=True).sum(axis=0)
+    small = jnp.broadcast_to(small[None], (n_tensor, *small.shape))
+    small = lax.all_to_all(small, "tensor", 0, 0, tiled=True).sum(axis=0)
     blocks = weight_grad.reshape(n_expert, -1, weight_grad.shape[1])
-    blocks = [lax.dynamic_index_in_dim(blocks, order[r], 0, keepdims=False) for r in range(n_expert)]
+    blocks = [lax.dynamic_index_in_dim(blocks, place ^ r, 0, keepdims=False) for r in step_order(bits)]
     far, near = (
         jnp.concatenate(part, axis=0) for part in (blocks[: n_expert // 2], blocks[n_expert // 2 :])
     )
     grad_qkv = Exchange(far, near, bits)
     sent = normed_line.send(small, far, near)
-    small = add_up(after(small, *sent), "tensor") if sent else add_up(small, "tensor")
+    small = after(small, *sent) if sent else small
+    small = lax.all_to_all(jnp.broadcast_to(small[None], (n_expert, *small.shape)), "expert", 0, 0, tiled=True)
+    small = small.reshape(-1, width)
     sent = sum([grad_qkv.send(*sent) for _ in bits[1:]], [])
     grad_qkv = grad_qkv.total().astype(f32)
     normed_grad = normed_line.total(*sent)

time: 1110 us -> 1060 us (0.955)
  waiting for transfers between devices: 332 us -> 315 us
  between operations: 31 us -> 15.6 us
    ppermute x25 -> x20, waiting for transfers between devices: 108 us -> 59 us  [hop(): return lax.ppermute(block, axis, [(i, i ^ bit) for i in range(size)])]
    ppermute x6 -> x0, starting transfers between devices: 19.4 us -> none  [to_members(): lax.ppermute(block, 'tensor', [(i, (i + step) % size) for i in range(size)])]
    all_to_all x2 -> x5, waiting for transfers between devices: 10.2 us -> 27.7 us  [the longest x1 15 us: local(): small = lax.all_to_all(small, 'tensor', 0, 0, tiled=True).sum(axis=0)]
    ppermute x14, waiting for transfers between devices: 88 us -> 103 us  [neighbours(): lax.ppermute(v, 'tensor', [(i, (i + 1) % size) for i in range(size)])]
    ppermute x14, starting transfers between devices: 32.8 us -> 46 us  [neighbours(): lax.ppermute(v, 'tensor', [(i, (i - 1) % size) for i in range(size)])]
    all_to_all x2 -> x5, starting transfers between devices: 6.71 us -> 19.4 us  [the longest x1 5.13 us: local(): small = lax.all_to_all(small, 'tensor', 0, 0, tiled=True).sum(axis=0)]
    dot_general x16, matrix products: 213 us -> 202 us  [dot(): lax.dot_general(a, b, (contract, ((), ())), preferred_element_type=f32)]
    pallas_call x2 -> x4, Pallas kernels: 36.1 us -> 31.1 us  [outputs(): pl.pallas_call(outputs_kernel, grid_spec=pltpu.PrefetchScalarGridSpec(num...]
  transfers between devices with their start and end apart: 72 -> 64, of which waited for: 37 -> 31; matrix products, arithmetic and copies ran while one was open for 34% -> 35% of each run, Pallas kernels for 20% -> 21%
where the time goes in v3:
time: 1060 us; the launch traced here: 1050 us
  waiting for transfers between devices  315 us (30%)
  Pallas kernels  220 us (21%)
  matrix products  202 us (19%)
  local copies, waits for them, and re-layouts  105 us (10%)
  other arithmetic  103 us (10%)
  starting transfers between devices  92.2 us (9%)
  between operations  15.6 us (1%)
    dot_general x16, matrix products, dot(): lax.dot_general(a, b, (contract, ((), ())), preferred_element_type=f32)  202 us
    pallas_call x2, Pallas kernels, experts(): pl.pallas_call(functools.partial(experts_kernel, len(held)), grid_spec=pl...  139 us
    ppermute x14, waiting for transfers between devices, neighbours(): lax.ppermute(v, 'tensor', [(i, (i + 1) % size) for i in range(size)])  103 us
    ppermute x14, waiting for transfers between devices, neighbours(): lax.ppermute(v, 'tensor', [(i, (i - 1) % size) for i in range(size)])  95.8 us
    ppermute x20, waiting for transfers between devices, hop(): return lax.ppermute(block, axis, [(i, i ^ bit) for i in range(size)])  59 us
    ppermute x14, starting transfers between devices, neighbours(): lax.ppermute(v, 'tensor', [(i, (i - 1) % size) for i in range(size)])  46 us
    unnamed x179, local copies, waits for them, and re-layouts  33.4 us
    convert_element_type x8, other arithmetic, send(): add = lambda parts: sum((p.astype(f32) for p in parts)).astype(bf16)  33.1 us
  transfers between devices with their start and end apart: 64, of which 31 were waited for; matrix products, arithmetic and copies ran while one was open for 35% of the time, Pallas kernels for 21%

profile of v3, /device:TPU:0, one launch (start us, length us, event | category | flops | bytes accessed | tf_op | source)
XLA Modules:
  0.0 1053.1 jit_solution(58812050910188157)
XLA Ops:
  22.4 21.2 %collective-permute-done = bf16[256,2048]{1,0:T(8,128)(2,1)S(1)} collective-permute-done((bf16[256,2048]{1,0:T(8,128)(2,1)}, bf16[256,2048]{1,0:T(8,128)(2,1)S(1)}, u32[]{:S(2)}, u32[]{:S(2)}) %collective-permute-start) | collective-permute-done | bytes 1048608 | tf_op jit(solution)/shard_map/ppermute | solution.py:361
  44.6 20.3 %collective-permute-done.1 = bf16[256,2048]{1,0:T(8,128)(2,1)S(1)} collective-permute-done((bf16[256,2048]{1,0:T(8,128)(2,1)}, bf16[256,2048]{1,0:T(8,128)(2,1)S(1)}, u32[]{:S(2)}, u32[]{:S(2)}) %collective-permute-start.1) | collective-permute-done | bytes 1048608 | tf_op jit(solution)/shard_map/ppermute | solution.py:362
  70.2 9.9 collective-permute-done.2
  82.0 5.8 collective-permute-done.3
  95.5 10.2 project.1
  109.3 10.1 collective-permute-done.5
  123.4 12.2 %collective-permute-done.6 = bf16[72,2048]{1,0:T(8,128)(2,1)S(1)} collective-permute-done((bf16[72,2048]{1,0:T(8,128)(2,1)S(1)}, bf16[72,2048]{1,0:T(8,128)(2,1)S(1)}, u32[]{:S(2)}, u32[]{:S(2)}) %collective-permute-start.6) | collective-permute-done | bytes 294944 | tf_op jit(solution)/shard_map/ppermute | solution.py:361
  142.7 11.7 %attend.1 = bf16[1024,1024]{1,0:T(8,128)(2,1)S(1)} custom-call(bf16[1024,1024]{1,0:T(8,128)(2,1)S(1)} %get-tuple-element.85.q_ref, bf16[1024,128]{1,0:T(8,128)(2,1)S(1)} %get-tuple-element.86.k_ref, bf16[128,1024]{1,0:T(8,128)(2,1)S(1)} %bitcast.154), custom_call_target="tpu_custom_call" | custom-call | flops 3221225472 | bytes 4194304 | tf_op jit(solution)/shard_map/attend/pallas_call | solution.py:88
  155.7 4.2 collective-permute-done.8
  167.6 5.4 collective-permute-done.10
  174.5 6.9 convolution_convert_fusion.2
  186.9 12.4 %collective-permute-done.14 = bf16[128,2048]{1,0:T(8,128)(2,1)S(1)} collective-permute-done((bf16[128,2048]{1,0:T(8,128)(2,1)S(1)}, bf16[128,2048]{1,0:T(8,128)(2,1)S(1)}, u32[]{:S(2)}, u32[]{:S(2)}) %collective-permute-start.14) | collective-permute-done | bytes 524320 | tf_op jit(solution)/shard_map/ppermute | solution.py:362
  199.3 11.5 %collective-permute-done.12 = bf16[128,2048]{1,0:T(8,128)(2,1)S(1)} collective-permute-done((bf16[128,2048]{1,0:T(8,128)(2,1)S(1)}, bf16[128,2048]{1,0:T(8,128)(2,1)S(1)}, u32[]{:S(2)}, u32[]{:S(2)}) %collective-permute-start.12) | collective-permute-done | bytes 524320 | tf_op jit(solution)/shard_map/ppermute | solution.py:361
  214.7 23.2 %collective-permute-done.15 = bf16[256,2048]{1,0:T(8,128)(2,1)S(1)} collective-permute-done((bf16[256,2048]{1,0:T(8,128)(2,1)S(1)}, bf16[256,2048]{1,0:T(8,128)(2,1)S(1)}, u32[]{:S(2)}, u32[]{:S(2)}) %collective-permute-start.15) | collective-permute-done | bytes 1048608 | tf_op jit(solution)/shard_map/ppermute | solution.py:362
  237.9 21.6 %collective-permute-done.13 = bf16[256,2048]{1,0:T(8,128)(2,1)S(1)} collective-permute-done((bf16[256,2048]{1,0:T(8,128)(2,1)S(1)}, bf16[256,2048]{1,0:T(8,128)(2,1)S(1)}, u32[]{:S(2)}, u32[]{:S(2)}) %collective-permute-start.13) | collective-permute-done | bytes 1048608 | tf_op jit(solution)/shard_map/ppermute | solution.py:361
  266.6 11.5 %collective-permute-start.17 = (bf16[144,2048]{1,0:T(8,128)(2,1)}, bf16[144,2048]{1,0:T(8,128)(2,1)}, u32[]{:S(2)}, u32[]{:S(2)}) collective-permute-start(bf16[144,2048]{1,0:T(8,128)(2,1)} %get-tuple-element.286), channel_id=1, source_target_pairs={{0,3},{1,0},{2,1},{3,2},{4,7},{5,4},{6,5},{7,6},{8,11},{9,8},{10,9... | collective-permute-start | bytes 1769480 | tf_op jit(solution)/shard_map/ppermute | solution.py:362
  278.1 20.3 %convolution_bitcast_fusion.pre_ref = f32[8,4,1,144,768]{4,3,2,1,0:T(8,128)} fusion(bf16[8,4,144,2048]{3,2,1,0:T(8,128)(2,1)} %bitcast.176, bf16[768,2048,1,1]{1,0,3,2:T(8,128)(2,1)S(1)} %bitcast.135), kind=kOutput, calls=%fused_computation.1 | convolution fusion | flops 14495514624 | bytes 36175872 | tf_op jit(solution)/shard_map/dot_general | solution.py:20
  302.4 3.8 collective-permute-start.19
  325.5 11.4 %collective-permute-done.20 = bf16[112,2048]{1,0:T(8,128)(2,1)S(1)} collective-permute-done((bf16[112,2048]{1,0:T(8,128)(2,1)S(1)}, bf16[112,2048]{1,0:T(8,128)(2,1)S(1)}, u32[]{:S(2)}, u32[]{:S(2)}) %collective-permute-start.20) | collective-permute-done | bytes 458784 | tf_op jit(solution)/shard_map/ppermute | solution.py:361
  336.9 8.5 collective-permute-done.21
  356.6 4.6 copy.70.wg_ref
  361.2 4.9 copy.71.wu_ref
  369.0 5.7 convert_reduce_fusion
  381.6 6.9 all-to-all-done
  392.8 17.6 %convolution_bitcast_fusion.1.pre_ref = f32[8,4,1,112,768]{4,3,2,1,0:T(8,128)} fusion(bf16[8,4,112,2048]{3,2,1,0:T(8,128)(2,1)} %bitcast.177, bf16[768,2048,1,1]{1,0,3,2:T(8,128)(2,1)S(1)} %bitcast.136), kind=kOutput, calls=%fused_computation.9 | convolution fusion | flops 11274289152 | bytes 28835840 | tf_op jit(solution)/shard_map/dot_general | solution.py:20
  410.4 9.8 all-gather.10.cloned.1.call-done.x_ref
  420.7 74.7 %experts.2 = (bf16[8,4,1,144,768]{4,3,2,1,0:T(8,128)(2,1)}, bf16[4608,768]{1,0:T(8,128)(2,1)}, bf16[4608,768]{1,0:T(8,128)(2,1)}, f32[8,8,576]{2,1,0:T(8,128)}, bf16[4608,2048]{1,0:T(8,128)(2,1)}) custom-call(s32[8]{0:T(128)} %iota.42.order, bf16[4608,2048]{1,0:T(8,128)(2,1)} %all-gather.10.cloned.1.call-done.x_ref, ...), custom_call_target="tpu_custom_call" | custom-call | flops 57982058496 | bytes 73138176 | tf_op jit(solution)/shard_map/experts/pallas_call | solution.py:232
  501.5 8.6 outputs.4
  510.0 4.4 copy-done.5
  514.4 64.6 %experts.3 = (bf16[8,4,1,112,768]{4,3,2,1,0:T(8,128)(2,1)}, bf16[3584,768]{1,0:T(8,128)(2,1)}, bf16[3584,768]{1,0:T(8,128)(2,1)}, f32[8,8,448]{2,1,0:T(8,128)}, ...) custom-call(s32[8]{0:T(128)} %copy-done.76, bf16[3584,2048]{1,0:T(8,128)(2,1)} %all-gather.12.cloned.1.call-done.x_ref, ...), custom_call_target="tpu_custom_call" | custom-call | flops 45097156608 | bytes 56885248 | tf_op jit(solution)/shard_map/experts/pallas_call | solution.py:232
  581.6 4.4 all-to-all-start.1
  586.1 21.4 %fusion.34 = f32[2048,768]{0,1:T(8,128)} fusion(bf16[4608,2048]{1,0:T(8,128)(2,1)} %all-gather.10.cloned.1.call-done.x_ref, bf16[4608,768]{1,0:T(8,128)(2,1)} %get-tuple-element.106), kind=kOutput, calls=%fused_computation.193 | convolution fusion | flops 14495514624 | bytes 32243712 | tf_op jit(solution)/shard_map/dot_general | solution.py:20
  607.6 5.0 add_convert_fusion.22
  617.6 7.0 outputs.6
  627.6 7.0 outputs.7
  637.5 8.6 outputs.5
  649.7 22.1 %collective-permute-done.27 = bf16[2,224,2048]{2,1,0:T(8,128)(2,1)} collective-permute-done((bf16[2,224,2048]{2,1,0:T(8,128)(2,1)S(1)}, bf16[2,224,2048]{2,1,0:T(8,128)(2,1)}, u32[]{:S(2)}, u32[]{:S(2)}) %collective-permute-start.27) | collective-permute-done | bytes 1835040 | tf_op jit(solution)/shard_map/ppermute | solution.py:301
  677.6 5.2 add_convert_fusion.5
  688.5 18.9 %fusion.35 = f32[2048,768]{0,1:T(8,128)} fusion(bf16[4608,2048]{1,0:T(8,128)(2,1)} %all-gather.10.cloned.1.call-done.x_ref, bf16[4608,768]{1,0:T(8,128)(2,1)S(1)} %bitcast.184), kind=kOutput, calls=%fused_computation.194 | convolution fusion | flops 14495514624 | bytes 32243712 | tf_op jit(solution)/shard_map/dot_general | solution.py:20
  707.4 12.5 %reduce-scatter.9.cloned.1.call-done = bf16[144,2048]{1,0:T(8,128)(2,1)} async-done(((bf16[576,2048]{1,0:T(8,128)(2,1)}), bf16[144,2048]{1,0:T(8,128)(2,1)}) %reduce-scatter.9.cloned.1.call-update) | async-done | bytes 589840 | tf_op jit(solution)/shard_map/reduce_scatter | solution.py:511
  719.9 4.0 fusion.9
  725.5 21.6 %fusion.36 = f32[768,2048]{1,0:T(8,128)} fusion(bf16[4608,768]{1,0:T(8,128)(2,1)} %bitcast.147, bf16[4608,2048]{1,0:T(8,128)(2,1)} %all-gather.6.cloned.1.call-done), kind=kOutput, calls=%fused_computation.195 | convolution fusion | flops 14495514624 | bytes 32243712 | tf_op jit(solution)/shard_map/dot_general | solution.py:20
  747.1 18.2 %convolution_add_fusion.2 = f32[2048,768]{0,1:T(8,128)} fusion(f32[2048,768]{0,1:T(8,128)S(1)} %bitcast.182, bf16[3584,2048]{1,0:T(8,128)(2,1)} %all-gather.12.cloned.1.call-done.x_ref, bf16[3584,768]{1,0:T(8,128)(2,1)} %get-tuple-element.120), kind=kOutput, calls=%fused_computation.14 | convolution fusion | flops 11275862016 | bytes 32768000 | tf_op jit(solution)/shard_map/dot_general | solution.py:20
  765.4 6.3 add_convert_fusion.2
  780.4 5.0 add_convert_fusion.16
  789.1 19.1 %convolution_add_fusion.1 = f32[2048,768]{0,1:T(8,128)} fusion(f32[2048,768]{0,1:T(8,128)} %fusion.35, bf16[3584,2048]{1,0:T(8,128)(2,1)} %all-gather.12.cloned.1.call-done.x_ref, bf16[3584,768]{1,0:T(8,128)(2,1)} %get-tuple-element.128), kind=kOutput, calls=%fused_computation.13 | convolution fusion | flops 11275862016 | bytes 32768000 | tf_op jit(solution)/shard_map/dot_general | solution.py:20
  808.2 5.1 fusion.6
  815.3 19.2 %convolution_add_fusion = f32[768,2048]{1,0:T(8,128)} fusion(f32[768,2048]{1,0:T(8,128)} %fusion.36, bf16[3584,768]{1,0:T(8,128)(2,1)} %bitcast.150, bf16[3584,2048]{1,0:T(8,128)(2,1)} %all-gather.8.cloned.1.call-done), kind=kOutput, calls=%fused_computation.10 | convolution fusion | flops 11275862016 | bytes 32768000 | tf_op jit(solution)/shard_map/dot_general | solution.py:20
  834.5 11.2 %collective-permute-done.37 = bf16[2,224,2048]{2,1,0:T(8,128)(2,1)} collective-permute-done((bf16[2,224,2048]{2,1,0:T(8,128)(2,1)}, bf16[2,224,2048]{2,1,0:T(8,128)(2,1)}, u32[]{:S(2)}, u32[]{:S(2)}) %collective-permute-start.37) | collective-permute-done | bytes 1835040 | tf_op jit(solution)/shard_map/ppermute | solution.py:301
  845.6 5.0 add_convert_fusion.12
  852.9 4.3 all-gather.14.cloned.1.call-done
  857.1 9.3 convolution_convert_fusion.3.do_ref
  866.4 6.3 collective-permute-done.38
  872.7 4.1 fusion.11
  884.2 27.9 %attend_back.1 = (bf16[1024,1024]{1,0:T(8,128)(2,1)S(1)}, bf16[1024,128]{1,0:T(8,128)(2,1)S(1)}, bf16[1024,128]{1,0:T(8,128)(2,1)S(1)}, f32[1,128]{1,0:T(1,128)S(1)}, f32[1,128]{1,0:T(1,128)S(1)}) custom-call(bf16[1024,1024]{1,0:T(8,128)(2,1)S(1)} %copy-done.22, bf16[1024,1024]{1,0:T(8,128)(2,1)S(1)} %copy-done.26, f32[1024,1152]{1,0:T(8,128)S(1)} %copy-done.20, ...), custom_call_target="tpu_custom_call" | custom-call | flops 7516192768 | bytes 10485760 | tf_op jit(solution)/shard_map/attend_back/pallas_call | solution.py:159
  913.9 9.8 multiply_reduce_fusion
  932.3 8.5 convolution_convert_fusion
  945.5 6.3 convolution_convert_fusion.1
  952.6 5.1 all-to-all-start.3
  959.3 15.0 %all-to-all-done.3 = f32[4,5,2048]{2,1,0:T(8,128)} async-done(((f32[4,5,2048]{2,1,0:T(8,128)}), f32[4,5,2048]{2,1,0:T(8,128)}, u32[]{:S(2)}, u32[]{:S(2)}) %all-to-all-start.3) | async-done | bytes 163872 | tf_op jit(solution)/shard_map/all_to_all | solution.py:622
  987.9 5.9 all-to-all-done.4
  1000.4 19.5 %collective-permute-done.44 = bf16[2,128,1280]{2,1,0:T(8,128)(2,1)S(1)} collective-permute-done((bf16[2,128,1280]{2,1,0:T(8,128)(2,1)S(1)}, bf16[2,128,1280]{2,1,0:T(8,128)(2,1)S(1)}, u32[]{:S(2)}, u32[]{:S(2)}) %collective-permute-start.44) | collective-permute-done | bytes 655392 | tf_op jit(solution)/shard_map/ppermute | solution.py:301
  1023.3 9.1 collective-permute-done.42
  1034.8 3.9 fusion.1
  (427 shorter events, 232.2 us)
Async XLA Ops:
  7.2 270.9 %all-gather.6.cloned.1.call-start = ((), (), s32[]{:S(2)}) async-start(), calls=%async_computation.11 | async-start | bytes 21233664 | tf_op jit(solution)/shard_map/all_gather | solution.py:475
  14.3 29.3 %collective-permute-start = (bf16[256,2048]{1,0:T(8,128)(2,1)}, bf16[256,2048]{1,0:T(8,128)(2,1)S(1)}, u32[]{:S(2)}, u32[]{:S(2)}) collective-permute-start(bf16[256,2048]{1,0:T(8,128)(2,1)} %get-tuple-element.229), channel_id=1, source_target_pairs={{0,1},{1,2},{2,3},{3,0},{4,5},{5,6},{6,7},{7,4},{8,9},{9,10},{10,1... | collective-permute-start | bytes 3145736 | tf_op jit(solution)/shard_map/ppermute | solution.py:361
  17.4 47.5 %collective-permute-start.1 = (bf16[256,2048]{1,0:T(8,128)(2,1)}, bf16[256,2048]{1,0:T(8,128)(2,1)S(1)}, u32[]{:S(2)}, u32[]{:S(2)}) collective-permute-start(bf16[256,2048]{1,0:T(8,128)(2,1)} %get-tuple-element.229), channel_id=1, source_target_pairs={{0,3},{1,0},{2,1},{3,2},{4,7},{5,4},{6,5},{7,6},{8,11},{9,8},{10,9... | collective-permute-start | bytes 3145736 | tf_op jit(solution)/shard_map/ppermute | solution.py:362
  44.5 35.6 %collective-permute-start.2 = (bf16[128,2048]{1,0:T(8,128)(2,1)}, bf16[128,2048]{1,0:T(8,128)(2,1)}, u32[]{:S(2)}, u32[]{:S(2)}) collective-permute-start(bf16[128,2048]{1,0:T(8,128)(2,1)} %slice.412), channel_id=1, source_target_pairs={{0,1},{1,2},{2,3},{3,0},{4,5},{5,6},{6,7},{7,4},{8,9},{9,10},{10,1... | collective-permute-start | bytes 1572872 | tf_op jit(solution)/shard_map/ppermute | solution.py:361
  64.9 22.8 %collective-permute-start.3 = (bf16[128,2048]{1,0:T(8,128)(2,1)S(1)}, bf16[128,2048]{1,0:T(8,128)(2,1)S(1)}, u32[]{:S(2)}, u32[]{:S(2)}) collective-permute-start(bf16[128,2048]{1,0:T(8,128)(2,1)S(1)} %slice.413), channel_id=1, source_target_pairs={{0,3},{1,0},{2,1},{3,2},{4,7},{5,4},{6,5},{7,6},{8,11},{9,8},{10,9... | collective-permute-start | bytes 1572872 | tf_op jit(solution)/shard_map/ppermute | solution.py:362
  91.3 18.0 %collective-permute-start.4 = (bf16[144,2048]{1,0:T(8,128)(2,1)S(1)}, bf16[144,2048]{1,0:T(8,128)(2,1)S(1)}, u32[]{:S(2)}, u32[]{:S(2)}) collective-permute-start(bf16[144,2048]{1,0:T(8,128)(2,1)S(1)} %get-tuple-element.288), channel_id=1, source_target_pairs={{0,1},{1,2},{2,3},{3,0},{4,5},{5,6},{6,7},{7,4},{8,9},{9,10},{10,1... | collective-permute-start | bytes 1769480 | tf_op jit(solution)/shard_map/ppermute | solution.py:361
  91.8 27.6 %collective-permute-start.5 = (bf16[144,2048]{1,0:T(8,128)(2,1)S(1)}, bf16[144,2048]{1,0:T(8,128)(2,1)S(1)}, u32[]{:S(2)}, u32[]{:S(2)}) collective-permute-start(bf16[144,2048]{1,0:T(8,128)(2,1)S(1)} %get-tuple-element.288), channel_id=1, source_target_pairs={{0,3},{1,0},{2,1},{3,2},{4,7},{5,4},{6,5},{7,6},{8,11},{9,8},{10,9... | collective-permute-start | bytes 1769480 | tf_op jit(solution)/shard_map/ppermute | solution.py:362
  119.5 16.8 %collective-permute-start.7 = (bf16[72,2048]{1,0:T(8,128)(2,1)S(1)}, bf16[72,2048]{1,0:T(8,128)(2,1)S(1)}, u32[]{:S(2)}, u32[]{:S(2)}) collective-permute-start(bf16[72,2048]{1,0:T(8,128)(2,1)S(1)} %slice.313), channel_id=1, source_target_pairs={{0,3},{1,0},{2,1},{3,2},{4,7},{5,4},{6,5},{7,6},{8,11},{9,8},{10,9... | collective-permute-start | bytes 884744 | tf_op jit(solution)/shard_map/ppermute | solution.py:362
  121.6 13.9 %collective-permute-start.6 = (bf16[72,2048]{1,0:T(8,128)(2,1)S(1)}, bf16[72,2048]{1,0:T(8,128)(2,1)S(1)}, u32[]{:S(2)}, u32[]{:S(2)}) collective-permute-start(bf16[72,2048]{1,0:T(8,128)(2,1)S(1)} %slice.312), channel_id=1, source_target_pairs={{0,1},{1,2},{2,3},{3,0},{4,5},{5,6},{6,7},{7,4},{8,9},{9,10},{10,1... | collective-permute-start | bytes 884744 | tf_op jit(solution)/shard_map/ppermute | solution.py:361
  137.0 181.2 %all-gather.8.cloned.1.call-start = ((), (), s32[]{:S(2)}) async-start(), calls=%async_computation.12 | async-start | bytes 16515072 | tf_op jit(solution)/shard_map/all_gather | solution.py:475
  138.2 17.5 %collective-permute-start.9 = (bf16[112,2048]{1,0:T(8,128)(2,1)S(1)}, bf16[112,2048]{1,0:T(8,128)(2,1)}, u32[]{:S(2)}, u32[]{:S(2)}) collective-permute-start(bf16[112,2048]{1,0:T(8,128)(2,1)S(1)} %slice.314), channel_id=1, source_target_pairs={{0,3},{1,0},{2,1},{3,2},{4,7},{5,4},{6,5},{7,6},{8,11},{9,8},{10,9... | collective-permute-start | bytes 1376264 | tf_op jit(solution)/shard_map/ppermute | solution.py:362
  139.9 19.9 %collective-permute-start.8 = (bf16[112,2048]{1,0:T(8,128)(2,1)S(1)}, bf16[112,2048]{1,0:T(8,128)(2,1)}, u32[]{:S(2)}, u32[]{:S(2)}) collective-permute-start(bf16[112,2048]{1,0:T(8,128)(2,1)S(1)} %slice.314), channel_id=1, source_target_pairs={{0,1},{1,2},{2,3},{3,0},{4,5},{5,6},{6,7},{7,4},{8,9},{9,10},{10,1... | collective-permute-start | bytes 1376264 | tf_op jit(solution)/shard_map/ppermute | solution.py:361
  161.8 11.9 %collective-permute-start.11 = (bf16[56,2048]{1,0:T(8,128)(2,1)S(1)}, bf16[56,2048]{1,0:T(8,128)(2,1)S(1)}, u32[]{:S(2)}, u32[]{:S(2)}) collective-permute-start(bf16[56,2048]{1,0:T(8,128)(2,1)S(1)} %slice.316), channel_id=1, source_target_pairs={{0,3},{1,0},{2,1},{3,2},{4,7},{5,4},{6,5},{7,6},{8,11},{9,8},{10,9... | collective-permute-start | bytes 688136 | tf_op jit(solution)/shard_map/ppermute | solution.py:362
  163.7 9.3 collective-permute-start.10
  174.5 245.7 %all-gather.10.cloned.1.call-start = ((), (), s32[]{:S(2)}) async-start(), calls=%async_computation.13 | async-start | bytes 21233664 | tf_op jit(solution)/shard_map/all_gather | solution.py:524
  183.9 15.4 %collective-permute-start.14 = (bf16[128,2048]{1,0:T(8,128)(2,1)S(1)}, bf16[128,2048]{1,0:T(8,128)(2,1)S(1)}, u32[]{:S(2)}, u32[]{:S(2)}) collective-permute-start(bf16[128,2048]{1,0:T(8,128)(2,1)S(1)} %get-tuple-element.280), channel_id=1, source_target_pairs={{0,3},{1,0},{2,1},{3,2},{4,7},{5,4},{6,5},{7,6},{8,11},{9,8},{10,9... | collective-permute-start | bytes 1572872 | tf_op jit(solution)/shard_map/ppermute | solution.py:362
  186.9 23.8 %collective-permute-start.12 = (bf16[128,2048]{1,0:T(8,128)(2,1)S(1)}, bf16[128,2048]{1,0:T(8,128)(2,1)S(1)}, u32[]{:S(2)}, u32[]{:S(2)}) collective-permute-start(bf16[128,2048]{1,0:T(8,128)(2,1)S(1)} %get-tuple-element.281), channel_id=1, source_target_pairs={{0,1},{1,2},{2,3},{3,0},{4,5},{5,6},{6,7},{7,4},{8,9},{9,10},{10,1... | collective-permute-start | bytes 1572872 | tf_op jit(solution)/shard_map/ppermute | solution.py:361
  212.5 25.4 %collective-permute-start.15 = (bf16[256,2048]{1,0:T(8,128)(2,1)S(1)}, bf16[256,2048]{1,0:T(8,128)(2,1)S(1)}, u32[]{:S(2)}, u32[]{:S(2)}) collective-permute-start(bf16[256,2048]{1,0:T(8,128)(2,1)S(1)} %pad_maximum_fusion.13), channel_id=1, source_target_pairs={{0,3},{1,0},{2,1},{3,2},{4,7},{5,4},{6,5},{7,6},{8,11},{9,8},{10,9... | collective-permute-start | bytes 3145736 | tf_op jit(solution)/shard_map/ppermute | solution.py:362
  214.4 45.1 %collective-permute-start.13 = (bf16[256,2048]{1,0:T(8,128)(2,1)S(1)}, bf16[256,2048]{1,0:T(8,128)(2,1)S(1)}, u32[]{:S(2)}, u32[]{:S(2)}) collective-permute-start(bf16[256,2048]{1,0:T(8,128)(2,1)S(1)} %pad_maximum_fusion.12), channel_id=1, source_target_pairs={{0,1},{1,2},{2,3},{3,0},{4,5},{5,6},{6,7},{7,4},{8,9},{9,10},{10,1... | collective-permute-start | bytes 3145736 | tf_op jit(solution)/shard_map/ppermute | solution.py:361
  264.8 33.6 %collective-permute-start.16 = (bf16[144,2048]{1,0:T(8,128)(2,1)}, bf16[144,2048]{1,0:T(8,128)(2,1)}, u32[]{:S(2)}, u32[]{:S(2)}) collective-permute-start(bf16[144,2048]{1,0:T(8,128)(2,1)} %get-tuple-element.286), channel_id=1, source_target_pairs={{0,1},{1,2},{2,3},{3,0},{4,5},{5,6},{6,7},{7,4},{8,9},{9,10},{10,1... | collective-permute-start | bytes 1769480 | tf_op jit(solution)/shard_map/ppermute | solution.py:361
  266.6 31.8 %collective-permute-start.17 = (bf16[144,2048]{1,0:T(8,128)(2,1)}, bf16[144,2048]{1,0:T(8,128)(2,1)}, u32[]{:S(2)}, u32[]{:S(2)}) collective-permute-start(bf16[144,2048]{1,0:T(8,128)(2,1)} %get-tuple-element.286), channel_id=1, source_target_pairs={{0,3},{1,0},{2,1},{3,2},{4,7},{5,4},{6,5},{7,6},{8,11},{9,8},{10,9... | collective-permute-start | bytes 1769480 | tf_op jit(solution)/shard_map/ppermute | solution.py:362
  299.3 11.8 %collective-permute-start.18 = (bf16[72,2048]{1,0:T(8,128)(2,1)S(1)}, bf16[72,2048]{1,0:T(8,128)(2,1)S(1)}, u32[]{:S(2)}, u32[]{:S(2)}) collective-permute-start(bf16[72,2048]{1,0:T(8,128)(2,1)S(1)} %slice.319), channel_id=1, source_target_pairs={{0,1},{1,2},{2,3},{3,0},{4,5},{5,6},{6,7},{7,4},{8,9},{9,10},{10,1... | collective-permute-start | bytes 884744 | tf_op jit(solution)/shard_map/ppermute | solution.py:361
  302.4 12.4 %collective-permute-start.19 = (bf16[72,2048]{1,0:T(8,128)(2,1)S(1)}, bf16[72,2048]{1,0:T(8,128)(2,1)S(1)}, u32[]{:S(2)}, u32[]{:S(2)}) collective-permute-start(bf16[72,2048]{1,0:T(8,128)(2,1)S(1)} %slice.320), channel_id=1, source_target_pairs={{0,3},{1,0},{2,1},{3,2},{4,7},{5,4},{6,5},{7,6},{8,11},{9,8},{10,9... | collective-permute-start | bytes 884744 | tf_op jit(solution)/shard_map/ppermute | solution.py:362
  318.2 196.2 %all-gather.12.cloned.1.call-start = ((), (), s32[]{:S(2)}) async-start(), calls=%async_computation.14 | async-start | bytes 16515072 | tf_op jit(solution)/shard_map/all_gather | solution.py:524
  321.6 15.2 %collective-permute-start.20 = (bf16[112,2048]{1,0:T(8,128)(2,1)S(1)}, bf16[112,2048]{1,0:T(8,128)(2,1)S(1)}, u32[]{:S(2)}, u32[]{:S(2)}) collective-permute-start(bf16[112,2048]{1,0:T(8,128)(2,1)S(1)} %get-tuple-element.284), channel_id=1, source_target_pairs={{0,1},{1,2},{2,3},{3,0},{4,5},{5,6},{6,7},{7,4},{8,9},{9,10},{10,1... | collective-permute-start | bytes 1376264 | tf_op jit(solution)/shard_map/ppermute | solution.py:361
  323.1 22.3 %collective-permute-start.21 = (bf16[112,2048]{1,0:T(8,128)(2,1)S(1)}, bf16[112,2048]{1,0:T(8,128)(2,1)S(1)}, u32[]{:S(2)}, u32[]{:S(2)}) collective-permute-start(bf16[112,2048]{1,0:T(8,128)(2,1)S(1)} %get-tuple-element.284), channel_id=1, source_target_pairs={{0,3},{1,0},{2,1},{3,2},{4,7},{5,4},{6,5},{7,6},{8,11},{9,8},{10,9... | collective-permute-start | bytes 1376264 | tf_op jit(solution)/shard_map/ppermute | solution.py:362
  336.9 14.7 %collective-permute-start.22 = (bf16[56,2048]{1,0:T(8,128)(2,1)S(1)}, bf16[56,2048]{1,0:T(8,128)(2,1)S(1)}, u32[]{:S(2)}, u32[]{:S(2)}) collective-permute-start(bf16[56,2048]{1,0:T(8,128)(2,1)S(1)} %slice.416), channel_id=1, source_target_pairs={{0,1},{1,2},{2,3},{3,0},{4,5},{5,6},{6,7},{7,4},{8,9},{9,10},{10,1... | collective-permute-start | bytes 688136 | tf_op jit(solution)/shard_map/ppermute | solution.py:361
  345.4 10.4 collective-permute-start.23
  378.3 10.1 all-to-all-start
  380.9 290.8 %reduce-scatter.7.cloned.1.call-start = ((), (), s32[]{:S(2)}) async-start(), calls=%async_computation.15 | async-start | bytes 21233664 | tf_op jit(solution)/shard_map/reduce_scatter | solution.py:529
  579.1 28.5 %collective-permute-start.24 = (bf16[1792,2048]{1,0:T(8,128)(2,1)}, bf16[1792,2048]{1,0:T(8,128)(2,1)}, u32[]{:S(2)}, u32[]{:S(2)}) collective-permute-start(bf16[1792,2048]{1,0:T(8,128)(2,1)} %get-tuple-element.103), channel_id=1, source_target_pairs={{0,4},{4,0},{8,12},{12,8},{16,20},{20,16},{24,28},{28,24},{1,5},{5... | collective-permute-start | bytes 22020104 | tf_op jit(solution)/shard_map/ppermute | solution.py:301
  579.3 98.4 %collective-permute-start.25 = (bf16[2304,2048]{1,0:T(8,128)(2,1)}, bf16[2304,2048]{1,0:T(8,128)(2,1)}, u32[]{:S(2)}, u32[]{:S(2)}) collective-permute-start(bf16[2304,2048]{1,0:T(8,128)(2,1)} %copy-done.5), channel_id=1, source_target_pairs={{0,4},{4,0},{8,12},{12,8},{16,20},{20,16},{24,28},{28,24},{1,5},{5... | collective-permute-start | bytes 28311560 | tf_op jit(solution)/shard_map/ppermute | solution.py:301
  581.6 25.8 %all-to-all-start.1 = ((f32[32,4,256]{2,1,0:T(4,128)}), f32[32,4,256]{2,1,0:T(4,128)S(1)}, u32[]{:S(2)}, u32[]{:S(2)}) async-start(f32[32,4,256]{2,1,0:T(4,128)} %bitcast.169), calls=%async_computation.1 | async-start | bytes 262144 | tf_op jit(solution)/shard_map/all_to_all | solution.py:516
  586.0 133.9 %reduce-scatter.9.cloned.1.call-start = ((), (), s32[]{:S(2)}) async-start(), calls=%async_computation.16 | async-start | bytes 2949120 | tf_op jit(solution)/shard_map/reduce_scatter | solution.py:511
  612.8 58.9 %collective-permute-start.27 = (bf16[2,224,2048]{2,1,0:T(8,128)(2,1)S(1)}, bf16[2,224,2048]{2,1,0:T(8,128)(2,1)}, u32[]{:S(2)}, u32[]{:S(2)}) collective-permute-start(bf16[2,224,2048]{2,1,0:T(8,128)(2,1)S(1)} %pad_maximum_fusion.7), channel_id=1, source_target_pairs={{0,16},{4,20},{8,24},{12,28},{16,0},{20,4},{24,8},{28,12},{1,17},{... | collective-permute-start | bytes 5505032 | tf_op jit(solution)/shard_map/ppermute | solution.py:301
  616.0 55.7 %collective-permute-start.26 = (bf16[2,224,2048]{2,1,0:T(8,128)(2,1)}, bf16[2,224,2048]{2,1,0:T(8,128)(2,1)}, u32[]{:S(2)}, u32[]{:S(2)}) collective-permute-start(bf16[2,224,2048]{2,1,0:T(8,128)(2,1)} %pad_maximum_fusion.6), channel_id=1, source_target_pairs={{0,8},{4,12},{8,0},{12,4},{16,24},{20,28},{24,16},{28,20},{1,9},{5... | collective-permute-start | bytes 5505032 | tf_op jit(solution)/shard_map/ppermute | solution.py:301
  637.5 142.9 %collective-permute-start.32 = (bf16[1792,2048]{1,0:T(8,128)(2,1)}, bf16[1792,2048]{1,0:T(8,128)(2,1)}, u32[]{:S(2)}, u32[]{:S(2)}) collective-permute-start(bf16[1792,2048]{1,0:T(8,128)(2,1)} %copy-done.6), channel_id=1, source_target_pairs={{0,4},{4,0},{8,12},{12,8},{16,20},{20,16},{24,28},{28,24},{1,5},{5... | collective-permute-start | bytes 22020104 | tf_op jit(solution)/shard_map/ppermute | solution.py:301
  671.7 99.9 %reduce-scatter.11.cloned.1.call-start = ((), (), s32[]{:S(2)}) async-start(), calls=%async_computation.17 | async-start | bytes 2293760 | tf_op jit(solution)/shard_map/reduce_scatter | solution.py:511
  675.5 44.4 %collective-permute-start.29 = (bf16[1,224,2048]{2,1,0:T(8,128)(2,1)S(1)}, bf16[1,224,2048]{2,1,0:T(8,128)(2,1)S(1)}, u32[]{:S(2)}, u32[]{:S(2)}) collective-permute-start(bf16[1,224,2048]{2,1,0:T(8,128)(2,1)S(1)} %get-tuple-element.248), channel_id=1, source_target_pairs={{0,16},{4,20},{8,24},{12,28},{16,0},{20,4},{24,8},{28,12},{1,17},{... | collective-permute-start | bytes 2752520 | tf_op jit(solution)/shard_map/ppermute | solution.py:301
  677.1 30.3 %collective-permute-start.30 = (bf16[1,224,2048]{2,1,0:T(8,128)(2,1)S(1)}, bf16[1,224,2048]{2,1,0:T(8,128)(2,1)S(1)}, u32[]{:S(2)}, u32[]{:S(2)}) collective-permute-start(bf16[1,224,2048]{2,1,0:T(8,128)(2,1)S(1)} %get-tuple-element.249), channel_id=1, source_target_pairs={{0,8},{4,12},{8,0},{12,4},{16,24},{20,28},{24,16},{28,20},{1,9},{5... | collective-permute-start | bytes 2752520 | tf_op jit(solution)/shard_map/ppermute | solution.py:301
  684.5 80.9 %collective-permute-start.28 = (bf16[2,288,2048]{2,1,0:T(8,128)(2,1)}, bf16[2,288,2048]{2,1,0:T(8,128)(2,1)}, u32[]{:S(2)}, u32[]{:S(2)}) collective-permute-start(bf16[2,288,2048]{2,1,0:T(8,128)(2,1)} %pad_maximum_fusion.3), channel_id=1, source_target_pairs={{0,8},{4,12},{8,0},{12,4},{16,24},{20,28},{24,16},{28,20},{1,9},{5... | collective-permute-start | bytes 7077896 | tf_op jit(solution)/shard_map/ppermute | solution.py:301
  687.7 77.7 %collective-permute-start.33 = (bf16[2,288,2048]{2,1,0:T(8,128)(2,1)}, bf16[2,288,2048]{2,1,0:T(8,128)(2,1)}, u32[]{:S(2)}, u32[]{:S(2)}) collective-permute-start(bf16[2,288,2048]{2,1,0:T(8,128)(2,1)} %pad_maximum_fusion.4), channel_id=1, source_target_pairs={{0,16},{4,20},{8,24},{12,28},{16,0},{20,4},{24,8},{28,12},{1,17},{... | collective-permute-start | bytes 7077896 | tf_op jit(solution)/shard_map/ppermute | solution.py:301
  725.5 131.7 %all-gather.14.cloned.1.call-start = ((), (), s32[]{:S(2)}) async-start(), calls=%async_computation.19 | async-start | bytes 5242880 | tf_op jit(solution)/shard_map/all_gather | solution.py:587
  776.7 137.2 %reduce-scatter.13.cloned.1.call-start = ((), (), s32[]{:S(2)}) async-start(), calls=%async_computation.18 | async-start | bytes 2949120 | tf_op jit(solution)/shard_map/reduce_scatter | solution.py:511
  777.4 30.8 %collective-permute-start.34 = (bf16[1,288,2048]{2,1,0:T(8,128)(2,1)}, bf16[1,288,2048]{2,1,0:T(8,128)(2,1)S(1)}, u32[]{:S(2)}, u32[]{:S(2)}) collective-permute-start(bf16[1,288,2048]{2,1,0:T(8,128)(2,1)} %get-tuple-element.232), channel_id=1, source_target_pairs={{0,8},{4,12},{8,0},{12,4},{16,24},{20,28},{24,16},{28,20},{1,9},{5... | collective-permute-start | bytes 3538952 | tf_op jit(solution)/shard_map/ppermute | solution.py:301
  778.9 29.3 %collective-permute-start.31 = (bf16[1,288,2048]{2,1,0:T(8,128)(2,1)S(1)}, bf16[1,288,2048]{2,1,0:T(8,128)(2,1)S(1)}, u32[]{:S(2)}, u32[]{:S(2)}) collective-permute-start(bf16[1,288,2048]{2,1,0:T(8,128)(2,1)S(1)} %copy-done.45), channel_id=1, source_target_pairs={{0,16},{4,20},{8,24},{12,28},{16,0},{20,4},{24,8},{28,12},{1,17},{... | collective-permute-start | bytes 3538952 | tf_op jit(solution)/shard_map/ppermute | solution.py:301
  786.9 58.7 %collective-permute-start.37 = (bf16[2,224,2048]{2,1,0:T(8,128)(2,1)}, bf16[2,224,2048]{2,1,0:T(8,128)(2,1)}, u32[]{:S(2)}, u32[]{:S(2)}) collective-permute-start(bf16[2,224,2048]{2,1,0:T(8,128)(2,1)} %pad_maximum_fusion.10), channel_id=1, source_target_pairs={{0,16},{4,20},{8,24},{12,28},{16,0},{20,4},{24,8},{28,12},{1,17},{... | collective-permute-start | bytes 5505032 | tf_op jit(solution)/shard_map/ppermute | solution.py:301
  788.5 57.1 %collective-permute-start.35 = (bf16[2,224,2048]{2,1,0:T(8,128)(2,1)}, bf16[2,224,2048]{2,1,0:T(8,128)(2,1)}, u32[]{:S(2)}, u32[]{:S(2)}) collective-permute-start(bf16[2,224,2048]{2,1,0:T(8,128)(2,1)} %pad_maximum_fusion.9), channel_id=1, source_target_pairs={{0,8},{4,12},{8,0},{12,4},{16,24},{20,28},{24,16},{28,20},{1,9},{5... | collective-permute-start | bytes 5505032 | tf_op jit(solution)/shard_map/ppermute | solution.py:301
  815.1 226.5 %reduce-scatter.15.cloned.1.call-start = ((), (), s32[]{:S(2)}) async-start(), calls=%async_computation.20 | async-start | bytes 2293760 | tf_op jit(solution)/shard_map/reduce_scatter | solution.py:511
  850.6 22.1 %collective-permute-start.36 = (bf16[1,224,2048]{2,1,0:T(8,128)(2,1)}, bf16[1,224,2048]{2,1,0:T(8,128)(2,1)S(1)}, u32[]{:S(2)}, u32[]{:S(2)}) collective-permute-start(bf16[1,224,2048]{2,1,0:T(8,128)(2,1)} %get-tuple-element.240), channel_id=1, source_target_pairs={{0,16},{4,20},{8,24},{12,28},{16,0},{20,4},{24,8},{28,12},{1,17},{... | collective-permute-start | bytes 2752520 | tf_op jit(solution)/shard_map/ppermute | solution.py:301
  852.1 20.7 %collective-permute-start.38 = (bf16[1,224,2048]{2,1,0:T(8,128)(2,1)}, bf16[1,224,2048]{2,1,0:T(8,128)(2,1)S(1)}, u32[]{:S(2)}, u32[]{:S(2)}) collective-permute-start(bf16[1,224,2048]{2,1,0:T(8,128)(2,1)} %get-tuple-element.241), channel_id=1, source_target_pairs={{0,8},{4,12},{8,0},{12,4},{16,24},{20,28},{24,16},{28,20},{1,9},{5... | collective-permute-start | bytes 2752520 | tf_op jit(solution)/shard_map/ppermute | solution.py:301
  925.1 50.2 %collective-permute-start.40 = (bf16[128,2048]{1,0:T(8,128)(2,1)}, bf16[128,2048]{1,0:T(8,128)(2,1)}, u32[]{:S(2)}, u32[]{:S(2)}) collective-permute-start(bf16[128,2048]{1,0:T(8,128)(2,1)} %get-tuple-element.275), channel_id=1, source_target_pairs={{0,3},{1,0},{2,1},{3,2},{4,7},{5,4},{6,5},{7,6},{8,11},{9,8},{10,9... | collective-permute-start | bytes 1572872 | tf_op jit(solution)/shard_map/ppermute | solution.py:362
  927.7 47.6 %collective-permute-start.39 = (bf16[128,2048]{1,0:T(8,128)(2,1)}, bf16[128,2048]{1,0:T(8,128)(2,1)}, u32[]{:S(2)}, u32[]{:S(2)}) collective-permute-start(bf16[128,2048]{1,0:T(8,128)(2,1)} %get-tuple-element.276), channel_id=1, source_target_pairs={{0,1},{1,2},{2,3},{3,0},{4,5},{5,6},{6,7},{7,4},{8,9},{9,10},{10,1... | collective-permute-start | bytes 1572872 | tf_op jit(solution)/shard_map/ppermute | solution.py:361
  928.8 23.0 %all-to-all-start.2 = ((f32[8,5,2048]{2,1,0:T(8,128)}), f32[8,5,2048]{2,1,0:T(8,128)S(1)}, u32[]{:S(2)}, u32[]{:S(2)}) async-start(f32[8,5,2048]{2,1,0:T(8,128)} %reshape.300), calls=%async_computation.7 | async-start | bytes 1048576 | tf_op jit(solution)/shard_map/all_to_all | solution.py:620
  932.3 111.6 %reduce-scatter.17.cloned.1.call-start = ((), (), s32[]{:S(2)}) async-start(), calls=%async_computation.21 | async-start | bytes 4718592 | tf_op jit(solution)/shard_map/reduce_scatter | solution.py:613
  943.9 52.3 %collective-permute-start.43 = (bf16[1024,1280]{1,0:T(8,128)(2,1)}, bf16[1024,1280]{1,0:T(8,128)(2,1)}, u32[]{:S(2)}, u32[]{:S(2)}) collective-permute-start(bf16[1024,1280]{1,0:T(8,128)(2,1)} %pad_maximum_fusion.1), channel_id=1, source_target_pairs={{0,4},{4,0},{8,12},{12,8},{16,20},{20,16},{24,28},{28,24},{1,5},{5... | collective-permute-start | bytes 7864328 | tf_op jit(solution)/shard_map/ppermute | solution.py:301
  952.6 21.7 %all-to-all-start.3 = ((f32[4,5,2048]{2,1,0:T(8,128)}), f32[4,5,2048]{2,1,0:T(8,128)}, u32[]{:S(2)}, u32[]{:S(2)}) async-start(f32[4,5,2048]{2,1,0:T(8,128)} %broadcast_in_dim.100), calls=%async_computation.8 | async-start | bytes 524288 | tf_op jit(solution)/shard_map/all_to_all | solution.py:622
  980.3 13.5 %all-to-all-start.4 = ((f32[8,5,2048]{2,1,0:T(8,128)}), f32[8,5,2048]{2,1,0:T(8,128)S(1)}, u32[]{:S(2)}, u32[]{:S(2)}) async-start(f32[8,5,2048]{2,1,0:T(8,128)} %broadcast_in_dim.102), calls=%async_computation.9 | async-start | bytes 1048576 | tf_op jit(solution)/shard_map/all_to_all | solution.py:631
  984.1 39.3 %collective-permute-start.41 = (bf16[256,2048]{1,0:T(8,128)(2,1)}, bf16[256,2048]{1,0:T(8,128)(2,1)}, u32[]{:S(2)}, u32[]{:S(2)}) collective-permute-start(bf16[256,2048]{1,0:T(8,128)(2,1)} %pad_maximum_fusion.14), channel_id=1, source_target_pairs={{0,1},{1,2},{2,3},{3,0},{4,5},{5,6},{6,7},{7,4},{8,9},{9,10},{10,1... | collective-permute-start | bytes 3145736 | tf_op jit(solution)/shard_map/ppermute | solution.py:361
  984.1 48.3 %collective-permute-start.42 = (bf16[256,2048]{1,0:T(8,128)(2,1)}, bf16[256,2048]{1,0:T(8,128)(2,1)}, u32[]{:S(2)}, u32[]{:S(2)}) collective-permute-start(bf16[256,2048]{1,0:T(8,128)(2,1)} %pad_maximum_fusion.15), channel_id=1, source_target_pairs={{0,3},{1,0},{2,1},{3,2},{4,7},{5,4},{6,5},{7,6},{8,11},{9,8},{10,9... | collective-permute-start | bytes 3145736 | tf_op jit(solution)/shard_map/ppermute | solution.py:362
  997.9 22.0 %collective-permute-start.44 = (bf16[2,128,1280]{2,1,0:T(8,128)(2,1)S(1)}, bf16[2,128,1280]{2,1,0:T(8,128)(2,1)S(1)}, u32[]{:S(2)}, u32[]{:S(2)}) collective-permute-start(bf16[2,128,1280]{2,1,0:T(8,128)(2,1)S(1)} %pad_maximum_fusion.16), channel_id=1, source_target_pairs={{0,8},{4,12},{8,0},{12,4},{16,24},{20,28},{24,16},{28,20},{1,9},{5... | collective-permute-start | bytes 1966088 | tf_op jit(solution)/shard_map/ppermute | solution.py:301
  998.6 21.4 %collective-permute-start.45 = (bf16[2,128,1280]{2,1,0:T(8,128)(2,1)S(1)}, bf16[2,128,1280]{2,1,0:T(8,128)(2,1)S(1)}, u32[]{:S(2)}, u32[]{:S(2)}) collective-permute-start(bf16[2,128,1280]{2,1,0:T(8,128)(2,1)S(1)} %pad_maximum_fusion.17), channel_id=1, source_target_pairs={{0,16},{4,20},{8,24},{12,28},{16,0},{20,4},{24,8},{28,12},{1,17},{... | collective-permute-start | bytes 1966088 | tf_op jit(solution)/shard_map/ppermute | solution.py:301
  1021.3 17.4 %collective-permute-start.47 = (bf16[1,128,1280]{2,1,0:T(8,128)(2,1)S(1)}, bf16[1,128,1280]{2,1,0:T(8,128)(2,1)S(1)}, u32[]{:S(2)}, u32[]{:S(2)}) collective-permute-start(bf16[1,128,1280]{2,1,0:T(8,128)(2,1)S(1)} %get-tuple-element.258), channel_id=1, source_target_pairs={{0,8},{4,12},{8,0},{12,4},{16,24},{20,28},{24,16},{28,20},{1,9},{5... | collective-permute-start | bytes 983048 | tf_op jit(solution)/shard_map/ppermute | solution.py:301
  1022.8 15.9 %collective-permute-start.46 = (bf16[1,128,1280]{2,1,0:T(8,128)(2,1)S(1)}, bf16[1,128,1280]{2,1,0:T(8,128)(2,1)S(1)}, u32[]{:S(2)}, u32[]{:S(2)}) collective-permute-start(bf16[1,128,1280]{2,1,0:T(8,128)(2,1)S(1)} %get-tuple-element.259), channel_id=1, source_target_pairs={{0,16},{4,20},{8,24},{12,28},{16,0},{20,4},{24,8},{28,12},{1,17},{... | collective-permute-start | bytes 983048 | tf_op jit(solution)/shard_map/ppermute | solution.py:301
  (89 other events, 1473.1 us)
Sparse Core Ops, SparseCore 0:
  137.1 98.1 all-gather.5
  237.2 80.9 all-gather.7
  320.7 99.4 all-gather.9
  421.9 80.9 all-gather.11
  506.4 143.9 reduce-scatter.6
  671.9 48.0 reduce-scatter.8
  725.6 38.9 reduce-scatter.10
  776.8 80.2 all-gather.13
  859.4 46.5 reduce-scatter.12
  908.2 56.2 reduce-scatter.14
  967.9 68.0 reduce-scatter.16

commit v4 on v3

--- a/solution.py
+++ b/solution.py
@@ -262,7 +262,7 @@
     out_ref[...] = dot(hidden, w_ref[...]).astype(bf16)
 
 
-def outputs(order, c, hidden_wt, down_w):
+def outputs(order, c, hidden_wt, down_w, flops=1):
     _, members, _, piece, hidden = hidden_wt.shape
     steps = order.shape[0]
     tile = members * piece
@@ -280,7 +280,7 @@
         ),
         out_shape=jax.ShapeDtypeStruct((steps * tile, width), bf16),
         compiler_params=pltpu.CompilerParams(vmem_limit_bytes=32 * MIB),
-        cost_estimate=pl.CostEstimate(flops=1, bytes_accessed=1, transcendentals=0),
+        cost_estimate=pl.CostEstimate(flops=flops, bytes_accessed=1, transcendentals=0),
         name="outputs",
     )(order, hidden_wt, down_w)
 
@@ -374,7 +374,7 @@
     if behind:
         low, high = after((low, high), *behind)
     far_low, far_high = up(low[:cut]), down(high[cut:])
-    whole = jnp.zeros((rows * size, block.shape[1]), block.dtype)
+    whole = after(jnp.zeros((rows * size, block.shape[1]), block.dtype), low)
     for part, member, shift in ((block, 0, 0), (low, 3, 0), (high, 1, 0), (far_low, 2, 0), (far_high, 2, cut)):
         at = lax.rem(me + member, size) * rows + shift
         whole = lax.dynamic_update_slice(whole, part, (at, 0))
@@ -468,11 +468,12 @@
     mixed_all = attend(queries, keys, values.T, local_q, local_kv)
     attn = mixed_all
     if chunks == 2:
-        grad_line = [
-            gather_line(given[:first], (queries,)),
-            gather_line(after(given[first:], queries), (mixed_all,)),
-        ]
-        grad_all = [lax.all_gather(part, "expert", axis=0, tiled=True) for part in grad_line]
+        line_1 = gather_line(given[first:], (queries,))
+        line_0 = gather_line(after(given[:first], queries), (mixed_all,))
+        grad_line = [line_0, line_1]
+        all_1 = lax.all_gather(line_1, "expert", axis=0, tiled=True)
+        all_0 = lax.all_gather(line_0, "expert", axis=0, tiled=True)
+        grad_all = [all_0, all_1]
         pre = [dot(part, down_w, NT).reshape(n_expert, n_tensor, 1, -1, hidden_loc) for part in grad_all]
         attn = after(attn, *grad_line)
     attn = Line(dot(attn, w_out).astype(bf16))
@@ -518,16 +519,15 @@
         return jnp.where(keep, scores.reshape(n_experts, tok_dev), 0.0)
 
     if chunks == 2:
-        moe_line = [gather_line(moe_in[:first], (pre[0],)), gather_line(moe_in[first:])]
+        moe_line = [gather_line(moe_in[:first], (pre[1],)), gather_line(moe_in[first:])]
         gates_0, gates_1 = gates_of(0, first), gates_of(first, tok_dev - first)
-        moe_line[0] = after(moe_line[0], grad_all[1])
+        moe_line[0] = after(moe_line[0], grad_all[0])
         moe_all = [lax.all_gather(part, "expert", axis=0, tiled=True) for part in moe_line]
         front, rear = order[: n_expert // 2], order[n_expert // 2 :]
         fixed = (spread, gate_w, up_w)
-        x_0 = after(moe_all[0], pre[1])
+        x_0 = moe_all[0]
         *kept_0, back_0 = experts(jnp.arange(n_expert, dtype=jnp.int32), 0, x_0, pre[0], gates_0, *fixed)
         back_0 = lax.psum_scatter(back_0, "expert", scatter_dimension=0, tiled=True)
-        back_own = [own_rows(back_0)]
         far_0 = outputs(front, 0, kept_0[0], down_w)
         x_1 = after(moe_all[1], far_0)
         *kept_1, far, near = experts(order, 0, x_1, pre[1], gates_1, *fixed, halves=True)
@@ -537,13 +537,15 @@
         scores = to_tokens([kept_0[3], kept_1[3]])
         sent = back_1.send(gate_grad, scores)
         hidden_0, hidden_1 = after((kept_0[0], kept_1[0]), *sent)
-        near_0 = outputs(rear, 0, hidden_0, down_w)
         far_1, near_1 = (outputs(part, 0, hidden_1, down_w) for part in (front, rear))
-        sent = back_1.send(near_0, far_1, near_1, back_0)
+        back_0 = after(back_0, far_1, near_1)
+        back_own = [own_rows(back_0)]
+        sent = back_1.send(far_1, near_1)
+        near_flops = 2 * 2 * n_expert // 2 * n_tensor * first * width * hidden_loc
+        near_0 = outputs(rear, 0, after(hidden_0, *sent), down_w, near_flops)
         out_0, out_1 = Exchange(far_0, near_0, bits), Exchange(far_1, near_1, bits)
         sent = out_0.send(*sent)
-        up_grad = dot(after(x_0, *sent), kept_0[2], TN)
-        back_1 = back_1.total(up_grad, back_own[0])
+        back_1 = back_1.total(*sent, back_own[0])
         back_own.append(own_rows(back_1))
         x_1, g_0 = after((moe_all[1], grad_all[0]), back_1)
         gate_grad = gate_grad + dot(x_1, kept_1[1], TN)
@@ -587,8 +589,8 @@
     middle_all = lax.all_gather(middle_grad.astype(bf16), "tensor", axis=0, tiled=True)
     if chunks == 2:
         sent = out_1.send(middle_grad)
-        x_1, g_1 = after((moe_all[1], grad_all[1]), *sent)
-        up_grad = up_grad + dot(x_1, kept_1[2], TN)
+        x_0, x_1, g_1 = after((moe_all[0], moe_all[1], grad_all[1]), *sent)
+        up_grad = dot(x_0, kept_0[2], TN) + dot(x_1, kept_1[2], TN)
         out_0 = out_0.total(up_grad)
         down_grad = down_grad + dot(kept_1[0].reshape(-1, hidden_loc), after(g_1, out_0), TN)
         sent = out_1.send(down_grad)

time: 1060 us -> 1040 us (0.981)
  waiting for transfers between devices: 315 us -> 285 us
    ppermute x14, waiting for transfers between devices: 95.8 us -> 80.9 us  [neighbours(): lax.ppermute(v, 'tensor', [(i, (i - 1) % size) for i in range(size)])]
    reduce_scatter x4, waiting for transfers between devices: 12.5 us -> 0.01 us  [own_rows(): return lax.psum_scatter(part, 'tensor', scatter_dimension=0, tiled=True)]
    unnamed x179 -> x181, local copies, waits for them, and re-layouts: 33.4 us -> 37.2 us
    dynamic_update_slice x21 -> x24, local copies, waits for them, and re-layouts: 22.3 us -> 22.8 us  [gather_line(): whole = lax.dynamic_update_slice(whole, part, (at, 0))]
  transfers between devices with their start and end apart: 64 -> 64, of which waited for: 31 -> 32; matrix products, arithmetic and copies ran while one was open for 35% -> 37% of each run, Pallas kernels for 21% -> 21%
where the time goes in v4:
time: 1040 us; the launch traced here: 1030 us
  waiting for transfers between devices  285 us (27%)
  Pallas kernels  220 us (21%)
  matrix products  208 us (20%)
  other arithmetic  109 us (10%)
  local copies, waits for them, and re-layouts  104 us (10%)
  starting transfers between devices  90.8 us (9%)
  between operations  15.6 us (2%)
    dot_general x16, matrix products, dot(): lax.dot_general(a, b, (contract, ((), ())), preferred_element_type=f32)  208 us
    pallas_call x2, Pallas kernels, experts(): pl.pallas_call(functools.partial(experts_kernel, len(held)), grid_spec=pl...  139 us
    ppermute x14, waiting for transfers between devices, neighbours(): lax.ppermute(v, 'tensor', [(i, (i + 1) % size) for i in range(size)])  111 us
    ppermute x14, waiting for transfers between devices, neighbours(): lax.ppermute(v, 'tensor', [(i, (i - 1) % size) for i in range(size)])  80.9 us
    ppermute x20, waiting for transfers between devices, hop(): return lax.ppermute(block, axis, [(i, i ^ bit) for i in range(size)])  54.8 us
    ppermute x14, starting transfers between devices, neighbours(): lax.ppermute(v, 'tensor', [(i, (i - 1) % size) for i in range(size)])  42.8 us
    unnamed x181, local copies, waits for them, and re-layouts  37.2 us
    convert_element_type x8, other arithmetic, send(): add = lambda parts: sum((p.astype(f32) for p in parts)).astype(bf16)  35.4 us
  transfers between devices with their start and end apart: 64, of which 32 were waited for; matrix products, arithmetic and copies ran while one was open for 37% of the time, Pallas kernels for 21%

profile of v4, /device:TPU:0, one launch (start us, length us, event | category | flops | bytes accessed | tf_op | source)
XLA Modules:
  0.0 1032.3 jit_solution(4746870453766761894)
XLA Ops:
  11.6 5.1 collective-permute-start.1
  19.1 21.2 %collective-permute-done.1 = bf16[256,2048]{1,0:T(8,128)(2,1)S(1)} collective-permute-done((bf16[256,2048]{1,0:T(8,128)(2,1)S(1)}, bf16[256,2048]{1,0:T(8,128)(2,1)S(1)}, u32[]{:S(2)}, u32[]{:S(2)}) %collective-permute-start.1) | collective-permute-done | bytes 1048608 | tf_op jit(solution)/shard_map/ppermute | solution.py:362
  40.3 4.3 collective-permute-start.3
  44.7 19.0 %collective-permute-done = bf16[256,2048]{1,0:T(8,128)(2,1)S(1)} collective-permute-done((bf16[256,2048]{1,0:T(8,128)(2,1)S(1)}, bf16[256,2048]{1,0:T(8,128)(2,1)S(1)}, u32[]{:S(2)}, u32[]{:S(2)}) %collective-permute-start) | collective-permute-done | bytes 1048608 | tf_op jit(solution)/shard_map/ppermute | solution.py:361
  66.4 18.6 %collective-permute-done.2 = bf16[128,2048]{1,0:T(8,128)(2,1)S(1)} collective-permute-done((bf16[128,2048]{1,0:T(8,128)(2,1)S(1)}, bf16[128,2048]{1,0:T(8,128)(2,1)S(1)}, u32[]{:S(2)}, u32[]{:S(2)}) %collective-permute-start.2) | collective-permute-done | bytes 524320 | tf_op jit(solution)/shard_map/ppermute | solution.py:361
  88.0 9.8 project.1
  98.9 9.9 collective-permute-done.8
  126.0 11.7 %attend.1 = bf16[1024,1024]{1,0:T(8,128)(2,1)S(1)} custom-call(bf16[1024,1024]{1,0:T(8,128)(2,1)S(1)} %get-tuple-element.92.q_ref, bf16[1024,128]{1,0:T(8,128)(2,1)S(1)} %get-tuple-element.93.k_ref, bf16[128,1024]{1,0:T(8,128)(2,1)S(1)} %bitcast.152), custom_call_target="tpu_custom_call" | custom-call | flops 3221225472 | bytes 4194304 | tf_op jit(solution)/shard_map/attend/pallas_call | solution.py:88
  139.9 10.9 %collective-permute-done.4 = bf16[144,2048]{1,0:T(8,128)(2,1)} collective-permute-done((bf16[144,2048]{1,0:T(8,128)(2,1)}, bf16[144,2048]{1,0:T(8,128)(2,1)}, u32[]{:S(2)}, u32[]{:S(2)}) %collective-permute-start.4) | collective-permute-done | bytes 589856 | tf_op jit(solution)/shard_map/ppermute | solution.py:361
  158.3 4.1 copy.86
  169.9 6.9 convolution_convert_fusion.2
  181.4 12.8 %collective-permute-done.14 = bf16[128,2048]{1,0:T(8,128)(2,1)S(1)} collective-permute-done((bf16[128,2048]{1,0:T(8,128)(2,1)S(1)}, bf16[128,2048]{1,0:T(8,128)(2,1)S(1)}, u32[]{:S(2)}, u32[]{:S(2)}) %collective-permute-start.14) | collective-permute-done | bytes 524320 | tf_op jit(solution)/shard_map/ppermute | solution.py:362
  194.2 8.4 collective-permute-done.12
  206.5 23.3 %collective-permute-done.15 = bf16[256,2048]{1,0:T(8,128)(2,1)S(1)} collective-permute-done((bf16[256,2048]{1,0:T(8,128)(2,1)S(1)}, bf16[256,2048]{1,0:T(8,128)(2,1)S(1)}, u32[]{:S(2)}, u32[]{:S(2)}) %collective-permute-start.15) | collective-permute-done | bytes 1048608 | tf_op jit(solution)/shard_map/ppermute | solution.py:362
  229.8 22.7 %collective-permute-done.13 = bf16[256,2048]{1,0:T(8,128)(2,1)S(1)} collective-permute-done((bf16[256,2048]{1,0:T(8,128)(2,1)S(1)}, bf16[256,2048]{1,0:T(8,128)(2,1)S(1)}, u32[]{:S(2)}, u32[]{:S(2)}) %collective-permute-start.13) | collective-permute-done | bytes 1048608 | tf_op jit(solution)/shard_map/ppermute | solution.py:361
  259.9 17.4 %convolution_bitcast_fusion.1.pre_ref = f32[8,4,1,112,768]{4,3,2,1,0:T(8,128)} fusion(bf16[8,4,112,2048]{3,2,1,0:T(8,128)(2,1)} %bitcast.175, bf16[768,2048,1,1]{1,0,3,2:T(8,128)(2,1)S(1)} %bitcast.138), kind=kOutput, calls=%fused_computation.10 | convolution fusion | flops 11274289152 | bytes 28835840 | tf_op jit(solution)/shard_map/dot_general | solution.py:20
  277.2 8.3 collective-permute-done.16
  297.1 4.4 collective-permute-done.19
  308.4 10.9 %collective-permute-done.21 = bf16[112,2048]{1,0:T(8,128)(2,1)S(1)} collective-permute-done((bf16[112,2048]{1,0:T(8,128)(2,1)S(1)}, bf16[112,2048]{1,0:T(8,128)(2,1)S(1)}, u32[]{:S(2)}, u32[]{:S(2)}) %collective-permute-start.21) | collective-permute-done | bytes 458784 | tf_op jit(solution)/shard_map/ppermute | solution.py:362
  319.3 4.3 collective-permute-start.23
  323.6 6.5 collective-permute-done.20
  335.2 4.1 collective-permute-done.22
  340.7 4.6 copy.70.wg_ref
  345.3 4.6 copy.71.wu_ref
  352.9 5.7 convert_reduce_fusion
  362.3 4.3 all-to-all-start
  367.7 6.4 all-to-all-done
  378.6 20.5 %convolution_bitcast_fusion.pre_ref = f32[8,4,1,144,768]{4,3,2,1,0:T(8,128)} fusion(bf16[8,4,144,2048]{3,2,1,0:T(8,128)(2,1)} %bitcast.174, bf16[768,2048,1,1]{1,0,3,2:T(8,128)(2,1)S(1)} %bitcast.139), kind=kOutput, calls=%fused_computation.1 | convolution fusion | flops 14495514624 | bytes 36175872 | tf_op jit(solution)/shard_map/dot_general | solution.py:20
  399.1 6.7 all-gather.10.cloned.1.call-done.x_ref
  406.3 74.6 %experts.2 = (bf16[8,4,1,144,768]{4,3,2,1,0:T(8,128)(2,1)}, bf16[4608,768]{1,0:T(8,128)(2,1)}, bf16[4608,768]{1,0:T(8,128)(2,1)}, f32[8,8,576]{2,1,0:T(8,128)}, bf16[4608,2048]{1,0:T(8,128)(2,1)}) custom-call(s32[8]{0:T(128)} %iota.42.order, bf16[4608,2048]{1,0:T(8,128)(2,1)} %all-gather.10.cloned.1.call-done.x_ref, ...), custom_call_target="tpu_custom_call" | custom-call | flops 57982058496 | bytes 73138176 | tf_op jit(solution)/shard_map/experts/pallas_call | solution.py:232
  487.0 8.6 outputs.4
  495.6 4.3 copy-done.4
  499.9 64.2 %experts.3 = (bf16[8,4,1,112,768]{4,3,2,1,0:T(8,128)(2,1)}, bf16[3584,768]{1,0:T(8,128)(2,1)}, bf16[3584,768]{1,0:T(8,128)(2,1)}, f32[8,8,448]{2,1,0:T(8,128)}, ...) custom-call(s32[8]{0:T(128)} %copy-done.80, bf16[3584,2048]{1,0:T(8,128)(2,1)} %all-gather.12.cloned.1.call-done.x_ref, ...), custom_call_target="tpu_custom_call" | custom-call | flops 45097156608 | bytes 56885248 | tf_op jit(solution)/shard_map/experts/pallas_call | solution.py:232
  569.7 4.5 all-to-all-start.1
  574.2 21.4 %fusion.30 = f32[2048,768]{0,1:T(8,128)} fusion(bf16[4608,2048]{1,0:T(8,128)(2,1)} %all-gather.10.cloned.1.call-done.x_ref, bf16[4608,768]{1,0:T(8,128)(2,1)} %get-tuple-element.116), kind=kOutput, calls=%fused_computation.190 | convolution fusion | flops 14495514624 | bytes 32243712 | tf_op jit(solution)/shard_map/dot_general | solution.py:20
  596.4 5.2 add_convert_fusion.22
  607.4 7.1 outputs.5
  617.4 7.0 outputs.6
  635.4 22.0 %collective-permute-done.26 = bf16[2,224,2048]{2,1,0:T(8,128)(2,1)} collective-permute-done((bf16[2,224,2048]{2,1,0:T(8,128)(2,1)}, bf16[2,224,2048]{2,1,0:T(8,128)(2,1)}, u32[]{:S(2)}, u32[]{:S(2)}) %collective-permute-start.26) | collective-permute-done | bytes 1835040 | tf_op jit(solution)/shard_map/ppermute | solution.py:301
  657.4 4.7 add_convert_fusion.20
  667.1 8.6 outputs.7
  675.7 6.8 add_convert_fusion.5
  687.7 4.6 fusion.9
  693.8 21.6 %fusion.31 = f32[768,2048]{1,0:T(8,128)} fusion(bf16[4608,768]{1,0:T(8,128)(2,1)} %bitcast.150, bf16[4608,2048]{1,0:T(8,128)(2,1)} %all-gather.8.cloned.1.call-done), kind=kOutput, calls=%fused_computation.191 | convolution fusion | flops 14495514624 | bytes 32243712 | tf_op jit(solution)/shard_map/dot_general | solution.py:20
  715.5 18.3 %convolution_add_fusion.2 = f32[2048,768]{0,1:T(8,128)} fusion(f32[2048,768]{0,1:T(8,128)S(1)} %bitcast.180, bf16[3584,2048]{1,0:T(8,128)(2,1)} %all-gather.12.cloned.1.call-done.x_ref, bf16[3584,768]{1,0:T(8,128)(2,1)} %get-tuple-element.130), kind=kOutput, calls=%fused_computation.14 | convolution fusion | flops 11275862016 | bytes 32768000 | tf_op jit(solution)/shard_map/dot_general | solution.py:20
  739.5 6.1 add_convert_fusion.2
  753.1 4.7 add_convert_fusion.16
  762.6 18.3 %fusion.32 = f32[2048,768]{0,1:T(8,128)} fusion(bf16[3584,2048]{1,0:T(8,128)(2,1)} %all-gather.12.cloned.1.call-done.x_ref, bf16[3584,768]{1,0:T(8,128)(2,1)} %get-tuple-element.140), kind=kOutput, calls=%fused_computation.192 | convolution fusion | flops 11274289152 | bytes 26476544 | tf_op jit(solution)/shard_map/dot_general | solution.py:20
  780.9 23.7 %convolution_add_fusion = f32[2048,768]{0,1:T(8,128)} fusion(f32[2048,768]{0,1:T(8,128)} %fusion.32, bf16[4608,2048]{1,0:T(8,128)(2,1)} %all-gather.10.cloned.1.call-done.x_ref, bf16[4608,768]{1,0:T(8,128)(2,1)} %get-tuple-element.138), kind=kOutput, calls=%fused_computation.9 | convolution fusion | flops 14497087488 | bytes 38535168 | tf_op jit(solution)/shard_map/dot_general | solution.py:20
  804.5 5.9 fusion.6
  812.1 19.4 %convolution_add_fusion.1 = f32[768,2048]{1,0:T(8,128)} fusion(f32[768,2048]{1,0:T(8,128)} %fusion.31, bf16[3584,768]{1,0:T(8,128)(2,1)} %bitcast.144, bf16[3584,2048]{1,0:T(8,128)(2,1)} %all-gather.6.cloned.1.call-done), kind=kOutput, calls=%fused_computation.11 | convolution fusion | flops 11275862016 | bytes 32768000 | tf_op jit(solution)/shard_map/dot_general | solution.py:20
  831.6 4.9 add_convert_fusion.12
  838.8 9.8 convolution_convert_fusion.3.do_ref
  848.5 8.6 collective-permute-done.38
  858.1 4.3 fusion.11
  869.9 27.9 %attend_back.1 = (bf16[1024,1024]{1,0:T(8,128)(2,1)S(1)}, bf16[1024,128]{1,0:T(8,128)(2,1)S(1)}, bf16[1024,128]{1,0:T(8,128)(2,1)S(1)}, f32[1,128]{1,0:T(1,128)S(1)}, f32[1,128]{1,0:T(1,128)S(1)}) custom-call(bf16[1024,1024]{1,0:T(8,128)(2,1)S(1)} %copy-done.25, bf16[1024,1024]{1,0:T(8,128)(2,1)S(1)} %copy-done.29, f32[1024,1152]{1,0:T(8,128)S(1)} %copy-done.23, ...), custom_call_target="tpu_custom_call" | custom-call | flops 7516192768 | bytes 10485760 | tf_op jit(solution)/shard_map/attend_back/pallas_call | solution.py:159
  899.6 9.8 multiply_reduce_fusion
  918.6 8.5 convolution_convert_fusion
  931.8 6.3 convolution_convert_fusion.1
  938.8 5.1 all-to-all-start.3
  945.5 7.9 all-to-all-done.3
  967.3 11.5 %all-to-all-done.4 = f32[8,5,2048]{2,1,0:T(8,128)S(1)} async-done(((f32[8,5,2048]{2,1,0:T(8,128)}), f32[8,5,2048]{2,1,0:T(8,128)S(1)}, u32[]{:S(2)}, u32[]{:S(2)}) %all-to-all-start.4) | async-done | bytes 327712 | tf_op jit(solution)/shard_map/all_to_all | solution.py:633
  985.3 17.6 %collective-permute-done.44 = bf16[2,128,1280]{2,1,0:T(8,128)(2,1)S(1)} collective-permute-done((bf16[2,128,1280]{2,1,0:T(8,128)(2,1)S(1)}, bf16[2,128,1280]{2,1,0:T(8,128)(2,1)S(1)}, u32[]{:S(2)}, u32[]{:S(2)}) %collective-permute-start.44) | collective-permute-done | bytes 655392 | tf_op jit(solution)/shard_map/ppermute | solution.py:301
  1007.1 4.7 collective-permute-done.42
  (429 shorter events, 230.9 us)
Async XLA Ops:
  7.2 252.7 %all-gather.6.cloned.1.call-start = ((), (), s32[]{:S(2)}) async-start(), calls=%async_computation.11 | async-start | bytes 16515072 | tf_op jit(solution)/shard_map/all_gather | solution.py:474
  11.6 28.7 %collective-permute-start.1 = (bf16[256,2048]{1,0:T(8,128)(2,1)S(1)}, bf16[256,2048]{1,0:T(8,128)(2,1)S(1)}, u32[]{:S(2)}, u32[]{:S(2)}) collective-permute-start(bf16[256,2048]{1,0:T(8,128)(2,1)S(1)} %fusion.4), channel_id=1, source_target_pairs={{0,3},{1,0},{2,1},{3,2},{4,7},{5,4},{6,5},{7,6},{8,11},{9,8},{10,9... | collective-permute-start | bytes 3145736 | tf_op jit(solution)/shard_map/ppermute | solution.py:362
  16.7 47.0 %collective-permute-start = (bf16[256,2048]{1,0:T(8,128)(2,1)S(1)}, bf16[256,2048]{1,0:T(8,128)(2,1)S(1)}, u32[]{:S(2)}, u32[]{:S(2)}) collective-permute-start(bf16[256,2048]{1,0:T(8,128)(2,1)S(1)} %fusion.4), channel_id=1, source_target_pairs={{0,1},{1,2},{2,3},{3,0},{4,5},{5,6},{6,7},{7,4},{8,9},{9,10},{10,1... | collective-permute-start | bytes 3145736 | tf_op jit(solution)/shard_map/ppermute | solution.py:361
  40.3 44.8 %collective-permute-start.3 = (bf16[128,2048]{1,0:T(8,128)(2,1)S(1)}, bf16[128,2048]{1,0:T(8,128)(2,1)S(1)}, u32[]{:S(2)}, u32[]{:S(2)}) collective-permute-start(bf16[128,2048]{1,0:T(8,128)(2,1)S(1)} %slice.413), channel_id=1, source_target_pairs={{0,3},{1,0},{2,1},{3,2},{4,7},{5,4},{6,5},{7,6},{8,11},{9,8},{10,9... | collective-permute-start | bytes 1572872 | tf_op jit(solution)/shard_map/ppermute | solution.py:362
  63.8 21.3 %collective-permute-start.2 = (bf16[128,2048]{1,0:T(8,128)(2,1)S(1)}, bf16[128,2048]{1,0:T(8,128)(2,1)S(1)}, u32[]{:S(2)}, u32[]{:S(2)}) collective-permute-start(bf16[128,2048]{1,0:T(8,128)(2,1)S(1)} %slice.412), channel_id=1, source_target_pairs={{0,1},{1,2},{2,3},{3,0},{4,5},{5,6},{6,7},{7,4},{8,9},{9,10},{10,1... | collective-permute-start | bytes 1572872 | tf_op jit(solution)/shard_map/ppermute | solution.py:361
  85.2 13.7 %collective-permute-start.9 = (bf16[112,2048]{1,0:T(8,128)(2,1)S(1)}, bf16[112,2048]{1,0:T(8,128)(2,1)S(1)}, u32[]{:S(2)}, u32[]{:S(2)}) collective-permute-start(bf16[112,2048]{1,0:T(8,128)(2,1)S(1)} %slice.314), channel_id=1, source_target_pairs={{0,3},{1,0},{2,1},{3,2},{4,7},{5,4},{6,5},{7,6},{8,11},{9,8},{10,9... | collective-permute-start | bytes 1376264 | tf_op jit(solution)/shard_map/ppermute | solution.py:362
  87.9 20.9 %collective-permute-start.8 = (bf16[112,2048]{1,0:T(8,128)(2,1)S(1)}, bf16[112,2048]{1,0:T(8,128)(2,1)S(1)}, u32[]{:S(2)}, u32[]{:S(2)}) collective-permute-start(bf16[112,2048]{1,0:T(8,128)(2,1)S(1)} %slice.314), channel_id=1, source_target_pairs={{0,1},{1,2},{2,3},{3,0},{4,5},{5,6},{6,7},{7,4},{8,9},{9,10},{10,1... | collective-permute-start | bytes 1376264 | tf_op jit(solution)/shard_map/ppermute | solution.py:361
  108.8 10.4 %collective-permute-start.10 = (bf16[56,2048]{1,0:T(8,128)(2,1)S(1)}, bf16[56,2048]{1,0:T(8,128)(2,1)S(1)}, u32[]{:S(2)}, u32[]{:S(2)}) collective-permute-start(bf16[56,2048]{1,0:T(8,128)(2,1)S(1)} %slice.315), channel_id=1, source_target_pairs={{0,1},{1,2},{2,3},{3,0},{4,5},{5,6},{6,7},{7,4},{8,9},{9,10},{10,1... | collective-permute-start | bytes 688136 | tf_op jit(solution)/shard_map/ppermute | solution.py:361
  109.5 10.7 %collective-permute-start.11 = (bf16[56,2048]{1,0:T(8,128)(2,1)S(1)}, bf16[56,2048]{1,0:T(8,128)(2,1)S(1)}, u32[]{:S(2)}, u32[]{:S(2)}) collective-permute-start(bf16[56,2048]{1,0:T(8,128)(2,1)S(1)} %slice.316), channel_id=1, source_target_pairs={{0,3},{1,0},{2,1},{3,2},{4,7},{5,4},{6,5},{7,6},{8,11},{9,8},{10,9... | collective-permute-start | bytes 688136 | tf_op jit(solution)/shard_map/ppermute | solution.py:362
  120.9 183.0 %all-gather.8.cloned.1.call-start = ((), (), s32[]{:S(2)}) async-start(), calls=%async_computation.12 | async-start | bytes 21233664 | tf_op jit(solution)/shard_map/all_gather | solution.py:475
  122.9 17.1 %collective-permute-start.5 = (bf16[144,2048]{1,0:T(8,128)(2,1)}, bf16[144,2048]{1,0:T(8,128)(2,1)}, u32[]{:S(2)}, u32[]{:S(2)}) collective-permute-start(bf16[144,2048]{1,0:T(8,128)(2,1)} %slice.311), channel_id=1, source_target_pairs={{0,3},{1,0},{2,1},{3,2},{4,7},{5,4},{6,5},{7,6},{8,11},{9,8},{10,9... | collective-permute-start | bytes 1769480 | tf_op jit(solution)/shard_map/ppermute | solution.py:362
  125.8 25.0 %collective-permute-start.4 = (bf16[144,2048]{1,0:T(8,128)(2,1)}, bf16[144,2048]{1,0:T(8,128)(2,1)}, u32[]{:S(2)}, u32[]{:S(2)}) collective-permute-start(bf16[144,2048]{1,0:T(8,128)(2,1)} %slice.311), channel_id=1, source_target_pairs={{0,1},{1,2},{2,3},{3,0},{4,5},{5,6},{6,7},{7,4},{8,9},{9,10},{10,1... | collective-permute-start | bytes 1769480 | tf_op jit(solution)/shard_map/ppermute | solution.py:361
  152.7 15.6 %collective-permute-start.6 = (bf16[72,2048]{1,0:T(8,128)(2,1)S(1)}, bf16[72,2048]{1,0:T(8,128)(2,1)S(1)}, u32[]{:S(2)}, u32[]{:S(2)}) collective-permute-start(bf16[72,2048]{1,0:T(8,128)(2,1)S(1)} %slice.312), channel_id=1, source_target_pairs={{0,1},{1,2},{2,3},{3,0},{4,5},{5,6},{6,7},{7,4},{8,9},{9,10},{10,1... | collective-permute-start | bytes 884744 | tf_op jit(solution)/shard_map/ppermute | solution.py:361
  153.6 15.5 %collective-permute-start.7 = (bf16[72,2048]{1,0:T(8,128)(2,1)S(1)}, bf16[72,2048]{1,0:T(8,128)(2,1)S(1)}, u32[]{:S(2)}, u32[]{:S(2)}) collective-permute-start(bf16[72,2048]{1,0:T(8,128)(2,1)S(1)} %slice.313), channel_id=1, source_target_pairs={{0,3},{1,0},{2,1},{3,2},{4,7},{5,4},{6,5},{7,6},{8,11},{9,8},{10,9... | collective-permute-start | bytes 884744 | tf_op jit(solution)/shard_map/ppermute | solution.py:362
  169.9 235.9 %all-gather.10.cloned.1.call-start = ((), (), s32[]{:S(2)}) async-start(), calls=%async_computation.13 | async-start | bytes 21233664 | tf_op jit(solution)/shard_map/all_gather | solution.py:525
  179.1 15.1 %collective-permute-start.14 = (bf16[128,2048]{1,0:T(8,128)(2,1)S(1)}, bf16[128,2048]{1,0:T(8,128)(2,1)S(1)}, u32[]{:S(2)}, u32[]{:S(2)}) collective-permute-start(bf16[128,2048]{1,0:T(8,128)(2,1)S(1)} %get-tuple-element.290), channel_id=1, source_target_pairs={{0,3},{1,0},{2,1},{3,2},{4,7},{5,4},{6,5},{7,6},{8,11},{9,8},{10,9... | collective-permute-start | bytes 1572872 | tf_op jit(solution)/shard_map/ppermute | solution.py:362
  179.7 22.8 %collective-permute-start.12 = (bf16[128,2048]{1,0:T(8,128)(2,1)S(1)}, bf16[128,2048]{1,0:T(8,128)(2,1)S(1)}, u32[]{:S(2)}, u32[]{:S(2)}) collective-permute-start(bf16[128,2048]{1,0:T(8,128)(2,1)S(1)} %get-tuple-element.291), channel_id=1, source_target_pairs={{0,1},{1,2},{2,3},{3,0},{4,5},{5,6},{6,7},{7,4},{8,9},{9,10},{10,1... | collective-permute-start | bytes 1572872 | tf_op jit(solution)/shard_map/ppermute | solution.py:361
  204.2 25.6 %collective-permute-start.15 = (bf16[256,2048]{1,0:T(8,128)(2,1)S(1)}, bf16[256,2048]{1,0:T(8,128)(2,1)S(1)}, u32[]{:S(2)}, u32[]{:S(2)}) collective-permute-start(bf16[256,2048]{1,0:T(8,128)(2,1)S(1)} %pad_maximum_fusion.13), channel_id=1, source_target_pairs={{0,3},{1,0},{2,1},{3,2},{4,7},{5,4},{6,5},{7,6},{8,11},{9,8},{10,9... | collective-permute-start | bytes 3145736 | tf_op jit(solution)/shard_map/ppermute | solution.py:362
  206.3 46.1 %collective-permute-start.13 = (bf16[256,2048]{1,0:T(8,128)(2,1)S(1)}, bf16[256,2048]{1,0:T(8,128)(2,1)S(1)}, u32[]{:S(2)}, u32[]{:S(2)}) collective-permute-start(bf16[256,2048]{1,0:T(8,128)(2,1)S(1)} %pad_maximum_fusion.12), channel_id=1, source_target_pairs={{0,1},{1,2},{2,3},{3,0},{4,5},{5,6},{6,7},{7,4},{8,9},{9,10},{10,1... | collective-permute-start | bytes 3145736 | tf_op jit(solution)/shard_map/ppermute | solution.py:361
  257.8 19.4 %collective-permute-start.17 = (bf16[144,2048]{1,0:T(8,128)(2,1)}, bf16[144,2048]{1,0:T(8,128)(2,1)}, u32[]{:S(2)}, u32[]{:S(2)}) collective-permute-start(bf16[144,2048]{1,0:T(8,128)(2,1)} %slice.414), channel_id=1, source_target_pairs={{0,3},{1,0},{2,1},{3,2},{4,7},{5,4},{6,5},{7,6},{8,11},{9,8},{10,9... | collective-permute-start | bytes 1769480 | tf_op jit(solution)/shard_map/ppermute | solution.py:362
  259.9 25.7 %collective-permute-start.16 = (bf16[144,2048]{1,0:T(8,128)(2,1)}, bf16[144,2048]{1,0:T(8,128)(2,1)}, u32[]{:S(2)}, u32[]{:S(2)}) collective-permute-start(bf16[144,2048]{1,0:T(8,128)(2,1)} %slice.414), channel_id=1, source_target_pairs={{0,1},{1,2},{2,3},{3,0},{4,5},{5,6},{6,7},{7,4},{8,9},{9,10},{10,1... | collective-permute-start | bytes 1769480 | tf_op jit(solution)/shard_map/ppermute | solution.py:361
  286.5 9.9 collective-permute-start.18
  292.1 9.4 collective-permute-start.19
  303.9 196.0 %all-gather.12.cloned.1.call-start = ((), (), s32[]{:S(2)}) async-start(), calls=%async_computation.14 | async-start | bytes 16515072 | tf_op jit(solution)/shard_map/all_gather | solution.py:525
  305.0 14.3 %collective-permute-start.21 = (bf16[112,2048]{1,0:T(8,128)(2,1)S(1)}, bf16[112,2048]{1,0:T(8,128)(2,1)S(1)}, u32[]{:S(2)}, u32[]{:S(2)}) collective-permute-start(bf16[112,2048]{1,0:T(8,128)(2,1)S(1)} %slice.415), channel_id=1, source_target_pairs={{0,3},{1,0},{2,1},{3,2},{4,7},{5,4},{6,5},{7,6},{8,11},{9,8},{10,9... | collective-permute-start | bytes 1376264 | tf_op jit(solution)/shard_map/ppermute | solution.py:362
  308.4 21.7 %collective-permute-start.20 = (bf16[112,2048]{1,0:T(8,128)(2,1)S(1)}, bf16[112,2048]{1,0:T(8,128)(2,1)S(1)}, u32[]{:S(2)}, u32[]{:S(2)}) collective-permute-start(bf16[112,2048]{1,0:T(8,128)(2,1)S(1)} %slice.415), channel_id=1, source_target_pairs={{0,1},{1,2},{2,3},{3,0},{4,5},{5,6},{6,7},{7,4},{8,9},{9,10},{10,1... | collective-permute-start | bytes 1376264 | tf_op jit(solution)/shard_map/ppermute | solution.py:361
  319.3 20.7 %collective-permute-start.23 = (bf16[56,2048]{1,0:T(8,128)(2,1)S(1)}, bf16[56,2048]{1,0:T(8,128)(2,1)S(1)}, u32[]{:S(2)}, u32[]{:S(2)}) collective-permute-start(bf16[56,2048]{1,0:T(8,128)(2,1)S(1)} %slice.417), channel_id=1, source_target_pairs={{0,3},{1,0},{2,1},{3,2},{4,7},{5,4},{6,5},{7,6},{8,11},{9,8},{10,9... | collective-permute-start | bytes 688136 | tf_op jit(solution)/shard_map/ppermute | solution.py:362
  330.1 9.1 collective-permute-start.22
  362.3 11.9 %all-to-all-start = ((bf16[32,4,256]{2,1,0:T(4,128)(2,1)}), bf16[32,4,256]{2,1,0:T(4,128)(2,1)S(1)}, u32[]{:S(2)}, u32[]{:S(2)}) async-start(bf16[32,4,256]{2,1,0:T(4,128)(2,1)} %bitcast.19), calls=%async_computation | async-start | bytes 131072 | tf_op jit(solution)/shard_map/all_to_all | solution.py:502
  366.7 264.7 %reduce-scatter.7.cloned.1.call-start = ((), (), s32[]{:S(2)}) async-start(), calls=%async_computation.15 | async-start | bytes 21233664 | tf_op jit(solution)/shard_map/reduce_scatter | solution.py:530
  564.1 32.3 %collective-permute-start.24 = (bf16[1792,2048]{1,0:T(8,128)(2,1)}, bf16[1792,2048]{1,0:T(8,128)(2,1)}, u32[]{:S(2)}, u32[]{:S(2)}) collective-permute-start(bf16[1792,2048]{1,0:T(8,128)(2,1)} %get-tuple-element.113), channel_id=1, source_target_pairs={{0,4},{4,0},{8,12},{12,8},{16,20},{20,16},{24,28},{28,24},{1,5},{5... | collective-permute-start | bytes 22020104 | tf_op jit(solution)/shard_map/ppermute | solution.py:301
  564.3 111.4 %collective-permute-start.27 = (bf16[2304,2048]{1,0:T(8,128)(2,1)}, bf16[2304,2048]{1,0:T(8,128)(2,1)}, u32[]{:S(2)}, u32[]{:S(2)}) collective-permute-start(bf16[2304,2048]{1,0:T(8,128)(2,1)} %copy-done.4), channel_id=1, source_target_pairs={{0,4},{4,0},{8,12},{12,8},{16,20},{20,16},{24,28},{28,24},{1,5},{5... | collective-permute-start | bytes 28311560 | tf_op jit(solution)/shard_map/ppermute | solution.py:301
  569.7 26.0 %all-to-all-start.1 = ((f32[32,4,256]{2,1,0:T(4,128)}), f32[32,4,256]{2,1,0:T(4,128)S(1)}, u32[]{:S(2)}, u32[]{:S(2)}) async-start(f32[32,4,256]{2,1,0:T(4,128)} %bitcast.167), calls=%async_computation.1 | async-start | bytes 262144 | tf_op jit(solution)/shard_map/all_to_all | solution.py:517
  574.1 113.6 %reduce-scatter.9.cloned.1.call-start = ((), (), s32[]{:S(2)}) async-start(), calls=%async_computation.16 | async-start | bytes 2949120 | tf_op jit(solution)/shard_map/reduce_scatter | solution.py:512
  603.1 54.3 %collective-permute-start.26 = (bf16[2,224,2048]{2,1,0:T(8,128)(2,1)}, bf16[2,224,2048]{2,1,0:T(8,128)(2,1)}, u32[]{:S(2)}, u32[]{:S(2)}) collective-permute-start(bf16[2,224,2048]{2,1,0:T(8,128)(2,1)} %pad_maximum_fusion.7), channel_id=1, source_target_pairs={{0,16},{4,20},{8,24},{12,28},{16,0},{20,4},{24,8},{28,12},{1,17},{... | collective-permute-start | bytes 5505032 | tf_op jit(solution)/shard_map/ppermute | solution.py:301
  606.2 51.2 %collective-permute-start.25 = (bf16[2,224,2048]{2,1,0:T(8,128)(2,1)}, bf16[2,224,2048]{2,1,0:T(8,128)(2,1)}, u32[]{:S(2)}, u32[]{:S(2)}) collective-permute-start(bf16[2,224,2048]{2,1,0:T(8,128)(2,1)} %pad_maximum_fusion.6), channel_id=1, source_target_pairs={{0,8},{4,12},{8,0},{12,4},{16,24},{20,28},{24,16},{28,20},{1,9},{5... | collective-permute-start | bytes 5505032 | tf_op jit(solution)/shard_map/ppermute | solution.py:301
  631.4 116.3 %reduce-scatter.11.cloned.1.call-start = ((), (), s32[]{:S(2)}) async-start(), calls=%async_computation.17 | async-start | bytes 2293760 | tf_op jit(solution)/shard_map/reduce_scatter | solution.py:512
  635.4 117.5 %collective-permute-start.32 = (bf16[1792,2048]{1,0:T(8,128)(2,1)}, bf16[1792,2048]{1,0:T(8,128)(2,1)}, u32[]{:S(2)}, u32[]{:S(2)}) collective-permute-start(bf16[1792,2048]{1,0:T(8,128)(2,1)} %copy-done.5), channel_id=1, source_target_pairs={{0,4},{4,0},{8,12},{12,8},{16,20},{20,16},{24,28},{28,24},{1,5},{5... | collective-permute-start | bytes 22020104 | tf_op jit(solution)/shard_map/ppermute | solution.py:301
  662.1 25.7 %collective-permute-start.29 = (bf16[1,224,2048]{2,1,0:T(8,128)(2,1)}, bf16[1,224,2048]{2,1,0:T(8,128)(2,1)}, u32[]{:S(2)}, u32[]{:S(2)}) collective-permute-start(bf16[1,224,2048]{2,1,0:T(8,128)(2,1)} %get-tuple-element.258), channel_id=1, source_target_pairs={{0,16},{4,20},{8,24},{12,28},{16,0},{20,4},{24,8},{28,12},{1,17},{... | collective-permute-start | bytes 2752520 | tf_op jit(solution)/shard_map/ppermute | solution.py:301
  663.5 24.2 %collective-permute-start.30 = (bf16[1,224,2048]{2,1,0:T(8,128)(2,1)S(1)}, bf16[1,224,2048]{2,1,0:T(8,128)(2,1)}, u32[]{:S(2)}, u32[]{:S(2)}) collective-permute-start(bf16[1,224,2048]{2,1,0:T(8,128)(2,1)S(1)} %get-tuple-element.259), channel_id=1, source_target_pairs={{0,8},{4,12},{8,0},{12,4},{16,24},{20,28},{24,16},{28,20},{1,9},{5... | collective-permute-start | bytes 2752520 | tf_op jit(solution)/shard_map/ppermute | solution.py:301
  684.1 52.8 %collective-permute-start.28 = (bf16[2,288,2048]{2,1,0:T(8,128)(2,1)}, bf16[2,288,2048]{2,1,0:T(8,128)(2,1)}, u32[]{:S(2)}, u32[]{:S(2)}) collective-permute-start(bf16[2,288,2048]{2,1,0:T(8,128)(2,1)} %pad_maximum_fusion.3), channel_id=1, source_target_pairs={{0,8},{4,12},{8,0},{12,4},{16,24},{20,28},{24,16},{28,20},{1,9},{5... | collective-permute-start | bytes 7077896 | tf_op jit(solution)/shard_map/ppermute | solution.py:301
  687.2 52.3 %collective-permute-start.33 = (bf16[2,288,2048]{2,1,0:T(8,128)(2,1)}, bf16[2,288,2048]{2,1,0:T(8,128)(2,1)}, u32[]{:S(2)}, u32[]{:S(2)}) collective-permute-start(bf16[2,288,2048]{2,1,0:T(8,128)(2,1)} %pad_maximum_fusion.4), channel_id=1, source_target_pairs={{0,16},{4,20},{8,24},{12,28},{16,0},{20,4},{24,8},{28,12},{1,17},{... | collective-permute-start | bytes 7077896 | tf_op jit(solution)/shard_map/ppermute | solution.py:301
  693.7 145.0 %all-gather.14.cloned.1.call-start = ((), (), s32[]{:S(2)}) async-start(), calls=%async_computation.19 | async-start | bytes 5242880 | tf_op jit(solution)/shard_map/all_gather | solution.py:589
  745.6 58.9 %collective-permute-start.34 = (bf16[1,288,2048]{2,1,0:T(8,128)(2,1)}, bf16[1,288,2048]{2,1,0:T(8,128)(2,1)}, u32[]{:S(2)}, u32[]{:S(2)}) collective-permute-start(bf16[1,288,2048]{2,1,0:T(8,128)(2,1)} %get-tuple-element.242), channel_id=1, source_target_pairs={{0,8},{4,12},{8,0},{12,4},{16,24},{20,28},{24,16},{28,20},{1,9},{5... | collective-permute-start | bytes 3538952 | tf_op jit(solution)/shard_map/ppermute | solution.py:301
  746.4 58.2 %collective-permute-start.31 = (bf16[1,288,2048]{2,1,0:T(8,128)(2,1)}, bf16[1,288,2048]{2,1,0:T(8,128)(2,1)}, u32[]{:S(2)}, u32[]{:S(2)}) collective-permute-start(bf16[1,288,2048]{2,1,0:T(8,128)(2,1)} %get-tuple-element.243), channel_id=1, source_target_pairs={{0,16},{4,20},{8,24},{12,28},{16,0},{20,4},{24,8},{28,12},{1,17},{... | collective-permute-start | bytes 3538952 | tf_op jit(solution)/shard_map/ppermute | solution.py:301
  752.9 146.7 %reduce-scatter.13.cloned.1.call-start = ((), (), s32[]{:S(2)}) async-start(), calls=%async_computation.18 | async-start | bytes 2949120 | tf_op jit(solution)/shard_map/reduce_scatter | solution.py:512
  759.2 72.3 %collective-permute-start.37 = (bf16[2,224,2048]{2,1,0:T(8,128)(2,1)}, bf16[2,224,2048]{2,1,0:T(8,128)(2,1)S(1)}, u32[]{:S(2)}, u32[]{:S(2)}) collective-permute-start(bf16[2,224,2048]{2,1,0:T(8,128)(2,1)} %pad_maximum_fusion.10), channel_id=1, source_target_pairs={{0,16},{4,20},{8,24},{12,28},{16,0},{20,4},{24,8},{28,12},{1,17},{... | collective-permute-start | bytes 5505032 | tf_op jit(solution)/shard_map/ppermute | solution.py:301
  761.3 70.2 %collective-permute-start.35 = (bf16[2,224,2048]{2,1,0:T(8,128)(2,1)}, bf16[2,224,2048]{2,1,0:T(8,128)(2,1)}, u32[]{:S(2)}, u32[]{:S(2)}) collective-permute-start(bf16[2,224,2048]{2,1,0:T(8,128)(2,1)} %pad_maximum_fusion.9), channel_id=1, source_target_pairs={{0,8},{4,12},{8,0},{12,4},{16,24},{20,28},{24,16},{28,20},{1,9},{5... | collective-permute-start | bytes 5505032 | tf_op jit(solution)/shard_map/ppermute | solution.py:301
  812.1 208.8 %reduce-scatter.15.cloned.1.call-start = ((), (), s32[]{:S(2)}) async-start(), calls=%async_computation.20 | async-start | bytes 2293760 | tf_op jit(solution)/shard_map/reduce_scatter | solution.py:512
  836.5 21.6 %collective-permute-start.36 = (bf16[1,224,2048]{2,1,0:T(8,128)(2,1)S(1)}, bf16[1,224,2048]{2,1,0:T(8,128)(2,1)S(1)}, u32[]{:S(2)}, u32[]{:S(2)}) collective-permute-start(bf16[1,224,2048]{2,1,0:T(8,128)(2,1)S(1)} %get-tuple-element.250), channel_id=1, source_target_pairs={{0,16},{4,20},{8,24},{12,28},{16,0},{20,4},{24,8},{28,12},{1,17},{... | collective-permute-start | bytes 2752520 | tf_op jit(solution)/shard_map/ppermute | solution.py:301
  837.3 19.8 %collective-permute-start.38 = (bf16[1,224,2048]{2,1,0:T(8,128)(2,1)}, bf16[1,224,2048]{2,1,0:T(8,128)(2,1)S(1)}, u32[]{:S(2)}, u32[]{:S(2)}) collective-permute-start(bf16[1,224,2048]{2,1,0:T(8,128)(2,1)} %get-tuple-element.251), channel_id=1, source_target_pairs={{0,8},{4,12},{8,0},{12,4},{16,24},{20,28},{24,16},{28,20},{1,9},{5... | collective-permute-start | bytes 2752520 | tf_op jit(solution)/shard_map/ppermute | solution.py:301
  910.8 43.6 %collective-permute-start.40 = (bf16[128,2048]{1,0:T(8,128)(2,1)}, bf16[128,2048]{1,0:T(8,128)(2,1)}, u32[]{:S(2)}, u32[]{:S(2)}) collective-permute-start(bf16[128,2048]{1,0:T(8,128)(2,1)} %get-tuple-element.285), channel_id=1, source_target_pairs={{0,3},{1,0},{2,1},{3,2},{4,7},{5,4},{6,5},{7,6},{8,11},{9,8},{10,9... | collective-permute-start | bytes 1572872 | tf_op jit(solution)/shard_map/ppermute | solution.py:362
  914.0 40.4 %collective-permute-start.39 = (bf16[128,2048]{1,0:T(8,128)(2,1)}, bf16[128,2048]{1,0:T(8,128)(2,1)}, u32[]{:S(2)}, u32[]{:S(2)}) collective-permute-start(bf16[128,2048]{1,0:T(8,128)(2,1)} %get-tuple-element.286), channel_id=1, source_target_pairs={{0,1},{1,2},{2,3},{3,0},{4,5},{5,6},{6,7},{7,4},{8,9},{9,10},{10,1... | collective-permute-start | bytes 1572872 | tf_op jit(solution)/shard_map/ppermute | solution.py:361
  915.1 23.0 %all-to-all-start.2 = ((f32[8,5,2048]{2,1,0:T(8,128)}), f32[8,5,2048]{2,1,0:T(8,128)S(1)}, u32[]{:S(2)}, u32[]{:S(2)}) async-start(f32[8,5,2048]{2,1,0:T(8,128)} %reshape.300), calls=%async_computation.7 | async-start | bytes 1048576 | tf_op jit(solution)/shard_map/all_to_all | solution.py:622
  918.6 104.6 %reduce-scatter.17.cloned.1.call-start = ((), (), s32[]{:S(2)}) async-start(), calls=%async_computation.21 | async-start | bytes 4718592 | tf_op jit(solution)/shard_map/reduce_scatter | solution.py:615
  930.2 50.8 %collective-permute-start.43 = (bf16[1024,1280]{1,0:T(8,128)(2,1)}, bf16[1024,1280]{1,0:T(8,128)(2,1)}, u32[]{:S(2)}, u32[]{:S(2)}) collective-permute-start(bf16[1024,1280]{1,0:T(8,128)(2,1)} %pad_maximum_fusion.1), channel_id=1, source_target_pairs={{0,4},{4,0},{8,12},{12,8},{16,20},{20,16},{24,28},{28,24},{1,5},{5... | collective-permute-start | bytes 7864328 | tf_op jit(solution)/shard_map/ppermute | solution.py:301
  938.8 14.6 %all-to-all-start.3 = ((f32[4,5,2048]{2,1,0:T(8,128)}), f32[4,5,2048]{2,1,0:T(8,128)}, u32[]{:S(2)}, u32[]{:S(2)}) async-start(f32[4,5,2048]{2,1,0:T(8,128)} %broadcast_in_dim.100), calls=%async_computation.8 | async-start | bytes 524288 | tf_op jit(solution)/shard_map/all_to_all | solution.py:624
  959.5 19.2 %all-to-all-start.4 = ((f32[8,5,2048]{2,1,0:T(8,128)}), f32[8,5,2048]{2,1,0:T(8,128)S(1)}, u32[]{:S(2)}, u32[]{:S(2)}) async-start(f32[8,5,2048]{2,1,0:T(8,128)} %broadcast_in_dim.102), calls=%async_computation.9 | async-start | bytes 1048576 | tf_op jit(solution)/shard_map/all_to_all | solution.py:633
  963.4 43.6 %collective-permute-start.41 = (bf16[256,2048]{1,0:T(8,128)(2,1)}, bf16[256,2048]{1,0:T(8,128)(2,1)}, u32[]{:S(2)}, u32[]{:S(2)}) collective-permute-start(bf16[256,2048]{1,0:T(8,128)(2,1)} %pad_maximum_fusion.14), channel_id=1, source_target_pairs={{0,1},{1,2},{2,3},{3,0},{4,5},{5,6},{6,7},{7,4},{8,9},{9,10},{10,1... | collective-permute-start | bytes 3145736 | tf_op jit(solution)/shard_map/ppermute | solution.py:361
  963.5 48.3 %collective-permute-start.42 = (bf16[256,2048]{1,0:T(8,128)(2,1)}, bf16[256,2048]{1,0:T(8,128)(2,1)}, u32[]{:S(2)}, u32[]{:S(2)}) collective-permute-start(bf16[256,2048]{1,0:T(8,128)(2,1)} %pad_maximum_fusion.15), channel_id=1, source_target_pairs={{0,3},{1,0},{2,1},{3,2},{4,7},{5,4},{6,5},{7,6},{8,11},{9,8},{10,9... | collective-permute-start | bytes 3145736 | tf_op jit(solution)/shard_map/ppermute | solution.py:362
  982.8 20.1 %collective-permute-start.44 = (bf16[2,128,1280]{2,1,0:T(8,128)(2,1)S(1)}, bf16[2,128,1280]{2,1,0:T(8,128)(2,1)S(1)}, u32[]{:S(2)}, u32[]{:S(2)}) collective-permute-start(bf16[2,128,1280]{2,1,0:T(8,128)(2,1)S(1)} %pad_maximum_fusion.16), channel_id=1, source_target_pairs={{0,8},{4,12},{8,0},{12,4},{16,24},{20,28},{24,16},{28,20},{1,9},{5... | collective-permute-start | bytes 1966088 | tf_op jit(solution)/shard_map/ppermute | solution.py:301
  982.9 20.7 %collective-permute-start.45 = (bf16[2,128,1280]{2,1,0:T(8,128)(2,1)S(1)}, bf16[2,128,1280]{2,1,0:T(8,128)(2,1)S(1)}, u32[]{:S(2)}, u32[]{:S(2)}) collective-permute-start(bf16[2,128,1280]{2,1,0:T(8,128)(2,1)S(1)} %pad_maximum_fusion.17), channel_id=1, source_target_pairs={{0,16},{4,20},{8,24},{12,28},{16,0},{20,4},{24,8},{28,12},{1,17},{... | collective-permute-start | bytes 1966088 | tf_op jit(solution)/shard_map/ppermute | solution.py:301
  1005.0 13.0 %collective-permute-start.47 = (bf16[1,128,1280]{2,1,0:T(8,128)(2,1)S(1)}, bf16[1,128,1280]{2,1,0:T(8,128)(2,1)S(1)}, u32[]{:S(2)}, u32[]{:S(2)}) collective-permute-start(bf16[1,128,1280]{2,1,0:T(8,128)(2,1)S(1)} %get-tuple-element.268), channel_id=1, source_target_pairs={{0,8},{4,12},{8,0},{12,4},{16,24},{20,28},{24,16},{28,20},{1,9},{5... | collective-permute-start | bytes 983048 | tf_op jit(solution)/shard_map/ppermute | solution.py:301
  1005.8 12.2 %collective-permute-start.46 = (bf16[1,128,1280]{2,1,0:T(8,128)(2,1)S(1)}, bf16[1,128,1280]{2,1,0:T(8,128)(2,1)S(1)}, u32[]{:S(2)}, u32[]{:S(2)}) collective-permute-start(bf16[1,128,1280]{2,1,0:T(8,128)(2,1)S(1)} %get-tuple-element.269), channel_id=1, source_target_pairs={{0,16},{4,20},{8,24},{12,28},{16,0},{20,4},{24,8},{28,12},{1,17},{... | collective-permute-start | bytes 983048 | tf_op jit(solution)/shard_map/ppermute | solution.py:301
  (89 other events, 1646.3 us)
Sparse Core Ops, SparseCore 0:
  121.0 81.5 all-gather.5
  205.1 98.7 all-gather.7
  306.3 99.4 all-gather.9
  407.5 80.9 all-gather.11
  492.0 139.2 reduce-scatter.6
  633.5 47.8 reduce-scatter.8
  693.9 39.4 reduce-scatter.10
  753.0 80.6 all-gather.13
  836.0 46.5 reduce-scatter.12
  884.7 47.8 reduce-scatter.14
  938.2 65.2 reduce-scatter.16

commit v5 on v4

--- a/solution.py
+++ b/solution.py
@@ -285,6 +285,30 @@
     )(order, hidden_wt, down_w)
 
 
+def rows_product_kernel(x_ref, g_ref, out_ref):
+    @pl.when(pl.program_id(0) == 0)
+    def _():
+        out_ref[...] = jnp.zeros_like(out_ref)
+
+    out_ref[...] += dot(x_ref[...], g_ref[...], TN)
+
+
+def rows_product(x, g):
+    rows, width = x.shape
+    columns = g.shape[1]
+    tile = rows // 4
+    return pl.pallas_call(
+        rows_product_kernel,
+        grid=(4,),
+        in_specs=[pl.BlockSpec((tile, width), lambda j: (j, 0)), pl.BlockSpec((tile, columns), lambda j: (j, 0))],
+        out_specs=pl.BlockSpec((width, columns), lambda j: (0, 0)),
+        out_shape=jax.ShapeDtypeStruct((width, columns), f32),
+        compiler_params=pltpu.CompilerParams(vmem_limit_bytes=52 * MIB),
+        cost_estimate=pl.CostEstimate(flops=1, bytes_accessed=1, transcendentals=0),
+        name="rows_product",
+    )(x, g)
+
+
 TOPK = 8
 
 
@@ -532,25 +556,24 @@
         x_1 = after(moe_all[1], far_0)
         *kept_1, far, near = experts(order, 0, x_1, pre[1], gates_1, *fixed, halves=True)
         back_1 = Exchange(far, near, bits)
-        x_0 = after(moe_all[0], kept_1[3])
-        gate_grad = dot(x_0, kept_0[1], TN)
         scores = to_tokens([kept_0[3], kept_1[3]])
-        sent = back_1.send(gate_grad, scores)
-        hidden_0, hidden_1 = after((kept_0[0], kept_1[0]), *sent)
-        far_1, near_1 = (outputs(part, 0, hidden_1, down_w) for part in (front, rear))
-        back_0 = after(back_0, far_1, near_1)
+        far_1, near_1 = (outputs(part, 0, kept_1[0], down_w) for part in (front, rear))
+        sent = back_1.send(far_1, near_1, scores)
+        x_0, hidden_0 = after((moe_all[0], kept_0[0]), *sent)
+        gate_grad = rows_product(x_0, kept_0[1])
+        back_0 = after(back_0, gate_grad)
         back_own = [own_rows(back_0)]
-        sent = back_1.send(far_1, near_1)
+        sent = back_1.send(gate_grad)
         near_flops = 2 * 2 * n_expert // 2 * n_tensor * first * width * hidden_loc
         near_0 = outputs(rear, 0, after(hidden_0, *sent), down_w, near_flops)
         out_0, out_1 = Exchange(far_0, near_0, bits), Exchange(far_1, near_1, bits)
-        sent = out_0.send(*sent)
-        back_1 = back_1.total(*sent, back_own[0])
+        sent = out_1.send(*sent)
+        back_1 = back_1.total(*sent, near_0, back_own[0])
         back_own.append(own_rows(back_1))
         x_1, g_0 = after((moe_all[1], grad_all[0]), back_1)
         gate_grad = gate_grad + dot(x_1, kept_1[1], TN)
         down_grad = dot(kept_0[0].reshape(-1, hidden_loc), g_0, TN)
-        sent = out_0.send(gate_grad, down_grad)
+        sent = out_1.send(gate_grad, down_grad)
         back_own = after(back_own, *sent)
     else:
         def one_chunk(sums, c):
@@ -588,24 +611,24 @@
 
     middle_all = lax.all_gather(middle_grad.astype(bf16), "tensor", axis=0, tiled=True)
     if chunks == 2:
-        sent = out_1.send(middle_grad)
+        sent = out_0.send(middle_grad)
         x_0, x_1, g_1 = after((moe_all[0], moe_all[1], grad_all[1]), *sent)
         up_grad = dot(x_0, kept_0[2], TN) + dot(x_1, kept_1[2], TN)
-        out_0 = out_0.total(up_grad)
-        down_grad = down_grad + dot(kept_1[0].reshape(-1, hidden_loc), after(g_1, out_0), TN)
-        sent = out_1.send(down_grad)
+        out_1 = out_1.total(up_grad)
+        down_grad = down_grad + dot(kept_1[0].reshape(-1, hidden_loc), after(g_1, out_1), TN)
+        sent = out_0.send(down_grad)
         middle_all = after(middle_all, *sent)
     mixed_grad = dot(middle_all, w_out, NT).astype(bf16)
     if chunks == 2:
-        out_1 = out_1.total(mixed_grad)
-        mixed_grad = after(mixed_grad, out_1)
+        out_0 = out_0.total(mixed_grad)
+        mixed_grad = after(mixed_grad, out_0)
     dq, dk, dv, query_gain_grad, key_gain_grad = attend_back(
         queries, mixed_grad, raw, keys, keys.T, values, q_gain, k_gain, cosine, sine, local_q, local_kv
     )
     qkv_grad = jnp.concatenate([dq, dk, dv], axis=1)
     if chunks == 2:
-        out_own = [own_rows(part) for part in (out_0, out_1)]
-        qkv_grad = after(qkv_grad, out_own[0])
+        out_own = [own_rows(part) for part in (out_1, out_0)][::-1]
+        qkv_grad = after(qkv_grad, out_own[1])
         moe_out = jnp.concatenate(out_own, axis=0)
     normed_part = dot(qkv_grad, w_qkv, NT)
     normed_low = normed_part.astype(bf16)
@@ -620,28 +643,28 @@
     small = jnp.concatenate([router_grad, *gain_rows], axis=0)
     small = jnp.pad(small, ((0, -small.shape[0] % n_expert), (0, 0))).reshape(n_expert, -1, width)
     small = lax.all_to_all(small, "expert", 0, 0, tiled=True).sum(axis=0)
-    small = jnp.broadcast_to(small[None], (n_tensor, *small.shape))
-    small = lax.all_to_all(small, "tensor", 0, 0, tiled=True).sum(axis=0)
     blocks = weight_grad.reshape(n_expert, -1, weight_grad.shape[1])
     blocks = [lax.dynamic_index_in_dim(blocks, place ^ r, 0, keepdims=False) for r in step_order(bits)]
     far, near = (
         jnp.concatenate(part, axis=0) for part in (blocks[: n_expert // 2], blocks[n_expert // 2 :])
     )
     grad_qkv = Exchange(far, near, bits)
-    sent = normed_line.send(small, far, near)
+    if chunks == 2:
+        grads = [down_grad, gate_grad, up_grad]
+    grad_down = grads[0].reshape(local_experts, quarter, width)
+    grad_gate, grad_up = (
+        part.reshape(width, local_experts, quarter).transpose(1, 0, 2) for part in grads[1:]
+    )
+    sent = normed_line.send(far, near, grad_gate, grad_up)
     small = after(small, *sent) if sent else small
+    for bit in bits_of(n_tensor):
+        small = small + hop(small, bit, "tensor")
     small = lax.all_to_all(jnp.broadcast_to(small[None], (n_expert, *small.shape)), "expert", 0, 0, tiled=True)
     small = small.reshape(-1, width)
     sent = sum([grad_qkv.send(*sent) for _ in bits[1:]], [])
     grad_qkv = grad_qkv.total().astype(f32)
     normed_grad = normed_line.total(*sent)
     layer_out = (middle + moe_out.astype(f32)).astype(bf16)
-    if chunks == 2:
-        grads = [down_grad, gate_grad, up_grad]
-    grad_down = grads[0].reshape(local_experts, quarter, width)
-    grad_gate, grad_up = (
-        part.reshape(width, local_experts, quarter).transpose(1, 0, 2) for part in grads[1:]
-    )
     hidden_part, _ = attn_pull(normed_grad)
     input_grad = middle_grad + hidden_part
     return (

time: 1040 us -> 1040 us (level)
  matrix products: 208 us -> 183 us
  Pallas kernels: 220 us -> 244 us
    dot_general x16 -> x15, matrix products: 208 us -> 183 us  [dot(): lax.dot_general(a, b, (contract, ((), ())), preferred_element_type=f32)]
    pallas_call x0 -> x1, Pallas kernels: none -> 23.5 us  [rows_product(): pl.pallas_call(rows_product_kernel, grid=(4,), in_specs=[pl.BlockSpec((ti...]
    unnamed x181 -> x175, local copies, waits for them, and re-layouts: 37.2 us -> 41.2 us
    ppermute x20 -> x22, waiting for transfers between devices: 54.8 us -> 58.8 us  [hop(): return lax.ppermute(block, axis, [(i, i ^ bit) for i in range(size)])]
  transfers between devices with their start and end apart: 64 -> 65, of which waited for: 32 -> 30; matrix products, arithmetic and copies ran while one was open for 37% -> 35% of each run, Pallas kernels for 21% -> 24%
where the time goes in v5:
time: 1040 us; the launch traced here: 1030 us
  waiting for transfers between devices  278 us (27%)
  Pallas kernels  244 us (23%)
  matrix products  183 us (18%)
  local copies, waits for them, and re-layouts  112 us (11%)
  other arithmetic  108 us (10%)
  starting transfers between devices  87.8 us (8%)
  between operations  15.6 us (2%)
    dot_general x15, matrix products, dot(): lax.dot_general(a, b, (contract, ((), ())), preferred_element_type=f32)  183 us
    pallas_call x2, Pallas kernels, experts(): pl.pallas_call(functools.partial(experts_kernel, len(held)), grid_spec=pl...  139 us
    ppermute x14, waiting for transfers between devices, neighbours(): lax.ppermute(v, 'tensor', [(i, (i + 1) % size) for i in range(size)])  111 us
    ppermute x14, waiting for transfers between devices, neighbours(): lax.ppermute(v, 'tensor', [(i, (i - 1) % size) for i in range(size)])  81.6 us
    ppermute x22, waiting for transfers between devices, hop(): return lax.ppermute(block, axis, [(i, i ^ bit) for i in range(size)])  58.8 us
    ppermute x14, starting transfers between devices, neighbours(): lax.ppermute(v, 'tensor', [(i, (i - 1) % size) for i in range(size)])  42.2 us
    unnamed x175, local copies, waits for them, and re-layouts  41.2 us
    convert_element_type x8, other arithmetic, send(): add = lambda parts: sum((p.astype(f32) for p in parts)).astype(bf16)  33.6 us
  transfers between devices with their start and end apart: 65, of which 30 were waited for; matrix products, arithmetic and copies ran while one was open for 35% of the time, Pallas kernels for 24%

profile of v5, /device:TPU:0, one launch (start us, length us, event | category | flops | bytes accessed | tf_op | source)
XLA Modules:
  0.0 1027.8 jit_solution(10781953461427383068)
XLA Ops:
  11.6 5.1 collective-permute-start.1
  19.1 21.2 %collective-permute-done.1 = bf16[256,2048]{1,0:T(8,128)(2,1)S(1)} collective-permute-done((bf16[256,2048]{1,0:T(8,128)(2,1)S(1)}, bf16[256,2048]{1,0:T(8,128)(2,1)S(1)}, u32[]{:S(2)}, u32[]{:S(2)}) %collective-permute-start.1) | collective-permute-done | bytes 1048608 | tf_op jit(solution)/shard_map/ppermute | solution.py:386
  40.3 4.3 collective-permute-start.3
  44.7 19.0 %collective-permute-done = bf16[256,2048]{1,0:T(8,128)(2,1)S(1)} collective-permute-done((bf16[256,2048]{1,0:T(8,128)(2,1)S(1)}, bf16[256,2048]{1,0:T(8,128)(2,1)S(1)}, u32[]{:S(2)}, u32[]{:S(2)}) %collective-permute-start) | collective-permute-done | bytes 1048608 | tf_op jit(solution)/shard_map/ppermute | solution.py:385
  66.4 18.6 %collective-permute-done.2 = bf16[128,2048]{1,0:T(8,128)(2,1)S(1)} collective-permute-done((bf16[128,2048]{1,0:T(8,128)(2,1)S(1)}, bf16[128,2048]{1,0:T(8,128)(2,1)S(1)}, u32[]{:S(2)}, u32[]{:S(2)}) %collective-permute-start.2) | collective-permute-done | bytes 524320 | tf_op jit(solution)/shard_map/ppermute | solution.py:385
  88.0 9.8 project.1
  98.9 9.9 collective-permute-done.8
  126.0 11.7 %attend.1 = bf16[1024,1024]{1,0:T(8,128)(2,1)S(1)} custom-call(bf16[1024,1024]{1,0:T(8,128)(2,1)S(1)} %get-tuple-element.91.q_ref, bf16[1024,128]{1,0:T(8,128)(2,1)S(1)} %get-tuple-element.92.k_ref, bf16[128,1024]{1,0:T(8,128)(2,1)S(1)} %bitcast.152), custom_call_target="tpu_custom_call" | custom-call | flops 3221225472 | bytes 4194304 | tf_op jit(solution)/shard_map/attend/pallas_call | solution.py:88
  139.9 10.9 %collective-permute-done.4 = bf16[144,2048]{1,0:T(8,128)(2,1)} collective-permute-done((bf16[144,2048]{1,0:T(8,128)(2,1)}, bf16[144,2048]{1,0:T(8,128)(2,1)}, u32[]{:S(2)}, u32[]{:S(2)}) %collective-permute-start.4) | collective-permute-done | bytes 589856 | tf_op jit(solution)/shard_map/ppermute | solution.py:385
  169.9 6.9 convolution_convert_fusion.2
  181.4 12.9 %collective-permute-done.14 = bf16[128,2048]{1,0:T(8,128)(2,1)S(1)} collective-permute-done((bf16[128,2048]{1,0:T(8,128)(2,1)S(1)}, bf16[128,2048]{1,0:T(8,128)(2,1)S(1)}, u32[]{:S(2)}, u32[]{:S(2)}) %collective-permute-start.14) | collective-permute-done | bytes 524320 | tf_op jit(solution)/shard_map/ppermute | solution.py:386
  194.3 8.3 collective-permute-done.12
  206.5 23.3 %collective-permute-done.15 = bf16[256,2048]{1,0:T(8,128)(2,1)S(1)} collective-permute-done((bf16[256,2048]{1,0:T(8,128)(2,1)S(1)}, bf16[256,2048]{1,0:T(8,128)(2,1)S(1)}, u32[]{:S(2)}, u32[]{:S(2)}) %collective-permute-start.15) | collective-permute-done | bytes 1048608 | tf_op jit(solution)/shard_map/ppermute | solution.py:386
  229.8 22.7 %collective-permute-done.13 = bf16[256,2048]{1,0:T(8,128)(2,1)S(1)} collective-permute-done((bf16[256,2048]{1,0:T(8,128)(2,1)S(1)}, bf16[256,2048]{1,0:T(8,128)(2,1)S(1)}, u32[]{:S(2)}, u32[]{:S(2)}) %collective-permute-start.13) | collective-permute-done | bytes 1048608 | tf_op jit(solution)/shard_map/ppermute | solution.py:385
  259.9 17.4 %convolution_bitcast_fusion.1.pre_ref = f32[8,4,1,112,768]{4,3,2,1,0:T(8,128)} fusion(bf16[8,4,112,2048]{3,2,1,0:T(8,128)(2,1)} %bitcast.176, bf16[768,2048,1,1]{1,0,3,2:T(8,128)(2,1)S(1)} %bitcast.136), kind=kOutput, calls=%fused_computation.10 | convolution fusion | flops 11274289152 | bytes 28835840 | tf_op jit(solution)/shard_map/dot_general | solution.py:20
  277.3 8.3 collective-permute-done.16
  297.2 4.4 collective-permute-done.19
  308.3 10.9 %collective-permute-done.21 = bf16[112,2048]{1,0:T(8,128)(2,1)S(1)} collective-permute-done((bf16[112,2048]{1,0:T(8,128)(2,1)S(1)}, bf16[112,2048]{1,0:T(8,128)(2,1)S(1)}, u32[]{:S(2)}, u32[]{:S(2)}) %collective-permute-start.21) | collective-permute-done | bytes 458784 | tf_op jit(solution)/shard_map/ppermute | solution.py:386
  319.3 4.3 collective-permute-start.23
  323.6 6.5 collective-permute-done.20
  335.1 4.2 collective-permute-done.22
  340.7 4.6 copy.65.wg_ref
  345.3 4.6 copy.66.wu_ref
  352.9 5.7 convert_reduce_fusion
  362.3 4.3 all-to-all-start
  367.7 6.4 all-to-all-done
  378.5 20.5 %convolution_bitcast_fusion.pre_ref = f32[8,4,1,144,768]{4,3,2,1,0:T(8,128)} fusion(bf16[8,4,144,2048]{3,2,1,0:T(8,128)(2,1)} %bitcast.175, bf16[768,2048,1,1]{1,0,3,2:T(8,128)(2,1)S(1)} %bitcast.137), kind=kOutput, calls=%fused_computation.1 | convolution fusion | flops 14495514624 | bytes 36175872 | tf_op jit(solution)/shard_map/dot_general | solution.py:20
  399.0 6.7 all-gather.10.cloned.1.call-done.x_ref
  406.3 74.6 %experts.2 = (bf16[8,4,1,144,768]{4,3,2,1,0:T(8,128)(2,1)}, bf16[4608,768]{1,0:T(8,128)(2,1)}, bf16[4608,768]{1,0:T(8,128)(2,1)}, f32[8,8,576]{2,1,0:T(8,128)}, bf16[4608,2048]{1,0:T(8,128)(2,1)}) custom-call(s32[8]{0:T(128)} %iota.42.order, bf16[4608,2048]{1,0:T(8,128)(2,1)} %all-gather.10.cloned.1.call-done.x_ref, ...), custom_call_target="tpu_custom_call" | custom-call | flops 57982058496 | bytes 73138176 | tf_op jit(solution)/shard_map/experts/pallas_call | solution.py:232
  487.0 8.6 outputs.4
  495.6 4.3 copy-done.6
  499.9 64.2 %experts.3 = (bf16[8,4,1,112,768]{4,3,2,1,0:T(8,128)(2,1)}, bf16[3584,768]{1,0:T(8,128)(2,1)}, bf16[3584,768]{1,0:T(8,128)(2,1)}, f32[8,8,448]{2,1,0:T(8,128)}, ...) custom-call(s32[8]{0:T(128)} %copy-done.77, bf16[3584,2048]{1,0:T(8,128)(2,1)} %all-gather.12.cloned.1.call-done.x_ref, ...), custom_call_target="tpu_custom_call" | custom-call | flops 45097156608 | bytes 56885248 | tf_op jit(solution)/shard_map/experts/pallas_call | solution.py:232
  567.1 8.2 outputs.5
  577.4 4.4 all-to-all-start.1
  584.6 7.2 outputs.6
  595.4 5.0 add_convert_fusion.22
  606.4 23.5 %rows_product.1 = f32[2048,768]{1,0:T(8,128)} custom-call(bf16[4608,2048]{1,0:T(8,128)(2,1)} %all-gather.10.cloned.1.call-done.x_ref, bf16[4608,768]{1,0:T(8,128)(2,1)} %get-tuple-element.118.g_ref), custom_call_target="tpu_custom_call" | custom-call | flops 1 | bytes 1 | tf_op jit(solution)/shard_map/rows_product/pallas_call | solution.py:300
  633.1 22.8 %collective-permute-done.25 = bf16[2,224,2048]{2,1,0:T(8,128)(2,1)} collective-permute-done((bf16[2,224,2048]{2,1,0:T(8,128)(2,1)}, bf16[2,224,2048]{2,1,0:T(8,128)(2,1)}, u32[]{:S(2)}, u32[]{:S(2)}) %collective-permute-start.25) | collective-permute-done | bytes 1835040 | tf_op jit(solution)/shard_map/ppermute | solution.py:325
  655.9 4.9 add_convert_fusion.19
  662.8 5.0 add_convert_fusion.18
  672.6 9.0 outputs.7
  685.8 4.6 fusion.9
  692.0 19.5 %convolution_add_fusion.1 = f32[2048,768]{1,0:T(8,128)} fusion(f32[2048,768]{1,0:T(8,128)} %rows_product.1, bf16[3584,2048]{1,0:T(8,128)(2,1)} %all-gather.12.cloned.1.call-done.x_ref, bf16[3584,768]{1,0:T(8,128)(2,1)} %get-tuple-element.128), kind=kOutput, calls=%fused_computation.11 | convolution fusion | flops 11275862016 | bytes 32768000 | tf_op jit(solution)/shard_map/dot_general | solution.py:20
  711.5 18.9 %fusion.30 = f32[768,2048]{1,0:T(8,128)} fusion(bf16[4608,768]{1,0:T(8,128)(2,1)S(1)} %bitcast.150, bf16[4608,2048]{1,0:T(8,128)(2,1)} %all-gather.8.cloned.1.call-done), kind=kOutput, calls=%fused_computation.190 | convolution fusion | flops 14495514624 | bytes 32243712 | tf_op jit(solution)/shard_map/dot_general | solution.py:20
  730.4 5.2 add_convert_fusion.12
  742.8 4.9 add_convert_fusion.5
  753.2 18.2 %fusion.31 = f32[2048,768]{0,1:T(8,128)} fusion(bf16[3584,2048]{1,0:T(8,128)(2,1)} %all-gather.12.cloned.1.call-done.x_ref, bf16[3584,768]{1,0:T(8,128)(2,1)} %get-tuple-element.139), kind=kOutput, calls=%fused_computation.191 | convolution fusion | flops 11274289152 | bytes 26476544 | tf_op jit(solution)/shard_map/dot_general | solution.py:20
  771.3 23.7 %convolution_add_fusion = f32[2048,768]{0,1:T(8,128)} fusion(f32[2048,768]{0,1:T(8,128)} %fusion.31, bf16[4608,2048]{1,0:T(8,128)(2,1)} %all-gather.10.cloned.1.call-done.x_ref, bf16[4608,768]{1,0:T(8,128)(2,1)} %get-tuple-element.137), kind=kOutput, calls=%fused_computation.9 | convolution fusion | flops 14497087488 | bytes 38535168 | tf_op jit(solution)/shard_map/dot_general | solution.py:20
  795.0 4.7 fusion.11
  801.1 19.4 %convolution_add_fusion.2 = f32[768,2048]{1,0:T(8,128)} fusion(f32[768,2048]{1,0:T(8,128)} %fusion.30, bf16[3584,768]{1,0:T(8,128)(2,1)} %bitcast.142, bf16[3584,2048]{1,0:T(8,128)(2,1)} %all-gather.6.cloned.1.call-done), kind=kOutput, calls=%fused_computation.12 | convolution fusion | flops 11275862016 | bytes 32768000 | tf_op jit(solution)/shard_map/dot_general | solution.py:20
  820.5 5.7 add_convert_fusion.3
  828.8 7.0 copy.73
  835.8 9.3 convolution_convert_fusion.3.do_ref
  845.2 8.0 collective-permute-done.38
  853.2 5.4 fusion.6
  867.2 27.5 %attend_back.1 = (bf16[1024,1024]{1,0:T(8,128)(2,1)S(1)}, bf16[1024,128]{1,0:T(8,128)(2,1)S(1)}, bf16[1024,128]{1,0:T(8,128)(2,1)S(1)}, f32[1,128]{1,0:T(1,128)S(1)}, f32[1,128]{1,0:T(1,128)S(1)}) custom-call(bf16[1024,1024]{1,0:T(8,128)(2,1)S(1)} %copy-done.25, bf16[1024,1024]{1,0:T(8,128)(2,1)S(1)} %copy-done.29, f32[1024,1152]{1,0:T(8,128)S(1)} %copy-done.23, ...), custom_call_target="tpu_custom_call" | custom-call | flops 7516192768 | bytes 10485760 | tf_op jit(solution)/shard_map/attend_back/pallas_call | solution.py:159
  896.4 9.8 multiply_reduce_fusion
  912.3 4.1 all-to-all-start.2
  916.5 8.3 convolution_convert_fusion
  929.5 6.3 convolution_convert_fusion.1
  943.4 4.2 collective-permute-done.46
  962.1 11.2 %all-to-all-done.3 = f32[8,5,2048]{2,1,0:T(8,128)S(1)} async-done(((f32[8,5,2048]{2,1,0:T(8,128)}), f32[8,5,2048]{2,1,0:T(8,128)S(1)}, u32[]{:S(2)}, u32[]{:S(2)}) %all-to-all-start.3) | async-done | bytes 327712 | tf_op jit(solution)/shard_map/all_to_all | solution.py:662
  979.9 19.4 %collective-permute-done.44 = bf16[2,128,1280]{2,1,0:T(8,128)(2,1)S(1)} collective-permute-done((bf16[2,128,1280]{2,1,0:T(8,128)(2,1)S(1)}, bf16[2,128,1280]{2,1,0:T(8,128)(2,1)S(1)}, u32[]{:S(2)}, u32[]{:S(2)}) %collective-permute-start.44) | collective-permute-done | bytes 655392 | tf_op jit(solution)/shard_map/ppermute | solution.py:325
  1001.9 5.3 collective-permute-done.42
  (426 shorter events, 226.3 us)
Async XLA Ops:
  7.2 252.7 %all-gather.6.cloned.1.call-start = ((), (), s32[]{:S(2)}) async-start(), calls=%async_computation.10 | async-start | bytes 16515072 | tf_op jit(solution)/shard_map/all_gather | solution.py:498
  11.6 28.7 %collective-permute-start.1 = (bf16[256,2048]{1,0:T(8,128)(2,1)S(1)}, bf16[256,2048]{1,0:T(8,128)(2,1)S(1)}, u32[]{:S(2)}, u32[]{:S(2)}) collective-permute-start(bf16[256,2048]{1,0:T(8,128)(2,1)S(1)} %fusion.4), channel_id=1, source_target_pairs={{0,3},{1,0},{2,1},{3,2},{4,7},{5,4},{6,5},{7,6},{8,11},{9,8},{10,9... | collective-permute-start | bytes 3145736 | tf_op jit(solution)/shard_map/ppermute | solution.py:386
  16.7 47.0 %collective-permute-start = (bf16[256,2048]{1,0:T(8,128)(2,1)S(1)}, bf16[256,2048]{1,0:T(8,128)(2,1)S(1)}, u32[]{:S(2)}, u32[]{:S(2)}) collective-permute-start(bf16[256,2048]{1,0:T(8,128)(2,1)S(1)} %fusion.4), channel_id=1, source_target_pairs={{0,1},{1,2},{2,3},{3,0},{4,5},{5,6},{6,7},{7,4},{8,9},{9,10},{10,1... | collective-permute-start | bytes 3145736 | tf_op jit(solution)/shard_map/ppermute | solution.py:385
  40.3 44.8 %collective-permute-start.3 = (bf16[128,2048]{1,0:T(8,128)(2,1)S(1)}, bf16[128,2048]{1,0:T(8,128)(2,1)S(1)}, u32[]{:S(2)}, u32[]{:S(2)}) collective-permute-start(bf16[128,2048]{1,0:T(8,128)(2,1)S(1)} %slice.413), channel_id=1, source_target_pairs={{0,3},{1,0},{2,1},{3,2},{4,7},{5,4},{6,5},{7,6},{8,11},{9,8},{10,9... | collective-permute-start | bytes 1572872 | tf_op jit(solution)/shard_map/ppermute | solution.py:386
  63.8 21.3 %collective-permute-start.2 = (bf16[128,2048]{1,0:T(8,128)(2,1)S(1)}, bf16[128,2048]{1,0:T(8,128)(2,1)S(1)}, u32[]{:S(2)}, u32[]{:S(2)}) collective-permute-start(bf16[128,2048]{1,0:T(8,128)(2,1)S(1)} %slice.412), channel_id=1, source_target_pairs={{0,1},{1,2},{2,3},{3,0},{4,5},{5,6},{6,7},{7,4},{8,9},{9,10},{10,1... | collective-permute-start | bytes 1572872 | tf_op jit(solution)/shard_map/ppermute | solution.py:385
  85.2 13.7 %collective-permute-start.9 = (bf16[112,2048]{1,0:T(8,128)(2,1)S(1)}, bf16[112,2048]{1,0:T(8,128)(2,1)S(1)}, u32[]{:S(2)}, u32[]{:S(2)}) collective-permute-start(bf16[112,2048]{1,0:T(8,128)(2,1)S(1)} %slice.314), channel_id=1, source_target_pairs={{0,3},{1,0},{2,1},{3,2},{4,7},{5,4},{6,5},{7,6},{8,11},{9,8},{10,9... | collective-permute-start | bytes 1376264 | tf_op jit(solution)/shard_map/ppermute | solution.py:386
  87.9 20.9 %collective-permute-start.8 = (bf16[112,2048]{1,0:T(8,128)(2,1)S(1)}, bf16[112,2048]{1,0:T(8,128)(2,1)S(1)}, u32[]{:S(2)}, u32[]{:S(2)}) collective-permute-start(bf16[112,2048]{1,0:T(8,128)(2,1)S(1)} %slice.314), channel_id=1, source_target_pairs={{0,1},{1,2},{2,3},{3,0},{4,5},{5,6},{6,7},{7,4},{8,9},{9,10},{10,1... | collective-permute-start | bytes 1376264 | tf_op jit(solution)/shard_map/ppermute | solution.py:385
  108.9 10.4 %collective-permute-start.10 = (bf16[56,2048]{1,0:T(8,128)(2,1)S(1)}, bf16[56,2048]{1,0:T(8,128)(2,1)S(1)}, u32[]{:S(2)}, u32[]{:S(2)}) collective-permute-start(bf16[56,2048]{1,0:T(8,128)(2,1)S(1)} %slice.315), channel_id=1, source_target_pairs={{0,1},{1,2},{2,3},{3,0},{4,5},{5,6},{6,7},{7,4},{8,9},{9,10},{10,1... | collective-permute-start | bytes 688136 | tf_op jit(solution)/shard_map/ppermute | solution.py:385
  109.5 10.7 %collective-permute-start.11 = (bf16[56,2048]{1,0:T(8,128)(2,1)S(1)}, bf16[56,2048]{1,0:T(8,128)(2,1)S(1)}, u32[]{:S(2)}, u32[]{:S(2)}) collective-permute-start(bf16[56,2048]{1,0:T(8,128)(2,1)S(1)} %slice.316), channel_id=1, source_target_pairs={{0,3},{1,0},{2,1},{3,2},{4,7},{5,4},{6,5},{7,6},{8,11},{9,8},{10,9... | collective-permute-start | bytes 688136 | tf_op jit(solution)/shard_map/ppermute | solution.py:386
  120.9 182.9 %all-gather.8.cloned.1.call-start = ((), (), s32[]{:S(2)}) async-start(), calls=%async_computation.11 | async-start | bytes 21233664 | tf_op jit(solution)/shard_map/all_gather | solution.py:499
  122.9 17.0 %collective-permute-start.5 = (bf16[144,2048]{1,0:T(8,128)(2,1)}, bf16[144,2048]{1,0:T(8,128)(2,1)}, u32[]{:S(2)}, u32[]{:S(2)}) collective-permute-start(bf16[144,2048]{1,0:T(8,128)(2,1)} %slice.311), channel_id=1, source_target_pairs={{0,3},{1,0},{2,1},{3,2},{4,7},{5,4},{6,5},{7,6},{8,11},{9,8},{10,9... | collective-permute-start | bytes 1769480 | tf_op jit(solution)/shard_map/ppermute | solution.py:386
  125.8 25.0 %collective-permute-start.4 = (bf16[144,2048]{1,0:T(8,128)(2,1)}, bf16[144,2048]{1,0:T(8,128)(2,1)}, u32[]{:S(2)}, u32[]{:S(2)}) collective-permute-start(bf16[144,2048]{1,0:T(8,128)(2,1)} %slice.311), channel_id=1, source_target_pairs={{0,1},{1,2},{2,3},{3,0},{4,5},{5,6},{6,7},{7,4},{8,9},{9,10},{10,1... | collective-permute-start | bytes 1769480 | tf_op jit(solution)/shard_map/ppermute | solution.py:385
  152.7 15.6 %collective-permute-start.6 = (bf16[72,2048]{1,0:T(8,128)(2,1)S(1)}, bf16[72,2048]{1,0:T(8,128)(2,1)S(1)}, u32[]{:S(2)}, u32[]{:S(2)}) collective-permute-start(bf16[72,2048]{1,0:T(8,128)(2,1)S(1)} %slice.312), channel_id=1, source_target_pairs={{0,1},{1,2},{2,3},{3,0},{4,5},{5,6},{6,7},{7,4},{8,9},{9,10},{10,1... | collective-permute-start | bytes 884744 | tf_op jit(solution)/shard_map/ppermute | solution.py:385
  153.6 15.6 %collective-permute-start.7 = (bf16[72,2048]{1,0:T(8,128)(2,1)S(1)}, bf16[72,2048]{1,0:T(8,128)(2,1)S(1)}, u32[]{:S(2)}, u32[]{:S(2)}) collective-permute-start(bf16[72,2048]{1,0:T(8,128)(2,1)S(1)} %slice.313), channel_id=1, source_target_pairs={{0,3},{1,0},{2,1},{3,2},{4,7},{5,4},{6,5},{7,6},{8,11},{9,8},{10,9... | collective-permute-start | bytes 884744 | tf_op jit(solution)/shard_map/ppermute | solution.py:386
  169.9 235.9 %all-gather.10.cloned.1.call-start = ((), (), s32[]{:S(2)}) async-start(), calls=%async_computation.12 | async-start | bytes 21233664 | tf_op jit(solution)/shard_map/all_gather | solution.py:549
  179.1 15.2 %collective-permute-start.14 = (bf16[128,2048]{1,0:T(8,128)(2,1)S(1)}, bf16[128,2048]{1,0:T(8,128)(2,1)S(1)}, u32[]{:S(2)}, u32[]{:S(2)}) collective-permute-start(bf16[128,2048]{1,0:T(8,128)(2,1)S(1)} %get-tuple-element.276), channel_id=1, source_target_pairs={{0,3},{1,0},{2,1},{3,2},{4,7},{5,4},{6,5},{7,6},{8,11},{9,8},{10,9... | collective-permute-start | bytes 1572872 | tf_op jit(solution)/shard_map/ppermute | solution.py:386
  179.7 22.8 %collective-permute-start.12 = (bf16[128,2048]{1,0:T(8,128)(2,1)S(1)}, bf16[128,2048]{1,0:T(8,128)(2,1)S(1)}, u32[]{:S(2)}, u32[]{:S(2)}) collective-permute-start(bf16[128,2048]{1,0:T(8,128)(2,1)S(1)} %get-tuple-element.277), channel_id=1, source_target_pairs={{0,1},{1,2},{2,3},{3,0},{4,5},{5,6},{6,7},{7,4},{8,9},{9,10},{10,1... | collective-permute-start | bytes 1572872 | tf_op jit(solution)/shard_map/ppermute | solution.py:385
  204.2 25.6 %collective-permute-start.15 = (bf16[256,2048]{1,0:T(8,128)(2,1)S(1)}, bf16[256,2048]{1,0:T(8,128)(2,1)S(1)}, u32[]{:S(2)}, u32[]{:S(2)}) collective-permute-start(bf16[256,2048]{1,0:T(8,128)(2,1)S(1)} %pad_maximum_fusion.13), channel_id=1, source_target_pairs={{0,3},{1,0},{2,1},{3,2},{4,7},{5,4},{6,5},{7,6},{8,11},{9,8},{10,9... | collective-permute-start | bytes 3145736 | tf_op jit(solution)/shard_map/ppermute | solution.py:386
  206.3 46.1 %collective-permute-start.13 = (bf16[256,2048]{1,0:T(8,128)(2,1)S(1)}, bf16[256,2048]{1,0:T(8,128)(2,1)S(1)}, u32[]{:S(2)}, u32[]{:S(2)}) collective-permute-start(bf16[256,2048]{1,0:T(8,128)(2,1)S(1)} %pad_maximum_fusion.12), channel_id=1, source_target_pairs={{0,1},{1,2},{2,3},{3,0},{4,5},{5,6},{6,7},{7,4},{8,9},{9,10},{10,1... | collective-permute-start | bytes 3145736 | tf_op jit(solution)/shard_map/ppermute | solution.py:385
  257.9 19.4 %collective-permute-start.17 = (bf16[144,2048]{1,0:T(8,128)(2,1)}, bf16[144,2048]{1,0:T(8,128)(2,1)}, u32[]{:S(2)}, u32[]{:S(2)}) collective-permute-start(bf16[144,2048]{1,0:T(8,128)(2,1)} %slice.414), channel_id=1, source_target_pairs={{0,3},{1,0},{2,1},{3,2},{4,7},{5,4},{6,5},{7,6},{8,11},{9,8},{10,9... | collective-permute-start | bytes 1769480 | tf_op jit(solution)/shard_map/ppermute | solution.py:386
  259.9 25.7 %collective-permute-start.16 = (bf16[144,2048]{1,0:T(8,128)(2,1)}, bf16[144,2048]{1,0:T(8,128)(2,1)}, u32[]{:S(2)}, u32[]{:S(2)}) collective-permute-start(bf16[144,2048]{1,0:T(8,128)(2,1)} %slice.414), channel_id=1, source_target_pairs={{0,1},{1,2},{2,3},{3,0},{4,5},{5,6},{6,7},{7,4},{8,9},{9,10},{10,1... | collective-permute-start | bytes 1769480 | tf_op jit(solution)/shard_map/ppermute | solution.py:385
  286.6 9.9 collective-permute-start.18
  292.2 9.3 collective-permute-start.19
  303.9 196.0 %all-gather.12.cloned.1.call-start = ((), (), s32[]{:S(2)}) async-start(), calls=%async_computation.13 | async-start | bytes 16515072 | tf_op jit(solution)/shard_map/all_gather | solution.py:549
  305.0 14.3 %collective-permute-start.21 = (bf16[112,2048]{1,0:T(8,128)(2,1)S(1)}, bf16[112,2048]{1,0:T(8,128)(2,1)S(1)}, u32[]{:S(2)}, u32[]{:S(2)}) collective-permute-start(bf16[112,2048]{1,0:T(8,128)(2,1)S(1)} %slice.415), channel_id=1, source_target_pairs={{0,3},{1,0},{2,1},{3,2},{4,7},{5,4},{6,5},{7,6},{8,11},{9,8},{10,9... | collective-permute-start | bytes 1376264 | tf_op jit(solution)/shard_map/ppermute | solution.py:386
  308.3 21.7 %collective-permute-start.20 = (bf16[112,2048]{1,0:T(8,128)(2,1)S(1)}, bf16[112,2048]{1,0:T(8,128)(2,1)S(1)}, u32[]{:S(2)}, u32[]{:S(2)}) collective-permute-start(bf16[112,2048]{1,0:T(8,128)(2,1)S(1)} %slice.415), channel_id=1, source_target_pairs={{0,1},{1,2},{2,3},{3,0},{4,5},{5,6},{6,7},{7,4},{8,9},{9,10},{10,1... | collective-permute-start | bytes 1376264 | tf_op jit(solution)/shard_map/ppermute | solution.py:385
  319.3 20.7 %collective-permute-start.23 = (bf16[56,2048]{1,0:T(8,128)(2,1)S(1)}, bf16[56,2048]{1,0:T(8,128)(2,1)S(1)}, u32[]{:S(2)}, u32[]{:S(2)}) collective-permute-start(bf16[56,2048]{1,0:T(8,128)(2,1)S(1)} %slice.417), channel_id=1, source_target_pairs={{0,3},{1,0},{2,1},{3,2},{4,7},{5,4},{6,5},{7,6},{8,11},{9,8},{10,9... | collective-permute-start | bytes 688136 | tf_op jit(solution)/shard_map/ppermute | solution.py:386
  330.1 9.1 collective-permute-start.22
  362.3 11.8 %all-to-all-start = ((bf16[32,4,256]{2,1,0:T(4,128)(2,1)}), bf16[32,4,256]{2,1,0:T(4,128)(2,1)S(1)}, u32[]{:S(2)}, u32[]{:S(2)}) async-start(bf16[32,4,256]{2,1,0:T(4,128)(2,1)} %bitcast.19), calls=%async_computation | async-start | bytes 131072 | tf_op jit(solution)/shard_map/all_to_all | solution.py:526
  366.6 263.3 %reduce-scatter.7.cloned.1.call-start = ((), (), s32[]{:S(2)}) async-start(), calls=%async_computation.14 | async-start | bytes 21233664 | tf_op jit(solution)/shard_map/reduce_scatter | solution.py:554
  564.0 31.4 %collective-permute-start.24 = (bf16[1792,2048]{1,0:T(8,128)(2,1)}, bf16[1792,2048]{1,0:T(8,128)(2,1)}, u32[]{:S(2)}, u32[]{:S(2)}) collective-permute-start(bf16[1792,2048]{1,0:T(8,128)(2,1)} %get-tuple-element.111), channel_id=1, source_target_pairs={{0,4},{4,0},{8,12},{12,8},{16,20},{20,16},{24,28},{28,24},{1,5},{5... | collective-permute-start | bytes 22020104 | tf_op jit(solution)/shard_map/ppermute | solution.py:325
  575.3 87.5 %collective-permute-start.29 = (bf16[1792,2048]{1,0:T(8,128)(2,1)}, bf16[1792,2048]{1,0:T(8,128)(2,1)}, u32[]{:S(2)}, u32[]{:S(2)}) collective-permute-start(bf16[1792,2048]{1,0:T(8,128)(2,1)} %outputs.5), channel_id=1, source_target_pairs={{0,4},{4,0},{8,12},{12,8},{16,20},{20,16},{24,28},{28,24},{1,5},{5... | collective-permute-start | bytes 22020104 | tf_op jit(solution)/shard_map/ppermute | solution.py:325
  577.4 17.3 %all-to-all-start.1 = ((f32[32,4,256]{2,1,0:T(4,128)}), f32[32,4,256]{2,1,0:T(4,128)S(1)}, u32[]{:S(2)}, u32[]{:S(2)}) async-start(f32[32,4,256]{2,1,0:T(4,128)} %bitcast.168), calls=%async_computation.1 | async-start | bytes 262144 | tf_op jit(solution)/shard_map/all_to_all | solution.py:541
  581.9 103.4 %reduce-scatter.9.cloned.1.call-start = ((), (), s32[]{:S(2)}) async-start(), calls=%async_computation.15 | async-start | bytes 2949120 | tf_op jit(solution)/shard_map/reduce_scatter | solution.py:536
  601.9 54.0 %collective-permute-start.25 = (bf16[2,224,2048]{2,1,0:T(8,128)(2,1)}, bf16[2,224,2048]{2,1,0:T(8,128)(2,1)}, u32[]{:S(2)}, u32[]{:S(2)}) collective-permute-start(bf16[2,224,2048]{2,1,0:T(8,128)(2,1)} %pad_maximum_fusion.6), channel_id=1, source_target_pairs={{0,8},{4,12},{8,0},{12,4},{16,24},{20,28},{24,16},{28,20},{1,9},{5... | collective-permute-start | bytes 5505032 | tf_op jit(solution)/shard_map/ppermute | solution.py:325
  604.9 51.0 %collective-permute-start.26 = (bf16[2,224,2048]{2,1,0:T(8,128)(2,1)}, bf16[2,224,2048]{2,1,0:T(8,128)(2,1)}, u32[]{:S(2)}, u32[]{:S(2)}) collective-permute-start(bf16[2,224,2048]{2,1,0:T(8,128)(2,1)} %pad_maximum_fusion.7), channel_id=1, source_target_pairs={{0,16},{4,20},{8,24},{12,28},{16,0},{20,4},{24,8},{28,12},{1,17},{... | collective-permute-start | bytes 5505032 | tf_op jit(solution)/shard_map/ppermute | solution.py:325
  629.9 107.7 %reduce-scatter.11.cloned.1.call-start = ((), (), s32[]{:S(2)}) async-start(), calls=%async_computation.16 | async-start | bytes 2293760 | tf_op jit(solution)/shard_map/reduce_scatter | solution.py:536
  631.7 111.0 %collective-permute-start.27 = (bf16[2304,2048]{1,0:T(8,128)(2,1)}, bf16[2304,2048]{1,0:T(8,128)(2,1)}, u32[]{:S(2)}, u32[]{:S(2)}) collective-permute-start(bf16[2304,2048]{1,0:T(8,128)(2,1)} %copy-done.6), channel_id=1, source_target_pairs={{0,4},{4,0},{8,12},{12,8},{16,20},{20,16},{24,28},{28,24},{1,5},{5... | collective-permute-start | bytes 28311560 | tf_op jit(solution)/shard_map/ppermute | solution.py:325
  660.8 24.4 %collective-permute-start.30 = (bf16[1,224,2048]{2,1,0:T(8,128)(2,1)S(1)}, bf16[1,224,2048]{2,1,0:T(8,128)(2,1)}, u32[]{:S(2)}, u32[]{:S(2)}) collective-permute-start(bf16[1,224,2048]{2,1,0:T(8,128)(2,1)S(1)} %get-tuple-element.244), channel_id=1, source_target_pairs={{0,8},{4,12},{8,0},{12,4},{16,24},{20,28},{24,16},{28,20},{1,9},{5... | collective-permute-start | bytes 2752520 | tf_op jit(solution)/shard_map/ppermute | solution.py:325
  662.2 23.6 %collective-permute-start.28 = (bf16[1,224,2048]{2,1,0:T(8,128)(2,1)}, bf16[1,224,2048]{2,1,0:T(8,128)(2,1)}, u32[]{:S(2)}, u32[]{:S(2)}) collective-permute-start(bf16[1,224,2048]{2,1,0:T(8,128)(2,1)} %get-tuple-element.245), channel_id=1, source_target_pairs={{0,16},{4,20},{8,24},{12,28},{16,0},{20,4},{24,8},{28,12},{1,17},{... | collective-permute-start | bytes 2752520 | tf_op jit(solution)/shard_map/ppermute | solution.py:325
  669.1 61.3 %collective-permute-start.32 = (bf16[2,224,2048]{2,1,0:T(8,128)(2,1)}, bf16[2,224,2048]{2,1,0:T(8,128)(2,1)}, u32[]{:S(2)}, u32[]{:S(2)}) collective-permute-start(bf16[2,224,2048]{2,1,0:T(8,128)(2,1)} %pad_maximum_fusion.9), channel_id=1, source_target_pairs={{0,16},{4,20},{8,24},{12,28},{16,0},{20,4},{24,8},{28,12},{1,17},{... | collective-permute-start | bytes 5505032 | tf_op jit(solution)/shard_map/ppermute | solution.py:325
  672.1 58.3 %collective-permute-start.31 = (bf16[2,224,2048]{2,1,0:T(8,128)(2,1)}, bf16[2,224,2048]{2,1,0:T(8,128)(2,1)}, u32[]{:S(2)}, u32[]{:S(2)}) collective-permute-start(bf16[2,224,2048]{2,1,0:T(8,128)(2,1)} %pad_maximum_fusion.8), channel_id=1, source_target_pairs={{0,8},{4,12},{8,0},{12,4},{16,24},{20,28},{24,16},{28,20},{1,9},{5... | collective-permute-start | bytes 5505032 | tf_op jit(solution)/shard_map/ppermute | solution.py:325
  691.9 143.9 %all-gather.14.cloned.1.call-start = ((), (), s32[]{:S(2)}) async-start(), calls=%async_computation.17 | async-start | bytes 5242880 | tf_op jit(solution)/shard_map/all_gather | solution.py:612
  735.6 59.4 %collective-permute-start.34 = (bf16[1,224,2048]{2,1,0:T(8,128)(2,1)}, bf16[1,224,2048]{2,1,0:T(8,128)(2,1)}, u32[]{:S(2)}, u32[]{:S(2)}) collective-permute-start(bf16[1,224,2048]{2,1,0:T(8,128)(2,1)} %get-tuple-element.236), channel_id=1, source_target_pairs={{0,16},{4,20},{8,24},{12,28},{16,0},{20,4},{24,8},{28,12},{1,17},{... | collective-permute-start | bytes 2752520 | tf_op jit(solution)/shard_map/ppermute | solution.py:325
  736.5 58.5 %collective-permute-start.35 = (bf16[1,224,2048]{2,1,0:T(8,128)(2,1)}, bf16[1,224,2048]{2,1,0:T(8,128)(2,1)}, u32[]{:S(2)}, u32[]{:S(2)}) collective-permute-start(bf16[1,224,2048]{2,1,0:T(8,128)(2,1)} %get-tuple-element.237), channel_id=1, source_target_pairs={{0,8},{4,12},{8,0},{12,4},{16,24},{20,28},{24,16},{28,20},{1,9},{5... | collective-permute-start | bytes 2752520 | tf_op jit(solution)/shard_map/ppermute | solution.py:325
  742.8 153.7 %reduce-scatter.15.cloned.1.call-start = ((), (), s32[]{:S(2)}) async-start(), calls=%async_computation.19 | async-start | bytes 2293760 | tf_op jit(solution)/shard_map/reduce_scatter | solution.py:536
  749.5 71.0 %collective-permute-start.33 = (bf16[2,288,2048]{2,1,0:T(8,128)(2,1)}, bf16[2,288,2048]{2,1,0:T(8,128)(2,1)S(1)}, u32[]{:S(2)}, u32[]{:S(2)}) collective-permute-start(bf16[2,288,2048]{2,1,0:T(8,128)(2,1)} %pad_maximum_fusion.3), channel_id=1, source_target_pairs={{0,8},{4,12},{8,0},{12,4},{16,24},{20,28},{24,16},{28,20},{1,9},{5... | collective-permute-start | bytes 7077896 | tf_op jit(solution)/shard_map/ppermute | solution.py:325
  752.0 68.5 %collective-permute-start.37 = (bf16[2,288,2048]{2,1,0:T(8,128)(2,1)}, bf16[2,288,2048]{2,1,0:T(8,128)(2,1)}, u32[]{:S(2)}, u32[]{:S(2)}) collective-permute-start(bf16[2,288,2048]{2,1,0:T(8,128)(2,1)} %pad_maximum_fusion.4), channel_id=1, source_target_pairs={{0,16},{4,20},{8,24},{12,28},{16,0},{20,4},{24,8},{28,12},{1,17},{... | collective-permute-start | bytes 7077896 | tf_op jit(solution)/shard_map/ppermute | solution.py:325
  801.0 215.2 %reduce-scatter.13.cloned.1.call-start = ((), (), s32[]{:S(2)}) async-start(), calls=%async_computation.18 | async-start | bytes 2949120 | tf_op jit(solution)/shard_map/reduce_scatter | solution.py:536
  826.2 27.0 %collective-permute-start.36 = (bf16[1,288,2048]{2,1,0:T(8,128)(2,1)}, bf16[1,288,2048]{2,1,0:T(8,128)(2,1)}, u32[]{:S(2)}, u32[]{:S(2)}) collective-permute-start(bf16[1,288,2048]{2,1,0:T(8,128)(2,1)} %get-tuple-element.228), channel_id=1, source_target_pairs={{0,16},{4,20},{8,24},{12,28},{16,0},{20,4},{24,8},{28,12},{1,17},{... | collective-permute-start | bytes 3538952 | tf_op jit(solution)/shard_map/ppermute | solution.py:325
  827.2 26.0 %collective-permute-start.38 = (bf16[1,288,2048]{2,1,0:T(8,128)(2,1)}, bf16[1,288,2048]{2,1,0:T(8,128)(2,1)}, u32[]{:S(2)}, u32[]{:S(2)}) collective-permute-start(bf16[1,288,2048]{2,1,0:T(8,128)(2,1)} %get-tuple-element.229), channel_id=1, source_target_pairs={{0,8},{4,12},{8,0},{12,4},{16,24},{20,28},{24,16},{28,20},{1,9},{5... | collective-permute-start | bytes 3538952 | tf_op jit(solution)/shard_map/ppermute | solution.py:325
  907.6 31.4 %collective-permute-start.40 = (bf16[128,2048]{1,0:T(8,128)(2,1)}, bf16[128,2048]{1,0:T(8,128)(2,1)}, u32[]{:S(2)}, u32[]{:S(2)}) collective-permute-start(bf16[128,2048]{1,0:T(8,128)(2,1)} %get-tuple-element.271), channel_id=1, source_target_pairs={{0,3},{1,0},{2,1},{3,2},{4,7},{5,4},{6,5},{7,6},{8,11},{9,8},{10,9... | collective-permute-start | bytes 1572872 | tf_op jit(solution)/shard_map/ppermute | solution.py:386
  911.1 28.0 %collective-permute-start.39 = (bf16[128,2048]{1,0:T(8,128)(2,1)}, bf16[128,2048]{1,0:T(8,128)(2,1)}, u32[]{:S(2)}, u32[]{:S(2)}) collective-permute-start(bf16[128,2048]{1,0:T(8,128)(2,1)} %get-tuple-element.272), channel_id=1, source_target_pairs={{0,1},{1,2},{2,3},{3,0},{4,5},{5,6},{6,7},{7,4},{8,9},{9,10},{10,1... | collective-permute-start | bytes 1572872 | tf_op jit(solution)/shard_map/ppermute | solution.py:385
  912.3 25.2 %all-to-all-start.2 = ((f32[8,5,2048]{2,1,0:T(8,128)}), f32[8,5,2048]{2,1,0:T(8,128)}, u32[]{:S(2)}, u32[]{:S(2)}) async-start(f32[8,5,2048]{2,1,0:T(8,128)} %reshape.304), calls=%async_computation.7 | async-start | bytes 1048576 | tf_op jit(solution)/shard_map/all_to_all | solution.py:645
  916.5 102.1 %reduce-scatter.17.cloned.1.call-start = ((), (), s32[]{:S(2)}) async-start(), calls=%async_computation.20 | async-start | bytes 4718592 | tf_op jit(solution)/shard_map/reduce_scatter | solution.py:638
  927.9 47.7 %collective-permute-start.43 = (bf16[1024,1280]{1,0:T(8,128)(2,1)}, bf16[1024,1280]{1,0:T(8,128)(2,1)}, u32[]{:S(2)}, u32[]{:S(2)}) collective-permute-start(bf16[1024,1280]{1,0:T(8,128)(2,1)} %pad_maximum_fusion.1), channel_id=1, source_target_pairs={{0,4},{4,0},{8,12},{12,8},{16,20},{20,16},{24,28},{28,24},{1,5},{5... | collective-permute-start | bytes 7864328 | tf_op jit(solution)/shard_map/ppermute | solution.py:325
  947.6 6.3 collective-permute-start.47
  954.7 18.6 %all-to-all-start.3 = ((f32[8,5,2048]{2,1,0:T(8,128)}), f32[8,5,2048]{2,1,0:T(8,128)S(1)}, u32[]{:S(2)}, u32[]{:S(2)}) async-start(f32[8,5,2048]{2,1,0:T(8,128)} %broadcast_in_dim.95), calls=%async_computation.8 | async-start | bytes 1048576 | tf_op jit(solution)/shard_map/all_to_all | solution.py:662
  958.2 43.6 %collective-permute-start.41 = (bf16[256,2048]{1,0:T(8,128)(2,1)}, bf16[256,2048]{1,0:T(8,128)(2,1)}, u32[]{:S(2)}, u32[]{:S(2)}) collective-permute-start(bf16[256,2048]{1,0:T(8,128)(2,1)} %pad_maximum_fusion.14), channel_id=1, source_target_pairs={{0,1},{1,2},{2,3},{3,0},{4,5},{5,6},{6,7},{7,4},{8,9},{9,10},{10,1... | collective-permute-start | bytes 3145736 | tf_op jit(solution)/shard_map/ppermute | solution.py:385
  959.1 48.1 %collective-permute-start.42 = (bf16[256,2048]{1,0:T(8,128)(2,1)}, bf16[256,2048]{1,0:T(8,128)(2,1)}, u32[]{:S(2)}, u32[]{:S(2)}) collective-permute-start(bf16[256,2048]{1,0:T(8,128)(2,1)} %pad_maximum_fusion.15), channel_id=1, source_target_pairs={{0,3},{1,0},{2,1},{3,2},{4,7},{5,4},{6,5},{7,6},{8,11},{9,8},{10,9... | collective-permute-start | bytes 3145736 | tf_op jit(solution)/shard_map/ppermute | solution.py:386
  977.4 22.0 %collective-permute-start.44 = (bf16[2,128,1280]{2,1,0:T(8,128)(2,1)S(1)}, bf16[2,128,1280]{2,1,0:T(8,128)(2,1)S(1)}, u32[]{:S(2)}, u32[]{:S(2)}) collective-permute-start(bf16[2,128,1280]{2,1,0:T(8,128)(2,1)S(1)} %pad_maximum_fusion.16), channel_id=1, source_target_pairs={{0,8},{4,12},{8,0},{12,4},{16,24},{20,28},{24,16},{28,20},{1,9},{5... | collective-permute-start | bytes 1966088 | tf_op jit(solution)/shard_map/ppermute | solution.py:325
  977.5 21.8 %collective-permute-start.45 = (bf16[2,128,1280]{2,1,0:T(8,128)(2,1)S(1)}, bf16[2,128,1280]{2,1,0:T(8,128)(2,1)S(1)}, u32[]{:S(2)}, u32[]{:S(2)}) collective-permute-start(bf16[2,128,1280]{2,1,0:T(8,128)(2,1)S(1)} %pad_maximum_fusion.17), channel_id=1, source_target_pairs={{0,16},{4,20},{8,24},{12,28},{16,0},{20,4},{24,8},{28,12},{1,17},{... | collective-permute-start | bytes 1966088 | tf_op jit(solution)/shard_map/ppermute | solution.py:325
  1000.7 12.7 %collective-permute-start.49 = (bf16[1,128,1280]{2,1,0:T(8,128)(2,1)S(1)}, bf16[1,128,1280]{2,1,0:T(8,128)(2,1)S(1)}, u32[]{:S(2)}, u32[]{:S(2)}) collective-permute-start(bf16[1,128,1280]{2,1,0:T(8,128)(2,1)S(1)} %get-tuple-element.254), channel_id=1, source_target_pairs={{0,8},{4,12},{8,0},{12,4},{16,24},{20,28},{24,16},{28,20},{1,9},{5... | collective-permute-start | bytes 983048 | tf_op jit(solution)/shard_map/ppermute | solution.py:325
  1001.8 11.6 %collective-permute-start.48 = (bf16[1,128,1280]{2,1,0:T(8,128)(2,1)S(1)}, bf16[1,128,1280]{2,1,0:T(8,128)(2,1)S(1)}, u32[]{:S(2)}, u32[]{:S(2)}) collective-permute-start(bf16[1,128,1280]{2,1,0:T(8,128)(2,1)S(1)} %get-tuple-element.255), channel_id=1, source_target_pairs={{0,16},{4,20},{8,24},{12,28},{16,0},{20,4},{24,8},{28,12},{1,17},{... | collective-permute-start | bytes 983048 | tf_op jit(solution)/shard_map/ppermute | solution.py:325
  (87 other events, 1498.2 us)
Sparse Core Ops, SparseCore 0:
  121.0 81.5 all-gather.5
  205.1 98.7 all-gather.7
  306.3 99.4 all-gather.9
  407.5 80.9 all-gather.11
  492.0 137.6 reduce-scatter.6
  631.8 47.8 reduce-scatter.8
  692.0 39.4 reduce-scatter.10
  742.9 80.6 all-gather.13
  825.9 37.9 reduce-scatter.14
  866.0 48.4 reduce-scatter.12
  936.0 63.3 reduce-scatter.16

commit v6 on v5

--- a/solution.py
+++ b/solution.py
@@ -656,12 +656,12 @@
         part.reshape(width, local_experts, quarter).transpose(1, 0, 2) for part in grads[1:]
     )
     sent = normed_line.send(far, near, grad_gate, grad_up)
+    sent = sum([grad_qkv.send(*sent) for _ in bits[1:]], [])
     small = after(small, *sent) if sent else small
     for bit in bits_of(n_tensor):
         small = small + hop(small, bit, "tensor")
     small = lax.all_to_all(jnp.broadcast_to(small[None], (n_expert, *small.shape)), "expert", 0, 0, tiled=True)
     small = small.reshape(-1, width)
-    sent = sum([grad_qkv.send(*sent) for _ in bits[1:]], [])
     grad_qkv = grad_qkv.total().astype(f32)
     normed_grad = normed_line.total(*sent)
     layer_out = (middle + moe_out.astype(f32)).astype(bf16)

time: 1040 us -> 1050 us (level)
  blocking collectives: 0 us -> 28.2 us
    all_to_all x0 -> x1, blocking collectives: none -> 28.2 us  [local(): small = lax.all_to_all(small, 'expert', 0, 0, tiled=True).sum(axis=0)]
    ppermute x22, waiting for transfers between devices: 58.8 us -> 44.1 us  [hop(): return lax.ppermute(block, axis, [(i, i ^ bit) for i in range(size)])]
    ppermute x14, waiting for transfers between devices: 111 us -> 122 us  [neighbours(): lax.ppermute(v, 'tensor', [(i, (i + 1) % size) for i in range(size)])]
    unnamed x175 -> x169, local copies, waits for them, and re-layouts: 41.2 us -> 42.1 us
  transfers between devices with their start and end apart: 65 -> 64, of which waited for: 30 -> 32; matrix products, arithmetic and copies ran while one was open for 35% -> 34% of each run, Pallas kernels for 24% -> 23%
where the time goes in v6:
time: 1050 us; the launch traced here: 1040 us
  waiting for transfers between devices  274 us (26%)
  Pallas kernels  244 us (23%)
  matrix products  184 us (18%)
  local copies, waits for them, and re-layouts  108 us (10%)
  other arithmetic  107 us (10%)
  starting transfers between devices  82.3 us (8%)
  blocking collectives  28.2 us (3%)
  between operations  15.7 us (1%)
    dot_general x15, matrix products, dot(): lax.dot_general(a, b, (contract, ((), ())), preferred_element_type=f32)  184 us
    pallas_call x2, Pallas kernels, experts(): pl.pallas_call(functools.partial(experts_kernel, len(held)), grid_spec=pl...  139 us
    ppermute x14, waiting for transfers between devices, neighbours(): lax.ppermute(v, 'tensor', [(i, (i + 1) % size) for i in range(size)])  122 us
    ppermute x14, waiting for transfers between devices, neighbours(): lax.ppermute(v, 'tensor', [(i, (i - 1) % size) for i in range(size)])  85.3 us
    ppermute x22, waiting for transfers between devices, hop(): return lax.ppermute(block, axis, [(i, i ^ bit) for i in range(size)])  44.1 us
    unnamed x169, local copies, waits for them, and re-layouts  42.1 us
    ppermute x14, starting transfers between devices, neighbours(): lax.ppermute(v, 'tensor', [(i, (i - 1) % size) for i in range(size)])  41.6 us
    convert_element_type x8, other arithmetic, send(): add = lambda parts: sum((p.astype(f32) for p in parts)).astype(bf16)  35.6 us
  transfers between devices with their start and end apart: 64, of which 32 were waited for; matrix products, arithmetic and copies ran while one was open for 34% of the time, Pallas kernels for 23%

profile of v6, /device:TPU:0, one launch (start us, length us, event | category | flops | bytes accessed | tf_op | source)
XLA Modules:
  0.0 1043.5 jit_solution(5833478159468107809)
XLA Ops:
  11.6 5.1 collective-permute-start.1
  19.0 21.2 %collective-permute-done.1 = bf16[256,2048]{1,0:T(8,128)(2,1)S(1)} collective-permute-done((bf16[256,2048]{1,0:T(8,128)(2,1)S(1)}, bf16[256,2048]{1,0:T(8,128)(2,1)S(1)}, u32[]{:S(2)}, u32[]{:S(2)}) %collective-permute-start.1) | collective-permute-done | bytes 1048608 | tf_op jit(solution)/shard_map/ppermute | solution.py:386
  40.3 4.3 collective-permute-start.3
  44.6 19.0 %collective-permute-done = bf16[256,2048]{1,0:T(8,128)(2,1)S(1)} collective-permute-done((bf16[256,2048]{1,0:T(8,128)(2,1)S(1)}, bf16[256,2048]{1,0:T(8,128)(2,1)S(1)}, u32[]{:S(2)}, u32[]{:S(2)}) %collective-permute-start) | collective-permute-done | bytes 1048608 | tf_op jit(solution)/shard_map/ppermute | solution.py:385
  66.4 18.6 %collective-permute-done.2 = bf16[128,2048]{1,0:T(8,128)(2,1)S(1)} collective-permute-done((bf16[128,2048]{1,0:T(8,128)(2,1)S(1)}, bf16[128,2048]{1,0:T(8,128)(2,1)S(1)}, u32[]{:S(2)}, u32[]{:S(2)}) %collective-permute-start.2) | collective-permute-done | bytes 524320 | tf_op jit(solution)/shard_map/ppermute | solution.py:385
  87.9 9.8 project.1
  98.9 9.9 collective-permute-done.8
  125.9 11.7 %attend.1 = bf16[1024,1024]{1,0:T(8,128)(2,1)S(1)} custom-call(bf16[1024,1024]{1,0:T(8,128)(2,1)S(1)} %get-tuple-element.91.q_ref, bf16[1024,128]{1,0:T(8,128)(2,1)S(1)} %get-tuple-element.92.k_ref, bf16[128,1024]{1,0:T(8,128)(2,1)S(1)} %bitcast.152), custom_call_target="tpu_custom_call" | custom-call | flops 3221225472 | bytes 4194304 | tf_op jit(solution)/shard_map/attend/pallas_call | solution.py:88
  139.8 10.9 %collective-permute-done.4 = bf16[144,2048]{1,0:T(8,128)(2,1)} collective-permute-done((bf16[144,2048]{1,0:T(8,128)(2,1)}, bf16[144,2048]{1,0:T(8,128)(2,1)}, u32[]{:S(2)}, u32[]{:S(2)}) %collective-permute-start.4) | collective-permute-done | bytes 589856 | tf_op jit(solution)/shard_map/ppermute | solution.py:385
  158.3 4.1 copy.82
  169.9 6.9 convolution_convert_fusion.2
  181.6 12.7 %collective-permute-done.14 = bf16[128,2048]{1,0:T(8,128)(2,1)S(1)} collective-permute-done((bf16[128,2048]{1,0:T(8,128)(2,1)S(1)}, bf16[128,2048]{1,0:T(8,128)(2,1)S(1)}, u32[]{:S(2)}, u32[]{:S(2)}) %collective-permute-start.14) | collective-permute-done | bytes 524320 | tf_op jit(solution)/shard_map/ppermute | solution.py:386
  194.3 8.2 collective-permute-done.12
  206.5 23.4 %collective-permute-done.15 = bf16[256,2048]{1,0:T(8,128)(2,1)S(1)} collective-permute-done((bf16[256,2048]{1,0:T(8,128)(2,1)S(1)}, bf16[256,2048]{1,0:T(8,128)(2,1)S(1)}, u32[]{:S(2)}, u32[]{:S(2)}) %collective-permute-start.15) | collective-permute-done | bytes 1048608 | tf_op jit(solution)/shard_map/ppermute | solution.py:386
  229.9 22.5 %collective-permute-done.13 = bf16[256,2048]{1,0:T(8,128)(2,1)S(1)} collective-permute-done((bf16[256,2048]{1,0:T(8,128)(2,1)S(1)}, bf16[256,2048]{1,0:T(8,128)(2,1)S(1)}, u32[]{:S(2)}, u32[]{:S(2)}) %collective-permute-start.13) | collective-permute-done | bytes 1048608 | tf_op jit(solution)/shard_map/ppermute | solution.py:385
  259.9 17.4 %convolution_bitcast_fusion.1.pre_ref = f32[8,4,1,112,768]{4,3,2,1,0:T(8,128)} fusion(bf16[8,4,112,2048]{3,2,1,0:T(8,128)(2,1)} %bitcast.176, bf16[768,2048,1,1]{1,0,3,2:T(8,128)(2,1)S(1)} %bitcast.136), kind=kOutput, calls=%fused_computation.10 | convolution fusion | flops 11274289152 | bytes 28835840 | tf_op jit(solution)/shard_map/dot_general | solution.py:20
  277.2 8.2 collective-permute-done.16
  296.8 4.6 collective-permute-done.19
  308.3 10.9 %collective-permute-done.21 = bf16[112,2048]{1,0:T(8,128)(2,1)S(1)} collective-permute-done((bf16[112,2048]{1,0:T(8,128)(2,1)S(1)}, bf16[112,2048]{1,0:T(8,128)(2,1)S(1)}, u32[]{:S(2)}, u32[]{:S(2)}) %collective-permute-start.21) | collective-permute-done | bytes 458784 | tf_op jit(solution)/shard_map/ppermute | solution.py:386
  319.2 4.3 collective-permute-start.23
  323.6 6.5 collective-permute-done.20
  335.0 4.2 collective-permute-done.22
  340.6 4.6 copy.65.wg_ref
  345.3 4.6 copy.66.wu_ref
  352.9 5.7 convert_reduce_fusion
  362.2 4.3 all-to-all-start
  367.4 6.7 all-to-all-done
  378.5 20.6 %convolution_bitcast_fusion.pre_ref = f32[8,4,1,144,768]{4,3,2,1,0:T(8,128)} fusion(bf16[8,4,144,2048]{3,2,1,0:T(8,128)(2,1)} %bitcast.175, bf16[768,2048,1,1]{1,0,3,2:T(8,128)(2,1)S(1)} %bitcast.137), kind=kOutput, calls=%fused_computation.1 | convolution fusion | flops 14495514624 | bytes 36175872 | tf_op jit(solution)/shard_map/dot_general | solution.py:20
  399.1 6.7 all-gather.10.cloned.1.call-done.x_ref
  406.2 74.6 %experts.2 = (bf16[8,4,1,144,768]{4,3,2,1,0:T(8,128)(2,1)}, bf16[4608,768]{1,0:T(8,128)(2,1)}, bf16[4608,768]{1,0:T(8,128)(2,1)}, f32[8,8,576]{2,1,0:T(8,128)}, bf16[4608,2048]{1,0:T(8,128)(2,1)}) custom-call(s32[8]{0:T(128)} %iota.42.order, bf16[4608,2048]{1,0:T(8,128)(2,1)} %all-gather.10.cloned.1.call-done.x_ref, ...), custom_call_target="tpu_custom_call" | custom-call | flops 57982058496 | bytes 73138176 | tf_op jit(solution)/shard_map/experts/pallas_call | solution.py:232
  487.0 8.6 outputs.4
  495.6 4.3 copy-done.6
  499.9 64.1 %experts.3 = (bf16[8,4,1,112,768]{4,3,2,1,0:T(8,128)(2,1)}, bf16[3584,768]{1,0:T(8,128)(2,1)}, bf16[3584,768]{1,0:T(8,128)(2,1)}, f32[8,8,448]{2,1,0:T(8,128)}, ...) custom-call(s32[8]{0:T(128)} %copy-done.75, bf16[3584,2048]{1,0:T(8,128)(2,1)} %all-gather.12.cloned.1.call-done.x_ref, ...), custom_call_target="tpu_custom_call" | custom-call | flops 45097156608 | bytes 56885248 | tf_op jit(solution)/shard_map/experts/pallas_call | solution.py:232
  567.1 8.2 outputs.5
  577.4 4.5 all-to-all-start.1
  584.6 7.4 outputs.6
  595.0 5.1 add_convert_fusion.22
  605.9 23.5 %rows_product.1 = f32[2048,768]{1,0:T(8,128)} custom-call(bf16[4608,2048]{1,0:T(8,128)(2,1)} %all-gather.10.cloned.1.call-done.x_ref, bf16[4608,768]{1,0:T(8,128)(2,1)} %get-tuple-element.118.g_ref), custom_call_target="tpu_custom_call" | custom-call | flops 1 | bytes 1 | tf_op jit(solution)/shard_map/rows_product/pallas_call | solution.py:300
  630.1 25.8 %collective-permute-done.25 = bf16[2,224,2048]{2,1,0:T(8,128)(2,1)} collective-permute-done((bf16[2,224,2048]{2,1,0:T(8,128)(2,1)}, bf16[2,224,2048]{2,1,0:T(8,128)(2,1)}, u32[]{:S(2)}, u32[]{:S(2)}) %collective-permute-start.25) | collective-permute-done | bytes 1835040 | tf_op jit(solution)/shard_map/ppermute | solution.py:325
  655.9 4.9 add_convert_fusion.19
  662.7 5.0 add_convert_fusion.18
  672.6 8.7 outputs.7
  685.8 4.6 fusion.9
  691.9 19.5 %convolution_add_fusion.1 = f32[2048,768]{1,0:T(8,128)} fusion(f32[2048,768]{1,0:T(8,128)} %rows_product.1, bf16[3584,2048]{1,0:T(8,128)(2,1)} %all-gather.12.cloned.1.call-done.x_ref, bf16[3584,768]{1,0:T(8,128)(2,1)} %get-tuple-element.128), kind=kOutput, calls=%fused_computation.11 | convolution fusion | flops 11275862016 | bytes 32768000 | tf_op jit(solution)/shard_map/dot_general | solution.py:20
  711.4 18.9 %fusion.30 = f32[768,2048]{1,0:T(8,128)} fusion(bf16[4608,768]{1,0:T(8,128)(2,1)S(1)} %bitcast.150, bf16[4608,2048]{1,0:T(8,128)(2,1)} %all-gather.8.cloned.1.call-done), kind=kOutput, calls=%fused_computation.190 | convolution fusion | flops 14495514624 | bytes 32243712 | tf_op jit(solution)/shard_map/dot_general | solution.py:20
  730.4 5.1 add_convert_fusion.12
  742.7 5.0 add_convert_fusion.5
  752.9 18.2 %fusion.31 = f32[2048,768]{0,1:T(8,128)} fusion(bf16[3584,2048]{1,0:T(8,128)(2,1)} %all-gather.12.cloned.1.call-done.x_ref, bf16[3584,768]{1,0:T(8,128)(2,1)} %get-tuple-element.139), kind=kOutput, calls=%fused_computation.191 | convolution fusion | flops 11274289152 | bytes 26476544 | tf_op jit(solution)/shard_map/dot_general | solution.py:20
  771.0 23.8 %convolution_add_fusion = f32[2048,768]{0,1:T(8,128)} fusion(f32[2048,768]{0,1:T(8,128)} %fusion.31, bf16[4608,2048]{1,0:T(8,128)(2,1)} %all-gather.10.cloned.1.call-done.x_ref, bf16[4608,768]{1,0:T(8,128)(2,1)} %get-tuple-element.137), kind=kOutput, calls=%fused_computation.9 | convolution fusion | flops 14497087488 | bytes 38535168 | tf_op jit(solution)/shard_map/dot_general | solution.py:20
  794.9 4.7 fusion.11
  801.0 19.3 %convolution_add_fusion.2 = f32[768,2048]{1,0:T(8,128)} fusion(f32[768,2048]{1,0:T(8,128)} %fusion.30, bf16[3584,768]{1,0:T(8,128)(2,1)} %bitcast.142, bf16[3584,2048]{1,0:T(8,128)(2,1)} %all-gather.6.cloned.1.call-done), kind=kOutput, calls=%fused_computation.12 | convolution fusion | flops 11275862016 | bytes 32768000 | tf_op jit(solution)/shard_map/dot_general | solution.py:20
  820.4 6.2 add_convert_fusion.3
  829.0 9.7 convolution_convert_fusion.3.do_ref
  838.7 13.3 %collective-permute-done.38 = bf16[1,288,2048]{2,1,0:T(8,128)(2,1)S(1)} collective-permute-done((bf16[1,288,2048]{2,1,0:T(8,128)(2,1)}, bf16[1,288,2048]{2,1,0:T(8,128)(2,1)S(1)}, u32[]{:S(2)}, u32[]{:S(2)}) %collective-permute-start.38) | collective-permute-done | bytes 1179680 | tf_op jit(solution)/shard_map/ppermute | solution.py:325
  853.3 5.4 fusion.6
  867.2 27.7 %attend_back.1 = (bf16[1024,1024]{1,0:T(8,128)(2,1)S(1)}, bf16[1024,128]{1,0:T(8,128)(2,1)S(1)}, bf16[1024,128]{1,0:T(8,128)(2,1)S(1)}, f32[1,128]{1,0:T(1,128)S(1)}, f32[1,128]{1,0:T(1,128)S(1)}) custom-call(bf16[1024,1024]{1,0:T(8,128)(2,1)S(1)} %copy-done.25, bf16[1024,1024]{1,0:T(8,128)(2,1)S(1)} %copy-done.28, f32[1024,1152]{1,0:T(8,128)S(1)} %copy-done.23, ...), custom_call_target="tpu_custom_call" | custom-call | flops 7516192768 | bytes 10485760 | tf_op jit(solution)/shard_map/attend_back/pallas_call | solution.py:159
  896.6 10.0 multiply_reduce_fusion
  910.9 5.9 convolution_convert_fusion
  918.8 6.6 copy.73
  929.0 9.5 convolution_convert_fusion.1
  941.3 11.8 %collective-permute-done.39 = bf16[128,2048]{1,0:T(8,128)(2,1)} collective-permute-done((bf16[128,2048]{1,0:T(8,128)(2,1)}, bf16[128,2048]{1,0:T(8,128)(2,1)}, u32[]{:S(2)}, u32[]{:S(2)}) %collective-permute-start.39) | collective-permute-done | bytes 524320 | tf_op jit(solution)/shard_map/ppermute | solution.py:385
  967.3 28.2 %all_to_all.20 = f32[8,5,2048]{2,1,0:T(8,128)S(1)} all-to-all(f32[8,5,2048]{2,1,0:T(8,128)S(1)} %reshape.304), channel_id=1, replica_groups=mesh['expert'=8,'tensor'=4] {'expert'}, dimensions={0} | all-to-all | bytes 655360 | tf_op jit(solution)/shard_map/all_to_all | solution.py:645
  999.1 6.6 collective-permute-done.42
  1023.1 6.7 all-to-all-done.3
  (419 shorter events, 219.1 us)
Async XLA Ops:
  7.2 252.6 %all-gather.6.cloned.1.call-start = ((), (), s32[]{:S(2)}) async-start(), calls=%async_computation.10 | async-start | bytes 16515072 | tf_op jit(solution)/shard_map/all_gather | solution.py:498
  11.6 28.7 %collective-permute-start.1 = (bf16[256,2048]{1,0:T(8,128)(2,1)S(1)}, bf16[256,2048]{1,0:T(8,128)(2,1)S(1)}, u32[]{:S(2)}, u32[]{:S(2)}) collective-permute-start(bf16[256,2048]{1,0:T(8,128)(2,1)S(1)} %fusion.4), channel_id=1, source_target_pairs={{0,3},{1,0},{2,1},{3,2},{4,7},{5,4},{6,5},{7,6},{8,11},{9,8},{10,9... | collective-permute-start | bytes 3145736 | tf_op jit(solution)/shard_map/ppermute | solution.py:386
  16.7 47.0 %collective-permute-start = (bf16[256,2048]{1,0:T(8,128)(2,1)S(1)}, bf16[256,2048]{1,0:T(8,128)(2,1)S(1)}, u32[]{:S(2)}, u32[]{:S(2)}) collective-permute-start(bf16[256,2048]{1,0:T(8,128)(2,1)S(1)} %fusion.4), channel_id=1, source_target_pairs={{0,1},{1,2},{2,3},{3,0},{4,5},{5,6},{6,7},{7,4},{8,9},{9,10},{10,1... | collective-permute-start | bytes 3145736 | tf_op jit(solution)/shard_map/ppermute | solution.py:385
  40.3 44.8 %collective-permute-start.3 = (bf16[128,2048]{1,0:T(8,128)(2,1)S(1)}, bf16[128,2048]{1,0:T(8,128)(2,1)S(1)}, u32[]{:S(2)}, u32[]{:S(2)}) collective-permute-start(bf16[128,2048]{1,0:T(8,128)(2,1)S(1)} %slice.413), channel_id=1, source_target_pairs={{0,3},{1,0},{2,1},{3,2},{4,7},{5,4},{6,5},{7,6},{8,11},{9,8},{10,9... | collective-permute-start | bytes 1572872 | tf_op jit(solution)/shard_map/ppermute | solution.py:386
  63.7 21.3 %collective-permute-start.2 = (bf16[128,2048]{1,0:T(8,128)(2,1)S(1)}, bf16[128,2048]{1,0:T(8,128)(2,1)S(1)}, u32[]{:S(2)}, u32[]{:S(2)}) collective-permute-start(bf16[128,2048]{1,0:T(8,128)(2,1)S(1)} %slice.412), channel_id=1, source_target_pairs={{0,1},{1,2},{2,3},{3,0},{4,5},{5,6},{6,7},{7,4},{8,9},{9,10},{10,1... | collective-permute-start | bytes 1572872 | tf_op jit(solution)/shard_map/ppermute | solution.py:385
  85.2 13.7 %collective-permute-start.9 = (bf16[112,2048]{1,0:T(8,128)(2,1)S(1)}, bf16[112,2048]{1,0:T(8,128)(2,1)S(1)}, u32[]{:S(2)}, u32[]{:S(2)}) collective-permute-start(bf16[112,2048]{1,0:T(8,128)(2,1)S(1)} %slice.314), channel_id=1, source_target_pairs={{0,3},{1,0},{2,1},{3,2},{4,7},{5,4},{6,5},{7,6},{8,11},{9,8},{10,9... | collective-permute-start | bytes 1376264 | tf_op jit(solution)/shard_map/ppermute | solution.py:386
  87.9 20.9 %collective-permute-start.8 = (bf16[112,2048]{1,0:T(8,128)(2,1)S(1)}, bf16[112,2048]{1,0:T(8,128)(2,1)S(1)}, u32[]{:S(2)}, u32[]{:S(2)}) collective-permute-start(bf16[112,2048]{1,0:T(8,128)(2,1)S(1)} %slice.314), channel_id=1, source_target_pairs={{0,1},{1,2},{2,3},{3,0},{4,5},{5,6},{6,7},{7,4},{8,9},{9,10},{10,1... | collective-permute-start | bytes 1376264 | tf_op jit(solution)/shard_map/ppermute | solution.py:385
  108.8 10.4 collective-permute-start.10
  109.5 10.7 %collective-permute-start.11 = (bf16[56,2048]{1,0:T(8,128)(2,1)S(1)}, bf16[56,2048]{1,0:T(8,128)(2,1)S(1)}, u32[]{:S(2)}, u32[]{:S(2)}) collective-permute-start(bf16[56,2048]{1,0:T(8,128)(2,1)S(1)} %slice.316), channel_id=1, source_target_pairs={{0,3},{1,0},{2,1},{3,2},{4,7},{5,4},{6,5},{7,6},{8,11},{9,8},{10,9... | collective-permute-start | bytes 688136 | tf_op jit(solution)/shard_map/ppermute | solution.py:386
  120.9 182.9 %all-gather.8.cloned.1.call-start = ((), (), s32[]{:S(2)}) async-start(), calls=%async_computation.11 | async-start | bytes 21233664 | tf_op jit(solution)/shard_map/all_gather | solution.py:499
  122.8 17.0 %collective-permute-start.5 = (bf16[144,2048]{1,0:T(8,128)(2,1)}, bf16[144,2048]{1,0:T(8,128)(2,1)}, u32[]{:S(2)}, u32[]{:S(2)}) collective-permute-start(bf16[144,2048]{1,0:T(8,128)(2,1)} %slice.311), channel_id=1, source_target_pairs={{0,3},{1,0},{2,1},{3,2},{4,7},{5,4},{6,5},{7,6},{8,11},{9,8},{10,9... | collective-permute-start | bytes 1769480 | tf_op jit(solution)/shard_map/ppermute | solution.py:386
  125.7 25.0 %collective-permute-start.4 = (bf16[144,2048]{1,0:T(8,128)(2,1)}, bf16[144,2048]{1,0:T(8,128)(2,1)}, u32[]{:S(2)}, u32[]{:S(2)}) collective-permute-start(bf16[144,2048]{1,0:T(8,128)(2,1)} %slice.311), channel_id=1, source_target_pairs={{0,1},{1,2},{2,3},{3,0},{4,5},{5,6},{6,7},{7,4},{8,9},{9,10},{10,1... | collective-permute-start | bytes 1769480 | tf_op jit(solution)/shard_map/ppermute | solution.py:385
  152.7 15.6 %collective-permute-start.6 = (bf16[72,2048]{1,0:T(8,128)(2,1)S(1)}, bf16[72,2048]{1,0:T(8,128)(2,1)S(1)}, u32[]{:S(2)}, u32[]{:S(2)}) collective-permute-start(bf16[72,2048]{1,0:T(8,128)(2,1)S(1)} %slice.312), channel_id=1, source_target_pairs={{0,1},{1,2},{2,3},{3,0},{4,5},{5,6},{6,7},{7,4},{8,9},{9,10},{10,1... | collective-permute-start | bytes 884744 | tf_op jit(solution)/shard_map/ppermute | solution.py:385
  153.5 15.6 %collective-permute-start.7 = (bf16[72,2048]{1,0:T(8,128)(2,1)S(1)}, bf16[72,2048]{1,0:T(8,128)(2,1)S(1)}, u32[]{:S(2)}, u32[]{:S(2)}) collective-permute-start(bf16[72,2048]{1,0:T(8,128)(2,1)S(1)} %slice.313), channel_id=1, source_target_pairs={{0,3},{1,0},{2,1},{3,2},{4,7},{5,4},{6,5},{7,6},{8,11},{9,8},{10,9... | collective-permute-start | bytes 884744 | tf_op jit(solution)/shard_map/ppermute | solution.py:386
  169.8 235.9 %all-gather.10.cloned.1.call-start = ((), (), s32[]{:S(2)}) async-start(), calls=%async_computation.12 | async-start | bytes 21233664 | tf_op jit(solution)/shard_map/all_gather | solution.py:549
  179.1 15.2 %collective-permute-start.14 = (bf16[128,2048]{1,0:T(8,128)(2,1)S(1)}, bf16[128,2048]{1,0:T(8,128)(2,1)S(1)}, u32[]{:S(2)}, u32[]{:S(2)}) collective-permute-start(bf16[128,2048]{1,0:T(8,128)(2,1)S(1)} %get-tuple-element.276), channel_id=1, source_target_pairs={{0,3},{1,0},{2,1},{3,2},{4,7},{5,4},{6,5},{7,6},{8,11},{9,8},{10,9... | collective-permute-start | bytes 1572872 | tf_op jit(solution)/shard_map/ppermute | solution.py:386
  179.7 22.8 %collective-permute-start.12 = (bf16[128,2048]{1,0:T(8,128)(2,1)S(1)}, bf16[128,2048]{1,0:T(8,128)(2,1)S(1)}, u32[]{:S(2)}, u32[]{:S(2)}) collective-permute-start(bf16[128,2048]{1,0:T(8,128)(2,1)S(1)} %get-tuple-element.277), channel_id=1, source_target_pairs={{0,1},{1,2},{2,3},{3,0},{4,5},{5,6},{6,7},{7,4},{8,9},{9,10},{10,1... | collective-permute-start | bytes 1572872 | tf_op jit(solution)/shard_map/ppermute | solution.py:385
  204.2 25.7 %collective-permute-start.15 = (bf16[256,2048]{1,0:T(8,128)(2,1)S(1)}, bf16[256,2048]{1,0:T(8,128)(2,1)S(1)}, u32[]{:S(2)}, u32[]{:S(2)}) collective-permute-start(bf16[256,2048]{1,0:T(8,128)(2,1)S(1)} %pad_maximum_fusion.13), channel_id=1, source_target_pairs={{0,3},{1,0},{2,1},{3,2},{4,7},{5,4},{6,5},{7,6},{8,11},{9,8},{10,9... | collective-permute-start | bytes 3145736 | tf_op jit(solution)/shard_map/ppermute | solution.py:386
  206.4 46.0 %collective-permute-start.13 = (bf16[256,2048]{1,0:T(8,128)(2,1)S(1)}, bf16[256,2048]{1,0:T(8,128)(2,1)S(1)}, u32[]{:S(2)}, u32[]{:S(2)}) collective-permute-start(bf16[256,2048]{1,0:T(8,128)(2,1)S(1)} %pad_maximum_fusion.12), channel_id=1, source_target_pairs={{0,1},{1,2},{2,3},{3,0},{4,5},{5,6},{6,7},{7,4},{8,9},{9,10},{10,1... | collective-permute-start | bytes 3145736 | tf_op jit(solution)/shard_map/ppermute | solution.py:385
  257.8 19.4 %collective-permute-start.17 = (bf16[144,2048]{1,0:T(8,128)(2,1)}, bf16[144,2048]{1,0:T(8,128)(2,1)}, u32[]{:S(2)}, u32[]{:S(2)}) collective-permute-start(bf16[144,2048]{1,0:T(8,128)(2,1)} %slice.414), channel_id=1, source_target_pairs={{0,3},{1,0},{2,1},{3,2},{4,7},{5,4},{6,5},{7,6},{8,11},{9,8},{10,9... | collective-permute-start | bytes 1769480 | tf_op jit(solution)/shard_map/ppermute | solution.py:386
  259.8 25.6 %collective-permute-start.16 = (bf16[144,2048]{1,0:T(8,128)(2,1)}, bf16[144,2048]{1,0:T(8,128)(2,1)}, u32[]{:S(2)}, u32[]{:S(2)}) collective-permute-start(bf16[144,2048]{1,0:T(8,128)(2,1)} %slice.414), channel_id=1, source_target_pairs={{0,1},{1,2},{2,3},{3,0},{4,5},{5,6},{6,7},{7,4},{8,9},{9,10},{10,1... | collective-permute-start | bytes 1769480 | tf_op jit(solution)/shard_map/ppermute | solution.py:385
  286.4 9.6 collective-permute-start.18
  292.0 9.3 collective-permute-start.19
  303.8 196.1 %all-gather.12.cloned.1.call-start = ((), (), s32[]{:S(2)}) async-start(), calls=%async_computation.13 | async-start | bytes 16515072 | tf_op jit(solution)/shard_map/all_gather | solution.py:549
  304.9 14.3 %collective-permute-start.21 = (bf16[112,2048]{1,0:T(8,128)(2,1)S(1)}, bf16[112,2048]{1,0:T(8,128)(2,1)S(1)}, u32[]{:S(2)}, u32[]{:S(2)}) collective-permute-start(bf16[112,2048]{1,0:T(8,128)(2,1)S(1)} %slice.415), channel_id=1, source_target_pairs={{0,3},{1,0},{2,1},{3,2},{4,7},{5,4},{6,5},{7,6},{8,11},{9,8},{10,9... | collective-permute-start | bytes 1376264 | tf_op jit(solution)/shard_map/ppermute | solution.py:386
  308.3 21.7 %collective-permute-start.20 = (bf16[112,2048]{1,0:T(8,128)(2,1)S(1)}, bf16[112,2048]{1,0:T(8,128)(2,1)S(1)}, u32[]{:S(2)}, u32[]{:S(2)}) collective-permute-start(bf16[112,2048]{1,0:T(8,128)(2,1)S(1)} %slice.415), channel_id=1, source_target_pairs={{0,1},{1,2},{2,3},{3,0},{4,5},{5,6},{6,7},{7,4},{8,9},{9,10},{10,1... | collective-permute-start | bytes 1376264 | tf_op jit(solution)/shard_map/ppermute | solution.py:385
  319.2 20.7 %collective-permute-start.23 = (bf16[56,2048]{1,0:T(8,128)(2,1)S(1)}, bf16[56,2048]{1,0:T(8,128)(2,1)S(1)}, u32[]{:S(2)}, u32[]{:S(2)}) collective-permute-start(bf16[56,2048]{1,0:T(8,128)(2,1)S(1)} %slice.417), channel_id=1, source_target_pairs={{0,3},{1,0},{2,1},{3,2},{4,7},{5,4},{6,5},{7,6},{8,11},{9,8},{10,9... | collective-permute-start | bytes 688136 | tf_op jit(solution)/shard_map/ppermute | solution.py:386
  330.0 9.1 collective-permute-start.22
  362.2 11.8 %all-to-all-start = ((bf16[32,4,256]{2,1,0:T(4,128)(2,1)}), bf16[32,4,256]{2,1,0:T(4,128)(2,1)S(1)}, u32[]{:S(2)}, u32[]{:S(2)}) async-start(bf16[32,4,256]{2,1,0:T(4,128)(2,1)} %bitcast.19), calls=%async_computation | async-start | bytes 131072 | tf_op jit(solution)/shard_map/all_to_all | solution.py:526
  366.6 263.4 %reduce-scatter.7.cloned.1.call-start = ((), (), s32[]{:S(2)}) async-start(), calls=%async_computation.14 | async-start | bytes 21233664 | tf_op jit(solution)/shard_map/reduce_scatter | solution.py:554
  564.0 31.0 %collective-permute-start.24 = (bf16[1792,2048]{1,0:T(8,128)(2,1)}, bf16[1792,2048]{1,0:T(8,128)(2,1)}, u32[]{:S(2)}, u32[]{:S(2)}) collective-permute-start(bf16[1792,2048]{1,0:T(8,128)(2,1)} %get-tuple-element.111), channel_id=1, source_target_pairs={{0,4},{4,0},{8,12},{12,8},{16,20},{20,16},{24,28},{28,24},{1,5},{5... | collective-permute-start | bytes 22020104 | tf_op jit(solution)/shard_map/ppermute | solution.py:325
  575.3 87.5 %collective-permute-start.29 = (bf16[1792,2048]{1,0:T(8,128)(2,1)}, bf16[1792,2048]{1,0:T(8,128)(2,1)}, u32[]{:S(2)}, u32[]{:S(2)}) collective-permute-start(bf16[1792,2048]{1,0:T(8,128)(2,1)} %outputs.5), channel_id=1, source_target_pairs={{0,4},{4,0},{8,12},{12,8},{16,20},{20,16},{24,28},{28,24},{1,5},{5... | collective-permute-start | bytes 22020104 | tf_op jit(solution)/shard_map/ppermute | solution.py:325
  577.4 17.5 %all-to-all-start.1 = ((f32[32,4,256]{2,1,0:T(4,128)}), f32[32,4,256]{2,1,0:T(4,128)S(1)}, u32[]{:S(2)}, u32[]{:S(2)}) async-start(f32[32,4,256]{2,1,0:T(4,128)} %bitcast.168), calls=%async_computation.1 | async-start | bytes 262144 | tf_op jit(solution)/shard_map/all_to_all | solution.py:541
  581.8 103.1 %reduce-scatter.9.cloned.1.call-start = ((), (), s32[]{:S(2)}) async-start(), calls=%async_computation.15 | async-start | bytes 2949120 | tf_op jit(solution)/shard_map/reduce_scatter | solution.py:536
  601.6 54.3 %collective-permute-start.25 = (bf16[2,224,2048]{2,1,0:T(8,128)(2,1)}, bf16[2,224,2048]{2,1,0:T(8,128)(2,1)}, u32[]{:S(2)}, u32[]{:S(2)}) collective-permute-start(bf16[2,224,2048]{2,1,0:T(8,128)(2,1)} %pad_maximum_fusion.6), channel_id=1, source_target_pairs={{0,8},{4,12},{8,0},{12,4},{16,24},{20,28},{24,16},{28,20},{1,9},{5... | collective-permute-start | bytes 5505032 | tf_op jit(solution)/shard_map/ppermute | solution.py:325
  604.7 51.2 %collective-permute-start.26 = (bf16[2,224,2048]{2,1,0:T(8,128)(2,1)}, bf16[2,224,2048]{2,1,0:T(8,128)(2,1)}, u32[]{:S(2)}, u32[]{:S(2)}) collective-permute-start(bf16[2,224,2048]{2,1,0:T(8,128)(2,1)} %pad_maximum_fusion.7), channel_id=1, source_target_pairs={{0,16},{4,20},{8,24},{12,28},{16,0},{20,4},{24,8},{28,12},{1,17},{... | collective-permute-start | bytes 5505032 | tf_op jit(solution)/shard_map/ppermute | solution.py:325
  630.0 107.6 %reduce-scatter.11.cloned.1.call-start = ((), (), s32[]{:S(2)}) async-start(), calls=%async_computation.16 | async-start | bytes 2293760 | tf_op jit(solution)/shard_map/reduce_scatter | solution.py:536
  630.0 112.6 %collective-permute-start.27 = (bf16[2304,2048]{1,0:T(8,128)(2,1)}, bf16[2304,2048]{1,0:T(8,128)(2,1)}, u32[]{:S(2)}, u32[]{:S(2)}) collective-permute-start(bf16[2304,2048]{1,0:T(8,128)(2,1)} %copy-done.6), channel_id=1, source_target_pairs={{0,4},{4,0},{8,12},{12,8},{16,20},{20,16},{24,28},{28,24},{1,5},{5... | collective-permute-start | bytes 28311560 | tf_op jit(solution)/shard_map/ppermute | solution.py:325
  660.8 24.2 %collective-permute-start.30 = (bf16[1,224,2048]{2,1,0:T(8,128)(2,1)S(1)}, bf16[1,224,2048]{2,1,0:T(8,128)(2,1)}, u32[]{:S(2)}, u32[]{:S(2)}) collective-permute-start(bf16[1,224,2048]{2,1,0:T(8,128)(2,1)S(1)} %get-tuple-element.244), channel_id=1, source_target_pairs={{0,8},{4,12},{8,0},{12,4},{16,24},{20,28},{24,16},{28,20},{1,9},{5... | collective-permute-start | bytes 2752520 | tf_op jit(solution)/shard_map/ppermute | solution.py:325
  662.2 23.6 %collective-permute-start.28 = (bf16[1,224,2048]{2,1,0:T(8,128)(2,1)}, bf16[1,224,2048]{2,1,0:T(8,128)(2,1)}, u32[]{:S(2)}, u32[]{:S(2)}) collective-permute-start(bf16[1,224,2048]{2,1,0:T(8,128)(2,1)} %get-tuple-element.245), channel_id=1, source_target_pairs={{0,16},{4,20},{8,24},{12,28},{16,0},{20,4},{24,8},{28,12},{1,17},{... | collective-permute-start | bytes 2752520 | tf_op jit(solution)/shard_map/ppermute | solution.py:325
  669.1 61.2 %collective-permute-start.32 = (bf16[2,224,2048]{2,1,0:T(8,128)(2,1)}, bf16[2,224,2048]{2,1,0:T(8,128)(2,1)}, u32[]{:S(2)}, u32[]{:S(2)}) collective-permute-start(bf16[2,224,2048]{2,1,0:T(8,128)(2,1)} %pad_maximum_fusion.9), channel_id=1, source_target_pairs={{0,16},{4,20},{8,24},{12,28},{16,0},{20,4},{24,8},{28,12},{1,17},{... | collective-permute-start | bytes 5505032 | tf_op jit(solution)/shard_map/ppermute | solution.py:325
  672.1 58.3 %collective-permute-start.31 = (bf16[2,224,2048]{2,1,0:T(8,128)(2,1)}, bf16[2,224,2048]{2,1,0:T(8,128)(2,1)}, u32[]{:S(2)}, u32[]{:S(2)}) collective-permute-start(bf16[2,224,2048]{2,1,0:T(8,128)(2,1)} %pad_maximum_fusion.8), channel_id=1, source_target_pairs={{0,8},{4,12},{8,0},{12,4},{16,24},{20,28},{24,16},{28,20},{1,9},{5... | collective-permute-start | bytes 5505032 | tf_op jit(solution)/shard_map/ppermute | solution.py:325
  691.8 137.2 %all-gather.14.cloned.1.call-start = ((), (), s32[]{:S(2)}) async-start(), calls=%async_computation.17 | async-start | bytes 5242880 | tf_op jit(solution)/shard_map/all_gather | solution.py:612
  735.5 59.4 %collective-permute-start.34 = (bf16[1,224,2048]{2,1,0:T(8,128)(2,1)}, bf16[1,224,2048]{2,1,0:T(8,128)(2,1)}, u32[]{:S(2)}, u32[]{:S(2)}) collective-permute-start(bf16[1,224,2048]{2,1,0:T(8,128)(2,1)} %get-tuple-element.236), channel_id=1, source_target_pairs={{0,16},{4,20},{8,24},{12,28},{16,0},{20,4},{24,8},{28,12},{1,17},{... | collective-permute-start | bytes 2752520 | tf_op jit(solution)/shard_map/ppermute | solution.py:325
  736.2 58.7 %collective-permute-start.35 = (bf16[1,224,2048]{2,1,0:T(8,128)(2,1)}, bf16[1,224,2048]{2,1,0:T(8,128)(2,1)}, u32[]{:S(2)}, u32[]{:S(2)}) collective-permute-start(bf16[1,224,2048]{2,1,0:T(8,128)(2,1)} %get-tuple-element.237), channel_id=1, source_target_pairs={{0,8},{4,12},{8,0},{12,4},{16,24},{20,28},{24,16},{28,20},{1,9},{5... | collective-permute-start | bytes 2752520 | tf_op jit(solution)/shard_map/ppermute | solution.py:325
  742.6 154.0 %reduce-scatter.15.cloned.1.call-start = ((), (), s32[]{:S(2)}) async-start(), calls=%async_computation.19 | async-start | bytes 2293760 | tf_op jit(solution)/shard_map/reduce_scatter | solution.py:536
  749.3 71.1 %collective-permute-start.33 = (bf16[2,288,2048]{2,1,0:T(8,128)(2,1)}, bf16[2,288,2048]{2,1,0:T(8,128)(2,1)}, u32[]{:S(2)}, u32[]{:S(2)}) collective-permute-start(bf16[2,288,2048]{2,1,0:T(8,128)(2,1)} %pad_maximum_fusion.3), channel_id=1, source_target_pairs={{0,8},{4,12},{8,0},{12,4},{16,24},{20,28},{24,16},{28,20},{1,9},{5... | collective-permute-start | bytes 7077896 | tf_op jit(solution)/shard_map/ppermute | solution.py:325
  751.5 68.8 %collective-permute-start.37 = (bf16[2,288,2048]{2,1,0:T(8,128)(2,1)}, bf16[2,288,2048]{2,1,0:T(8,128)(2,1)}, u32[]{:S(2)}, u32[]{:S(2)}) collective-permute-start(bf16[2,288,2048]{2,1,0:T(8,128)(2,1)} %pad_maximum_fusion.4), channel_id=1, source_target_pairs={{0,16},{4,20},{8,24},{12,28},{16,0},{20,4},{24,8},{28,12},{1,17},{... | collective-permute-start | bytes 7077896 | tf_op jit(solution)/shard_map/ppermute | solution.py:325
  800.9 230.8 %reduce-scatter.13.cloned.1.call-start = ((), (), s32[]{:S(2)}) async-start(), calls=%async_computation.18 | async-start | bytes 2949120 | tf_op jit(solution)/shard_map/reduce_scatter | solution.py:536
  826.5 25.5 %collective-permute-start.38 = (bf16[1,288,2048]{2,1,0:T(8,128)(2,1)}, bf16[1,288,2048]{2,1,0:T(8,128)(2,1)S(1)}, u32[]{:S(2)}, u32[]{:S(2)}) collective-permute-start(bf16[1,288,2048]{2,1,0:T(8,128)(2,1)} %get-tuple-element.229), channel_id=1, source_target_pairs={{0,8},{4,12},{8,0},{12,4},{16,24},{20,28},{24,16},{28,20},{1,9},{5... | collective-permute-start | bytes 3538952 | tf_op jit(solution)/shard_map/ppermute | solution.py:325
  827.4 25.9 %collective-permute-start.36 = (bf16[1,288,2048]{2,1,0:T(8,128)(2,1)}, bf16[1,288,2048]{2,1,0:T(8,128)(2,1)}, u32[]{:S(2)}, u32[]{:S(2)}) collective-permute-start(bf16[1,288,2048]{2,1,0:T(8,128)(2,1)} %get-tuple-element.228), channel_id=1, source_target_pairs={{0,16},{4,20},{8,24},{12,28},{16,0},{20,4},{24,8},{28,12},{1,17},{... | collective-permute-start | bytes 3538952 | tf_op jit(solution)/shard_map/ppermute | solution.py:325
  860.4 173.7 %reduce-scatter.17.cloned.1.call-start = ((), (), s32[]{:S(2)}) async-start(), calls=%async_computation.20 | async-start | bytes 4718592 | tf_op jit(solution)/shard_map/reduce_scatter | solution.py:638
  918.8 42.3 %collective-permute-start.43 = (bf16[1024,1280]{1,0:T(8,128)(2,1)}, bf16[1024,1280]{1,0:T(8,128)(2,1)}, u32[]{:S(2)}, u32[]{:S(2)}) collective-permute-start(bf16[1024,1280]{1,0:T(8,128)(2,1)} %pad_maximum_fusion.1), channel_id=1, source_target_pairs={{0,4},{4,0},{8,12},{12,8},{16,20},{20,16},{24,28},{28,24},{1,5},{5... | collective-permute-start | bytes 7864328 | tf_op jit(solution)/shard_map/ppermute | solution.py:325
  925.3 16.0 %collective-permute-start.40 = (bf16[128,2048]{1,0:T(8,128)(2,1)}, bf16[128,2048]{1,0:T(8,128)(2,1)}, u32[]{:S(2)}, u32[]{:S(2)}) collective-permute-start(bf16[128,2048]{1,0:T(8,128)(2,1)} %get-tuple-element.271), channel_id=1, source_target_pairs={{0,3},{1,0},{2,1},{3,2},{4,7},{5,4},{6,5},{7,6},{8,11},{9,8},{10,9... | collective-permute-start | bytes 1572872 | tf_op jit(solution)/shard_map/ppermute | solution.py:386
  928.7 24.4 %collective-permute-start.39 = (bf16[128,2048]{1,0:T(8,128)(2,1)}, bf16[128,2048]{1,0:T(8,128)(2,1)}, u32[]{:S(2)}, u32[]{:S(2)}) collective-permute-start(bf16[128,2048]{1,0:T(8,128)(2,1)} %get-tuple-element.272), channel_id=1, source_target_pairs={{0,1},{1,2},{2,3},{3,0},{4,5},{5,6},{6,7},{7,4},{8,9},{9,10},{10,1... | collective-permute-start | bytes 1572872 | tf_op jit(solution)/shard_map/ppermute | solution.py:385
  956.2 42.9 %collective-permute-start.41 = (bf16[256,2048]{1,0:T(8,128)(2,1)}, bf16[256,2048]{1,0:T(8,128)(2,1)S(1)}, u32[]{:S(2)}, u32[]{:S(2)}) collective-permute-start(bf16[256,2048]{1,0:T(8,128)(2,1)} %pad_maximum_fusion.14), channel_id=1, source_target_pairs={{0,1},{1,2},{2,3},{3,0},{4,5},{5,6},{6,7},{7,4},{8,9},{9,10},{10,1... | collective-permute-start | bytes 3145736 | tf_op jit(solution)/shard_map/ppermute | solution.py:385
  958.8 46.8 %collective-permute-start.42 = (bf16[256,2048]{1,0:T(8,128)(2,1)}, bf16[256,2048]{1,0:T(8,128)(2,1)}, u32[]{:S(2)}, u32[]{:S(2)}) collective-permute-start(bf16[256,2048]{1,0:T(8,128)(2,1)} %pad_maximum_fusion.15), channel_id=1, source_target_pairs={{0,3},{1,0},{2,1},{3,2},{4,7},{5,4},{6,5},{7,6},{8,11},{9,8},{10,9... | collective-permute-start | bytes 3145736 | tf_op jit(solution)/shard_map/ppermute | solution.py:386
  964.0 31.5 %collective-permute-start.44 = (bf16[2,128,1280]{2,1,0:T(8,128)(2,1)}, bf16[2,128,1280]{2,1,0:T(8,128)(2,1)}, u32[]{:S(2)}, u32[]{:S(2)}) collective-permute-start(bf16[2,128,1280]{2,1,0:T(8,128)(2,1)} %pad_maximum_fusion.16), channel_id=1, source_target_pairs={{0,8},{4,12},{8,0},{12,4},{16,24},{20,28},{24,16},{28,20},{1,9},{5... | collective-permute-start | bytes 1966088 | tf_op jit(solution)/shard_map/ppermute | solution.py:325
  965.3 30.3 %collective-permute-start.45 = (bf16[2,128,1280]{2,1,0:T(8,128)(2,1)}, bf16[2,128,1280]{2,1,0:T(8,128)(2,1)}, u32[]{:S(2)}, u32[]{:S(2)}) collective-permute-start(bf16[2,128,1280]{2,1,0:T(8,128)(2,1)} %pad_maximum_fusion.17), channel_id=1, source_target_pairs={{0,16},{4,20},{8,24},{12,28},{16,0},{20,4},{24,8},{28,12},{1,17},{... | collective-permute-start | bytes 1966088 | tf_op jit(solution)/shard_map/ppermute | solution.py:325
  998.0 22.2 %collective-permute-start.49 = (bf16[1,128,1280]{2,1,0:T(8,128)(2,1)}, bf16[1,128,1280]{2,1,0:T(8,128)(2,1)S(1)}, u32[]{:S(2)}, u32[]{:S(2)}) collective-permute-start(bf16[1,128,1280]{2,1,0:T(8,128)(2,1)} %get-tuple-element.254), channel_id=1, source_target_pairs={{0,8},{4,12},{8,0},{12,4},{16,24},{20,28},{24,16},{28,20},{1,9},{5... | collective-permute-start | bytes 983048 | tf_op jit(solution)/shard_map/ppermute | solution.py:325
  998.5 21.6 %collective-permute-start.48 = (bf16[1,128,1280]{2,1,0:T(8,128)(2,1)S(1)}, bf16[1,128,1280]{2,1,0:T(8,128)(2,1)S(1)}, u32[]{:S(2)}, u32[]{:S(2)}) collective-permute-start(bf16[1,128,1280]{2,1,0:T(8,128)(2,1)S(1)} %get-tuple-element.255), channel_id=1, source_target_pairs={{0,16},{4,20},{8,24},{12,28},{16,0},{20,4},{24,8},{28,12},{1,17},{... | collective-permute-start | bytes 983048 | tf_op jit(solution)/shard_map/ppermute | solution.py:325
  1005.6 4.3 collective-permute-start.46
  1009.9 5.9 collective-permute-start.47
  1016.6 13.2 %all-to-all-start.3 = ((f32[8,5,2048]{2,1,0:T(8,128)}), f32[8,5,2048]{2,1,0:T(8,128)S(1)}, u32[]{:S(2)}, u32[]{:S(2)}) async-start(f32[8,5,2048]{2,1,0:T(8,128)} %broadcast_in_dim.95), calls=%async_computation.8 | async-start | bytes 1048576 | tf_op jit(solution)/shard_map/all_to_all | solution.py:663
  (83 other events, 1604.6 us)
Sparse Core Ops, SparseCore 0:
  121.0 81.5 all-gather.5
  205.0 98.7 all-gather.7
  306.2 99.4 all-gather.9
  407.5 80.9 all-gather.11
  491.9 137.9 reduce-scatter.6
  632.1 47.8 reduce-scatter.8
  692.0 39.4 reduce-scatter.10
  742.8 80.6 all-gather.13
  825.8 37.9 reduce-scatter.14
  865.9 47.1 reduce-scatter.12
  938.6 63.6 reduce-scatter.16
